TPU v7x, 32 devices: a whole 2x2x4 slice. The times are simulated.
32 devices in a mesh: gz: 4 (over y, x), gx: 8 (over z, core).
Axes of the slice: x: 2, y: 2, z: 4, core: 2. Of those that a mesh axis runs over, the one named last changes fastest.
Arguments:
- populations: float32 [27, 8, 64, 128], P(None, 'gz', 'gx'), may hold values from 0 to 1, as said below
- rates: float32 [27], replicated, may hold values from 0.5 to 1.8
- grain_fraction: bfloat16 [16384, 128], P(('gz', 'gx')), may hold values from 0 to 0.3984375
- grain_velocity: bfloat16 [3, 16384], P(None, ('gz', 'gx')), may hold values from -0.29882812 to 0.29882812
- grain_dest: int32 [16384, 1], P(('gz', 'gx')), may hold values from 0 to 31; in each aligned block of 512 rows (0 to 511, 512 to 1023, ...) at most 32 rows name the same one
- grain_line: int32 [16384], P(('gz', 'gx')), may hold values from 0 to 15
Outputs:
- scaled: float32 [27, 8, 64, 128], P(None, 'gz', 'gx')
- grain_force: float32 [3, 16384], P(None, ('gz', 'gx'))
Inputs may be any that keep to these rules, and one draw needn't show every extreme that they name: populations are positive. grain_dest is a linear index of gz+gx, gz slowest; among the rows of one device at most 32 name the same device, and exactly 32 do in some device's rows.
All inputs are finite; a program needn't handle non-finite values.
Results may differ from a plain program's by a relative error of at most 0.0003.
Values may be sent and summed in bfloat16 or wider, within the bound.
No kernel may reach another device: no remote copies, remote signals or barrier semaphores. Data moves between devices by JAX's collectives and lax.ppermute only.
A program may use at most 64 MiB of HBM per device.

v0:
```python
import jax
import jax.numpy as jnp
import numpy as np
from jax import lax
from jax.sharding import PartitionSpec as P

STEPS = 2


highest = lax.Precision.HIGHEST


def extended_2(shard, sides, width):
    for axis, dim in sides:
        peers, length = (lax.axis_size(axis), shard.shape[dim])
        up = [(i, (i + 1) % peers) for i in range(peers)]
        down = [(j, i) for i, j in up]
        last = lax.slice_in_dim(shard, length - width, length, axis=dim)
        first = lax.slice_in_dim(shard, 0, width, axis=dim)
        before = lax.ppermute(last, axis, up)
        after = lax.ppermute(first, axis, down)
        shard = jnp.concatenate([before, shard, after], axis=dim)
    return shard


def lattice_tables():
    labels = np.arange(27)
    digits = [labels // 9, labels // 3 % 3, labels % 3]
    velocity = np.stack([digit - 1 for digit in digits]).astype(np.float32)
    count = np.abs(digits[0] - 1) + np.abs(digits[1] - 1) + np.abs(digits[2] - 1)
    weights = np.array([8.0 / 27, 2.0 / 27, 1.0 / 54, 1.0 / 216], dtype=np.float32)[count]
    vander = np.array([[1.0, 1.0, 1.0], [-1.0, 0.0, 1.0], [1.0, 0.0, 1.0]], dtype=np.float32)
    vander_inv = np.array([[0.0, -0.5, 0.5], [1.0, 0.0, -1.0], [0.0, 0.5, 0.5]], dtype=np.float32)
    moments = np.ones((27, 27), dtype=np.float32)
    inverse = np.ones((27, 27), dtype=np.float32)
    for digit in digits:
        moments = moments * vander[digit[:, None], digit[None, :]]
        inverse = inverse * vander_inv[digit[:, None], digit[None, :]]
    return (velocity, weights, moments, inverse)


def equilibrium(density, speed, velocity, weights):
    along = jnp.dot(velocity.T, speed, precision=highest)
    square = jnp.sum(speed * speed, axis=0)
    return (
        weights[:, None]
        * density[None, :]
        * (1.0 + 3.0 * along + 4.5 * along * along - 1.5 * square[None, :])
    )


def collide(fields, rates, solid, carried):
    velocity_np, weights_np, moments_np, inverse_np = lattice_tables()
    velocity = jnp.asarray(velocity_np)
    weights = jnp.asarray(weights_np)
    density = jnp.sum(fields, axis=0)
    momentum = jnp.dot(velocity, fields, precision=highest)
    speed = momentum / density[None, :]
    equil = equilibrium(density, speed, velocity, weights)
    departure = fields - equil
    projected = jnp.dot(jnp.asarray(moments_np), departure, precision=highest)
    fluid = -jnp.dot(jnp.asarray(inverse_np), rates[:, None] * projected, precision=highest)
    cover = 1.0 + solid
    share = solid / cover
    solid_equil = equilibrium(density, carried / cover[None, :], velocity, weights)
    exchange_term = departure[::-1] - (fields - solid_equil)
    post = fields + (1.0 - share)[None, :] * fluid + share[None, :] * exchange_term
    push = jnp.dot(velocity, exchange_term, precision=highest) / cover[None, :]
    return (post, push)


def stream_local(block, extended, level, top):
    depth, length = (block.shape[1], block.shape[2])
    moved_list = []
    for population in range(27):
        step_z = population // 9 - 1
        step_x = population // 3 % 3 - 1
        step_y = population % 3 - 1
        moved = extended[
            population, 1 - step_z : 1 - step_z + depth, 1 - step_x : 1 - step_x + length
        ]
        moved = jnp.roll(moved, step_y, axis=2)
        if step_z == 1:
            moved = jnp.where((level == 0)[:, None, None], block[26 - population], moved)
        if step_z == -1:
            moved = jnp.where((level == top)[:, None, None], block[26 - population], moved)
        moved_list.append(moved)
    return jnp.stack(moved_list)


def per_device(populations, rates, grain_fraction, grain_velocity, grain_dest, grain_line):
    depth, length, width = (populations.shape[1], populations.shape[2], populations.shape[3])
    lines = depth * length
    cells = lines * width
    devices = lax.axis_size("gz") * lax.axis_size("gx")
    grains = grain_fraction.shape[0]
    capacity = 2 * grains // devices
    slots = devices * capacity
    target = grain_dest[:, 0]
    chosen = (target[:, None] == jnp.arange(devices, dtype=jnp.int32)[None, :]).astype(jnp.int32)
    before = jnp.cumsum(chosen, axis=0) - chosen
    rank = jnp.sum(before * chosen, axis=1)
    position = target * capacity + rank
    send_fraction = (
        jnp.zeros((slots, width), jnp.bfloat16)
        .at[position]
        .set(grain_fraction)
        .reshape(devices, capacity, width)
    )
    send_speed = (
        jnp.zeros((devices, 3, capacity), jnp.bfloat16).at[target, :, rank].set(grain_velocity.T)
    )
    send_line = (
        jnp.full((slots,), -1, jnp.int32).at[position].set(grain_line).reshape(devices, capacity)
    )
    recv_fraction, recv_speed = (
        lax.all_to_all(send_fraction, ("gz", "gx"), split_axis=0, concat_axis=0, tiled=True),
        lax.all_to_all(send_speed, ("gz", "gx"), split_axis=0, concat_axis=0, tiled=True),
    )
    recv_line = lax.all_to_all(
        send_line, ("gz", "gx"), split_axis=0, concat_axis=0, tiled=True
    ).reshape(slots)
    fraction = recv_fraction.reshape(slots, width)
    speed = jnp.moveaxis(recv_speed, 1, 0).reshape(3, slots).astype(jnp.float32)
    matches = jnp.arange(lines, dtype=jnp.int32)[:, None] == recv_line[None, :]
    solid = jnp.dot(matches.astype(jnp.bfloat16), fraction, preferred_element_type=jnp.float32)
    weighted = fraction.astype(jnp.float32)[None, :, :] * speed[:, :, None]
    carried = jnp.einsum("ls,ksy->kly", matches.astype(jnp.float32), weighted, precision=highest)
    solid_flat = solid.reshape(cells)
    carried_flat = carried.reshape(3, cells)
    fields = populations.reshape(27, cells)
    push_total = jnp.zeros((3, cells), jnp.float32)
    level = lax.axis_index("gz") * depth + jnp.arange(depth, dtype=jnp.int32)
    top = lax.axis_size("gz") * depth - 1
    for turn_index in range(STEPS):
        post, push = collide(fields, rates, solid_flat, carried_flat)
        push_total = push_total + push
        block = post.reshape(27, depth, length, width)
        extended = extended_2(block, (("gz", 1), ("gx", 2)), 1)
        fields = stream_local(block, extended, level, top).reshape(27, cells)
    weights = jnp.asarray(lattice_tables()[1])
    scaled = fields.reshape(27, depth, length, width) / weights[:, None, None, None]
    push_lines = push_total.reshape(3, lines, width)
    safe_line = jnp.where(recv_line >= 0, recv_line, 0).reshape(devices, capacity)
    picked = push_lines[:, safe_line, :]
    slot_force = -jnp.einsum(
        "kjcy,jcy->jkc",
        picked,
        fraction.reshape(devices, capacity, width).astype(jnp.float32),
        precision=highest,
    )
    returned = lax.all_to_all(slot_force, ("gz", "gx"), split_axis=0, concat_axis=0, tiled=True)
    grain_force = returned[target, :, rank].T
    return (scaled, grain_force)


def solution(mesh):
    in_specs = (
        P(None, "gz", "gx", None),
        P(),
        P(("gz", "gx"), None),
        P(None, ("gz", "gx")),
        P(("gz", "gx"), None),
        P(("gz", "gx")),
    )
    out_specs = (P(None, "gz", "gx", None), P(None, ("gz", "gx")))
    return jax.shard_map(
        per_device, mesh=mesh, in_specs=in_specs, out_specs=out_specs, check_vma=False
    )
```

profile of v0, /device:TPU:0, one launch (start us, length us, event | category | flops | bytes accessed | tf_op | source)
XLA Modules:
  0.0 131.5 jit_solution(6016120446037944495)
XLA Ops:
  1.4 1.2 reduce-window.6
  2.8 0.8 fusion.32
  4.3 2.6 %scatter_custom_fusion = s32[1024]{0:T(1024)S(1)} fusion(s32[512]{0:T(512)S(1)} %bitcast.562, s32[512]{0:T(512)} %param.20, s32[]{:T(128)} %constant.22.clone.1), kind=kCustom, calls=%fused_computation.312 | custom fusion | bytes 4608 | tf_op jit(solution)/shard_map/scatter | solution.py:114
  7.6 7.3 %all-to-all-start = ((s32[32,1,32]{2,1,0:T(1,128)}), s32[32,1,32]{2,1,0:T(1,128)S(1)}, u32[]{:S(2)}, u32[]{:S(2)}) async-start(s32[32,1,32]{2,1,0:T(1,128)} %all_to_all.17), calls=%async_computation | async-start | bytes 32768 | tf_op jit(solution)/shard_map/all_to_all | solution.py:120
  14.9 1.0 reduce_sum.189
  15.9 1.0 pad.153
  16.9 0.9 multiply_reduce_fusion.1
  17.9 1.2 fusion.16
  19.7 24.7 %scatter_fusion = bf16[32,3,32]{1,2,0:T(8,128)(2,1)S(1)} fusion(bf16[32,3,32]{1,2,0:T(8,128)(2,1)S(1)} %broadcast_in_dim.211, s32[512]{0:T(512)S(1)} %bitcast.429, bf16[512,3]{1,0:T(8,128)(2,1)S(1)} %copy.135), kind=kCustom, calls=%fused_computation.4 | custom fusion | bytes 13312 | tf_op jit(solution)/shard_map/scatter | solution.py:111
  44.4 0.9 copy.136
  45.3 5.9 %all-to-all-start.2 = ((bf16[32,3,32]{2,1,0:T(4,128)(2,1)}), bf16[32,3,32]{2,1,0:T(4,128)(2,1)S(1)}, u32[]{:S(2)}, u32[]{:S(2)}) async-start(bf16[32,3,32]{2,1,0:T(4,128)(2,1)} %copy.136), calls=%async_computation.2 | async-start | bytes 65536 | tf_op jit(solution)/shard_map/all_to_all | solution.py:118
  51.8 2.8 %scatter_custom_fusion.1 = bf16[1024,128]{1,0:T(8,128)(2,1)} fusion(s32[512]{0:T(512)S(1)} %bitcast.563, bf16[512,128]{1,0:T(8,128)(2,1)} %param.17, bf16[]{:T(256)} %constant.9.clone.1), kind=kCustom, calls=%fused_computation.49 | custom fusion | bytes 262656 | tf_op jit(solution)/shard_map/scatter | solution.py:107
  54.6 3.7 %all-to-all-done.2 = bf16[32,3,32]{2,1,0:T(4,128)(2,1)S(1)} async-done(((bf16[32,3,32]{2,1,0:T(4,128)(2,1)}), bf16[32,3,32]{2,1,0:T(4,128)(2,1)S(1)}, u32[]{:S(2)}, u32[]{:S(2)}) %all-to-all-start.2) | async-done | bytes 6176 | tf_op jit(solution)/shard_map/all_to_all | solution.py:118
  58.4 2.6 %all-to-all-start.1 = ((bf16[32,32,128]{2,1,0:T(8,128)(2,1)}), bf16[32,32,128]{2,1,0:T(8,128)(2,1)S(1)}, u32[]{:S(2)}, u32[]{:S(2)}) async-start(bf16[32,32,128]{2,1,0:T(8,128)(2,1)} %bitcast.5), calls=%async_computation.1 | async-start | bytes 524288 | tf_op jit(solution)/shard_map/all_to_all | solution.py:117
  63.0 8.3 %all-to-all-done.1 = bf16[32,32,128]{2,1,0:T(8,128)(2,1)S(1)} async-done(((bf16[32,32,128]{2,1,0:T(8,128)(2,1)}), bf16[32,32,128]{2,1,0:T(8,128)(2,1)S(1)}, u32[]{:S(2)}, u32[]{:S(2)}) %all-to-all-start.1) | async-done | bytes 262176 | tf_op jit(solution)/shard_map/all_to_all | solution.py:117
  71.6 0.8 fusion.47
  74.3 2.5 %collective-permute-start.1 = (f32[27,1,8,128]{3,2,1,0:T(8,128)S(1)}, f32[27,1,8,128]{3,2,1,0:T(8,128)S(1)}, u32[]{:S(2)}, u32[]{:S(2)}) collective-permute-start(f32[27,1,8,128]{3,2,1,0:T(8,128)S(1)} %get-tuple-element.133), channel_id=1, source_target_pairs={{8,0},{16,8},{24,16},{0,24},{9,1},{17,9},{25,17},{1,25},{10,2},{18... | collective-permute-start | bytes 331784 | tf_op jit(solution)/shard_map/ppermute | solution.py:21
  76.8 3.4 %collective-permute-done = f32[27,1,8,128]{3,2,1,0:T(8,128)S(1)} collective-permute-done((f32[27,1,8,128]{3,2,1,0:T(8,128)S(1)}, f32[27,1,8,128]{3,2,1,0:T(8,128)S(1)}, u32[]{:S(2)}, u32[]{:S(2)}) %collective-permute-start) | collective-permute-done | bytes 110624 | tf_op jit(solution)/shard_map/ppermute | solution.py:20
  80.3 1.2 collective-permute-done.1
  82.2 3.5 %collective-permute-start.2 = (f32[27,4,1,128]{3,2,1,0:T(1,128)S(1)}, f32[27,4,1,128]{3,2,1,0:T(1,128)S(1)}, u32[]{:S(2)}, u32[]{:S(2)}) collective-permute-start(f32[27,4,1,128]{3,2,1,0:T(1,128)S(1)} %get-tuple-element.62), channel_id=1, source_target_pairs={{1,0},{2,1},{3,2},{4,3},{5,4},{6,5},{7,6},{0,7},{9,8},{10,9},{11,1... | collective-permute-start | bytes 165896 | tf_op jit(solution)/shard_map/ppermute | solution.py:21
  86.0 1.5 %collective-permute-done.3 = f32[27,4,1,128]{3,2,1,0:T(1,128)S(1)} collective-permute-done((f32[27,4,1,128]{3,2,1,0:T(1,128)S(1)}, f32[27,4,1,128]{3,2,1,0:T(1,128)S(1)}, u32[]{:S(2)}, u32[]{:S(2)}) %collective-permute-start.3) | collective-permute-done | bytes 55328 | tf_op jit(solution)/shard_map/ppermute | solution.py:20
  94.0 0.9 collective-permute-start.4
  94.9 4.0 %gather_fusion = f32[1024,3,128]{2,1,0:T(4,128)S(1)} fusion(f32[3,16,128]{2,0,1:T(4,128)S(1)} %fusion.11, s32[1024]{0:T(1024)} %broadcast_clamp_fusion), kind=kCustom, calls=%fused_computation | custom fusion | bytes 3149824 | tf_op jit(solution)/shard_map/gather | solution.py:145
  98.9 3.6 %fusion.14 = f32[32,32,1,3]{3,2,1,0:T(1,128)S(1)} fusion(f32[3,32,32,128]{3,0,2,1:T(4,128)S(1)} %bitcast.442, bf16[32,32,128,1]{2,1,0,3:T(8,128)(2,1)S(1)} %bitcast.435), kind=kOutput, calls=%fused_computation.26 | convolution fusion | flops 4718592 | bytes 1847296 | tf_op jit(solution)/shard_map/kjcy,jcy->jkc/dot_general | solution.py:146
  103.6 4.8 %all-to-all-start.3 = ((f32[32,3,32]{2,1,0:T(4,128)}), f32[32,3,32]{2,1,0:T(4,128)S(1)}, u32[]{:S(2)}, u32[]{:S(2)}) async-start(f32[32,3,32]{2,1,0:T(4,128)} %fusion.33), calls=%async_computation.3 | async-start | bytes 131072 | tf_op jit(solution)/shard_map/all_to_all | solution.py:152
  108.6 2.7 %collective-permute-start.5 = (f32[27,1,8,128]{3,2,1,0:T(8,128)S(1)}, f32[27,1,8,128]{3,2,1,0:T(8,128)S(1)}, u32[]{:S(2)}, u32[]{:S(2)}) collective-permute-start(f32[27,1,8,128]{3,2,1,0:T(8,128)S(1)} %get-tuple-element.131), channel_id=1, source_target_pairs={{8,0},{16,8},{24,16},{0,24},{9,1},{17,9},{25,17},{1,25},{10,2},{18... | collective-permute-start | bytes 331784 | tf_op jit(solution)/shard_map/ppermute | solution.py:21
  111.3 4.5 %all-to-all-done.3 = f32[32,3,32]{2,1,0:T(4,128)S(1)} async-done(((f32[32,3,32]{2,1,0:T(4,128)}), f32[32,3,32]{2,1,0:T(4,128)S(1)}, u32[]{:S(2)}, u32[]{:S(2)}) %all-to-all-start.3) | async-done | bytes 12320 | tf_op jit(solution)/shard_map/all_to_all | solution.py:152
  116.1 3.7 %gather_fusion.1 = f32[512,3]{1,0:T(8,128)S(1)} fusion(f32[32,3,32]{1,2,0:T(8,128)S(1)} %copy.163, s32[512]{0:T(512)S(1)} %bitcast.428), kind=kCustom, calls=%fused_computation.1 | custom fusion | bytes 16384 | tf_op jit(solution)/shard_map/gather | solution.py:153
  120.6 0.9 constant_dynamic-update-slice_fusion.13
  122.5 1.7 %collective-permute-done.6 = f32[27,4,1,128]{3,2,1,0:T(1,128)S(1)} collective-permute-done((f32[27,4,1,128]{3,2,1,0:T(1,128)S(1)}, f32[27,4,1,128]{3,2,1,0:T(1,128)S(1)}, u32[]{:S(2)}, u32[]{:S(2)}) %collective-permute-start.6) | collective-permute-done | bytes 55328 | tf_op jit(solution)/shard_map/ppermute | solution.py:21
  124.4 3.5 %collective-permute-done.7 = f32[27,4,1,128]{3,2,1,0:T(1,128)S(1)} collective-permute-done((f32[27,4,1,128]{3,2,1,0:T(1,128)S(1)}, f32[27,4,1,128]{3,2,1,0:T(1,128)S(1)}, u32[]{:S(2)}, u32[]{:S(2)}) %collective-permute-start.7) | collective-permute-done | bytes 55328 | tf_op jit(solution)/shard_map/ppermute | solution.py:20
  130.7 0.8 broadcast_multiply_fusion
  (275 shorter events, 21.0 us)
Async XLA Ops:
  0.6 18.4 %copy-start.3 = (f32[27,27]{1,0:T(8,128)S(1)}, f32[27,27]{1,0:T(8,128)}, u32[]{:S(2)}) copy-start(f32[27,27]{1,0:T(8,128)} %constant.17.clone) | copy-start | bytes 8752
  0.6 18.4 %copy-start.28 = (f32[27]{0:T(128)S(1)}, f32[27]{0:T(128)}, u32[]{:S(2)}) copy-start(f32[27]{0:T(128)} %param.16) | copy-start | bytes 328
  0.7 18.8 %copy-start.27 = (bf16[3,512]{1,0:T(4,128)(2,1)S(1)}, bf16[3,512]{1,0:T(4,128)(2,1)}, u32[]{:S(2)}) copy-start(bf16[3,512]{1,0:T(4,128)(2,1)} %param.18) | copy-start | bytes 9220
  7.6 37.7 %all-to-all-start = ((s32[32,1,32]{2,1,0:T(1,128)}), s32[32,1,32]{2,1,0:T(1,128)S(1)}, u32[]{:S(2)}, u32[]{:S(2)}) async-start(s32[32,1,32]{2,1,0:T(1,128)} %all_to_all.17), calls=%async_computation | async-start | bytes 32768 | tf_op jit(solution)/shard_map/all_to_all | solution.py:120
  19.7 52.7 %copy-start.25 = (f32[3,27]{1,0:T(4,128)S(1)}, f32[3,27]{1,0:T(4,128)}, u32[]{:S(2)}) copy-start(f32[3,27]{1,0:T(4,128)} %constant.15.clone) | copy-start | bytes 976
  45.3 13.1 %all-to-all-start.2 = ((bf16[32,3,32]{2,1,0:T(4,128)(2,1)}), bf16[32,3,32]{2,1,0:T(4,128)(2,1)S(1)}, u32[]{:S(2)}, u32[]{:S(2)}) async-start(bf16[32,3,32]{2,1,0:T(4,128)(2,1)} %copy.136), calls=%async_computation.2 | async-start | bytes 65536 | tf_op jit(solution)/shard_map/all_to_all | solution.py:118
  51.1 38.3 %copy-start.4 = (pred[2]{0:T(512)(128)(4,1)}, pred[2]{0:T(512)(128)(4,1)S(1)}, u32[]{:S(2)}) copy-start(pred[2]{0:T(512)(128)(4,1)S(1)} %get-tuple-element.152) | copy-start | bytes 10
  51.2 38.3 %copy-start.6 = (pred[2]{0:T(512)(128)(4,1)}, pred[2]{0:T(512)(128)(4,1)S(1)}, u32[]{:S(2)}) copy-start(pred[2]{0:T(512)(128)(4,1)S(1)} %get-tuple-element.153) | copy-start | bytes 10
  51.2 21.7 %copy-start.2 = (f32[27,27]{1,0:T(8,128)S(1)}, f32[27,27]{1,0:T(8,128)}, u32[]{:S(2)}) copy-start(f32[27,27]{1,0:T(8,128)} %constant.52.clone) | copy-start | bytes 8752
  51.2 21.7 %copy-start.26 = (f32[27]{0:T(128)S(1)}, f32[27]{0:T(128)}, u32[]{:S(2)}) copy-start(f32[27]{0:T(128)} %constant.16.clone) | copy-start | bytes 328
  58.4 13.0 %all-to-all-start.1 = ((bf16[32,32,128]{2,1,0:T(8,128)(2,1)}), bf16[32,32,128]{2,1,0:T(8,128)(2,1)S(1)}, u32[]{:S(2)}, u32[]{:S(2)}) async-start(bf16[32,32,128]{2,1,0:T(8,128)(2,1)} %bitcast.5), calls=%async_computation.1 | async-start | bytes 524288 | tf_op jit(solution)/shard_map/all_to_all | solution.py:117
  73.4 6.8 %collective-permute-start = (f32[27,1,8,128]{3,2,1,0:T(8,128)S(1)}, f32[27,1,8,128]{3,2,1,0:T(8,128)S(1)}, u32[]{:S(2)}, u32[]{:S(2)}) collective-permute-start(f32[27,1,8,128]{3,2,1,0:T(8,128)S(1)} %get-tuple-element.134), channel_id=1, source_target_pairs={{0,8},{8,16},{16,24},{24,0},{1,9},{9,17},{17,25},{25,1},{2,10},{10... | collective-permute-start | bytes 331784 | tf_op jit(solution)/shard_map/ppermute | solution.py:20
  74.3 7.1 %collective-permute-start.1 = (f32[27,1,8,128]{3,2,1,0:T(8,128)S(1)}, f32[27,1,8,128]{3,2,1,0:T(8,128)S(1)}, u32[]{:S(2)}, u32[]{:S(2)}) collective-permute-start(f32[27,1,8,128]{3,2,1,0:T(8,128)S(1)} %get-tuple-element.133), channel_id=1, source_target_pairs={{8,0},{16,8},{24,16},{0,24},{9,1},{17,9},{25,17},{1,25},{10,2},{18... | collective-permute-start | bytes 331784 | tf_op jit(solution)/shard_map/ppermute | solution.py:21
  82.1 5.4 %collective-permute-start.3 = (f32[27,4,1,128]{3,2,1,0:T(1,128)S(1)}, f32[27,4,1,128]{3,2,1,0:T(1,128)S(1)}, u32[]{:S(2)}, u32[]{:S(2)}) collective-permute-start(f32[27,4,1,128]{3,2,1,0:T(1,128)S(1)} %get-tuple-element.61), channel_id=1, source_target_pairs={{0,1},{1,2},{2,3},{3,4},{4,5},{5,6},{6,7},{7,0},{8,9},{9,10},{10,1... | collective-permute-start | bytes 165896 | tf_op jit(solution)/shard_map/ppermute | solution.py:20
  82.2 5.7 %collective-permute-start.2 = (f32[27,4,1,128]{3,2,1,0:T(1,128)S(1)}, f32[27,4,1,128]{3,2,1,0:T(1,128)S(1)}, u32[]{:S(2)}, u32[]{:S(2)}) collective-permute-start(f32[27,4,1,128]{3,2,1,0:T(1,128)S(1)} %get-tuple-element.62), channel_id=1, source_target_pairs={{1,0},{2,1},{3,2},{4,3},{5,4},{6,5},{7,6},{0,7},{9,8},{10,9},{11,1... | collective-permute-start | bytes 165896 | tf_op jit(solution)/shard_map/ppermute | solution.py:21
  94.0 26.6 %collective-permute-start.4 = (f32[27,1,8,128]{3,2,1,0:T(8,128)}, f32[27,1,8,128]{3,2,1,0:T(8,128)}, u32[]{:S(2)}, u32[]{:S(2)}) collective-permute-start(f32[27,1,8,128]{3,2,1,0:T(8,128)} %get-tuple-element.132), channel_id=1, source_target_pairs={{0,8},{8,16},{16,24},{24,0},{1,9},{9,17},{17,25},{25,1},{2,10},{10... | collective-permute-start | bytes 331784 | tf_op jit(solution)/shard_map/ppermute | solution.py:20
  98.9 9.6 %copy-start = (f32[1,2048]{1,0:T(1,128)S(1)}, f32[1,2048]{1,0:T(1,128)}, u32[]{:S(2)}) copy-start(f32[1,2048]{1,0:T(1,128)} %get-tuple-element.92) | copy-start | bytes 24580
  98.9 9.6 %copy-start.1 = (f32[1,2048]{1,0:T(1,128)S(1)}, f32[1,2048]{1,0:T(1,128)}, u32[]{:S(2)}) copy-start(f32[1,2048]{1,0:T(1,128)} %get-tuple-element.94) | copy-start | bytes 24580
  103.6 12.2 %all-to-all-start.3 = ((f32[32,3,32]{2,1,0:T(4,128)}), f32[32,3,32]{2,1,0:T(4,128)S(1)}, u32[]{:S(2)}, u32[]{:S(2)}) async-start(f32[32,3,32]{2,1,0:T(4,128)} %fusion.33), calls=%async_computation.3 | async-start | bytes 131072 | tf_op jit(solution)/shard_map/all_to_all | solution.py:152
  108.6 13.0 %collective-permute-start.5 = (f32[27,1,8,128]{3,2,1,0:T(8,128)S(1)}, f32[27,1,8,128]{3,2,1,0:T(8,128)S(1)}, u32[]{:S(2)}, u32[]{:S(2)}) collective-permute-start(f32[27,1,8,128]{3,2,1,0:T(8,128)S(1)} %get-tuple-element.131), channel_id=1, source_target_pairs={{8,0},{16,8},{24,16},{0,24},{9,1},{17,9},{25,17},{1,25},{10,2},{18... | collective-permute-start | bytes 331784 | tf_op jit(solution)/shard_map/ppermute | solution.py:21
  119.8 8.3 %copy-start.23 = (f32[1,2048]{1,0:T(1,128)S(1)}, f32[1,2048]{1,0:T(1,128)}, u32[]{:S(2)}) copy-start(f32[1,2048]{1,0:T(1,128)} %get-tuple-element.100) | copy-start | bytes 24580
  119.8 8.4 %copy-start.22 = (f32[1,2048]{1,0:T(1,128)S(1)}, f32[1,2048]{1,0:T(1,128)}, u32[]{:S(2)}) copy-start(f32[1,2048]{1,0:T(1,128)} %get-tuple-element.99) | copy-start | bytes 24580
  119.8 8.6 %copy-start.21 = (f32[1,2048]{1,0:T(1,128)S(1)}, f32[1,2048]{1,0:T(1,128)}, u32[]{:S(2)}) copy-start(f32[1,2048]{1,0:T(1,128)} %get-tuple-element.98) | copy-start | bytes 24580
  119.8 8.7 %copy-start.20 = (f32[1,2048]{1,0:T(1,128)S(1)}, f32[1,2048]{1,0:T(1,128)}, u32[]{:S(2)}) copy-start(f32[1,2048]{1,0:T(1,128)} %get-tuple-element.97) | copy-start | bytes 24580
  119.8 8.7 %copy-start.10 = (f32[1,2048]{1,0:T(1,128)S(1)}, f32[1,2048]{1,0:T(1,128)}, u32[]{:S(2)}) copy-start(f32[1,2048]{1,0:T(1,128)} %get-tuple-element.96) | copy-start | bytes 24580
  119.8 9.0 %copy-start.19 = (f32[1,2048]{1,0:T(1,128)S(1)}, f32[1,2048]{1,0:T(1,128)}, u32[]{:S(2)}) copy-start(f32[1,2048]{1,0:T(1,128)} %get-tuple-element.95) | copy-start | bytes 24580
  121.5 8.3 %copy-start.5 = (pred[2]{0:T(512)(128)(4,1)S(1)}, pred[2]{0:T(512)(128)(4,1)}, u32[]{:S(2)}) copy-start(pred[2]{0:T(512)(128)(4,1)} %copy-done.4) | copy-start | bytes 10
  121.6 8.4 %copy-start.9 = (f32[1,2048]{1,0:T(1,128)S(1)}, f32[1,2048]{1,0:T(1,128)}, u32[]{:S(2)}) copy-start(f32[1,2048]{1,0:T(1,128)} %get-tuple-element.90) | copy-start | bytes 24580
  121.8 8.4 %copy-start.16 = (f32[1,2048]{1,0:T(1,128)S(1)}, f32[1,2048]{1,0:T(1,128)}, u32[]{:S(2)}) copy-start(f32[1,2048]{1,0:T(1,128)} %get-tuple-element.88) | copy-start | bytes 24580
  121.8 8.4 %copy-start.15 = (f32[1,2048]{1,0:T(1,128)S(1)}, f32[1,2048]{1,0:T(1,128)}, u32[]{:S(2)}) copy-start(f32[1,2048]{1,0:T(1,128)} %get-tuple-element.87) | copy-start | bytes 24580
  121.8 2.4 %collective-permute-start.6 = (f32[27,4,1,128]{3,2,1,0:T(1,128)S(1)}, f32[27,4,1,128]{3,2,1,0:T(1,128)S(1)}, u32[]{:S(2)}, u32[]{:S(2)}) collective-permute-start(f32[27,4,1,128]{3,2,1,0:T(1,128)S(1)} %get-tuple-element.60), channel_id=1, source_target_pairs={{1,0},{2,1},{3,2},{4,3},{5,4},{6,5},{7,6},{0,7},{9,8},{10,9},{11,1... | collective-permute-start | bytes 165896 | tf_op jit(solution)/shard_map/ppermute | solution.py:21
  122.5 5.4 %collective-permute-start.7 = (f32[27,4,1,128]{3,2,1,0:T(1,128)S(1)}, f32[27,4,1,128]{3,2,1,0:T(1,128)S(1)}, u32[]{:S(2)}, u32[]{:S(2)}) collective-permute-start(f32[27,4,1,128]{3,2,1,0:T(1,128)S(1)} %get-tuple-element.59), channel_id=1, source_target_pairs={{0,1},{1,2},{2,3},{3,4},{4,5},{5,6},{6,7},{7,0},{8,9},{9,10},{10,1... | collective-permute-start | bytes 165896 | tf_op jit(solution)/shard_map/ppermute | solution.py:20
  (34 other events, 265.9 us)
where the time goes:
time: 132 us
  local copies, waits for them, and re-layouts  50.1 us (38%)
  starting transfers between devices  31.3 us (24%)
  waiting for transfers between devices  27.9 us (21%)
  other arithmetic  10.5 us (8%)
  matrix products  9.93 us (8%)
  between operations  1.8 us (1%)
    scatter x2, local copies, waits for them, and re-layouts, per_device(): jnp.zeros((devices, 3, capacity), jnp.bfloat16).at[target, :, rank]  25.6 us
    ppermute x4, starting transfers between devices, extended_2(): after = lax.ppermute(first, axis, down)  9.23 us
    ppermute x4, waiting for transfers between devices, extended_2(): before = lax.ppermute(last, axis, up)  8.45 us
    all_to_all x1, waiting for transfers between devices, per_device(): lax.all_to_all(send_fraction, ('gz', 'gx'), split_axis=0, concat_axis=0,...  8.3 us
    all_to_all x1, starting transfers between devices, per_device(): lax.all_to_all(send_line, ('gz', 'gx'), split_axis=0, concat_axis=0, tile...  7.3 us
    all_to_all x1, starting transfers between devices, per_device(): lax.all_to_all(send_speed, ('gz', 'gx'), split_axis=0, concat_axis=0, til...  5.85 us
    all_to_all x1, starting transfers between devices, per_device(): lax.all_to_all(slot_force, ('gz', 'gx'), split_axis=0, concat_axis=0, til...  4.82 us
    all_to_all x1, waiting for transfers between devices, per_device(): lax.all_to_all(slot_force, ('gz', 'gx'), split_axis=0, concat_axis=0, til...  4.53 us
  transfers between devices with their start and end apart: 12, of which 8 were waited for; matrix products, arithmetic and copies ran while one was open for 39% of the time, Pallas kernels for 0%

commit v1 on v0

v1 whole, which is shorter than its diff:
```python
import functools

import jax
import jax.numpy as jnp
import numpy as np
from jax import lax
from jax.experimental import pallas as pl
from jax.experimental.pallas import tpu as pltpu
from jax.sharding import PartitionSpec as P

STEPS = 2
LANES = 128
f32, bf16, i32 = jnp.float32, jnp.bfloat16, jnp.int32
DIGITS = [(i // 9, i // 3 % 3, i % 3) for i in range(27)]
STEP = [tuple(d - 1 for d in digits) for digits in DIGITS]
WEIGHT = [(8.0 / 27, 2.0 / 27, 1.0 / 54, 1.0 / 216)[sum(abs(s) for s in step)] for step in STEP]


def iota(shape, dim):
    return lax.broadcasted_iota(i32, shape, dim)


def call(kernel, outs, *operands, scalars=0, flops=0):
    smem, vmem = pl.BlockSpec(memory_space=pltpu.SMEM), pl.BlockSpec(memory_space=pltpu.VMEM)
    size = sum(o.size * o.dtype.itemsize for o in operands) + sum(
        int(np.prod(o.shape)) * o.dtype.itemsize for o in outs
    )
    return pl.pallas_call(
        kernel,
        out_shape=list(outs),
        in_specs=[smem] * scalars + [vmem] * (len(operands) - scalars),
        out_specs=[vmem] * len(outs),
        compiler_params=pltpu.CompilerParams(vmem_limit_bytes=24 * 1024 * 1024),
        cost_estimate=pl.CostEstimate(flops=flops, bytes_accessed=size, transcendentals=0),
    )(*operands)


def split3(x):
    high = x.astype(bf16)
    rest = x - high.astype(f32)
    mid = rest.astype(bf16)
    return high, mid, (rest - mid.astype(f32)).astype(bf16)


def pack_kernel(devices, capacity, dest_ref, line_ref, speed_ref, fraction_ref, send_ref, rank_ref):
    grains, width = fraction_ref.shape
    slots = devices * capacity
    dest = dest_ref[...]
    hot = jnp.where(iota((devices, grains), 0) == dest, 1.0, 0.0)
    earlier = jnp.where(iota((LANES, LANES), 0) < iota((LANES, LANES), 1), 1.0, 0.0).astype(bf16)
    total = jnp.zeros((devices, 1), f32)
    ranks = []
    for start in range(0, grains, LANES):
        part = hot[:, start : start + LANES]
        before = jnp.dot(part.astype(bf16), earlier, preferred_element_type=f32) + total
        ranks.append(jnp.sum(part * before, axis=0, keepdims=True))
        total = total + jnp.sum(part, axis=1, keepdims=True)
    rank = jnp.concatenate(ranks, axis=1).astype(i32)
    rank_ref[...] = rank
    position = dest * capacity + rank
    place = jnp.where(iota((slots, grains), 0) == position, 1.0, 0.0).astype(bf16)
    rows = jnp.dot(place, fraction_ref[...], preferred_element_type=f32)
    speed = speed_ref[...].astype(f32)
    values = [speed[0:1], speed[1:2], speed[2:3], line_ref[...].astype(f32)]
    at_rank = iota((capacity, grains), 0) == rank
    facts = [jnp.where(at_rank, value, 0.0) for value in values]
    if 4 * capacity < width:
        facts.append(jnp.zeros((width - 4 * capacity, grains), f32))
    fact_rows = lax.dot_general(
        hot.astype(bf16),
        jnp.concatenate(facts, axis=0).astype(bf16),
        (((1,), (1,)), ((), ())),
        preferred_element_type=f32,
    )
    send_ref[...] = jnp.concatenate(
        [rows.reshape(devices, capacity, width), fact_rows.reshape(devices, 1, width)], axis=1
    ).astype(bf16)


def equilibrium_parts(density, speed, i):
    step = STEP[i]
    along = None
    for s, v in zip(step, speed):
        if s:
            term = v if s > 0 else -v
            along = term if along is None else along + term
    return along


def collide(fields, rate, solid, carried):
    density = functools.reduce(lambda a, b: a + b, fields)
    momentum = []
    for axis in range(3):
        plus = functools.reduce(lambda a, b: a + b, [fields[i] for i in range(27) if STEP[i][axis] == 1])
        minus = functools.reduce(lambda a, b: a + b, [fields[i] for i in range(27) if STEP[i][axis] == -1])
        momentum.append(plus - minus)
    inverse = 1.0 / density
    speed = [m * inverse for m in momentum]
    cover = 1.0 + solid
    inv_cover = 1.0 / cover
    share = solid * inv_cover
    solid_speed = [c * inv_cover for c in carried]
    base = 1.0 - 1.5 * (speed[0] * speed[0] + speed[1] * speed[1] + speed[2] * speed[2])
    solid_base = 1.0 - 1.5 * sum(v * v for v in solid_speed[1:]) - 1.5 * solid_speed[0] * solid_speed[0]
    departure, exchange = [None] * 27, [None] * 27
    for i in range(13, 27):
        j = 26 - i
        scale = WEIGHT[i] * density
        if i == 13:
            departure[13] = fields[13] - scale * base
            exchange[13] = departure[13] - (fields[13] - scale * solid_base)
            continue
        along = equilibrium_parts(density, speed, i)
        even, odd = scale * (base + 4.5 * along * along), scale * (3.0 * along)
        departure[i] = fields[i] - (even + odd)
        departure[j] = fields[j] - (even - odd)
        along = equilibrium_parts(density, solid_speed, i)
        even, odd = scale * (solid_base + 4.5 * along * along), scale * (3.0 * along)
        exchange[i] = departure[j] - (fields[i] - (even + odd))
        exchange[j] = departure[i] - (fields[j] - (even - odd))
    push = [
        (density * v - m) * inv_cover for v, m in zip(solid_speed, momentum)
    ]
    moments = list(departure)
    for stride in (1, 3, 9):
        for i in range(27):
            if i // stride % 3 == 0:
                low, mid, high = moments[i], moments[i + stride], moments[i + 2 * stride]
                both = low + high
                moments[i], moments[i + stride], moments[i + 2 * stride] = both + mid, high - low, both
    moments = [rate[a] * moments[a] for a in range(27)]
    for stride in (9, 3, 1):
        for i in range(27):
            if i // stride % 3 == 0:
                m0, m1, m2 = moments[i], moments[i + stride], moments[i + 2 * stride]
                half1, half2 = 0.5 * m1, 0.5 * m2
                moments[i], moments[i + stride], moments[i + 2 * stride] = half2 - half1, m0 - m2, half2 + half1
    keep = 1.0 - share
    post = [fields[i] - keep * moments[i] + share * exchange[i] for i in range(27)]
    return post, push


def collide_levels(read, rates_ref, held_ref, post_ref, up_ref, down_ref):
    depth, length = post_ref.shape[1], post_ref.shape[2]
    lines = depth * length
    rate = [rates_ref[a] for a in range(27)]
    pushes = []
    for z in range(depth):
        cells = lambda k: held_ref[k * lines + z * length : k * lines + (z + 1) * length, :]
        post, push = collide(read(z), rate, cells(0), [cells(1), cells(2), cells(3)])
        pushes.append(push)
        for i in range(27):
            post_ref[i, z] = post[i]
            if STEP[i][0] == 1 and z == depth - 1:
                up_ref[i - 18] = post[i]
            if STEP[i][0] == -1 and z == 0:
                down_ref[i] = post[i]
    return pushes


def first_kernel(
    capacity, rates_ref, recv_ref, fields_ref,
    post_ref, up_ref, down_ref, push_ref, held_ref, line_ref, slot_ref,
):
    devices, _, width = recv_ref.shape
    slots = devices * capacity
    depth, length = fields_ref.shape[1], fields_ref.shape[2]
    lines = depth * length
    received = recv_ref[...].astype(f32)
    slot_rows = received[:, :capacity].reshape(slots, width).astype(bf16)
    slot_ref[...] = slot_rows
    facts = received[:, capacity:].reshape(devices, width)
    group = iota((devices, width), 1) // capacity
    stacked = jnp.concatenate([jnp.where(group == m, facts, 0.0) for m in range(4)], axis=0)
    spread = jnp.where(
        iota((width, slots), 0) % capacity == iota((width, slots), 1) % capacity, 1.0, 0.0
    ).astype(bf16)
    wide = jnp.dot(stacked.astype(bf16), spread, preferred_element_type=f32)
    own = iota((devices, slots), 0) == iota((devices, slots), 1) // capacity
    fact = [
        jnp.sum(jnp.where(own, wide[m * devices : (m + 1) * devices], 0.0), axis=0, keepdims=True)
        for m in range(4)
    ]
    line_ref[...] = fact[3].astype(i32)
    on_line = iota((lines, slots), 0) == fact[3].astype(i32)
    gather = [jnp.where(on_line, 1.0, 0.0)] + [jnp.where(on_line, fact[k], 0.0) for k in range(3)]
    held_ref[...] = jnp.dot(
        jnp.concatenate(gather, axis=0).astype(bf16), slot_rows, preferred_element_type=f32
    )
    read = lambda z: [fields_ref[i, z] for i in range(27)]
    pushes = collide_levels(read, rates_ref, held_ref, post_ref, up_ref, down_ref)
    for z in range(depth):
        for k in range(3):
            push_ref[k, z] = pushes[z][k]


def ends_kernel(place_ref, post_ref, below_ref, above_ref, inner_ref, outer_ref):
    depth, length = post_ref.shape[1], post_ref.shape[2]
    even = place_ref[1] % 2 == 0

    def row(i, z, x):
        source = z - STEP[i][0]
        if source < 0:
            return below_ref[i - 18, x : x + 1]
        if source >= depth:
            return above_ref[i, x : x + 1]
        return post_ref[i, source, x : x + 1]

    for i in range(27):
        if STEP[i][1] != 1:
            continue
        j = i - 6
        for z in range(depth):
            n = ((STEP[i][0] + 1) * 3 + STEP[i][2] + 1) * depth + z
            right, left = row(i, z, length - 1), row(j, z, 0)
            inner_ref[n : n + 1] = jnp.where(even, right, left)
            outer_ref[n : n + 1] = jnp.where(even, left, right)


def streamed(place_ref, post_ref, below_ref, above_ref, inner_ref, outer_ref, z):
    depth, length, width = post_ref.shape[1:]
    even = place_ref[1] % 2 == 0
    rows = iota((length, width), 0)
    moved_list = []
    for i in range(27):
        cz, cx, cy = STEP[i]
        source = z - cz
        if source < 0:
            moved = below_ref[i - 18]
        elif source >= depth:
            moved = above_ref[i]
        else:
            moved = post_ref[i, source]
        if cx:
            n = ((cz + 1) * 3 + cy + 1) * depth + z
            inner, outer = inner_ref[n : n + 1], outer_ref[n : n + 1]
            edge = jnp.where(even, outer, inner) if cx > 0 else jnp.where(even, inner, outer)
            moved = pltpu.roll(moved, cx % length, 0)
            moved = jnp.where(rows == (0 if cx > 0 else length - 1), edge, moved)
        if cy:
            moved = pltpu.roll(moved, cy % width, 1)
        if source < 0:
            moved = jnp.where(place_ref[0] == 0, post_ref[26 - i, z], moved)
        elif source >= depth:
            moved = jnp.where(place_ref[0] == place_ref[2] - 1, post_ref[26 - i, z], moved)
        moved_list.append(moved)
    return moved_list


def second_kernel(
    capacity, place_ref, rates_ref, post_ref, below_ref, above_ref, inner_ref, outer_ref,
    held_ref, push_ref, line_ref, slot_ref, next_ref, up_ref, down_ref, force_ref,
):
    depth, length, width = post_ref.shape[1:]
    lines = depth * length
    slots = slot_ref.shape[0]
    halo = (below_ref, above_ref, inner_ref, outer_ref)
    read = lambda z: streamed(place_ref, post_ref, *halo, z)
    pushes = collide_levels(read, rates_ref, held_ref, next_ref, up_ref, down_ref)
    total = jnp.concatenate(
        [push_ref[k, z] + pushes[z][k] for k in range(3) for z in range(depth)], axis=0
    )
    along = lax.dot_general(
        jnp.concatenate(split3(total), axis=0),
        slot_ref[...],
        (((1,), (1,)), ((), ())),
        preferred_element_type=f32,
    )
    along = along[: 3 * lines] + along[3 * lines : 6 * lines] + along[6 * lines :]
    on_line = iota((lines, slots), 0) == line_ref[...]
    tiles, per_tile = slots // LANES, LANES // capacity
    group = iota((tiles, LANES), 1) // capacity
    force = []
    for k in range(3):
        picked = -jnp.sum(jnp.where(on_line, along[k * lines : (k + 1) * lines], 0.0), axis=0, keepdims=True)
        force.append(
            jnp.concatenate([picked[:, t * LANES : (t + 1) * LANES] for t in range(tiles)], axis=0)
        )
    for a in range(per_tile):
        block = jnp.zeros((tiles, LANES), f32)
        for k in range(3):
            shift = (k - a) * capacity % LANES
            turned = pltpu.roll(force[k], shift, 1) if shift else force[k]
            block = jnp.where(group == k, turned, block)
        force_ref[pl.ds(a, tiles, stride=per_tile), :] = block


def last_kernel(place_ref, post_ref, below_ref, above_ref, inner_ref, outer_ref, scaled_ref):
    for z in range(post_ref.shape[1]):
        halo = (below_ref, above_ref, inner_ref, outer_ref)
        fields = streamed(place_ref, post_ref, *halo, z)
        for i in range(27):
            scaled_ref[i, z] = fields[i] * (1.0 / WEIGHT[i])


def unpack_kernel(capacity, dest_ref, rank_ref, back_ref, force_ref):
    devices, grains = back_ref.shape[0], dest_ref.shape[1]
    hot = jnp.where(iota((devices, grains), 0) == dest_ref[...], 1.0, 0.0).astype(bf16)
    parts = jnp.concatenate([part.astype(f32) for part in split3(back_ref[...])], axis=1).T
    picked = jnp.dot(parts.astype(bf16), hot, preferred_element_type=f32)
    picked = picked[:LANES] + picked[LANES : 2 * LANES] + picked[2 * LANES :]
    at_rank = iota((capacity, grains), 0) == rank_ref[...]
    for k in range(3):
        mine = jnp.where(at_rank, picked[k * capacity : (k + 1) * capacity], 0.0)
        force_ref[k : k + 1] = jnp.sum(mine, axis=0, keepdims=True)


def exchange_halo(place, post, up, down):
    peers, length = lax.axis_size("gz"), lax.axis_size("gx")
    below = lax.ppermute(up, "gz", [(i, (i + 1) % peers) for i in range(peers)])
    above = lax.ppermute(down, "gz", [((i + 1) % peers, i) for i in range(peers)])
    depth, width = post.shape[1], post.shape[3]
    ends = jax.ShapeDtypeStruct((9 * depth, width), f32)
    inner, outer = call(ends_kernel, [ends, ends], place, post, below, above, scalars=1)
    inner = lax.ppermute(inner, "gx", [(i, i ^ 1) for i in range(length)])
    outer = lax.ppermute(
        outer, "gx", [(i, (i + 1) % length if i % 2 else (i - 1) % length) for i in range(length)]
    )
    return below, above, inner, outer


def per_device(populations, rates, grain_fraction, grain_velocity, grain_dest, grain_line):
    _, depth, length, width = populations.shape
    lines = depth * length
    devices = lax.axis_size("gz") * lax.axis_size("gx")
    grains = grain_fraction.shape[0]
    capacity = 2 * grains // devices
    slots = devices * capacity
    shape = jax.ShapeDtypeStruct
    dest, line = grain_dest.reshape(1, grains), grain_line.reshape(1, grains)
    place = jnp.stack(
        [lax.axis_index("gz"), lax.axis_index("gx"), jnp.int32(lax.axis_size("gz"))]
    ).astype(i32)
    send, rank = call(
        functools.partial(pack_kernel, devices, capacity),
        [shape((devices, capacity + 1, width), bf16), shape((1, grains), i32)],
        dest, line, grain_velocity, grain_fraction,
    )
    recv = lax.all_to_all(send, ("gz", "gx"), split_axis=0, concat_axis=0, tiled=True)
    state = shape(populations.shape, f32)
    face = shape((9, length, width), f32)
    post, up, down, push, held, slot_line, slot_rows = call(
        functools.partial(first_kernel, capacity),
        [
            state, face, face, shape((3, depth, length, width), f32),
            shape((4 * lines, width), f32), shape((1, slots), i32), shape((slots, width), bf16),
        ],
        rates, recv, populations, scalars=1,
    )
    halo = exchange_halo(place, post, up, down)
    post, up, down, slot_force = call(
        functools.partial(second_kernel, capacity),
        [state, face, face, shape((devices, LANES), f32)],
        place, rates, post, *halo, held, push, slot_line, slot_rows, scalars=2,
    )
    back = lax.all_to_all(slot_force, ("gz", "gx"), split_axis=0, concat_axis=0, tiled=True)
    halo = exchange_halo(place, post, up, down)
    (scaled,) = call(last_kernel, [state], place, post, *halo, scalars=1)
    (grain_force,) = call(
        functools.partial(unpack_kernel, capacity), [shape((3, grains), f32)], dest, rank, back
    )
    return (scaled, grain_force)


def solution(mesh):
    in_specs = (
        P(None, "gz", "gx", None),
        P(),
        P(("gz", "gx"), None),
        P(None, ("gz", "gx")),
        P(("gz", "gx"), None),
        P(("gz", "gx")),
    )
    out_specs = (P(None, "gz", "gx", None), P(None, ("gz", "gx")))
    return jax.shard_map(
        per_device, mesh=mesh, in_specs=in_specs, out_specs=out_specs, check_vma=False
    )
```

time: 132 us -> 52.9 us (0.40)
  local copies, waits for them, and re-layouts: 50.1 us -> 2.96 us
  starting transfers between devices: 31.3 us -> 20 us
  other arithmetic: 10.5 us -> 0.08 us
  matrix products: 9.93 us -> 0 us
  Pallas kernels: 0 us -> 7.52 us
  waiting for transfers between devices: 27.9 us -> 21.2 us
    scatter x4 -> x0, local copies, waits for them, and re-layouts: 31 us -> none  [the longest x2 25.6 us: per_device(): jnp.zeros((devices, 3, capacity), jnp.bfloat16).at[target, :, rank]]
    dot_general x13 -> x0, matrix products: 9.93 us -> none  [the longest x1 3.65 us: per_device(): jnp.einsum('kjcy,jcy->jkc', picked, fraction.reshape(devices, capacity, w...]
    all_to_all x3 -> x1, starting transfers between devices: 15.7 us -> 7.3 us  [per_device(): lax.all_to_all(send, ('gz', 'gx'), split_axis=0, concat_axis=0, tiled=True)]
    gather x2 -> x0, local copies, waits for them, and re-layouts: 7.7 us -> none  [the longest x1 4.04 us: per_device(): picked = push_lines[:, safe_line, :]]
    pallas_call x0 -> x7, Pallas kernels: none -> 7.52 us  [call(): pl.pallas_call(kernel, out_shape=list(outs), in_specs=[smem] * scalars +...]
    ppermute x8, waiting for transfers between devices: 11.3 us -> 6.43 us  [the longest x2 3.82 us: exchange_halo(): lax.ppermute(outer, 'gx', [(i, (i + 1) % length if i % 2 else (i - 1) % l...]
    slice x18 -> x0, local copies, waits for them, and re-layouts: 2.42 us -> none  [the longest x12 0.87 us: stream_local(): moved = jnp.roll(moved, step_y, axis=2)]
    all_to_all x1, starting transfers between devices: 4.82 us -> 2.54 us  [per_device(): lax.all_to_all(slot_force, ('gz', 'gx'), split_axis=0, concat_axis=0, til...]
  transfers between devices with their start and end apart: 12 -> 10, of which waited for: 8 -> 6; matrix products, arithmetic and copies ran while one was open for 39% -> 0% of each run, Pallas kernels for 0% -> 3%
where the time goes in v1:
time: 52.9 us; the launch traced here: 52.6 us
  waiting for transfers between devices  21.2 us (40%)
  starting transfers between devices  20 us (38%)
  Pallas kernels  7.52 us (14%)
  local copies, waits for them, and re-layouts  2.96 us (6%)
  between operations  0.74 us (1%)
    all_to_all x1, waiting for transfers between devices, per_device(): lax.all_to_all(send, ('gz', 'gx'), split_axis=0, concat_axis=0, tiled=True)  12.1 us
    pallas_call x7, Pallas kernels, call(): pl.pallas_call(kernel, out_shape=list(outs), in_specs=[smem] * scalars +...  7.52 us
    all_to_all x1, starting transfers between devices, per_device(): lax.all_to_all(send, ('gz', 'gx'), split_axis=0, concat_axis=0, tiled=True)  7.3 us
    ppermute x2, starting transfers between devices, exchange_halo(): lax.ppermute(outer, 'gx', [(i, (i + 1) % length if i % 2 else (i - 1) % l...  4.16 us
    ppermute x2, starting transfers between devices, exchange_halo(): lax.ppermute(down, 'gz', [((i + 1) % peers, i) for i in range(peers)])  3.84 us
    ppermute x2, waiting for transfers between devices, exchange_halo(): lax.ppermute(outer, 'gx', [(i, (i + 1) % length if i % 2 else (i - 1) % l...  3.82 us
    unnamed x12, local copies, waits for them, and re-layouts  2.96 us
    all_to_all x1, waiting for transfers between devices, per_device(): lax.all_to_all(slot_force, ('gz', 'gx'), split_axis=0, concat_axis=0, til...  2.68 us
  transfers between devices with their start and end apart: 10, of which 6 were waited for; matrix products, arithmetic and copies ran while one was open for 0% of the time, Pallas kernels for 3%

profile of v1, /device:TPU:0, one launch (start us, length us, event | category | flops | bytes accessed | tf_op | source)
XLA Modules:
  0.0 52.6 jit_solution(14217757053817806186)
XLA Ops:
  0.6 0.7 %copy-done.2 = s32[512,1]{0,1:T(1,128)S(1)} copy-done((s32[512,1]{0,1:T(1,128)S(1)}, s32[512,1]{0,1:T(1,128)}, u32[]{:S(2)}) %copy-start.2) | copy-done | bytes 2072
  1.3 0.9 %copy-done.1 = bf16[512,128]{1,0:T(8,128)(2,1)S(1)} copy-done((bf16[512,128]{1,0:T(8,128)(2,1)S(1)}, bf16[512,128]{1,0:T(8,128)(2,1)}, u32[]{:S(2)}) %copy-start.1) | copy-done | bytes 131096
  2.2 0.7 %copy-done.3 = bf16[3,512]{1,0:T(4,128)(2,1)S(1)} copy-done((bf16[3,512]{1,0:T(4,128)(2,1)S(1)}, bf16[3,512]{1,0:T(4,128)(2,1)}, u32[]{:S(2)}) %copy-start.3) | copy-done | bytes 3096
  2.9 0.7 %copy-done.4 = s32[512]{0:T(512)S(1)} copy-done((s32[512]{0:T(512)S(1)}, s32[512]{0:T(512)}, u32[]{:S(2)}) %copy-start.4) | copy-done | bytes 2072
  3.6 1.3 %shard_map.77 = (bf16[32,33,128]{2,1,0:T(8,128)(2,1)}, s32[1,512]{1,0:T(1,128)S(1)}) custom-call(s32[1,512]{1,0:T(1,128)S(1)} %bitcast.9, s32[1,512]{1,0:T(1,128)S(1)} %bitcast.11, bf16[3,512]{1,0:T(4,128)(2,1)S(1)} %copy-done.3, bf16[512,128]{1,0:T(8,128)(2,1)S(1)} %copy-done.1), custom_call_target="tpu_custom_call" | custom-call | bytes 410624 | tf_op jit(solution)/shard_map/pallas_call | solution.py:28
  4.9 7.3 %all-to-all-start = ((bf16[32,33,128]{2,1,0:T(8,128)(2,1)}), bf16[32,33,128]{2,1,0:T(8,128)(2,1)S(1)}, u32[]{:S(2)}, u32[]{:S(2)}) async-start(bf16[32,33,128]{2,1,0:T(8,128)(2,1)} %get-tuple-element.19), calls=%async_computation | async-start | bytes 655360 | tf_op jit(solution)/shard_map/all_to_all | solution.py:339
  12.2 0.0 copy-start.5
  12.2 12.1 %all-to-all-done.recv_ref = bf16[32,33,128]{2,1,0:T(8,128)(2,1)S(1)} async-done(((bf16[32,33,128]{2,1,0:T(8,128)(2,1)}), bf16[32,33,128]{2,1,0:T(8,128)(2,1)S(1)}, u32[]{:S(2)}, u32[]{:S(2)}) %all-to-all-start) | async-done | bytes 270368 | tf_op jit(solution)/shard_map/all_to_all | solution.py:339
  24.4 1.1 %shard_map.78 = (f32[27,2,8,128]{3,2,1,0:T(8,128)S(1)}, f32[9,8,128]{2,1,0:T(8,128)S(1)}, f32[9,8,128]{2,1,0:T(8,128)S(1)}, f32[3,2,8,128]{3,2,1,0:T(8,128)S(1)}...) custom-call(f32[27]{0:T(128)S(1)} %copy-done.5, ...), custom_call_target="tpu_custom_call" | custom-call | bytes 1110124 | tf_op jit(solution)/shard_map/pallas_call | solution.py:28
  25.4 0.1 collective-permute-start
  25.5 2.9 %collective-permute-start.1 = (f32[9,8,128]{2,1,0:T(8,128)S(1)}, f32[9,8,128]{2,1,0:T(8,128)S(1)}, u32[]{:S(2)}, u32[]{:S(2)}) collective-permute-start(f32[9,8,128]{2,1,0:T(8,128)S(1)} %get-tuple-element.22), channel_id=1, source_target_pairs={{8,0},{16,8},{24,16},{0,24},{9,1},{17,9},{25,17},{1,25},{10,2},{18... | collective-permute-start | bytes 110600 | tf_op jit(solution)/shard_map/ppermute | solution.py:311
  28.4 0.1 pad_add_fusion.place_ref
  28.5 1.9 %collective-permute-done.below_ref = f32[9,8,128]{2,1,0:T(8,128)S(1)} collective-permute-done((f32[9,8,128]{2,1,0:T(8,128)S(1)}, f32[9,8,128]{2,1,0:T(8,128)S(1)}, u32[]{:S(2)}, u32[]{:S(2)}) %collective-permute-start) | collective-permute-done | bytes 36896 | tf_op jit(solution)/shard_map/ppermute | solution.py:310
  30.3 0.0 collective-permute-done.1.above_ref
  30.4 0.6 %shard_map.79 = (f32[18,128]{1,0:T(8,128)S(1)}, f32[18,128]{1,0:T(8,128)S(1)}) custom-call(s32[3]{0:T(128)S(1)} %pad_add_fusion.place_ref, f32[27,2,8,128]{3,2,1,0:T(8,128)S(1)} %get-tuple-element.20.post_ref, f32[9,8,128]{2,1,0:T(8,128)S(1)} %collective-permute-done.below_ref, f32[9,8,128]{2,1,0:T(8,128)S(1)} %collective-permute-done.1.above_ref), custom_call_target="tpu_custom_call" | custom-call | bytes 313356 | tf_op jit(solution)/shard_map/pallas_call | solution.py:28
  30.9 0.1 collective-permute-start.2
  31.0 0.9 %collective-permute-start.3 = (f32[18,128]{1,0:T(8,128)S(1)}, f32[18,128]{1,0:T(8,128)S(1)}, u32[]{:S(2)}, u32[]{:S(2)}) collective-permute-start(f32[18,128]{1,0:T(8,128)S(1)} %get-tuple-element.24), channel_id=1, source_target_pairs={{0,7},{1,2},{2,1},{3,4},{4,3},{5,6},{6,5},{7,0},{8,15},{9,10},{10,... | collective-permute-start | bytes 27656 | tf_op jit(solution)/shard_map/ppermute | solution.py:316
  31.9 0.3 collective-permute-done.2.inner_ref
  32.2 3.8 %collective-permute-done.3.outer_ref = f32[18,128]{1,0:T(8,128)S(1)} collective-permute-done((f32[18,128]{1,0:T(8,128)S(1)}, f32[18,128]{1,0:T(8,128)S(1)}, u32[]{:S(2)}, u32[]{:S(2)}) %collective-permute-start.3) | collective-permute-done | bytes 9248 | tf_op jit(solution)/shard_map/ppermute | solution.py:316
  36.0 1.8 %shard_map.80 = (f32[27,2,8,128]{3,2,1,0:T(8,128)S(1)}, f32[9,8,128]{2,1,0:T(8,128)S(1)}, f32[9,8,128]{2,1,0:T(8,128)S(1)}, f32[32,128]{1,0:T(8,128)}) custom-call(s32[3]{0:T(128)S(1)} %pad_add_fusion.place_ref, f32[27]{0:T(128)S(1)} %copy-done.5, f32[27,2,8,128]{3,2,1,0:T(8,128)S(1)} %get-tuple-element.20.post_ref, ...), custom_call_target="tpu_custom_call" | custom-call | bytes 948344 | tf_op jit(solution)/shard_map/pallas_call | solution.py:28
  37.7 2.0 %collective-permute-start.4 = (f32[9,8,128]{2,1,0:T(8,128)S(1)}, f32[9,8,128]{2,1,0:T(8,128)S(1)}, u32[]{:S(2)}, u32[]{:S(2)}) collective-permute-start(f32[9,8,128]{2,1,0:T(8,128)S(1)} %get-tuple-element.30), channel_id=1, source_target_pairs={{0,8},{8,16},{16,24},{24,0},{1,9},{9,17},{17,25},{25,1},{2,10},{10... | collective-permute-start | bytes 110600 | tf_op jit(solution)/shard_map/ppermute | solution.py:310
  39.7 0.9 %collective-permute-start.5 = (f32[9,8,128]{2,1,0:T(8,128)S(1)}, f32[9,8,128]{2,1,0:T(8,128)S(1)}, u32[]{:S(2)}, u32[]{:S(2)}) collective-permute-start(f32[9,8,128]{2,1,0:T(8,128)S(1)} %get-tuple-element.31), channel_id=1, source_target_pairs={{8,0},{16,8},{24,16},{0,24},{9,1},{17,9},{25,17},{1,25},{10,2},{18... | collective-permute-start | bytes 110600 | tf_op jit(solution)/shard_map/ppermute | solution.py:311
  40.7 2.5 %all-to-all-start.1 = ((f32[32,1,128]{2,1,0:T(1,128)}), f32[32,1,128]{2,1,0:T(1,128)S(1)}, u32[]{:S(2)}, u32[]{:S(2)}) async-start(f32[32,1,128]{2,1,0:T(1,128)} %bitcast.5), calls=%async_computation.1 | async-start | bytes 32768 | tf_op jit(solution)/shard_map/all_to_all | solution.py:356
  43.2 0.0 collective-permute-done.4.below_ref
  43.2 0.5 collective-permute-done.5.above_ref
  43.7 0.6 %shard_map.81 = (f32[18,128]{1,0:T(8,128)S(1)}, f32[18,128]{1,0:T(8,128)S(1)}) custom-call(s32[3]{0:T(128)S(1)} %pad_add_fusion.place_ref, f32[27,2,8,128]{3,2,1,0:T(8,128)S(1)} %get-tuple-element.29.post_ref, f32[9,8,128]{2,1,0:T(8,128)S(1)} %collective-permute-done.4.below_ref, f32[9,8,128]{2,1,0:T(8,128)S(1)} %collective-permute-done.5.above_ref), custom_call_target="tpu_custom_call" | custom-call | bytes 313356 | tf_op jit(solution)/shard_map/pallas_call | solution.py:28
  44.3 0.1 collective-permute-start.6
  44.3 3.3 %collective-permute-start.7 = (f32[18,128]{1,0:T(8,128)S(1)}, f32[18,128]{1,0:T(8,128)S(1)}, u32[]{:S(2)}, u32[]{:S(2)}) collective-permute-start(f32[18,128]{1,0:T(8,128)S(1)} %get-tuple-element.33), channel_id=1, source_target_pairs={{0,7},{1,2},{2,1},{3,4},{4,3},{5,6},{6,5},{7,0},{8,15},{9,10},{10,... | collective-permute-start | bytes 27656 | tf_op jit(solution)/shard_map/ppermute | solution.py:316
  47.6 2.7 %all-to-all-done.1 = f32[32,1,128]{2,1,0:T(1,128)S(1)} async-done(((f32[32,1,128]{2,1,0:T(1,128)}), f32[32,1,128]{2,1,0:T(1,128)S(1)}, u32[]{:S(2)}, u32[]{:S(2)}) %all-to-all-start.1) | async-done | bytes 16416 | tf_op jit(solution)/shard_map/all_to_all | solution.py:356
  50.3 0.9 %shard_map.83 = f32[3,512]{1,0:T(4,128)} custom-call(s32[1,512]{1,0:T(1,128)S(1)} %bitcast.10, s32[1,512]{1,0:T(1,128)S(1)} %get-tuple-element.34.rank_ref, f32[32,128]{1,0:T(8,128)S(1)} %bitcast.8), custom_call_target="tpu_custom_call" | custom-call | bytes 26624 | tf_op jit(solution)/shard_map/pallas_call | solution.py:28
  51.2 0.0 collective-permute-done.7.outer_ref
  51.2 1.3 %shard_map.82 = f32[27,2,8,128]{3,2,1,0:T(8,128)} custom-call(s32[3]{0:T(128)S(1)} %pad_add_fusion.place_ref, f32[27,2,8,128]{3,2,1,0:T(8,128)S(1)} %get-tuple-element.29.post_ref, f32[9,8,128]{2,1,0:T(8,128)S(1)} %collective-permute-done.4.below_ref, f32[9,8,128]{2,1,0:T(8,128)S(1)} %collective-permute-done.5.above_ref, ...), custom_call_target="tpu_custom_call" | custom-call | bytes 534540 | tf_op jit(solution)/shard_map/pallas_call | solution.py:28
  (8 shorter events, 0.0 us)
Async XLA Ops:
  0.6 0.7 %copy-start.2 = (s32[512,1]{0,1:T(1,128)S(1)}, s32[512,1]{0,1:T(1,128)}, u32[]{:S(2)}) copy-start(s32[512,1]{0,1:T(1,128)} %param.10) | copy-start | bytes 6148
  1.3 0.9 %copy-start.1 = (bf16[512,128]{1,0:T(8,128)(2,1)S(1)}, bf16[512,128]{1,0:T(8,128)(2,1)}, u32[]{:S(2)}) copy-start(bf16[512,128]{1,0:T(8,128)(2,1)} %fraction_ref.1) | copy-start | bytes 393220
  2.2 0.7 %copy-start.3 = (bf16[3,512]{1,0:T(4,128)(2,1)S(1)}, bf16[3,512]{1,0:T(4,128)(2,1)}, u32[]{:S(2)}) copy-start(bf16[3,512]{1,0:T(4,128)(2,1)} %speed_ref.1) | copy-start | bytes 9220
  2.9 0.7 %copy-start.4 = (s32[512]{0:T(512)S(1)}, s32[512]{0:T(512)}, u32[]{:S(2)}) copy-start(s32[512]{0:T(512)} %param.11) | copy-start | bytes 6148
  4.9 19.5 %copy-start = (f32[27,2,8,128]{3,2,1,0:T(8,128)S(1)}, f32[27,2,8,128]{3,2,1,0:T(8,128)}, u32[]{:S(2)}) copy-start(f32[27,2,8,128]{3,2,1,0:T(8,128)} %fields_ref.1) | copy-start | bytes 663556
  4.9 19.4 %all-to-all-start = ((bf16[32,33,128]{2,1,0:T(8,128)(2,1)}), bf16[32,33,128]{2,1,0:T(8,128)(2,1)S(1)}, u32[]{:S(2)}, u32[]{:S(2)}) async-start(bf16[32,33,128]{2,1,0:T(8,128)(2,1)} %get-tuple-element.19), calls=%async_computation | async-start | bytes 655360 | tf_op jit(solution)/shard_map/all_to_all | solution.py:339
  12.2 12.1 %copy-start.5 = (f32[27]{0:T(128)S(1)}, f32[27]{0:T(128)}, u32[]{:S(2)}) copy-start(f32[27]{0:T(128)} %rates_ref.3) | copy-start | bytes 328
  25.4 4.9 %collective-permute-start = (f32[9,8,128]{2,1,0:T(8,128)S(1)}, f32[9,8,128]{2,1,0:T(8,128)S(1)}, u32[]{:S(2)}, u32[]{:S(2)}) collective-permute-start(f32[9,8,128]{2,1,0:T(8,128)S(1)} %get-tuple-element.21), channel_id=1, source_target_pairs={{0,8},{8,16},{16,24},{24,0},{1,9},{9,17},{17,25},{25,1},{2,10},{10... | collective-permute-start | bytes 110600 | tf_op jit(solution)/shard_map/ppermute | solution.py:310
  25.5 4.8 %collective-permute-start.1 = (f32[9,8,128]{2,1,0:T(8,128)S(1)}, f32[9,8,128]{2,1,0:T(8,128)S(1)}, u32[]{:S(2)}, u32[]{:S(2)}) collective-permute-start(f32[9,8,128]{2,1,0:T(8,128)S(1)} %get-tuple-element.22), channel_id=1, source_target_pairs={{8,0},{16,8},{24,16},{0,24},{9,1},{17,9},{25,17},{1,25},{10,2},{18... | collective-permute-start | bytes 110600 | tf_op jit(solution)/shard_map/ppermute | solution.py:311
  30.9 1.2 %collective-permute-start.2 = (f32[18,128]{1,0:T(8,128)S(1)}, f32[18,128]{1,0:T(8,128)S(1)}, u32[]{:S(2)}, u32[]{:S(2)}) collective-permute-start(f32[18,128]{1,0:T(8,128)S(1)} %get-tuple-element.23), channel_id=1, source_target_pairs={{0,1},{1,0},{2,3},{3,2},{4,5},{5,4},{6,7},{7,6},{8,9},{9,8},{10,11... | collective-permute-start | bytes 27656 | tf_op jit(solution)/shard_map/ppermute | solution.py:315
  31.0 5.0 %collective-permute-start.3 = (f32[18,128]{1,0:T(8,128)S(1)}, f32[18,128]{1,0:T(8,128)S(1)}, u32[]{:S(2)}, u32[]{:S(2)}) collective-permute-start(f32[18,128]{1,0:T(8,128)S(1)} %get-tuple-element.24), channel_id=1, source_target_pairs={{0,7},{1,2},{2,1},{3,4},{4,3},{5,6},{6,5},{7,0},{8,15},{9,10},{10,... | collective-permute-start | bytes 27656 | tf_op jit(solution)/shard_map/ppermute | solution.py:316
  37.7 5.5 %collective-permute-start.4 = (f32[9,8,128]{2,1,0:T(8,128)S(1)}, f32[9,8,128]{2,1,0:T(8,128)S(1)}, u32[]{:S(2)}, u32[]{:S(2)}) collective-permute-start(f32[9,8,128]{2,1,0:T(8,128)S(1)} %get-tuple-element.30), channel_id=1, source_target_pairs={{0,8},{8,16},{16,24},{24,0},{1,9},{9,17},{17,25},{25,1},{2,10},{10... | collective-permute-start | bytes 110600 | tf_op jit(solution)/shard_map/ppermute | solution.py:310
  39.7 4.0 %collective-permute-start.5 = (f32[9,8,128]{2,1,0:T(8,128)S(1)}, f32[9,8,128]{2,1,0:T(8,128)S(1)}, u32[]{:S(2)}, u32[]{:S(2)}) collective-permute-start(f32[9,8,128]{2,1,0:T(8,128)S(1)} %get-tuple-element.31), channel_id=1, source_target_pairs={{8,0},{16,8},{24,16},{0,24},{9,1},{17,9},{25,17},{1,25},{10,2},{18... | collective-permute-start | bytes 110600 | tf_op jit(solution)/shard_map/ppermute | solution.py:311
  40.7 9.6 %all-to-all-start.1 = ((f32[32,1,128]{2,1,0:T(1,128)}), f32[32,1,128]{2,1,0:T(1,128)S(1)}, u32[]{:S(2)}, u32[]{:S(2)}) async-start(f32[32,1,128]{2,1,0:T(1,128)} %bitcast.5), calls=%async_computation.1 | async-start | bytes 32768 | tf_op jit(solution)/shard_map/all_to_all | solution.py:356
  44.3 6.9 %collective-permute-start.6 = (f32[18,128]{1,0:T(8,128)S(1)}, f32[18,128]{1,0:T(8,128)S(1)}, u32[]{:S(2)}, u32[]{:S(2)}) collective-permute-start(f32[18,128]{1,0:T(8,128)S(1)} %get-tuple-element.32), channel_id=1, source_target_pairs={{0,1},{1,0},{2,3},{3,2},{4,5},{5,4},{6,7},{7,6},{8,9},{9,8},{10,11... | collective-permute-start | bytes 27656 | tf_op jit(solution)/shard_map/ppermute | solution.py:315
  44.3 6.9 %collective-permute-start.7 = (f32[18,128]{1,0:T(8,128)S(1)}, f32[18,128]{1,0:T(8,128)S(1)}, u32[]{:S(2)}, u32[]{:S(2)}) collective-permute-start(f32[18,128]{1,0:T(8,128)S(1)} %get-tuple-element.33), channel_id=1, source_target_pairs={{0,7},{1,2},{2,1},{3,4},{4,3},{5,6},{6,5},{7,0},{8,15},{9,10},{10,... | collective-permute-start | bytes 27656 | tf_op jit(solution)/shard_map/ppermute | solution.py:316

commit v2 on v1

--- a/solution.py
+++ b/solution.py
@@ -20,19 +20,27 @@
     return lax.broadcasted_iota(i32, shape, dim)
 
 
-def call(kernel, outs, *operands, scalars=0, flops=0):
-    smem, vmem = pl.BlockSpec(memory_space=pltpu.SMEM), pl.BlockSpec(memory_space=pltpu.VMEM)
+def call(kernel, outs, *operands, smem=(), hbm=(), scratch=(), flops=0, vmem=24):
+    space = [pltpu.SMEM if n in smem else pltpu.HBM if n in hbm else pltpu.VMEM for n in range(len(operands))]
     size = sum(o.size * o.dtype.itemsize for o in operands) + sum(
         int(np.prod(o.shape)) * o.dtype.itemsize for o in outs
     )
     return pl.pallas_call(
         kernel,
         out_shape=list(outs),
-        in_specs=[smem] * scalars + [vmem] * (len(operands) - scalars),
-        out_specs=[vmem] * len(outs),
-        compiler_params=pltpu.CompilerParams(vmem_limit_bytes=24 * 1024 * 1024),
+        in_specs=[pl.BlockSpec(memory_space=where) for where in space],
+        out_specs=[pl.BlockSpec(memory_space=pltpu.VMEM)] * len(outs),
+        scratch_shapes=list(scratch),
+        compiler_params=pltpu.CompilerParams(vmem_limit_bytes=vmem * 1024 * 1024),
         cost_estimate=pl.CostEstimate(flops=flops, bytes_accessed=size, transcendentals=0),
     )(*operands)
+
+
+def device_at(step_z, step_x):
+    depth, length = lax.axis_size("gz"), lax.axis_size("gx")
+    z = lax.rem(lax.axis_index("gz") + step_z + depth, depth)
+    x = lax.rem(lax.axis_index("gx") + step_x + length, length)
+    return z * length + x
 
 
 def split3(x):
@@ -42,9 +50,15 @@
     return high, mid, (rest - mid.astype(f32)).astype(bf16)
 
 
-def pack_kernel(devices, capacity, dest_ref, line_ref, speed_ref, fraction_ref, send_ref, rank_ref):
+def pack_kernel(devices, capacity, *refs):
+    sources, (send_ref, rank_ref), held, sem = refs[:4], refs[4:6], refs[6:10], refs[10]
+    copies = [pltpu.make_async_copy(sources[n], held[n], sem.at[n]) for n in range(4)]
+    for copy in copies:
+        copy.start()
+    dest_ref, line_ref, speed_ref, fraction_ref = held
     grains, width = fraction_ref.shape
     slots = devices * capacity
+    copies[0].wait()
     dest = dest_ref[...]
     hot = jnp.where(iota((devices, grains), 0) == dest, 1.0, 0.0)
     earlier = jnp.where(iota((LANES, LANES), 0) < iota((LANES, LANES), 1), 1.0, 0.0).astype(bf16)
@@ -59,7 +73,10 @@
     rank_ref[...] = rank
     position = dest * capacity + rank
     place = jnp.where(iota((slots, grains), 0) == position, 1.0, 0.0).astype(bf16)
+    copies[3].wait()
     rows = jnp.dot(place, fraction_ref[...], preferred_element_type=f32)
+    copies[1].wait()
+    copies[2].wait()
     speed = speed_ref[...].astype(f32)
     values = [speed[0:1], speed[1:2], speed[2:3], line_ref[...].astype(f32)]
     at_rank = iota((capacity, grains), 0) == rank
@@ -194,9 +211,9 @@
             push_ref[k, z] = pushes[z][k]
 
 
-def ends_kernel(place_ref, post_ref, below_ref, above_ref, inner_ref, outer_ref):
+def ends_kernel(post_ref, below_ref, above_ref, inner_ref, outer_ref):
     depth, length = post_ref.shape[1], post_ref.shape[2]
-    even = place_ref[1] % 2 == 0
+    even = lax.axis_index("gx") % 2 == 0
 
     def row(i, z, x):
         source = z - STEP[i][0]
@@ -211,20 +228,25 @@
             continue
         j = i - 6
         for z in range(depth):
-            n = ((STEP[i][0] + 1) * 3 + STEP[i][2] + 1) * depth + z
+            n = end_row(i, z, depth)
             right, left = row(i, z, length - 1), row(j, z, 0)
             inner_ref[n : n + 1] = jnp.where(even, right, left)
             outer_ref[n : n + 1] = jnp.where(even, left, right)
 
 
-def streamed(place_ref, post_ref, below_ref, above_ref, inner_ref, outer_ref, z):
+def end_row(i, z, depth):
+    return ((STEP[i][0] + 1) * 3 + STEP[i][2] + 1) * depth + z
+
+
+def streamed(post_ref, below_ref, above_ref, inner_ref, outer_ref, z, back_ref=None):
     depth, length, width = post_ref.shape[1:]
-    even = place_ref[1] % 2 == 0
+    even = lax.axis_index("gx") % 2 == 0
     rows = iota((length, width), 0)
     moved_list = []
     for i in range(27):
         cz, cx, cy = STEP[i]
         source = z - cz
+        inside = 0 <= source < depth
         if source < 0:
             moved = below_ref[i - 18]
         elif source >= depth:
@@ -232,31 +254,55 @@
         else:
             moved = post_ref[i, source]
         if cx:
-            n = ((cz + 1) * 3 + cy + 1) * depth + z
+            n = end_row(i, z, depth)
             inner, outer = inner_ref[n : n + 1], outer_ref[n : n + 1]
             edge = jnp.where(even, outer, inner) if cx > 0 else jnp.where(even, inner, outer)
+            if not inside and back_ref is not None:
+                edge = back_ref[pl.ds(4 * device_at(-cz, -cx) + 2 + cy, 1)]
             moved = pltpu.roll(moved, cx % length, 0)
             moved = jnp.where(rows == (0 if cx > 0 else length - 1), edge, moved)
         if cy:
             moved = pltpu.roll(moved, cy % width, 1)
         if source < 0:
-            moved = jnp.where(place_ref[0] == 0, post_ref[26 - i, z], moved)
+            moved = jnp.where(lax.axis_index("gz") == 0, post_ref[26 - i, z], moved)
         elif source >= depth:
-            moved = jnp.where(place_ref[0] == place_ref[2] - 1, post_ref[26 - i, z], moved)
+            top = lax.axis_size("gz") - 1
+            moved = jnp.where(lax.axis_index("gz") == top, post_ref[26 - i, z], moved)
         moved_list.append(moved)
     return moved_list
 
 
 def second_kernel(
-    capacity, place_ref, rates_ref, post_ref, below_ref, above_ref, inner_ref, outer_ref,
-    held_ref, push_ref, line_ref, slot_ref, next_ref, up_ref, down_ref, force_ref,
+    capacity, rates_ref, post_ref, below_ref, above_ref, inner_ref, outer_ref,
+    held_ref, push_ref, line_ref, slot_ref,
+    next_ref, up_ref, down_ref, next_inner_ref, next_outer_ref, back_ref, right_ref, left_ref,
 ):
     depth, length, width = post_ref.shape[1:]
     lines = depth * length
     slots = slot_ref.shape[0]
     halo = (below_ref, above_ref, inner_ref, outer_ref)
-    read = lambda z: streamed(place_ref, post_ref, *halo, z)
+    read = lambda z: streamed(post_ref, *halo, z)
     pushes = collide_levels(read, rates_ref, held_ref, next_ref, up_ref, down_ref)
+    back_ref[...] = jnp.zeros(back_ref.shape, f32)
+    right_ref[...] = jnp.zeros(right_ref.shape, f32)
+    left_ref[...] = jnp.zeros(left_ref.shape, f32)
+    for i in range(27):
+        cz, cx, cy = STEP[i]
+        if cx == 0:
+            continue
+        x = length - 1 if cx > 0 else 0
+        face_ref = right_ref if cx > 0 else left_ref
+        for z in range(depth):
+            if 0 <= z - cz < depth:
+                n = end_row(i, z, depth)
+                face_ref[n : n + 1] = next_ref[i, z - cz, x : x + 1]
+        if cz:
+            z = depth - 1 if cz > 0 else 0
+            back_ref[pl.ds(4 * device_at(cz, cx) + 2 + cy, 1)] = next_ref[i, z, x : x + 1]
+    even = lax.axis_index("gx") % 2 == 0
+    right, left = right_ref[...], left_ref[...]
+    next_inner_ref[...] = jnp.where(even, right, left)
+    next_outer_ref[...] = jnp.where(even, left, right)
     total = jnp.concatenate(
         [push_ref[k, z] + pushes[z][k] for k in range(3) for z in range(depth)], axis=0
     )
@@ -282,21 +328,22 @@
             shift = (k - a) * capacity % LANES
             turned = pltpu.roll(force[k], shift, 1) if shift else force[k]
             block = jnp.where(group == k, turned, block)
-        force_ref[pl.ds(a, tiles, stride=per_tile), :] = block
-
-
-def last_kernel(place_ref, post_ref, below_ref, above_ref, inner_ref, outer_ref, scaled_ref):
+        back_ref[pl.ds(4 * a, tiles, stride=4 * per_tile), :] = block
+
+
+def last_kernel(post_ref, below_ref, above_ref, inner_ref, outer_ref, back_ref, scaled_ref):
     for z in range(post_ref.shape[1]):
         halo = (below_ref, above_ref, inner_ref, outer_ref)
-        fields = streamed(place_ref, post_ref, *halo, z)
+        fields = streamed(post_ref, *halo, z, back_ref)
         for i in range(27):
             scaled_ref[i, z] = fields[i] * (1.0 / WEIGHT[i])
 
 
 def unpack_kernel(capacity, dest_ref, rank_ref, back_ref, force_ref):
-    devices, grains = back_ref.shape[0], dest_ref.shape[1]
+    devices, grains = back_ref.shape[0] // 4, dest_ref.shape[1]
     hot = jnp.where(iota((devices, grains), 0) == dest_ref[...], 1.0, 0.0).astype(bf16)
-    parts = jnp.concatenate([part.astype(f32) for part in split3(back_ref[...])], axis=1).T
+    back = back_ref[pl.ds(0, devices, stride=4), :]
+    parts = jnp.concatenate([part.astype(f32) for part in split3(back)], axis=1).T
     picked = jnp.dot(parts.astype(bf16), hot, preferred_element_type=f32)
     picked = picked[:LANES] + picked[LANES : 2 * LANES] + picked[2 * LANES :]
     at_rank = iota((capacity, grains), 0) == rank_ref[...]
@@ -305,18 +352,20 @@
         force_ref[k : k + 1] = jnp.sum(mine, axis=0, keepdims=True)
 
 
-def exchange_halo(place, post, up, down):
-    peers, length = lax.axis_size("gz"), lax.axis_size("gx")
+def swap_faces(up, down):
+    peers = lax.axis_size("gz")
     below = lax.ppermute(up, "gz", [(i, (i + 1) % peers) for i in range(peers)])
     above = lax.ppermute(down, "gz", [((i + 1) % peers, i) for i in range(peers)])
-    depth, width = post.shape[1], post.shape[3]
-    ends = jax.ShapeDtypeStruct((9 * depth, width), f32)
-    inner, outer = call(ends_kernel, [ends, ends], place, post, below, above, scalars=1)
+    return below, above
+
+
+def swap_ends(inner, outer):
+    length = lax.axis_size("gx")
     inner = lax.ppermute(inner, "gx", [(i, i ^ 1) for i in range(length)])
     outer = lax.ppermute(
         outer, "gx", [(i, (i + 1) % length if i % 2 else (i - 1) % length) for i in range(length)]
     )
-    return below, above, inner, outer
+    return inner, outer
 
 
 def per_device(populations, rates, grain_fraction, grain_velocity, grain_dest, grain_line):
@@ -328,37 +377,42 @@
     slots = devices * capacity
     shape = jax.ShapeDtypeStruct
     dest, line = grain_dest.reshape(1, grains), grain_line.reshape(1, grains)
-    place = jnp.stack(
-        [lax.axis_index("gz"), lax.axis_index("gx"), jnp.int32(lax.axis_size("gz"))]
-    ).astype(i32)
+    inputs = (dest, line, grain_velocity, grain_fraction)
     send, rank = call(
         functools.partial(pack_kernel, devices, capacity),
         [shape((devices, capacity + 1, width), bf16), shape((1, grains), i32)],
-        dest, line, grain_velocity, grain_fraction,
+        *inputs,
+        hbm=range(4), vmem=60,
+        scratch=[pltpu.VMEM(x.shape, x.dtype) for x in inputs] + [pltpu.SemaphoreType.DMA((4,))],
     )
     recv = lax.all_to_all(send, ("gz", "gx"), split_axis=0, concat_axis=0, tiled=True)
     state = shape(populations.shape, f32)
-    face = shape((9, length, width), f32)
+    face, ends = shape((9, length, width), f32), shape((9 * depth, width), f32)
     post, up, down, push, held, slot_line, slot_rows = call(
         functools.partial(first_kernel, capacity),
         [
             state, face, face, shape((3, depth, length, width), f32),
             shape((4 * lines, width), f32), shape((1, slots), i32), shape((slots, width), bf16),
         ],
-        rates, recv, populations, scalars=1,
-    )
-    halo = exchange_halo(place, post, up, down)
-    post, up, down, slot_force = call(
+        rates, recv, populations, smem=(0,),
+    )
+    below, above = swap_faces(up, down)
+    inner, outer = swap_ends(*call(ends_kernel, [ends, ends], post, below, above))
+    post, up, down, inner, outer, back = call(
         functools.partial(second_kernel, capacity),
-        [state, face, face, shape((devices, LANES), f32)],
-        place, rates, post, *halo, held, push, slot_line, slot_rows, scalars=2,
-    )
-    back = lax.all_to_all(slot_force, ("gz", "gx"), split_axis=0, concat_axis=0, tiled=True)
-    halo = exchange_halo(place, post, up, down)
-    (scaled,) = call(last_kernel, [state], place, post, *halo, scalars=1)
+        [state, face, face, ends, ends, shape((4 * devices, LANES), f32)],
+        rates, post, below, above, inner, outer, held, push, slot_line, slot_rows,
+        smem=(0,), scratch=[pltpu.VMEM(ends.shape, f32)] * 2,
+    )
+    back = lax.all_to_all(
+        back.reshape(devices, 4, LANES), ("gz", "gx"), split_axis=0, concat_axis=0, tiled=True
+    ).reshape(4 * devices, LANES)
+    below, above = swap_faces(up, down)
+    inner, outer = swap_ends(inner, outer)
     (grain_force,) = call(
         functools.partial(unpack_kernel, capacity), [shape((3, grains), f32)], dest, rank, back
     )
+    (scaled,) = call(last_kernel, [state], post, below, above, inner, outer, back)
     return (scaled, grain_force)
 
 

time: 52.9 us -> 48.3 us (0.913)
  blocking collectives: 0 us -> 19.5 us
  waiting for transfers between devices: 21.2 us -> 6.71 us
  starting transfers between devices: 20 us -> 13.9 us
  local copies, waits for them, and re-layouts: 2.96 us -> 0.02 us
    all_to_all x0 -> x1, blocking collectives: none -> 19.5 us  [per_device(): lax.all_to_all(send, ('gz', 'gx'), split_axis=0, concat_axis=0, tiled=True)]
    all_to_all x2 -> x1, waiting for transfers between devices: 14.8 us -> 0.67 us  [per_device(): lax.all_to_all(back.reshape(devices, 4, LANES), ('gz', 'gx'), split_axis=...]
    all_to_all x2 -> x1, starting transfers between devices: 9.85 us -> 3.29 us  [per_device(): lax.all_to_all(back.reshape(devices, 4, LANES), ('gz', 'gx'), split_axis=...]
    unnamed x12 -> x8, local copies, waits for them, and re-layouts: 2.96 us -> 0.02 us
    pallas_call x7 -> x6, Pallas kernels: 7.52 us -> 7.13 us  [call(): pl.pallas_call(kernel, out_shape=list(outs), in_specs=[pl.BlockSpec(memor...]
  transfers between devices with their start and end apart: 10 -> 9, of which waited for: 6 -> 4; matrix products, arithmetic and copies ran while one was open for 0% -> 0% of each run, Pallas kernels for 3% -> 2%
where the time goes in v2:
time: 48.3 us; the launch traced here: 48 us
  blocking collectives  19.5 us (40%)
  starting transfers between devices  13.9 us (29%)
  Pallas kernels  7.13 us (15%)
  waiting for transfers between devices  6.71 us (14%)
  between operations  0.72 us (1%)
    all_to_all x1, blocking collectives, per_device(): lax.all_to_all(send, ('gz', 'gx'), split_axis=0, concat_axis=0, tiled=True)  19.5 us
    pallas_call x6, Pallas kernels, call(): pl.pallas_call(kernel, out_shape=list(outs), in_specs=[pl.BlockSpec(memor...  7.13 us
    ppermute x2, starting transfers between devices, swap_ends(): lax.ppermute(outer, 'gx', [(i, (i + 1) % length if i % 2 else (i - 1) % l...  4.62 us
    ppermute x2, starting transfers between devices, swap_faces(): lax.ppermute(down, 'gz', [((i + 1) % peers, i) for i in range(peers)])  4.07 us
    ppermute x2, waiting for transfers between devices, swap_ends(): lax.ppermute(outer, 'gx', [(i, (i + 1) % length if i % 2 else (i - 1) % l...  3.82 us
    all_to_all x1, starting transfers between devices, per_device(): lax.all_to_all(back.reshape(devices, 4, LANES), ('gz', 'gx'), split_axis=...  3.29 us
    ppermute x2, waiting for transfers between devices, swap_faces(): below = lax.ppermute(up, 'gz', [(i, (i + 1) % peers) for i in range(peers)])  1.93 us
    ppermute x2, starting transfers between devices, swap_faces(): below = lax.ppermute(up, 'gz', [(i, (i + 1) % peers) for i in range(peers)])  1.88 us
  transfers between devices with their start and end apart: 9, of which 4 were waited for; matrix products, arithmetic and copies ran while one was open for 0% of the time, Pallas kernels for 2%

profile of v2, /device:TPU:0, one launch (start us, length us, event | category | flops | bytes accessed | tf_op | source)
XLA Modules:
  0.0 48.0 jit_solution(12281805929795771700)
XLA Ops:
  0.6 2.5 %shard_map.77 = (bf16[32,33,128]{2,1,0:T(8,128)(2,1)}, s32[1,512]{1,0:T(1,128)}) custom-call(s32[1,512]{1,0:T(1,128)} %bitcast.6, s32[1,512]{1,0:T(1,128)} %bitcast.8, bf16[3,512]{1,0:T(4,128)(2,1)} %refs_2_.1, bf16[512,128]{1,0:T(8,128)(2,1)} %refs_3_.1), custom_call_target="tpu_custom_call" | custom-call | bytes 410624 | tf_op jit(solution)/shard_map/pallas_call | solution.py:28
  3.2 0.0 copy-start
  3.2 0.0 copy-start.3
  3.2 19.5 %all_to_all.10.recv_ref = bf16[32,33,128]{2,1,0:T(8,128)(2,1)S(1)} all-to-all(bf16[32,33,128]{2,1,0:T(8,128)(2,1)} %get-tuple-element.19), channel_id=1, replica_groups=mesh['gz'=4,'gx'=8] {'gz','gx'}, dimensions={0} | all-to-all | bytes 540672 | tf_op jit(solution)/shard_map/all_to_all | solution.py:388
  22.6 0.0 copy-done
  22.7 0.0 copy-done.3
  22.7 1.1 %shard_map.78 = (f32[27,2,8,128]{3,2,1,0:T(8,128)S(1)}, f32[9,8,128]{2,1,0:T(8,128)S(1)}, f32[9,8,128]{2,1,0:T(8,128)S(1)}, f32[3,2,8,128]{3,2,1,0:T(8,128)S(1)}...) custom-call(f32[27]{0:T(128)S(1)} %copy-done.3, ...), custom_call_target="tpu_custom_call" | custom-call | bytes 1110124 | tf_op jit(solution)/shard_map/pallas_call | solution.py:28
  23.7 0.1 collective-permute-start
  23.8 2.9 %collective-permute-start.1 = (f32[9,8,128]{2,1,0:T(8,128)S(1)}, f32[9,8,128]{2,1,0:T(8,128)S(1)}, u32[]{:S(2)}, u32[]{:S(2)}) collective-permute-start(f32[9,8,128]{2,1,0:T(8,128)S(1)} %get-tuple-element.22), channel_id=1, source_target_pairs={{8,0},{16,8},{24,16},{0,24},{9,1},{17,9},{25,17},{1,25},{10,2},{18... | collective-permute-start | bytes 110600 | tf_op jit(solution)/shard_map/ppermute | solution.py:358
  26.7 1.9 %collective-permute-done.below_ref = f32[9,8,128]{2,1,0:T(8,128)S(1)} collective-permute-done((f32[9,8,128]{2,1,0:T(8,128)S(1)}, f32[9,8,128]{2,1,0:T(8,128)S(1)}, u32[]{:S(2)}, u32[]{:S(2)}) %collective-permute-start) | collective-permute-done | bytes 36896 | tf_op jit(solution)/shard_map/ppermute | solution.py:357
  28.6 0.0 collective-permute-done.1.above_ref
  28.7 0.1 collective-permute-start.2
  28.7 0.9 %collective-permute-start.3 = (f32[18,128]{1,0:T(8,128)S(1)}, f32[18,128]{1,0:T(8,128)S(1)}, u32[]{:S(2)}, u32[]{:S(2)}) collective-permute-start(f32[18,128]{1,0:T(8,128)S(1)} %get-tuple-element.24), channel_id=1, source_target_pairs={{0,7},{1,2},{2,1},{3,4},{4,3},{5,6},{6,5},{7,0},{8,15},{9,10},{10,... | collective-permute-start | bytes 27656 | tf_op jit(solution)/shard_map/ppermute | solution.py:365
  29.6 0.3 collective-permute-done.2.inner_ref
  29.9 3.8 %collective-permute-done.3.outer_ref = f32[18,128]{1,0:T(8,128)S(1)} collective-permute-done((f32[18,128]{1,0:T(8,128)S(1)}, f32[18,128]{1,0:T(8,128)S(1)}, u32[]{:S(2)}, u32[]{:S(2)}) %collective-permute-start.3) | collective-permute-done | bytes 9248 | tf_op jit(solution)/shard_map/ppermute | solution.py:365
  33.7 1.8 %shard_map.80 = (f32[27,2,8,128]{3,2,1,0:T(8,128)S(1)}, f32[9,8,128]{2,1,0:T(8,128)S(1)}, f32[9,8,128]{2,1,0:T(8,128)S(1)}, f32[18,128]{1,0:T(8,128)S(1)}, f32[18,128]{1,0:T(8,128)S(1)}, /*index=5*/f32[128,128]{1,0:T(8,128)}) custom-call(f32[27]{0:T(128)S(1)} %copy-done.3, f32[27,2,8,128]{3,2,1,0:T(8,128)S(1)} %get-tuple-element.20.post_ref, ...), custom_call_target="tpu_custom_call" | custom-call | bytes 1015916 | tf_op jit(solution)/shard_map/pallas_call | solution.py:28
  35.5 3.3 %all-to-all-start.1 = ((f32[32,4,128]{2,1,0:T(4,128)}), f32[32,4,128]{2,1,0:T(4,128)S(1)}, u32[]{:S(2)}, u32[]{:S(2)}) async-start(f32[32,4,128]{2,1,0:T(4,128)} %bitcast.2), calls=%async_computation.1 | async-start | bytes 131072 | tf_op jit(solution)/shard_map/all_to_all | solution.py:407
  38.8 1.8 %collective-permute-start.4 = (f32[9,8,128]{2,1,0:T(8,128)S(1)}, f32[9,8,128]{2,1,0:T(8,128)S(1)}, u32[]{:S(2)}, u32[]{:S(2)}) collective-permute-start(f32[9,8,128]{2,1,0:T(8,128)S(1)} %get-tuple-element.30), channel_id=1, source_target_pairs={{0,8},{8,16},{16,24},{24,0},{1,9},{9,17},{17,25},{25,1},{2,10},{10... | collective-permute-start | bytes 110600 | tf_op jit(solution)/shard_map/ppermute | solution.py:357
  40.6 1.2 %collective-permute-start.5 = (f32[9,8,128]{2,1,0:T(8,128)S(1)}, f32[9,8,128]{2,1,0:T(8,128)S(1)}, u32[]{:S(2)}, u32[]{:S(2)}) collective-permute-start(f32[9,8,128]{2,1,0:T(8,128)S(1)} %get-tuple-element.31), channel_id=1, source_target_pairs={{8,0},{16,8},{24,16},{0,24},{9,1},{17,9},{25,17},{1,25},{10,2},{18... | collective-permute-start | bytes 110600 | tf_op jit(solution)/shard_map/ppermute | solution.py:358
  41.8 0.0 collective-permute-start.6
  41.8 0.0 copy-start.2
  41.8 0.0 copy-start.1
  41.8 3.7 %collective-permute-start.7 = (f32[18,128]{1,0:T(8,128)S(1)}, f32[18,128]{1,0:T(8,128)S(1)}, u32[]{:S(2)}, u32[]{:S(2)}) collective-permute-start(f32[18,128]{1,0:T(8,128)S(1)} %get-tuple-element.33), channel_id=1, source_target_pairs={{0,7},{1,2},{2,1},{3,4},{4,3},{5,6},{6,5},{7,0},{8,15},{9,10},{10,... | collective-permute-start | bytes 27656 | tf_op jit(solution)/shard_map/ppermute | solution.py:365
  45.5 0.7 %all-to-all-done.1 = f32[32,4,128]{2,1,0:T(4,128)S(1)} async-done(((f32[32,4,128]{2,1,0:T(4,128)}), f32[32,4,128]{2,1,0:T(4,128)S(1)}, u32[]{:S(2)}, u32[]{:S(2)}) %all-to-all-start.1) | async-done | bytes 65568 | tf_op jit(solution)/shard_map/all_to_all | solution.py:407
  46.2 0.0 copy-done.2
  46.2 0.0 copy-done.1
  46.2 0.9 %shard_map.82 = f32[3,512]{1,0:T(4,128)} custom-call(s32[1,512]{1,0:T(1,128)S(1)} %bitcast.7, s32[1,512]{1,0:T(1,128)S(1)} %copy-done.2, f32[128,128]{1,0:T(8,128)S(1)} %bitcast.4), custom_call_target="tpu_custom_call" | custom-call | bytes 75776 | tf_op jit(solution)/shard_map/pallas_call | solution.py:28
  47.1 0.0 collective-permute-done.6.inner_ref
  47.1 0.0 collective-permute-done.7.outer_ref
  47.1 0.0 collective-permute-done.4.below_ref
  47.1 0.0 collective-permute-done.5.above_ref
  47.1 0.8 %shard_map.81 = f32[27,2,8,128]{3,2,1,0:T(8,128)} custom-call(f32[27,2,8,128]{3,2,1,0:T(8,128)S(1)} %get-tuple-element.29.post_ref, f32[9,8,128]{2,1,0:T(8,128)S(1)} %collective-permute-done.4.below_ref, f32[9,8,128]{2,1,0:T(8,128)S(1)} %collective-permute-done.5.above_ref, f32[18,128]{1,0:T(8,128)S(1)} %collective-permute-done.6.inner_ref, ...), custom_call_target="tpu_custom_call" | custom-call | bytes 600064 | tf_op jit(solution)/shard_map/pallas_call | solution.py:28
  (1 shorter events, 0.0 us)
Async XLA Ops:
  3.2 19.5 %copy-start = (f32[27,2,8,128]{3,2,1,0:T(8,128)S(1)}, f32[27,2,8,128]{3,2,1,0:T(8,128)}, u32[]{:S(2)}) copy-start(f32[27,2,8,128]{3,2,1,0:T(8,128)} %fields_ref.1) | copy-start | bytes 663556
  3.2 19.5 %copy-start.3 = (f32[27]{0:T(128)S(1)}, f32[27]{0:T(128)}, u32[]{:S(2)}) copy-start(f32[27]{0:T(128)} %rates_ref.3) | copy-start | bytes 328
  23.7 4.9 %collective-permute-start = (f32[9,8,128]{2,1,0:T(8,128)S(1)}, f32[9,8,128]{2,1,0:T(8,128)S(1)}, u32[]{:S(2)}, u32[]{:S(2)}) collective-permute-start(f32[9,8,128]{2,1,0:T(8,128)S(1)} %get-tuple-element.21), channel_id=1, source_target_pairs={{0,8},{8,16},{16,24},{24,0},{1,9},{9,17},{17,25},{25,1},{2,10},{10... | collective-permute-start | bytes 110600 | tf_op jit(solution)/shard_map/ppermute | solution.py:357
  23.8 4.8 %collective-permute-start.1 = (f32[9,8,128]{2,1,0:T(8,128)S(1)}, f32[9,8,128]{2,1,0:T(8,128)S(1)}, u32[]{:S(2)}, u32[]{:S(2)}) collective-permute-start(f32[9,8,128]{2,1,0:T(8,128)S(1)} %get-tuple-element.22), channel_id=1, source_target_pairs={{8,0},{16,8},{24,16},{0,24},{9,1},{17,9},{25,17},{1,25},{10,2},{18... | collective-permute-start | bytes 110600 | tf_op jit(solution)/shard_map/ppermute | solution.py:358
  28.7 1.2 %collective-permute-start.2 = (f32[18,128]{1,0:T(8,128)S(1)}, f32[18,128]{1,0:T(8,128)S(1)}, u32[]{:S(2)}, u32[]{:S(2)}) collective-permute-start(f32[18,128]{1,0:T(8,128)S(1)} %get-tuple-element.23), channel_id=1, source_target_pairs={{0,1},{1,0},{2,3},{3,2},{4,5},{5,4},{6,7},{7,6},{8,9},{9,8},{10,11... | collective-permute-start | bytes 27656 | tf_op jit(solution)/shard_map/ppermute | solution.py:364
  28.7 5.0 %collective-permute-start.3 = (f32[18,128]{1,0:T(8,128)S(1)}, f32[18,128]{1,0:T(8,128)S(1)}, u32[]{:S(2)}, u32[]{:S(2)}) collective-permute-start(f32[18,128]{1,0:T(8,128)S(1)} %get-tuple-element.24), channel_id=1, source_target_pairs={{0,7},{1,2},{2,1},{3,4},{4,3},{5,6},{6,5},{7,0},{8,15},{9,10},{10,... | collective-permute-start | bytes 27656 | tf_op jit(solution)/shard_map/ppermute | solution.py:365
  35.5 10.7 %all-to-all-start.1 = ((f32[32,4,128]{2,1,0:T(4,128)}), f32[32,4,128]{2,1,0:T(4,128)S(1)}, u32[]{:S(2)}, u32[]{:S(2)}) async-start(f32[32,4,128]{2,1,0:T(4,128)} %bitcast.2), calls=%async_computation.1 | async-start | bytes 131072 | tf_op jit(solution)/shard_map/all_to_all | solution.py:407
  38.8 8.3 %collective-permute-start.4 = (f32[9,8,128]{2,1,0:T(8,128)S(1)}, f32[9,8,128]{2,1,0:T(8,128)S(1)}, u32[]{:S(2)}, u32[]{:S(2)}) collective-permute-start(f32[9,8,128]{2,1,0:T(8,128)S(1)} %get-tuple-element.30), channel_id=1, source_target_pairs={{0,8},{8,16},{16,24},{24,0},{1,9},{9,17},{17,25},{25,1},{2,10},{10... | collective-permute-start | bytes 110600 | tf_op jit(solution)/shard_map/ppermute | solution.py:357
  40.6 6.5 %collective-permute-start.5 = (f32[9,8,128]{2,1,0:T(8,128)S(1)}, f32[9,8,128]{2,1,0:T(8,128)S(1)}, u32[]{:S(2)}, u32[]{:S(2)}) collective-permute-start(f32[9,8,128]{2,1,0:T(8,128)S(1)} %get-tuple-element.31), channel_id=1, source_target_pairs={{8,0},{16,8},{24,16},{0,24},{9,1},{17,9},{25,17},{1,25},{10,2},{18... | collective-permute-start | bytes 110600 | tf_op jit(solution)/shard_map/ppermute | solution.py:358
  41.8 5.3 %collective-permute-start.6 = (f32[18,128]{1,0:T(8,128)S(1)}, f32[18,128]{1,0:T(8,128)S(1)}, u32[]{:S(2)}, u32[]{:S(2)}) collective-permute-start(f32[18,128]{1,0:T(8,128)S(1)} %get-tuple-element.32), channel_id=1, source_target_pairs={{0,1},{1,0},{2,3},{3,2},{4,5},{5,4},{6,7},{7,6},{8,9},{9,8},{10,11... | collective-permute-start | bytes 27656 | tf_op jit(solution)/shard_map/ppermute | solution.py:364
  41.8 4.4 %copy-start.2 = (s32[1,512]{1,0:T(1,128)S(1)}, s32[1,512]{1,0:T(1,128)}, u32[]{:S(2)}) copy-start(s32[1,512]{1,0:T(1,128)} %get-tuple-element.35.rank_ref) | copy-start | bytes 6148
  41.8 4.4 %copy-start.1 = (s32[512,1]{0,1:T(1,128)S(1)}, s32[512,1]{0,1:T(1,128)}, u32[]{:S(2)}) copy-start(s32[512,1]{0,1:T(1,128)} %param.10) | copy-start | bytes 6148
  41.8 5.3 %collective-permute-start.7 = (f32[18,128]{1,0:T(8,128)S(1)}, f32[18,128]{1,0:T(8,128)S(1)}, u32[]{:S(2)}, u32[]{:S(2)}) collective-permute-start(f32[18,128]{1,0:T(8,128)S(1)} %get-tuple-element.33), channel_id=1, source_target_pairs={{0,7},{1,2},{2,1},{3,4},{4,3},{5,6},{6,5},{7,0},{8,15},{9,10},{10,... | collective-permute-start | bytes 27656 | tf_op jit(solution)/shard_map/ppermute | solution.py:365

commit v3 on v2

v3 whole, which is shorter than its diff:
```python
import functools

import jax
import jax.numpy as jnp
import numpy as np
from jax import lax
from jax.experimental import pallas as pl
from jax.experimental.pallas import tpu as pltpu
from jax.sharding import PartitionSpec as P

STEPS = 2
LANES = 128
f32, bf16, i32 = jnp.float32, jnp.bfloat16, jnp.int32
DIGITS = [(i // 9, i // 3 % 3, i % 3) for i in range(27)]
STEP = [tuple(d - 1 for d in digits) for digits in DIGITS]
WEIGHT = [(8.0 / 27, 2.0 / 27, 1.0 / 54, 1.0 / 216)[sum(abs(s) for s in step)] for step in STEP]


def iota(shape, dim):
    return lax.broadcasted_iota(i32, shape, dim)


def call(kernel, outs, *operands, smem=(), hbm=(), hbm_out=(), scratch=(), vmem=24):
    space = [pltpu.SMEM if n in smem else pltpu.HBM if n in hbm else pltpu.VMEM for n in range(len(operands))]
    size = sum(o.size * o.dtype.itemsize for o in operands) + sum(
        int(np.prod(o.shape)) * o.dtype.itemsize for o in outs
    )
    return pl.pallas_call(
        kernel,
        out_shape=list(outs),
        in_specs=[pl.BlockSpec(memory_space=where) for where in space],
        out_specs=[
            pl.BlockSpec(memory_space=pltpu.HBM if n in hbm_out else pltpu.VMEM) for n in range(len(outs))
        ],
        scratch_shapes=list(scratch),
        compiler_params=pltpu.CompilerParams(vmem_limit_bytes=vmem * 1024 * 1024),
        cost_estimate=pl.CostEstimate(flops=0, bytes_accessed=size, transcendentals=0),
    )(*operands)


def device_at(step_z, step_x):
    depth, length = lax.axis_size("gz"), lax.axis_size("gx")
    z = lax.rem(lax.axis_index("gz") + step_z + depth, depth)
    x = lax.rem(lax.axis_index("gx") + step_x + length, length)
    return z * length + x


def split3(x):
    high = x.astype(bf16)
    rest = x - high.astype(f32)
    mid = rest.astype(bf16)
    return high, mid, (rest - mid.astype(f32)).astype(bf16)


def pack_kernel(devices, capacity, parts, *refs):
    sources, (send_ref, rank_ref), held = refs[:4], refs[4:6], refs[6:10]
    staged_ref, rows_ref, sem, out_sem = refs[10:]
    copies = [pltpu.make_async_copy(sources[n], held[n], sem.at[n]) for n in range(4)]
    for copy in copies:
        copy.start()
    dest_ref, line_ref, speed_ref, fraction_ref = held
    grains, width = fraction_ref.shape
    block = capacity + 2
    copies[0].wait()
    dest = dest_ref[...]
    hot = jnp.where(iota((devices, grains), 0) == dest, 1.0, 0.0)
    earlier = jnp.where(iota((LANES, LANES), 0) < iota((LANES, LANES), 1), 1.0, 0.0).astype(bf16)
    total = jnp.zeros((devices, 1), f32)
    ranks = []
    for start in range(0, grains, LANES):
        part = hot[:, start : start + LANES]
        before = jnp.dot(part.astype(bf16), earlier, preferred_element_type=f32) + total
        ranks.append(jnp.sum(part * before, axis=0, keepdims=True))
        total = total + jnp.sum(part, axis=1, keepdims=True)
    rank = jnp.concatenate(ranks, axis=1).astype(i32)
    rank_ref[...] = rank
    position = dest * block + rank
    copies[1].wait()
    copies[2].wait()
    speed = speed_ref[...].astype(f32)
    values = [speed[0:1], speed[1:2], speed[2:3], line_ref[...].astype(f32)]
    at_rank = iota((capacity, grains), 0) == rank
    facts = [jnp.where(at_rank, value, 0.0) for value in values]
    if 4 * capacity < width:
        facts.append(jnp.zeros((width - 4 * capacity, grains), f32))
    fact_rows = lax.dot_general(
        hot.astype(bf16),
        jnp.concatenate(facts, axis=0).astype(bf16),
        (((1,), (1,)), ((), ())),
        preferred_element_type=f32,
    )
    copies[3].wait()
    fraction = fraction_ref[...]
    size, some = devices * block // parts, devices // parts
    out = []
    for n in range(parts):
        place = jnp.where(iota((size, grains), 0) == position - n * size, 1.0, 0.0).astype(bf16)
        rows_ref[n] = jnp.dot(place, fraction, preferred_element_type=f32)
        rows_ref[n, pl.ds(capacity, some, stride=block), :] = fact_rows[n * some : (n + 1) * some]
        staged_ref[n * size : (n + 1) * size] = rows_ref[n].astype(bf16)
        rows = pl.ds(n * size, size)
        out.append(pltpu.make_async_copy(staged_ref.at[rows], send_ref.at[rows], out_sem.at[n]))
        out[n].start()
    for copy in out:
        copy.wait()


def total_of(values):
    return functools.reduce(lambda a, b: a + b, values)


def along(speed, i):
    return total_of([v if s > 0 else -v for s, v in zip(STEP[i], speed) if s])


def relax(fields, rate):
    density = total_of(fields)
    momentum = [
        total_of([fields[i] for i in range(27) if STEP[i][axis] == 1])
        - total_of([fields[i] for i in range(27) if STEP[i][axis] == -1])
        for axis in range(3)
    ]
    inverse = 1.0 / density
    speed = [m * inverse for m in momentum]
    base = 1.0 - 1.5 * total_of([v * v for v in speed])
    departure = [None] * 27
    for i in range(13, 27):
        scale = WEIGHT[i] * density
        if i == 13:
            departure[i] = fields[i] - scale * base
            continue
        dot = along(speed, i)
        even, odd = scale * (base + 4.5 * dot * dot), scale * (3.0 * dot)
        departure[i] = fields[i] - (even + odd)
        departure[26 - i] = fields[26 - i] - (even - odd)
    moments = list(departure)
    for stride in (1, 3, 9):
        for i in range(27):
            if i // stride % 3 == 0:
                low, mid, high = moments[i], moments[i + stride], moments[i + 2 * stride]
                both = low + high
                moments[i], moments[i + stride], moments[i + 2 * stride] = both + mid, high - low, both
    moments = [rate[a] * moments[a] for a in range(27)]
    for stride in (9, 3, 1):
        for i in range(27):
            if i // stride % 3 == 0:
                m0, m1, m2 = moments[i], moments[i + stride], moments[i + 2 * stride]
                half1, half2 = 0.5 * m1, 0.5 * m2
                moments[i], moments[i + stride], moments[i + 2 * stride] = half2 - half1, m0 - m2, half2 + half1
    kept = [fields[i] - moments[i] for i in range(27)]
    swapped = [departure[26 - i] - kept[i] for i in range(27)]
    return density, momentum, kept, swapped


def exchange(density, momentum, kept, swapped, solid, carried):
    inverse = 1.0 / (1.0 + solid)
    share = solid * inverse
    speed = [c * inverse for c in carried]
    base = 1.0 - 1.5 * total_of([v * v for v in speed])
    push = [(density * v - m) * inverse for v, m in zip(speed, momentum)]
    post = [None] * 27
    for i in range(13, 27):
        scale = WEIGHT[i] * density
        if i == 13:
            post[i] = kept[i] + share * (swapped[i] + scale * base)
            continue
        dot = along(speed, i)
        even, odd = scale * (base + 4.5 * dot * dot), scale * (3.0 * dot)
        post[i] = kept[i] + share * (swapped[i] + (even + odd))
        post[26 - i] = kept[26 - i] + share * (swapped[26 - i] + (even - odd))
    return post, push


def grains_at(held_ref, z, depth, length):
    lines = depth * length
    first = [held_ref[k * lines + z * length : k * lines + (z + 1) * length, :] for k in range(4)]
    return first[0], first[1:]


def store_post(post, z, post_ref, up_ref, down_ref):
    for i in range(27):
        post_ref[i, z] = post[i]
        if STEP[i][0] == 1 and z == post_ref.shape[1] - 1:
            up_ref[i - 18] = post[i]
        if STEP[i][0] == -1 and z == 0:
            down_ref[i] = post[i]


def relax_kernel(rates_ref, fields_ref, kept_ref, swapped_ref, sums_ref):
    rate = [rates_ref[a] for a in range(27)]
    for z in range(fields_ref.shape[1]):
        density, momentum, kept, swapped = relax([fields_ref[i, z] for i in range(27)], rate)
        for n, value in enumerate([density] + momentum):
            sums_ref[n, z] = value
        for i in range(27):
            kept_ref[i, z] = kept[i]
            swapped_ref[i, z] = swapped[i]


def first_kernel(
    devices, capacity, recv_ref, kept_ref, swapped_ref, sums_ref,
    post_ref, up_ref, down_ref, push_ref, held_ref, line_ref, slot_ref, wide_ref,
):
    width = recv_ref.shape[1]
    block, slots = capacity + 2, devices * capacity
    depth, length = kept_ref.shape[1], kept_ref.shape[2]
    lines = depth * length
    wide_ref[...] = recv_ref[...].astype(f32)
    facts = wide_ref[pl.ds(capacity, devices, stride=block), :]
    slot_rows = jnp.concatenate(
        [wide_ref[j * block : j * block + capacity] for j in range(devices)], axis=0
    ).astype(bf16)
    slot_ref[...] = slot_rows
    group = iota((devices, width), 1) // capacity
    stacked = jnp.concatenate([jnp.where(group == m, facts, 0.0) for m in range(4)], axis=0)
    spread = jnp.where(
        iota((width, slots), 0) % capacity == iota((width, slots), 1) % capacity, 1.0, 0.0
    ).astype(bf16)
    wide = jnp.dot(stacked.astype(bf16), spread, preferred_element_type=f32)
    own = iota((devices, slots), 0) == iota((devices, slots), 1) // capacity
    fact = [
        jnp.sum(jnp.where(own, wide[m * devices : (m + 1) * devices], 0.0), axis=0, keepdims=True)
        for m in range(4)
    ]
    line_ref[...] = fact[3].astype(i32)
    on_line = iota((lines, slots), 0) == fact[3].astype(i32)
    gather = [jnp.where(on_line, 1.0, 0.0)] + [jnp.where(on_line, fact[k], 0.0) for k in range(3)]
    held_ref[...] = jnp.dot(
        jnp.concatenate(gather, axis=0).astype(bf16), slot_rows, preferred_element_type=f32
    )
    for z in range(depth):
        sums = [sums_ref[n, z] for n in range(4)]
        kept, swapped = [kept_ref[i, z] for i in range(27)], [swapped_ref[i, z] for i in range(27)]
        grains = grains_at(held_ref, z, depth, length)
        post, push = exchange(sums[0], sums[1:], kept, swapped, *grains)
        store_post(post, z, post_ref, up_ref, down_ref)
        for k in range(3):
            push_ref[k, z] = push[k]


def turn_kernel(slot_ref, dest_ref, rank_ref, turned_ref, hot_ref, at_rank_ref):
    turned_ref[...] = slot_ref[...].astype(f32).T.astype(bf16)
    hot_ref[...] = jnp.where(iota(hot_ref.shape, 0) == dest_ref[...], 1.0, 0.0).astype(bf16)
    at_rank_ref[...] = jnp.where(iota(at_rank_ref.shape, 0) == rank_ref[...], 1.0, 0.0)


def ends_kernel(post_ref, below_ref, above_ref, inner_ref, outer_ref):
    depth, length = post_ref.shape[1], post_ref.shape[2]
    even = lax.axis_index("gx") % 2 == 0

    def row(i, z, x):
        source = z - STEP[i][0]
        if source < 0:
            return below_ref[i - 18, x : x + 1]
        if source >= depth:
            return above_ref[i, x : x + 1]
        return post_ref[i, source, x : x + 1]

    for i in range(27):
        if STEP[i][1] != 1:
            continue
        j = i - 6
        for z in range(depth):
            n = end_row(i, z, depth)
            right, left = row(i, z, length - 1), row(j, z, 0)
            inner_ref[n : n + 1] = jnp.where(even, right, left)
            outer_ref[n : n + 1] = jnp.where(even, left, right)


def end_row(i, z, depth):
    return ((STEP[i][0] + 1) * 3 + STEP[i][2] + 1) * depth + z


def streamed(post_ref, below_ref, above_ref, inner_ref, outer_ref, z, back_ref=None, part=range(27)):
    depth, length, width = post_ref.shape[1:]
    even = lax.axis_index("gx") % 2 == 0
    rows = iota((length, width), 0)
    moved_list = []
    for i in part:
        cz, cx, cy = STEP[i]
        source = z - cz
        inside = 0 <= source < depth
        if source < 0:
            moved = below_ref[i - 18]
        elif source >= depth:
            moved = above_ref[i]
        else:
            moved = post_ref[i, source]
        if cx:
            n = end_row(i, z, depth)
            inner, outer = inner_ref[n : n + 1], outer_ref[n : n + 1]
            edge = jnp.where(even, outer, inner) if cx > 0 else jnp.where(even, inner, outer)
            if not inside and back_ref is not None:
                edge = back_ref[pl.ds(4 * device_at(-cz, -cx) + 2 + cy, 1)]
            moved = pltpu.roll(moved, cx % length, 0)
            moved = jnp.where(rows == (0 if cx > 0 else length - 1), edge, moved)
        if cy:
            moved = pltpu.roll(moved, cy % width, 1)
        if source < 0:
            moved = jnp.where(lax.axis_index("gz") == 0, post_ref[26 - i, z], moved)
        elif source >= depth:
            top = lax.axis_size("gz") - 1
            moved = jnp.where(lax.axis_index("gz") == top, post_ref[26 - i, z], moved)
        moved_list.append(moved)
    return moved_list


def second_kernel(
    capacity, rates_ref, post_ref, below_ref, above_ref, inner_ref, outer_ref,
    held_ref, push_ref, line_ref, turned_ref,
    next_ref, up_ref, down_ref, next_inner_ref, next_outer_ref, back_ref, right_ref, left_ref,
):
    depth, length, width = post_ref.shape[1:]
    lines = depth * length
    slots = turned_ref.shape[1]
    halo = (below_ref, above_ref, inner_ref, outer_ref)
    rate = [rates_ref[a] for a in range(27)]
    pushes = []
    for z in range(depth):
        relaxed = relax(streamed(post_ref, *halo, z), rate)
        post, push = exchange(*relaxed, *grains_at(held_ref, z, depth, length))
        store_post(post, z, next_ref, up_ref, down_ref)
        pushes.append(push)
    back_ref[...] = jnp.zeros(back_ref.shape, f32)
    right_ref[...] = jnp.zeros(right_ref.shape, f32)
    left_ref[...] = jnp.zeros(left_ref.shape, f32)
    for i in range(27):
        cz, cx, cy = STEP[i]
        if cx == 0:
            continue
        x = length - 1 if cx > 0 else 0
        face_ref = right_ref if cx > 0 else left_ref
        for z in range(depth):
            if 0 <= z - cz < depth:
                n = end_row(i, z, depth)
                face_ref[n : n + 1] = next_ref[i, z - cz, x : x + 1]
        if cz:
            z = depth - 1 if cz > 0 else 0
            back_ref[pl.ds(4 * device_at(cz, cx) + 2 + cy, 1)] = next_ref[i, z, x : x + 1]
    even = lax.axis_index("gx") % 2 == 0
    right, left = right_ref[...], left_ref[...]
    next_inner_ref[...] = jnp.where(even, right, left)
    next_outer_ref[...] = jnp.where(even, left, right)
    total = jnp.concatenate(
        [push_ref[k, z] + pushes[z][k] for k in range(3) for z in range(depth)], axis=0
    )
    along_y = jnp.dot(
        jnp.concatenate(split3(total), axis=0), turned_ref[...], preferred_element_type=f32
    )
    along_y = along_y[: 3 * lines] + along_y[3 * lines : 6 * lines] + along_y[6 * lines :]
    on_line = iota((lines, slots), 0) == line_ref[...]
    tiles, per_tile = slots // LANES, LANES // capacity
    group = iota((tiles, LANES), 1) // capacity
    force = []
    for k in range(3):
        picked = -jnp.sum(jnp.where(on_line, along_y[k * lines : (k + 1) * lines], 0.0), axis=0, keepdims=True)
        force.append(
            jnp.concatenate([picked[:, t * LANES : (t + 1) * LANES] for t in range(tiles)], axis=0)
        )
    for a in range(per_tile):
        block = jnp.zeros((tiles, LANES), f32)
        for k in range(3):
            shift = (k - a) * capacity % LANES
            turned = pltpu.roll(force[k], shift, 1) if shift else force[k]
            block = jnp.where(group == k, turned, block)
        back_ref[pl.ds(4 * a, tiles, stride=4 * per_tile), :] = block


def last_kernel(
    capacity, post_ref, below_ref, above_ref, inner_ref, outer_ref, back_ref, hot_ref, at_rank_ref,
    scaled_ref, force_ref, staged_ref, sem,
):
    depth = post_ref.shape[1]
    halo = (below_ref, above_ref, inner_ref, outer_ref)
    copies = []
    for cz in (0, 1, -1):
        part = [i for i in range(27) if STEP[i][0] == cz]
        for z in range(depth):
            for i, field in zip(part, streamed(post_ref, *halo, z, back_ref, part)):
                staged_ref[i, z] = field * (1.0 / WEIGHT[i])
        rows = pl.ds(part[0], len(part))
        copies.append(pltpu.make_async_copy(staged_ref.at[rows], scaled_ref.at[rows], sem.at[cz + 1]))
        copies[-1].start()
    back = back_ref[pl.ds(0, hot_ref.shape[0], stride=4), :]
    parts = jnp.concatenate([part.astype(f32) for part in split3(back)], axis=1).T
    picked = jnp.dot(parts.astype(bf16), hot_ref[...], preferred_element_type=f32)
    picked = picked[:LANES] + picked[LANES : 2 * LANES] + picked[2 * LANES :]
    for k in range(3):
        mine = at_rank_ref[...] * picked[k * capacity : (k + 1) * capacity]
        force_ref[k : k + 1] = jnp.sum(mine, axis=0, keepdims=True)
    for copy in copies:
        copy.wait()


def swap_faces(up, down):
    peers = lax.axis_size("gz")
    below = lax.ppermute(up, "gz", [(i, (i + 1) % peers) for i in range(peers)])
    above = lax.ppermute(down, "gz", [((i + 1) % peers, i) for i in range(peers)])
    return below, above


def swap_ends(inner, outer):
    length = lax.axis_size("gx")
    inner = lax.ppermute(inner, "gx", [(i, i ^ 1) for i in range(length)])
    outer = lax.ppermute(
        outer, "gx", [(i, (i + 1) % length if i % 2 else (i - 1) % length) for i in range(length)]
    )
    return inner, outer


def per_device(populations, rates, grain_fraction, grain_velocity, grain_dest, grain_line):
    _, depth, length, width = populations.shape
    lines = depth * length
    devices = lax.axis_size("gz") * lax.axis_size("gx")
    grains = grain_fraction.shape[0]
    capacity = 2 * grains // devices
    slots = devices * capacity
    shape, both = jax.ShapeDtypeStruct, ("gz", "gx")
    dest, line = grain_dest.reshape(1, grains), grain_line.reshape(1, grains)
    inputs, rows, parts = (dest, line, grain_velocity, grain_fraction), devices * (capacity + 2), 4
    send, rank = call(
        functools.partial(pack_kernel, devices, capacity, parts),
        [shape((rows, width), bf16), shape((1, grains), i32)],
        *inputs,
        hbm=range(4),
        hbm_out=(0,),
        scratch=[pltpu.VMEM(x.shape, x.dtype) for x in inputs]
        + [pltpu.VMEM((rows, width), bf16), pltpu.VMEM((parts, rows // parts, width), f32)]
        + [pltpu.SemaphoreType.DMA((n,)) for n in (4, parts)],
        vmem=60,
    )
    recv = lax.all_to_all(
        send.reshape(devices, capacity // 2 + 1, 2, width), both, split_axis=0, concat_axis=0, tiled=True
    ).reshape(rows, width)
    state, sums = shape(populations.shape, f32), shape((4, depth, length, width), f32)
    face, ends = shape((9, length, width), f32), shape((9 * depth, width), f32)
    kept, swapped, sums = call(relax_kernel, [state, state, sums], rates, populations, smem=(0,))
    post, up, down, push, held, slot_line, slot_rows = call(
        functools.partial(first_kernel, devices, capacity),
        [
            state, face, face, shape((3, depth, length, width), f32),
            shape((4 * lines, width), f32), shape((1, slots), i32), shape((slots, width), bf16),
        ],
        recv, kept, swapped, sums, scratch=[pltpu.VMEM((rows, width), f32)],
    )
    below, above = swap_faces(up, down)
    turned, hot, at_rank = call(
        turn_kernel,
        [shape((width, slots), bf16), shape((devices, grains), bf16), shape((capacity, grains), f32)],
        slot_rows, dest, rank,
    )
    inner, outer = swap_ends(*call(ends_kernel, [ends, ends], post, below, above))
    post, up, down, inner, outer, back = call(
        functools.partial(second_kernel, capacity),
        [state, face, face, ends, ends, shape((4 * devices, LANES), f32)],
        rates, post, below, above, inner, outer, held, push, slot_line, turned,
        smem=(0,), scratch=[pltpu.VMEM(ends.shape, f32)] * 2,
    )
    back = lax.all_to_all(
        back.reshape(devices, 4, LANES), both, split_axis=0, concat_axis=0, tiled=True
    ).reshape(4 * devices, LANES)
    below, above = swap_faces(up, down)
    inner, outer = swap_ends(inner, outer)
    scaled, grain_force = call(
        functools.partial(last_kernel, capacity),
        [state, shape((3, grains), f32)],
        post, below, above, inner, outer, back, hot, at_rank,
        hbm_out=(0,), scratch=[pltpu.VMEM(state.shape, f32), pltpu.SemaphoreType.DMA((3,))],
    )
    return (scaled, grain_force)


def solution(mesh):
    in_specs = (
        P(None, "gz", "gx", None),
        P(),
        P(("gz", "gx"), None),
        P(None, ("gz", "gx")),
        P(("gz", "gx"), None),
        P(("gz", "gx")),
    )
    out_specs = (P(None, "gz", "gx", None), P(None, ("gz", "gx")))
    return jax.shard_map(
        per_device, mesh=mesh, in_specs=in_specs, out_specs=out_specs, check_vma=False
    )
```

time: 48.3 us -> 47.4 us (0.981)
  blocking collectives: 19.5 us -> 0 us
  waiting for transfers between devices: 6.71 us -> 17.6 us
  starting transfers between devices: 13.9 us -> 21.2 us
    all_to_all x1 -> x0, blocking collectives: 19.5 us -> none  [per_device(): lax.all_to_all(send, ('gz', 'gx'), split_axis=0, concat_axis=0, tiled=True)]
    all_to_all x1 -> x2, waiting for transfers between devices: 0.67 us -> 10.3 us  [the longest x1 10.3 us: per_device(): lax.all_to_all(send.reshape(devices, capacity // 2 + 1, 2, width), both,...]
    all_to_all x1 -> x2, starting transfers between devices: 3.29 us -> 10.6 us  [the longest x1 7.3 us: per_device(): lax.all_to_all(send.reshape(devices, capacity // 2 + 1, 2, width), both,...]
    ppermute x2, waiting for transfers between devices: 3.82 us -> 5.25 us  [swap_ends(): lax.ppermute(outer, 'gx', [(i, (i + 1) % length if i % 2 else (i - 1) % l...]
    pallas_call x6 -> x7, Pallas kernels: 7.13 us -> 7.44 us  [call(): pl.pallas_call(kernel, out_shape=list(outs), in_specs=[pl.BlockSpec(memor...]
  transfers between devices with their start and end apart: 9 -> 10, of which waited for: 4 -> 5; matrix products, arithmetic and copies ran while one was open for 0% -> 0% of each run, Pallas kernels for 2% -> 2%
where the time goes in v3:
time: 47.4 us; the launch traced here: 47.1 us
  starting transfers between devices  21.2 us (45%)
  waiting for transfers between devices  17.6 us (37%)
  Pallas kernels  7.44 us (16%)
  between operations  0.75 us (2%)
    all_to_all x1, waiting for transfers between devices, per_device(): lax.all_to_all(send.reshape(devices, capacity // 2 + 1, 2, width), both,...  10.3 us
    pallas_call x7, Pallas kernels, call(): pl.pallas_call(kernel, out_shape=list(outs), in_specs=[pl.BlockSpec(memor...  7.44 us
    all_to_all x1, starting transfers between devices, per_device(): lax.all_to_all(send.reshape(devices, capacity // 2 + 1, 2, width), both,...  7.3 us
    ppermute x2, waiting for transfers between devices, swap_ends(): lax.ppermute(outer, 'gx', [(i, (i + 1) % length if i % 2 else (i - 1) % l...  5.25 us
    ppermute x2, starting transfers between devices, swap_ends(): lax.ppermute(outer, 'gx', [(i, (i + 1) % length if i % 2 else (i - 1) % l...  4.61 us
    ppermute x2, starting transfers between devices, swap_faces(): lax.ppermute(down, 'gz', [((i + 1) % peers, i) for i in range(peers)])  4.05 us
    all_to_all x1, starting transfers between devices, per_device(): lax.all_to_all(back.reshape(devices, 4, LANES), both, split_axis=0, conca...  3.29 us
    ppermute x2, waiting for transfers between devices, swap_faces(): below = lax.ppermute(up, 'gz', [(i, (i + 1) % peers) for i in range(peers)])  1.93 us
  transfers between devices with their start and end apart: 10, of which 5 were waited for; matrix products, arithmetic and copies ran while one was open for 0% of the time, Pallas kernels for 2%

profile of v3, /device:TPU:0, one launch (start us, length us, event | category | flops | bytes accessed | tf_op | source)
XLA Modules:
  0.0 47.1 jit_solution(927952681680667599)
XLA Ops:
  0.6 2.8 %shard_map.77 = (bf16[1088,128]{1,0:T(8,128)(2,1)}, s32[1,512]{1,0:T(1,128)}) custom-call(s32[1,512]{1,0:T(1,128)} %bitcast.8, s32[1,512]{1,0:T(1,128)} %bitcast.11, bf16[3,512]{1,0:T(4,128)(2,1)} %refs_2_.1, bf16[512,128]{1,0:T(8,128)(2,1)} %refs_3_.1), custom_call_target="tpu_custom_call" | custom-call | bytes 418816 | tf_op jit(solution)/shard_map/pallas_call | solution.py:28
  3.4 0.0 copy-start
  3.4 0.0 copy-start.3
  3.5 7.3 %all-to-all-start = ((bf16[32,17,2,128]{3,2,1,0:T(2,128)(2,1)}), bf16[32,17,2,128]{3,2,1,0:T(2,128)(2,1)S(1)}, u32[]{:S(2)}, u32[]{:S(2)}) async-start(bf16[32,17,2,128]{3,2,1,0:T(2,128)(2,1)} %bitcast.10), calls=%async_computation | async-start | bytes 557056 | tf_op jit(solution)/shard_map/all_to_all | solution.py:432
  10.8 0.0 copy-done
  10.8 0.0 copy-done.3
  10.8 0.7 %shard_map.78 = (f32[27,2,8,128]{3,2,1,0:T(8,128)S(1)}, f32[27,2,8,128]{3,2,1,0:T(8,128)S(1)}, f32[4,2,8,128]{3,2,1,0:T(8,128)S(1)}) custom-call(f32[27]{0:T(128)S(1)} %copy-done.3, f32[27,2,8,128]{3,2,1,0:T(8,128)S(1)} %copy-done), custom_call_target="tpu_custom_call" | custom-call | bytes 696428 | tf_op jit(solution)/shard_map/pallas_call | solution.py:28
  11.5 10.3 %all-to-all-done = bf16[32,17,2,128]{3,2,1,0:T(2,128)(2,1)S(1)} async-done(((bf16[32,17,2,128]{3,2,1,0:T(2,128)(2,1)}), bf16[32,17,2,128]{3,2,1,0:T(2,128)(2,1)S(1)}, u32[]{:S(2)}, u32[]{:S(2)}) %all-to-all-start) | async-done | bytes 278560 | tf_op jit(solution)/shard_map/all_to_all | solution.py:432
  21.9 0.4 shard_map.79
  22.3 0.1 collective-permute-start
  22.4 2.9 %collective-permute-start.1 = (f32[9,8,128]{2,1,0:T(8,128)S(1)}, f32[9,8,128]{2,1,0:T(8,128)S(1)}, u32[]{:S(2)}, u32[]{:S(2)}) collective-permute-start(f32[9,8,128]{2,1,0:T(8,128)S(1)} %get-tuple-element.31), channel_id=1, source_target_pairs={{8,0},{16,8},{24,16},{0,24},{9,1},{17,9},{25,17},{1,25},{10,2},{18... | collective-permute-start | bytes 110600 | tf_op jit(solution)/shard_map/ppermute | solution.py:398
  25.3 1.9 %collective-permute-done.below_ref = f32[9,8,128]{2,1,0:T(8,128)S(1)} collective-permute-done((f32[9,8,128]{2,1,0:T(8,128)S(1)}, f32[9,8,128]{2,1,0:T(8,128)S(1)}, u32[]{:S(2)}, u32[]{:S(2)}) %collective-permute-start) | collective-permute-done | bytes 36896 | tf_op jit(solution)/shard_map/ppermute | solution.py:397
  27.2 0.0 collective-permute-done.1.above_ref
  27.2 0.1 collective-permute-start.2
  27.3 0.0 copy-start.2
  27.3 0.0 copy-start.1
  27.3 0.9 %collective-permute-start.3 = (f32[18,128]{1,0:T(8,128)S(1)}, f32[18,128]{1,0:T(8,128)S(1)}, u32[]{:S(2)}, u32[]{:S(2)}) collective-permute-start(f32[18,128]{1,0:T(8,128)S(1)} %get-tuple-element.33), channel_id=1, source_target_pairs={{0,7},{1,2},{2,1},{3,4},{4,3},{5,6},{6,5},{7,0},{8,15},{9,10},{10,... | collective-permute-start | bytes 27656 | tf_op jit(solution)/shard_map/ppermute | solution.py:405
  28.2 0.1 shard_map.81
  28.4 0.1 collective-permute-done.2.inner_ref
  28.5 3.8 %collective-permute-done.3.outer_ref = f32[18,128]{1,0:T(8,128)S(1)} collective-permute-done((f32[18,128]{1,0:T(8,128)S(1)}, f32[18,128]{1,0:T(8,128)S(1)}, u32[]{:S(2)}, u32[]{:S(2)}) %collective-permute-start.3) | collective-permute-done | bytes 9248 | tf_op jit(solution)/shard_map/ppermute | solution.py:405
  32.3 1.8 %shard_map.82 = (f32[27,2,8,128]{3,2,1,0:T(8,128)S(1)}, f32[9,8,128]{2,1,0:T(8,128)S(1)}, f32[9,8,128]{2,1,0:T(8,128)S(1)}, f32[18,128]{1,0:T(8,128)S(1)}, f32[18,128]{1,0:T(8,128)S(1)}, /*index=5*/f32[128,128]{1,0:T(8,128)}) custom-call(f32[27]{0:T(128)S(1)} %copy-done.3, f32[27,2,8,128]{3,2,1,0:T(8,128)S(1)} %get-tuple-element.29.post_ref, ...), custom_call_target="tpu_custom_call" | custom-call | bytes 1015916 | tf_op jit(solution)/shard_map/pallas_call | solution.py:28
  34.1 3.3 %all-to-all-start.1 = ((f32[32,4,128]{2,1,0:T(4,128)}), f32[32,4,128]{2,1,0:T(4,128)S(1)}, u32[]{:S(2)}, u32[]{:S(2)}) async-start(f32[32,4,128]{2,1,0:T(4,128)} %bitcast.4), calls=%async_computation.1 | async-start | bytes 131072 | tf_op jit(solution)/shard_map/all_to_all | solution.py:459
  37.4 1.8 %collective-permute-start.4 = (f32[9,8,128]{2,1,0:T(8,128)S(1)}, f32[9,8,128]{2,1,0:T(8,128)S(1)}, u32[]{:S(2)}, u32[]{:S(2)}) collective-permute-start(f32[9,8,128]{2,1,0:T(8,128)S(1)} %get-tuple-element.41), channel_id=1, source_target_pairs={{0,8},{8,16},{16,24},{24,0},{1,9},{9,17},{17,25},{25,1},{2,10},{10... | collective-permute-start | bytes 110600 | tf_op jit(solution)/shard_map/ppermute | solution.py:397
  39.3 1.2 %collective-permute-start.5 = (f32[9,8,128]{2,1,0:T(8,128)S(1)}, f32[9,8,128]{2,1,0:T(8,128)S(1)}, u32[]{:S(2)}, u32[]{:S(2)}) collective-permute-start(f32[9,8,128]{2,1,0:T(8,128)S(1)} %get-tuple-element.42), channel_id=1, source_target_pairs={{8,0},{16,8},{24,16},{0,24},{9,1},{17,9},{25,17},{1,25},{10,2},{18... | collective-permute-start | bytes 110600 | tf_op jit(solution)/shard_map/ppermute | solution.py:398
  40.4 0.0 collective-permute-start.6
  40.4 3.7 %collective-permute-start.7 = (f32[18,128]{1,0:T(8,128)S(1)}, f32[18,128]{1,0:T(8,128)S(1)}, u32[]{:S(2)}, u32[]{:S(2)}) collective-permute-start(f32[18,128]{1,0:T(8,128)S(1)} %get-tuple-element.44), channel_id=1, source_target_pairs={{0,7},{1,2},{2,1},{3,4},{4,3},{5,6},{6,5},{7,0},{8,15},{9,10},{10,... | collective-permute-start | bytes 27656 | tf_op jit(solution)/shard_map/ppermute | solution.py:405
  44.1 0.0 collective-permute-done.6.inner_ref
  44.1 1.4 %collective-permute-done.7.outer_ref = f32[18,128]{1,0:T(8,128)S(1)} collective-permute-done((f32[18,128]{1,0:T(8,128)S(1)}, f32[18,128]{1,0:T(8,128)S(1)}, u32[]{:S(2)}, u32[]{:S(2)}) %collective-permute-start.7) | collective-permute-done | bytes 9248 | tf_op jit(solution)/shard_map/ppermute | solution.py:405
  45.6 0.0 collective-permute-done.4.below_ref
  45.6 0.0 collective-permute-done.5.above_ref
  45.6 0.0 all-to-all-done.1
  45.6 1.5 %shard_map.83 = (f32[27,2,8,128]{3,2,1,0:T(8,128)}, f32[3,512]{1,0:T(4,128)}) custom-call(f32[27,2,8,128]{3,2,1,0:T(8,128)S(1)} %get-tuple-element.40.post_ref, f32[9,8,128]{2,1,0:T(8,128)S(1)} %collective-permute-done.4.below_ref, f32[9,8,128]{2,1,0:T(8,128)S(1)} %collective-permute-done.5.above_ref, f32[18,128]{1,0:T(8,128)S(1)} %collective-permute-done.6.inner_ref, ...), custom_call_target="tpu_custom_call" | custom-call | bytes 704512 | tf_op jit(solution)/shard_map/pallas_call | solution.py:28
  (3 shorter events, 0.0 us)
Async XLA Ops:
  3.4 7.3 %copy-start = (f32[27,2,8,128]{3,2,1,0:T(8,128)S(1)}, f32[27,2,8,128]{3,2,1,0:T(8,128)}, u32[]{:S(2)}) copy-start(f32[27,2,8,128]{3,2,1,0:T(8,128)} %fields_ref.1) | copy-start | bytes 663556
  3.4 7.3 %copy-start.3 = (f32[27]{0:T(128)S(1)}, f32[27]{0:T(128)}, u32[]{:S(2)}) copy-start(f32[27]{0:T(128)} %rates_ref.3) | copy-start | bytes 328
  3.5 18.4 %all-to-all-start = ((bf16[32,17,2,128]{3,2,1,0:T(2,128)(2,1)}), bf16[32,17,2,128]{3,2,1,0:T(2,128)(2,1)S(1)}, u32[]{:S(2)}, u32[]{:S(2)}) async-start(bf16[32,17,2,128]{3,2,1,0:T(2,128)(2,1)} %bitcast.10), calls=%async_computation | async-start | bytes 557056 | tf_op jit(solution)/shard_map/all_to_all | solution.py:432
  22.3 4.9 %collective-permute-start = (f32[9,8,128]{2,1,0:T(8,128)S(1)}, f32[9,8,128]{2,1,0:T(8,128)S(1)}, u32[]{:S(2)}, u32[]{:S(2)}) collective-permute-start(f32[9,8,128]{2,1,0:T(8,128)S(1)} %get-tuple-element.30), channel_id=1, source_target_pairs={{0,8},{8,16},{16,24},{24,0},{1,9},{9,17},{17,25},{25,1},{2,10},{10... | collective-permute-start | bytes 110600 | tf_op jit(solution)/shard_map/ppermute | solution.py:397
  22.4 4.8 %collective-permute-start.1 = (f32[9,8,128]{2,1,0:T(8,128)S(1)}, f32[9,8,128]{2,1,0:T(8,128)S(1)}, u32[]{:S(2)}, u32[]{:S(2)}) collective-permute-start(f32[9,8,128]{2,1,0:T(8,128)S(1)} %get-tuple-element.31), channel_id=1, source_target_pairs={{8,0},{16,8},{24,16},{0,24},{9,1},{17,9},{25,17},{1,25},{10,2},{18... | collective-permute-start | bytes 110600 | tf_op jit(solution)/shard_map/ppermute | solution.py:398
  27.2 1.2 %collective-permute-start.2 = (f32[18,128]{1,0:T(8,128)S(1)}, f32[18,128]{1,0:T(8,128)S(1)}, u32[]{:S(2)}, u32[]{:S(2)}) collective-permute-start(f32[18,128]{1,0:T(8,128)S(1)} %get-tuple-element.32), channel_id=1, source_target_pairs={{0,1},{1,0},{2,3},{3,2},{4,5},{5,4},{6,7},{7,6},{8,9},{9,8},{10,11... | collective-permute-start | bytes 27656 | tf_op jit(solution)/shard_map/ppermute | solution.py:404
  27.3 0.9 %copy-start.2 = (s32[1,512]{1,0:T(1,128)S(1)}, s32[1,512]{1,0:T(1,128)}, u32[]{:S(2)}) copy-start(s32[1,512]{1,0:T(1,128)} %get-tuple-element.38.rank_ref) | copy-start | bytes 6148
  27.3 0.9 %copy-start.1 = (s32[512,1]{0,1:T(1,128)S(1)}, s32[512,1]{0,1:T(1,128)}, u32[]{:S(2)}) copy-start(s32[512,1]{0,1:T(1,128)} %param.10) | copy-start | bytes 6148
  27.3 5.0 %collective-permute-start.3 = (f32[18,128]{1,0:T(8,128)S(1)}, f32[18,128]{1,0:T(8,128)S(1)}, u32[]{:S(2)}, u32[]{:S(2)}) collective-permute-start(f32[18,128]{1,0:T(8,128)S(1)} %get-tuple-element.33), channel_id=1, source_target_pairs={{0,7},{1,2},{2,1},{3,4},{4,3},{5,6},{6,5},{7,0},{8,15},{9,10},{10,... | collective-permute-start | bytes 27656 | tf_op jit(solution)/shard_map/ppermute | solution.py:405
  34.1 11.4 %all-to-all-start.1 = ((f32[32,4,128]{2,1,0:T(4,128)}), f32[32,4,128]{2,1,0:T(4,128)S(1)}, u32[]{:S(2)}, u32[]{:S(2)}) async-start(f32[32,4,128]{2,1,0:T(4,128)} %bitcast.4), calls=%async_computation.1 | async-start | bytes 131072 | tf_op jit(solution)/shard_map/all_to_all | solution.py:459
  37.4 8.1 %collective-permute-start.4 = (f32[9,8,128]{2,1,0:T(8,128)S(1)}, f32[9,8,128]{2,1,0:T(8,128)S(1)}, u32[]{:S(2)}, u32[]{:S(2)}) collective-permute-start(f32[9,8,128]{2,1,0:T(8,128)S(1)} %get-tuple-element.41), channel_id=1, source_target_pairs={{0,8},{8,16},{16,24},{24,0},{1,9},{9,17},{17,25},{25,1},{2,10},{10... | collective-permute-start | bytes 110600 | tf_op jit(solution)/shard_map/ppermute | solution.py:397
  39.3 6.3 %collective-permute-start.5 = (f32[9,8,128]{2,1,0:T(8,128)S(1)}, f32[9,8,128]{2,1,0:T(8,128)S(1)}, u32[]{:S(2)}, u32[]{:S(2)}) collective-permute-start(f32[9,8,128]{2,1,0:T(8,128)S(1)} %get-tuple-element.42), channel_id=1, source_target_pairs={{8,0},{16,8},{24,16},{0,24},{9,1},{17,9},{25,17},{1,25},{10,2},{18... | collective-permute-start | bytes 110600 | tf_op jit(solution)/shard_map/ppermute | solution.py:398
  40.4 3.7 %collective-permute-start.6 = (f32[18,128]{1,0:T(8,128)S(1)}, f32[18,128]{1,0:T(8,128)S(1)}, u32[]{:S(2)}, u32[]{:S(2)}) collective-permute-start(f32[18,128]{1,0:T(8,128)S(1)} %get-tuple-element.43), channel_id=1, source_target_pairs={{0,1},{1,0},{2,3},{3,2},{4,5},{5,4},{6,7},{7,6},{8,9},{9,8},{10,11... | collective-permute-start | bytes 27656 | tf_op jit(solution)/shard_map/ppermute | solution.py:404
  40.4 5.1 %collective-permute-start.7 = (f32[18,128]{1,0:T(8,128)S(1)}, f32[18,128]{1,0:T(8,128)S(1)}, u32[]{:S(2)}, u32[]{:S(2)}) collective-permute-start(f32[18,128]{1,0:T(8,128)S(1)} %get-tuple-element.44), channel_id=1, source_target_pairs={{0,7},{1,2},{2,1},{3,4},{4,3},{5,6},{6,5},{7,0},{8,15},{9,10},{10,... | collective-permute-start | bytes 27656 | tf_op jit(solution)/shard_map/ppermute | solution.py:405

commit v4 on v3

--- a/solution.py
+++ b/solution.py
@@ -20,21 +20,20 @@
     return lax.broadcasted_iota(i32, shape, dim)
 
 
-def call(kernel, outs, *operands, smem=(), hbm=(), hbm_out=(), scratch=(), vmem=24):
-    space = [pltpu.SMEM if n in smem else pltpu.HBM if n in hbm else pltpu.VMEM for n in range(len(operands))]
+def call(kernel, outs, *operands, smem=(), scratch=(), flops=0):
     size = sum(o.size * o.dtype.itemsize for o in operands) + sum(
         int(np.prod(o.shape)) * o.dtype.itemsize for o in outs
     )
     return pl.pallas_call(
         kernel,
         out_shape=list(outs),
-        in_specs=[pl.BlockSpec(memory_space=where) for where in space],
-        out_specs=[
-            pl.BlockSpec(memory_space=pltpu.HBM if n in hbm_out else pltpu.VMEM) for n in range(len(outs))
+        in_specs=[
+            pl.BlockSpec(memory_space=pltpu.SMEM if n in smem else pltpu.VMEM) for n in range(len(operands))
         ],
+        out_specs=[pl.BlockSpec(memory_space=pltpu.VMEM)] * len(outs),
         scratch_shapes=list(scratch),
-        compiler_params=pltpu.CompilerParams(vmem_limit_bytes=vmem * 1024 * 1024),
-        cost_estimate=pl.CostEstimate(flops=0, bytes_accessed=size, transcendentals=0),
+        compiler_params=pltpu.CompilerParams(vmem_limit_bytes=24 * 1024 * 1024),
+        cost_estimate=pl.CostEstimate(flops=flops, bytes_accessed=size, transcendentals=0),
     )(*operands)
 
 
@@ -52,31 +51,33 @@
     return high, mid, (rest - mid.astype(f32)).astype(bf16)
 
 
-def pack_kernel(devices, capacity, parts, *refs):
-    sources, (send_ref, rank_ref), held = refs[:4], refs[4:6], refs[6:10]
-    staged_ref, rows_ref, sem, out_sem = refs[10:]
-    copies = [pltpu.make_async_copy(sources[n], held[n], sem.at[n]) for n in range(4)]
-    for copy in copies:
-        copy.start()
-    dest_ref, line_ref, speed_ref, fraction_ref = held
-    grains, width = fraction_ref.shape
-    block = capacity + 2
-    copies[0].wait()
-    dest = dest_ref[...]
-    hot = jnp.where(iota((devices, grains), 0) == dest, 1.0, 0.0)
-    earlier = jnp.where(iota((LANES, LANES), 0) < iota((LANES, LANES), 1), 1.0, 0.0).astype(bf16)
+def tables_kernel(capacity, earlier_ref, spread_ref, own_ref):
+    width, slots = spread_ref.shape
+    order = iota(earlier_ref.shape, 0) < iota(earlier_ref.shape, 1)
+    earlier_ref[...] = jnp.where(order, 1.0, 0.0).astype(bf16)
+    same = iota((width, slots), 0) % capacity == iota((width, slots), 1) % capacity
+    spread_ref[...] = jnp.where(same, 1.0, 0.0).astype(bf16)
+    own_ref[...] = jnp.where(iota(own_ref.shape, 0) == iota(own_ref.shape, 1) // capacity, 1.0, 0.0)
+
+
+def ranks(hot, earlier):
+    devices, grains = hot.shape
     total = jnp.zeros((devices, 1), f32)
-    ranks = []
+    parts = []
     for start in range(0, grains, LANES):
         part = hot[:, start : start + LANES]
         before = jnp.dot(part.astype(bf16), earlier, preferred_element_type=f32) + total
-        ranks.append(jnp.sum(part * before, axis=0, keepdims=True))
+        parts.append(jnp.sum(part * before, axis=0, keepdims=True))
         total = total + jnp.sum(part, axis=1, keepdims=True)
-    rank = jnp.concatenate(ranks, axis=1).astype(i32)
-    rank_ref[...] = rank
-    position = dest * block + rank
-    copies[1].wait()
-    copies[2].wait()
+    return jnp.concatenate(parts, axis=1)
+
+
+def pack_kernel(devices, capacity, dest_ref, line_ref, speed_ref, fraction_ref, earlier_ref, send_ref, rows_ref):
+    grains, width = fraction_ref.shape
+    block = capacity + 2
+    dest = dest_ref[...]
+    hot = jnp.where(iota((devices, grains), 0) == dest, 1.0, 0.0)
+    rank = ranks(hot, earlier_ref[...]).astype(i32)
     speed = speed_ref[...].astype(f32)
     values = [speed[0:1], speed[1:2], speed[2:3], line_ref[...].astype(f32)]
     at_rank = iota((capacity, grains), 0) == rank
@@ -89,20 +90,10 @@
         (((1,), (1,)), ((), ())),
         preferred_element_type=f32,
     )
-    copies[3].wait()
-    fraction = fraction_ref[...]
-    size, some = devices * block // parts, devices // parts
-    out = []
-    for n in range(parts):
-        place = jnp.where(iota((size, grains), 0) == position - n * size, 1.0, 0.0).astype(bf16)
-        rows_ref[n] = jnp.dot(place, fraction, preferred_element_type=f32)
-        rows_ref[n, pl.ds(capacity, some, stride=block), :] = fact_rows[n * some : (n + 1) * some]
-        staged_ref[n * size : (n + 1) * size] = rows_ref[n].astype(bf16)
-        rows = pl.ds(n * size, size)
-        out.append(pltpu.make_async_copy(staged_ref.at[rows], send_ref.at[rows], out_sem.at[n]))
-        out[n].start()
-    for copy in out:
-        copy.wait()
+    place = jnp.where(iota((devices * block, grains), 0) == dest * block + rank, 1.0, 0.0).astype(bf16)
+    rows_ref[...] = jnp.dot(place, fraction_ref[...], preferred_element_type=f32)
+    rows_ref[pl.ds(capacity, devices, stride=block), :] = fact_rows
+    send_ref[...] = rows_ref[...].astype(bf16)
 
 
 def total_of(values):
@@ -177,17 +168,29 @@
     return first[0], first[1:]
 
 
-def store_post(post, z, post_ref, up_ref, down_ref):
-    for i in range(27):
-        post_ref[i, z] = post[i]
-        if STEP[i][0] == 1 and z == post_ref.shape[1] - 1:
-            up_ref[i - 18] = post[i]
-        if STEP[i][0] == -1 and z == 0:
-            down_ref[i] = post[i]
-
-
-def relax_kernel(rates_ref, fields_ref, kept_ref, swapped_ref, sums_ref):
+def even_place(axis):
+    return lax.axis_index(axis) % 2 == 0
+
+
+def store_faces(post_ref, near_ref, far_ref):
+    top = post_ref.shape[1] - 1
+    for n in range(9):
+        up, down = post_ref[n + 18, top], post_ref[n, 0]
+        near_ref[n] = jnp.where(even_place("gz"), up, down)
+        far_ref[n] = jnp.where(even_place("gz"), down, up)
+
+
+def across(near_ref, far_ref, i, x=slice(None)):
+    n = i % 9
+    if STEP[i][0] > 0:
+        return jnp.where(even_place("gz"), far_ref[n, x], near_ref[n, x])
+    return jnp.where(even_place("gz"), near_ref[n, x], far_ref[n, x])
+
+
+def relax_kernel(rates_ref, fields_ref, kept_ref, swapped_ref, sums_ref, rate_rows_ref):
     rate = [rates_ref[a] for a in range(27)]
+    for a in range(27):
+        rate_rows_ref[a : a + 1] = jnp.full((1, rate_rows_ref.shape[1]), rate[a], f32)
     for z in range(fields_ref.shape[1]):
         density, momentum, kept, swapped = relax([fields_ref[i, z] for i in range(27)], rate)
         for n, value in enumerate([density] + momentum):
@@ -198,8 +201,8 @@
 
 
 def first_kernel(
-    devices, capacity, recv_ref, kept_ref, swapped_ref, sums_ref,
-    post_ref, up_ref, down_ref, push_ref, held_ref, line_ref, slot_ref, wide_ref,
+    devices, capacity, recv_ref, kept_ref, swapped_ref, sums_ref, spread_ref, own_ref,
+    post_ref, near_ref, far_ref, push_ref, held_ref, line_ref, slot_ref, wide_ref,
 ):
     width = recv_ref.shape[1]
     block, slots = capacity + 2, devices * capacity
@@ -213,14 +216,10 @@
     slot_ref[...] = slot_rows
     group = iota((devices, width), 1) // capacity
     stacked = jnp.concatenate([jnp.where(group == m, facts, 0.0) for m in range(4)], axis=0)
-    spread = jnp.where(
-        iota((width, slots), 0) % capacity == iota((width, slots), 1) % capacity, 1.0, 0.0
-    ).astype(bf16)
-    wide = jnp.dot(stacked.astype(bf16), spread, preferred_element_type=f32)
-    own = iota((devices, slots), 0) == iota((devices, slots), 1) // capacity
+    wide = jnp.dot(stacked.astype(bf16), spread_ref[...], preferred_element_type=f32)
+    own = own_ref[...]
     fact = [
-        jnp.sum(jnp.where(own, wide[m * devices : (m + 1) * devices], 0.0), axis=0, keepdims=True)
-        for m in range(4)
+        jnp.sum(own * wide[m * devices : (m + 1) * devices], axis=0, keepdims=True) for m in range(4)
     ]
     line_ref[...] = fact[3].astype(i32)
     on_line = iota((lines, slots), 0) == fact[3].astype(i32)
@@ -233,28 +232,30 @@
         kept, swapped = [kept_ref[i, z] for i in range(27)], [swapped_ref[i, z] for i in range(27)]
         grains = grains_at(held_ref, z, depth, length)
         post, push = exchange(sums[0], sums[1:], kept, swapped, *grains)
-        store_post(post, z, post_ref, up_ref, down_ref)
+        for i in range(27):
+            post_ref[i, z] = post[i]
         for k in range(3):
             push_ref[k, z] = push[k]
-
-
-def turn_kernel(slot_ref, dest_ref, rank_ref, turned_ref, hot_ref, at_rank_ref):
+    store_faces(post_ref, near_ref, far_ref)
+
+
+def turn_kernel(slot_ref, dest_ref, earlier_ref, turned_ref, hot_ref, at_rank_ref):
     turned_ref[...] = slot_ref[...].astype(f32).T.astype(bf16)
-    hot_ref[...] = jnp.where(iota(hot_ref.shape, 0) == dest_ref[...], 1.0, 0.0).astype(bf16)
-    at_rank_ref[...] = jnp.where(iota(at_rank_ref.shape, 0) == rank_ref[...], 1.0, 0.0)
-
-
-def ends_kernel(post_ref, below_ref, above_ref, inner_ref, outer_ref):
+    hot = jnp.where(iota(hot_ref.shape, 0) == dest_ref[...], 1.0, 0.0)
+    hot_ref[...] = hot.astype(bf16)
+    rank = ranks(hot, earlier_ref[...]).astype(i32)
+    at_rank_ref[...] = jnp.where(iota(at_rank_ref.shape, 0) == rank, 1.0, 0.0)
+
+
+def ends_kernel(post_ref, near_ref, far_ref, inner_ref, outer_ref):
     depth, length = post_ref.shape[1], post_ref.shape[2]
-    even = lax.axis_index("gx") % 2 == 0
+    even = even_place("gx")
 
     def row(i, z, x):
         source = z - STEP[i][0]
-        if source < 0:
-            return below_ref[i - 18, x : x + 1]
-        if source >= depth:
-            return above_ref[i, x : x + 1]
-        return post_ref[i, source, x : x + 1]
+        if 0 <= source < depth:
+            return post_ref[i, source, x : x + 1]
+        return across(near_ref, far_ref, i, slice(x, x + 1))
 
     for i in range(27):
         if STEP[i][1] != 1:
@@ -271,21 +272,16 @@
     return ((STEP[i][0] + 1) * 3 + STEP[i][2] + 1) * depth + z
 
 
-def streamed(post_ref, below_ref, above_ref, inner_ref, outer_ref, z, back_ref=None, part=range(27)):
+def streamed(post_ref, near_ref, far_ref, inner_ref, outer_ref, z, back_ref=None):
     depth, length, width = post_ref.shape[1:]
-    even = lax.axis_index("gx") % 2 == 0
+    even = even_place("gx")
     rows = iota((length, width), 0)
     moved_list = []
-    for i in part:
+    for i in range(27):
         cz, cx, cy = STEP[i]
         source = z - cz
         inside = 0 <= source < depth
-        if source < 0:
-            moved = below_ref[i - 18]
-        elif source >= depth:
-            moved = above_ref[i]
-        else:
-            moved = post_ref[i, source]
+        moved = post_ref[i, source] if inside else across(near_ref, far_ref, i)
         if cx:
             n = end_row(i, z, depth)
             inner, outer = inner_ref[n : n + 1], outer_ref[n : n + 1]
@@ -306,21 +302,23 @@
 
 
 def second_kernel(
-    capacity, rates_ref, post_ref, below_ref, above_ref, inner_ref, outer_ref,
+    capacity, rates_ref, post_ref, near_ref, far_ref, inner_ref, outer_ref,
     held_ref, push_ref, line_ref, turned_ref,
-    next_ref, up_ref, down_ref, next_inner_ref, next_outer_ref, back_ref, right_ref, left_ref,
+    next_ref, next_near_ref, next_far_ref, next_inner_ref, next_outer_ref, back_ref, right_ref, left_ref,
 ):
     depth, length, width = post_ref.shape[1:]
     lines = depth * length
     slots = turned_ref.shape[1]
-    halo = (below_ref, above_ref, inner_ref, outer_ref)
-    rate = [rates_ref[a] for a in range(27)]
+    halo = (near_ref, far_ref, inner_ref, outer_ref)
+    rate = [rates_ref[a : a + 1] for a in range(27)]
     pushes = []
     for z in range(depth):
         relaxed = relax(streamed(post_ref, *halo, z), rate)
         post, push = exchange(*relaxed, *grains_at(held_ref, z, depth, length))
-        store_post(post, z, next_ref, up_ref, down_ref)
+        for i in range(27):
+            next_ref[i, z] = post[i]
         pushes.append(push)
+    store_faces(next_ref, next_near_ref, next_far_ref)
     back_ref[...] = jnp.zeros(back_ref.shape, f32)
     right_ref[...] = jnp.zeros(right_ref.shape, f32)
     left_ref[...] = jnp.zeros(left_ref.shape, f32)
@@ -337,7 +335,7 @@
         if cz:
             z = depth - 1 if cz > 0 else 0
             back_ref[pl.ds(4 * device_at(cz, cx) + 2 + cy, 1)] = next_ref[i, z, x : x + 1]
-    even = lax.axis_index("gx") % 2 == 0
+    even = even_place("gx")
     right, left = right_ref[...], left_ref[...]
     next_inner_ref[...] = jnp.where(even, right, left)
     next_outer_ref[...] = jnp.where(even, left, right)
@@ -367,20 +365,13 @@
 
 
 def last_kernel(
-    capacity, post_ref, below_ref, above_ref, inner_ref, outer_ref, back_ref, hot_ref, at_rank_ref,
-    scaled_ref, force_ref, staged_ref, sem,
+    capacity, post_ref, near_ref, far_ref, inner_ref, outer_ref, back_ref, hot_ref, at_rank_ref,
+    scaled_ref, force_ref,
 ):
-    depth = post_ref.shape[1]
-    halo = (below_ref, above_ref, inner_ref, outer_ref)
-    copies = []
-    for cz in (0, 1, -1):
-        part = [i for i in range(27) if STEP[i][0] == cz]
-        for z in range(depth):
-            for i, field in zip(part, streamed(post_ref, *halo, z, back_ref, part)):
-                staged_ref[i, z] = field * (1.0 / WEIGHT[i])
-        rows = pl.ds(part[0], len(part))
-        copies.append(pltpu.make_async_copy(staged_ref.at[rows], scaled_ref.at[rows], sem.at[cz + 1]))
-        copies[-1].start()
+    for z in range(post_ref.shape[1]):
+        fields = streamed(post_ref, near_ref, far_ref, inner_ref, outer_ref, z, back_ref)
+        for i in range(27):
+            scaled_ref[i, z] = fields[i] * (1.0 / WEIGHT[i])
     back = back_ref[pl.ds(0, hot_ref.shape[0], stride=4), :]
     parts = jnp.concatenate([part.astype(f32) for part in split3(back)], axis=1).T
     picked = jnp.dot(parts.astype(bf16), hot_ref[...], preferred_element_type=f32)
@@ -388,24 +379,30 @@
     for k in range(3):
         mine = at_rank_ref[...] * picked[k * capacity : (k + 1) * capacity]
         force_ref[k : k + 1] = jnp.sum(mine, axis=0, keepdims=True)
-    for copy in copies:
-        copy.wait()
-
-
-def swap_faces(up, down):
-    peers = lax.axis_size("gz")
-    below = lax.ppermute(up, "gz", [(i, (i + 1) % peers) for i in range(peers)])
-    above = lax.ppermute(down, "gz", [((i + 1) % peers, i) for i in range(peers)])
-    return below, above
-
-
-def swap_ends(inner, outer):
+
+
+def swap_faces(near, far):
+    depth, length = lax.axis_size("gz"), lax.axis_size("gx")
+    received = []
+    for face, odd in ((far, 1), (near, 0)):
+        pairs = []
+        for z in range(depth):
+            other = z + 1 if z % 2 == odd else z - 1
+            for x in range(length):
+                to = other * length + x if 0 <= other < depth else z * length + (x ^ 1)
+                pairs.append((z * length + x, to))
+        received.append(lax.ppermute(face, ("gz", "gx"), pairs))
+    return received[1], received[0]
+
+
+def swap_inner(inner):
+    return lax.ppermute(inner, "gx", [(i, i ^ 1) for i in range(lax.axis_size("gx"))])
+
+
+def swap_outer(outer):
     length = lax.axis_size("gx")
-    inner = lax.ppermute(inner, "gx", [(i, i ^ 1) for i in range(length)])
-    outer = lax.ppermute(
-        outer, "gx", [(i, (i + 1) % length if i % 2 else (i - 1) % length) for i in range(length)]
-    )
-    return inner, outer
+    pairs = [(i, (i + 1) % length if i % 2 else (i - 1) % length) for i in range(length)]
+    return lax.ppermute(outer, "gx", pairs)
 
 
 def per_device(populations, rates, grain_fraction, grain_velocity, grain_dest, grain_line):
@@ -417,55 +414,58 @@
     slots = devices * capacity
     shape, both = jax.ShapeDtypeStruct, ("gz", "gx")
     dest, line = grain_dest.reshape(1, grains), grain_line.reshape(1, grains)
-    inputs, rows, parts = (dest, line, grain_velocity, grain_fraction), devices * (capacity + 2), 4
-    send, rank = call(
-        functools.partial(pack_kernel, devices, capacity, parts),
-        [shape((rows, width), bf16), shape((1, grains), i32)],
-        *inputs,
-        hbm=range(4),
-        hbm_out=(0,),
-        scratch=[pltpu.VMEM(x.shape, x.dtype) for x in inputs]
-        + [pltpu.VMEM((rows, width), bf16), pltpu.VMEM((parts, rows // parts, width), f32)]
-        + [pltpu.SemaphoreType.DMA((n,)) for n in (4, parts)],
-        vmem=60,
+    rows = devices * (capacity + 2)
+    earlier, spread, own = call(
+        functools.partial(tables_kernel, capacity),
+        [shape((LANES, LANES), bf16), shape((width, slots), bf16), shape((devices, slots), f32)],
+        flops=10**9,
+    )
+    (send,) = call(
+        functools.partial(pack_kernel, devices, capacity),
+        [shape((rows, width), bf16)],
+        dest, line, grain_velocity, grain_fraction, earlier,
+        scratch=[pltpu.VMEM((rows, width), f32)],
     )
     recv = lax.all_to_all(
         send.reshape(devices, capacity // 2 + 1, 2, width), both, split_axis=0, concat_axis=0, tiled=True
     ).reshape(rows, width)
     state, sums = shape(populations.shape, f32), shape((4, depth, length, width), f32)
     face, ends = shape((9, length, width), f32), shape((9 * depth, width), f32)
-    kept, swapped, sums = call(relax_kernel, [state, state, sums], rates, populations, smem=(0,))
-    post, up, down, push, held, slot_line, slot_rows = call(
+    kept, swapped, sums, rate_rows = call(
+        relax_kernel, [state, state, sums, shape((27, width), f32)], rates, populations, smem=(0,)
+    )
+    post, near, far, push, held, slot_line, slot_rows = call(
         functools.partial(first_kernel, devices, capacity),
         [
             state, face, face, shape((3, depth, length, width), f32),
             shape((4 * lines, width), f32), shape((1, slots), i32), shape((slots, width), bf16),
         ],
-        recv, kept, swapped, sums, scratch=[pltpu.VMEM((rows, width), f32)],
-    )
-    below, above = swap_faces(up, down)
+        recv, kept, swapped, sums, spread, own, scratch=[pltpu.VMEM((rows, width), f32)],
+    )
+    near, far = swap_faces(near, far)
     turned, hot, at_rank = call(
         turn_kernel,
         [shape((width, slots), bf16), shape((devices, grains), bf16), shape((capacity, grains), f32)],
-        slot_rows, dest, rank,
-    )
-    inner, outer = swap_ends(*call(ends_kernel, [ends, ends], post, below, above))
-    post, up, down, inner, outer, back = call(
+        slot_rows, dest, earlier,
+    )
+    inner, outer = call(ends_kernel, [ends, ends], post, near, far)
+    inner, outer = swap_inner(inner), swap_outer(outer)
+    post, next_near, next_far, inner, outer, back = call(
         functools.partial(second_kernel, capacity),
         [state, face, face, ends, ends, shape((4 * devices, LANES), f32)],
-        rates, post, below, above, inner, outer, held, push, slot_line, turned,
-        smem=(0,), scratch=[pltpu.VMEM(ends.shape, f32)] * 2,
+        rate_rows, post, near, far, inner, outer, held, push, slot_line, turned,
+        scratch=[pltpu.VMEM(ends.shape, f32)] * 2,
     )
     back = lax.all_to_all(
         back.reshape(devices, 4, LANES), both, split_axis=0, concat_axis=0, tiled=True
     ).reshape(4 * devices, LANES)
-    below, above = swap_faces(up, down)
-    inner, outer = swap_ends(inner, outer)
+    outer = swap_outer(outer)
+    near, far = swap_faces(next_near, next_far)
+    inner = swap_inner(inner)
     scaled, grain_force = call(
         functools.partial(last_kernel, capacity),
         [state, shape((3, grains), f32)],
-        post, below, above, inner, outer, back, hot, at_rank,
-        hbm_out=(0,), scratch=[pltpu.VMEM(state.shape, f32), pltpu.SemaphoreType.DMA((3,))],
+        post, near, far, inner, outer, back, hot, at_rank,
     )
     return (scaled, grain_force)
 

time: 47.4 us -> 44.5 us (0.939)
  starting transfers between devices: 21.2 us -> 17 us
  waiting for transfers between devices: 17.6 us -> 20.6 us
  Pallas kernels: 7.44 us -> 5.04 us
  local copies, waits for them, and re-layouts: 0.03 us -> 0.82 us
    ppermute x8, starting transfers between devices: 10.6 us -> 6.07 us  [the longest x2 3.01 us: swap_outer(): return lax.ppermute(outer, 'gx', pairs)]
    ppermute x8, waiting for transfers between devices: 7.31 us -> 10.1 us  [the longest x2 5.79 us: swap_outer(): return lax.ppermute(outer, 'gx', pairs)]
    pallas_call x7 -> x8, Pallas kernels: 7.44 us -> 5.04 us  [call(): pl.pallas_call(kernel, out_shape=list(outs), in_specs=[pl.BlockSpec(memor...]
    unnamed x8 -> x12, local copies, waits for them, and re-layouts: 0.03 us -> 0.82 us
  transfers between devices with their start and end apart: 10 -> 10, of which waited for: 5 -> 6; matrix products, arithmetic and copies ran while one was open for 0% -> 0% of each run, Pallas kernels for 2% -> 2%
where the time goes in v4:
time: 44.5 us; the launch traced here: 44.3 us
  waiting for transfers between devices  20.6 us (46%)
  starting transfers between devices  17 us (38%)
  Pallas kernels  5.04 us (11%)
  local copies, waits for them, and re-layouts  0.82 us (2%)
  between operations  0.76 us (2%)
    all_to_all x1, waiting for transfers between devices, per_device(): lax.all_to_all(send.reshape(devices, capacity // 2 + 1, 2, width), both,...  10.3 us
    all_to_all x1, starting transfers between devices, per_device(): lax.all_to_all(send.reshape(devices, capacity // 2 + 1, 2, width), both,...  7.3 us
    ppermute x2, waiting for transfers between devices, swap_outer(): return lax.ppermute(outer, 'gx', pairs)  5.79 us
    pallas_call x8, Pallas kernels, call(): pl.pallas_call(kernel, out_shape=list(outs), in_specs=[pl.BlockSpec(memor...  5.04 us
    all_to_all x1, starting transfers between devices, per_device(): lax.all_to_all(back.reshape(devices, 4, LANES), both, split_axis=0, conca...  3.67 us
    ppermute x4, waiting for transfers between devices, swap_faces(): received.append(lax.ppermute(face, ('gz', 'gx'), pairs))  3.38 us
    ppermute x2, starting transfers between devices, swap_outer(): return lax.ppermute(outer, 'gx', pairs)  3.01 us
    ppermute x4, starting transfers between devices, swap_faces(): received.append(lax.ppermute(face, ('gz', 'gx'), pairs))  2.48 us
  transfers between devices with their start and end apart: 10, of which 6 were waited for; matrix products, arithmetic and copies ran while one was open for 0% of the time, Pallas kernels for 2%

profile of v4, /device:TPU:0, one launch (start us, length us, event | category | flops | bytes accessed | tf_op | source)
XLA Modules:
  0.0 44.3 jit_solution(7779716355214553170)
XLA Ops:
  0.6 0.1 shard_map.78
  0.7 0.0 copy-start.4
  0.7 0.0 copy-start.2
  0.7 0.8 %copy-done.1 = bf16[512,128]{1,0:T(8,128)(2,1)S(1)} copy-done((bf16[512,128]{1,0:T(8,128)(2,1)S(1)}, bf16[512,128]{1,0:T(8,128)(2,1)}, u32[]{:S(2)}) %copy-start.1) | copy-done | bytes 131096
  1.5 0.0 copy-done.3
  1.5 0.0 copy-done.2
  1.5 1.4 %shard_map.79 = bf16[1088,128]{1,0:T(8,128)(2,1)} custom-call(s32[1,512]{1,0:T(1,128)S(1)} %bitcast.8, s32[1,512]{1,0:T(1,128)S(1)} %bitcast.10, bf16[3,512]{1,0:T(4,128)(2,1)S(1)} %copy-done.3, bf16[512,128]{1,0:T(8,128)(2,1)S(1)} %copy-done.1, bf16[128,128]{1,0:T(8,128)(2,1)S(1)} %get-tuple-element.28.earlier_ref), custom_call_target="tpu_custom_call" | custom-call | bytes 449536 | tf_op jit(solution)/shard_map/pallas_call | solution.py:27
  2.9 7.3 %all-to-all-start = ((bf16[32,17,2,128]{3,2,1,0:T(2,128)(2,1)}), bf16[32,17,2,128]{3,2,1,0:T(2,128)(2,1)S(1)}, u32[]{:S(2)}, u32[]{:S(2)}) async-start(bf16[32,17,2,128]{3,2,1,0:T(2,128)(2,1)} %bitcast.2), calls=%async_computation | async-start | bytes 557056 | tf_op jit(solution)/shard_map/all_to_all | solution.py:429
  10.3 0.7 %shard_map.77 = (f32[27,2,8,128]{3,2,1,0:T(8,128)S(1)}, f32[27,2,8,128]{3,2,1,0:T(8,128)S(1)}, f32[4,2,8,128]{3,2,1,0:T(8,128)S(1)}, f32[27,128]{1,0:T(8,128)S(1)}) custom-call(f32[27]{0:T(128)S(1)} %copy-done.5, f32[27,2,8,128]{3,2,1,0:T(8,128)S(1)} %copy-done), custom_call_target="tpu_custom_call" | custom-call | bytes 710252 | tf_op jit(solution)/shard_map/pallas_call | solution.py:27
  11.0 10.3 %all-to-all-done = bf16[32,17,2,128]{3,2,1,0:T(2,128)(2,1)S(1)} async-done(((bf16[32,17,2,128]{3,2,1,0:T(2,128)(2,1)}), bf16[32,17,2,128]{3,2,1,0:T(2,128)(2,1)S(1)}, u32[]{:S(2)}, u32[]{:S(2)}) %all-to-all-start) | async-done | bytes 278560 | tf_op jit(solution)/shard_map/all_to_all | solution.py:429
  21.3 0.4 %shard_map.80 = (f32[27,2,8,128]{3,2,1,0:T(8,128)S(1)}, f32[9,8,128]{2,1,0:T(8,128)S(1)}, f32[9,8,128]{2,1,0:T(8,128)S(1)}, f32[3,2,8,128]{3,2,1,0:T(8,128)S(1)}...) custom-call(bf16[1088,128]{1,0:T(8,128)(2,1)S(1)} %bitcast.6, ...), custom_call_target="tpu_custom_call" | custom-call | bytes 1765376 | tf_op jit(solution)/shard_map/pallas_call | solution.py:27
  21.8 0.1 collective-permute-start
  21.9 0.5 %collective-permute-start.1 = (f32[9,8,128]{2,1,0:T(8,128)S(1)}, f32[9,8,128]{2,1,0:T(8,128)S(1)}, u32[]{:S(2)}, u32[]{:S(2)}) collective-permute-start(f32[9,8,128]{2,1,0:T(8,128)S(1)} %get-tuple-element.36), channel_id=1, source_target_pairs={{0,1},{1,0},{2,3},{3,2},{4,5},{5,4},{6,7},{7,6},{8,16},{9,17},{10,... | collective-permute-start | bytes 110600 | tf_op jit(solution)/shard_map/ppermute | solution.py:394
  22.4 3.4 %collective-permute-done.near_ref = f32[9,8,128]{2,1,0:T(8,128)S(1)} collective-permute-done((f32[9,8,128]{2,1,0:T(8,128)S(1)}, f32[9,8,128]{2,1,0:T(8,128)S(1)}, u32[]{:S(2)}, u32[]{:S(2)}) %collective-permute-start) | collective-permute-done | bytes 36896 | tf_op jit(solution)/shard_map/ppermute | solution.py:394
  25.8 0.0 collective-permute-done.1.far_ref
  25.8 0.1 collective-permute-start.2
  25.9 0.1 collective-permute-start.3
  26.0 0.2 shard_map.82
  26.2 0.9 %collective-permute-done.2.inner_ref = f32[18,128]{1,0:T(8,128)S(1)} collective-permute-done((f32[18,128]{1,0:T(8,128)S(1)}, f32[18,128]{1,0:T(8,128)S(1)}, u32[]{:S(2)}, u32[]{:S(2)}) %collective-permute-start.2) | collective-permute-done | bytes 9248 | tf_op jit(solution)/shard_map/ppermute | solution.py:399
  27.1 3.8 %collective-permute-done.3.outer_ref = f32[18,128]{1,0:T(8,128)S(1)} collective-permute-done((f32[18,128]{1,0:T(8,128)S(1)}, f32[18,128]{1,0:T(8,128)S(1)}, u32[]{:S(2)}, u32[]{:S(2)}) %collective-permute-start.3) | collective-permute-done | bytes 9248 | tf_op jit(solution)/shard_map/ppermute | solution.py:405
  30.9 1.3 %shard_map.83 = (f32[27,2,8,128]{3,2,1,0:T(8,128)S(1)}, f32[9,8,128]{2,1,0:T(8,128)S(1)}, f32[9,8,128]{2,1,0:T(8,128)S(1)}, f32[18,128]{1,0:T(8,128)S(1)}, f32[18,128]{1,0:T(8,128)S(1)}, /*index=5*/f32[128,128]{1,0:T(8,128)}) custom-call(f32[27,128]{1,0:T(8,128)S(1)} %get-tuple-element.27.rates_ref, f32[27,2,8,128]{3,2,1,0:T(8,128)S(1)} %get-tuple-element.34.post_ref, ...), custom_call_target="tpu_custom_call" | custom-call | bytes 1029632 | tf_op jit(solution)/shard_map/pallas_call | solution.py:27
  32.2 3.7 %all-to-all-start.1 = ((f32[32,4,128]{2,1,0:T(4,128)}), f32[32,4,128]{2,1,0:T(4,128)S(1)}, u32[]{:S(2)}, u32[]{:S(2)}) async-start(f32[32,4,128]{2,1,0:T(4,128)} %bitcast.4), calls=%async_computation.1 | async-start | bytes 131072 | tf_op jit(solution)/shard_map/all_to_all | solution.py:459
  35.8 1.8 %collective-permute-start.4 = (f32[9,8,128]{2,1,0:T(8,128)S(1)}, f32[9,8,128]{2,1,0:T(8,128)S(1)}, u32[]{:S(2)}, u32[]{:S(2)}) collective-permute-start(f32[9,8,128]{2,1,0:T(8,128)S(1)} %get-tuple-element.45), channel_id=1, source_target_pairs={{0,8},{1,9},{2,10},{3,11},{4,12},{5,13},{6,14},{7,15},{8,0},{9,1},... | collective-permute-start | bytes 110600 | tf_op jit(solution)/shard_map/ppermute | solution.py:394
  37.7 0.0 collective-permute-start.5
  37.7 0.5 %collective-permute-start.6 = (f32[18,128]{1,0:T(8,128)S(1)}, f32[18,128]{1,0:T(8,128)S(1)}, u32[]{:S(2)}, u32[]{:S(2)}) collective-permute-start(f32[18,128]{1,0:T(8,128)S(1)} %get-tuple-element.47), channel_id=1, source_target_pairs={{0,1},{1,0},{2,3},{3,2},{4,5},{5,4},{6,7},{7,6},{8,9},{9,8},{10,11... | collective-permute-start | bytes 27656 | tf_op jit(solution)/shard_map/ppermute | solution.py:399
  38.2 2.9 %collective-permute-start.7 = (f32[18,128]{1,0:T(8,128)S(1)}, f32[18,128]{1,0:T(8,128)S(1)}, u32[]{:S(2)}, u32[]{:S(2)}) collective-permute-start(f32[18,128]{1,0:T(8,128)S(1)} %get-tuple-element.48), channel_id=1, source_target_pairs={{0,7},{1,2},{2,1},{3,4},{4,3},{5,6},{6,5},{7,0},{8,15},{9,10},{10,... | collective-permute-start | bytes 27656 | tf_op jit(solution)/shard_map/ppermute | solution.py:405
  41.1 0.0 collective-permute-done.6.inner_ref
  41.1 2.0 %collective-permute-done.7.outer_ref = f32[18,128]{1,0:T(8,128)S(1)} collective-permute-done((f32[18,128]{1,0:T(8,128)S(1)}, f32[18,128]{1,0:T(8,128)S(1)}, u32[]{:S(2)}, u32[]{:S(2)}) %collective-permute-start.7) | collective-permute-done | bytes 9248 | tf_op jit(solution)/shard_map/ppermute | solution.py:405
  43.1 0.0 collective-permute-done.4.near_ref
  43.1 0.0 collective-permute-done.5.far_ref
  43.1 0.2 all-to-all-done.1
  43.3 1.0 %shard_map.84 = (f32[27,2,8,128]{3,2,1,0:T(8,128)}, f32[3,512]{1,0:T(4,128)}) custom-call(f32[27,2,8,128]{3,2,1,0:T(8,128)S(1)} %get-tuple-element.44.post_ref, f32[9,8,128]{2,1,0:T(8,128)S(1)} %collective-permute-done.4.near_ref, f32[9,8,128]{2,1,0:T(8,128)S(1)} %collective-permute-done.5.far_ref, f32[18,128]{1,0:T(8,128)S(1)} %collective-permute-done.6.inner_ref, ...), custom_call_target="tpu_custom_call" | custom-call | bytes 704512 | tf_op jit(solution)/shard_map/pallas_call | solution.py:27
  (8 shorter events, 0.0 us)
Async XLA Ops:
  0.6 0.9 %copy-start.1 = (bf16[512,128]{1,0:T(8,128)(2,1)S(1)}, bf16[512,128]{1,0:T(8,128)(2,1)}, u32[]{:S(2)}) copy-start(bf16[512,128]{1,0:T(8,128)(2,1)} %fraction_ref.1) | copy-start | bytes 393220
  0.6 0.9 %copy-start.3 = (bf16[3,512]{1,0:T(4,128)(2,1)S(1)}, bf16[3,512]{1,0:T(4,128)(2,1)}, u32[]{:S(2)}) copy-start(bf16[3,512]{1,0:T(4,128)(2,1)} %speed_ref.1) | copy-start | bytes 9220
  0.7 0.8 %copy-start.4 = (s32[512]{0:T(512)S(1)}, s32[512]{0:T(512)}, u32[]{:S(2)}) copy-start(s32[512]{0:T(512)} %param.11) | copy-start | bytes 6148
  0.7 0.8 %copy-start.2 = (s32[512,1]{0,1:T(1,128)S(1)}, s32[512,1]{0,1:T(1,128)}, u32[]{:S(2)}) copy-start(s32[512,1]{0,1:T(1,128)} %param.10) | copy-start | bytes 6148
  2.9 7.3 %copy-start = (f32[27,2,8,128]{3,2,1,0:T(8,128)S(1)}, f32[27,2,8,128]{3,2,1,0:T(8,128)}, u32[]{:S(2)}) copy-start(f32[27,2,8,128]{3,2,1,0:T(8,128)} %fields_ref.1) | copy-start | bytes 663556
  2.9 7.3 %copy-start.5 = (f32[27]{0:T(128)S(1)}, f32[27]{0:T(128)}, u32[]{:S(2)}) copy-start(f32[27]{0:T(128)} %rates_ref.1) | copy-start | bytes 328
  2.9 18.4 %all-to-all-start = ((bf16[32,17,2,128]{3,2,1,0:T(2,128)(2,1)}), bf16[32,17,2,128]{3,2,1,0:T(2,128)(2,1)S(1)}, u32[]{:S(2)}, u32[]{:S(2)}) async-start(bf16[32,17,2,128]{3,2,1,0:T(2,128)(2,1)} %bitcast.2), calls=%async_computation | async-start | bytes 557056 | tf_op jit(solution)/shard_map/all_to_all | solution.py:429
  21.8 4.0 %collective-permute-start = (f32[9,8,128]{2,1,0:T(8,128)S(1)}, f32[9,8,128]{2,1,0:T(8,128)S(1)}, u32[]{:S(2)}, u32[]{:S(2)}) collective-permute-start(f32[9,8,128]{2,1,0:T(8,128)S(1)} %get-tuple-element.35), channel_id=1, source_target_pairs={{0,8},{1,9},{2,10},{3,11},{4,12},{5,13},{6,14},{7,15},{8,0},{9,1},... | collective-permute-start | bytes 110600 | tf_op jit(solution)/shard_map/ppermute | solution.py:394
  21.9 3.9 %collective-permute-start.1 = (f32[9,8,128]{2,1,0:T(8,128)S(1)}, f32[9,8,128]{2,1,0:T(8,128)S(1)}, u32[]{:S(2)}, u32[]{:S(2)}) collective-permute-start(f32[9,8,128]{2,1,0:T(8,128)S(1)} %get-tuple-element.36), channel_id=1, source_target_pairs={{0,1},{1,0},{2,3},{3,2},{4,5},{5,4},{6,7},{7,6},{8,16},{9,17},{10,... | collective-permute-start | bytes 110600 | tf_op jit(solution)/shard_map/ppermute | solution.py:394
  25.8 1.2 %collective-permute-start.2 = (f32[18,128]{1,0:T(8,128)S(1)}, f32[18,128]{1,0:T(8,128)S(1)}, u32[]{:S(2)}, u32[]{:S(2)}) collective-permute-start(f32[18,128]{1,0:T(8,128)S(1)} %get-tuple-element.37), channel_id=1, source_target_pairs={{0,1},{1,0},{2,3},{3,2},{4,5},{5,4},{6,7},{7,6},{8,9},{9,8},{10,11... | collective-permute-start | bytes 27656 | tf_op jit(solution)/shard_map/ppermute | solution.py:399
  25.9 5.0 %collective-permute-start.3 = (f32[18,128]{1,0:T(8,128)S(1)}, f32[18,128]{1,0:T(8,128)S(1)}, u32[]{:S(2)}, u32[]{:S(2)}) collective-permute-start(f32[18,128]{1,0:T(8,128)S(1)} %get-tuple-element.38), channel_id=1, source_target_pairs={{0,7},{1,2},{2,1},{3,4},{4,3},{5,6},{6,5},{7,0},{8,15},{9,10},{10,... | collective-permute-start | bytes 27656 | tf_op jit(solution)/shard_map/ppermute | solution.py:405
  32.2 11.2 %all-to-all-start.1 = ((f32[32,4,128]{2,1,0:T(4,128)}), f32[32,4,128]{2,1,0:T(4,128)S(1)}, u32[]{:S(2)}, u32[]{:S(2)}) async-start(f32[32,4,128]{2,1,0:T(4,128)} %bitcast.4), calls=%async_computation.1 | async-start | bytes 131072 | tf_op jit(solution)/shard_map/all_to_all | solution.py:459
  35.8 7.3 %collective-permute-start.4 = (f32[9,8,128]{2,1,0:T(8,128)S(1)}, f32[9,8,128]{2,1,0:T(8,128)S(1)}, u32[]{:S(2)}, u32[]{:S(2)}) collective-permute-start(f32[9,8,128]{2,1,0:T(8,128)S(1)} %get-tuple-element.45), channel_id=1, source_target_pairs={{0,8},{1,9},{2,10},{3,11},{4,12},{5,13},{6,14},{7,15},{8,0},{9,1},... | collective-permute-start | bytes 110600 | tf_op jit(solution)/shard_map/ppermute | solution.py:394
  37.7 5.4 %collective-permute-start.5 = (f32[9,8,128]{2,1,0:T(8,128)S(1)}, f32[9,8,128]{2,1,0:T(8,128)S(1)}, u32[]{:S(2)}, u32[]{:S(2)}) collective-permute-start(f32[9,8,128]{2,1,0:T(8,128)S(1)} %get-tuple-element.46), channel_id=1, source_target_pairs={{0,1},{1,0},{2,3},{3,2},{4,5},{5,4},{6,7},{7,6},{8,16},{9,17},{10,... | collective-permute-start | bytes 110600 | tf_op jit(solution)/shard_map/ppermute | solution.py:394
  37.7 3.5 %collective-permute-start.6 = (f32[18,128]{1,0:T(8,128)S(1)}, f32[18,128]{1,0:T(8,128)S(1)}, u32[]{:S(2)}, u32[]{:S(2)}) collective-permute-start(f32[18,128]{1,0:T(8,128)S(1)} %get-tuple-element.47), channel_id=1, source_target_pairs={{0,1},{1,0},{2,3},{3,2},{4,5},{5,4},{6,7},{7,6},{8,9},{9,8},{10,11... | collective-permute-start | bytes 27656 | tf_op jit(solution)/shard_map/ppermute | solution.py:399
  38.2 4.9 %collective-permute-start.7 = (f32[18,128]{1,0:T(8,128)S(1)}, f32[18,128]{1,0:T(8,128)S(1)}, u32[]{:S(2)}, u32[]{:S(2)}) collective-permute-start(f32[18,128]{1,0:T(8,128)S(1)} %get-tuple-element.48), channel_id=1, source_target_pairs={{0,7},{1,2},{2,1},{3,4},{4,3},{5,6},{6,5},{7,0},{8,15},{9,10},{10,... | collective-permute-start | bytes 27656 | tf_op jit(solution)/shard_map/ppermute | solution.py:405

commit v5 on v4

--- a/solution.py
+++ b/solution.py
@@ -20,16 +20,14 @@
     return lax.broadcasted_iota(i32, shape, dim)
 
 
-def call(kernel, outs, *operands, smem=(), scratch=(), flops=0):
+def call(kernel, outs, *operands, scratch=(), flops=0):
     size = sum(o.size * o.dtype.itemsize for o in operands) + sum(
         int(np.prod(o.shape)) * o.dtype.itemsize for o in outs
     )
     return pl.pallas_call(
         kernel,
         out_shape=list(outs),
-        in_specs=[
-            pl.BlockSpec(memory_space=pltpu.SMEM if n in smem else pltpu.VMEM) for n in range(len(operands))
-        ],
+        in_specs=[pl.BlockSpec(memory_space=pltpu.VMEM)] * len(operands),
         out_specs=[pl.BlockSpec(memory_space=pltpu.VMEM)] * len(outs),
         scratch_shapes=list(scratch),
         compiler_params=pltpu.CompilerParams(vmem_limit_bytes=24 * 1024 * 1024),
@@ -187,27 +185,15 @@
     return jnp.where(even_place("gz"), near_ref[n, x], far_ref[n, x])
 
 
-def relax_kernel(rates_ref, fields_ref, kept_ref, swapped_ref, sums_ref, rate_rows_ref):
-    rate = [rates_ref[a] for a in range(27)]
-    for a in range(27):
-        rate_rows_ref[a : a + 1] = jnp.full((1, rate_rows_ref.shape[1]), rate[a], f32)
-    for z in range(fields_ref.shape[1]):
-        density, momentum, kept, swapped = relax([fields_ref[i, z] for i in range(27)], rate)
-        for n, value in enumerate([density] + momentum):
-            sums_ref[n, z] = value
-        for i in range(27):
-            kept_ref[i, z] = kept[i]
-            swapped_ref[i, z] = swapped[i]
-
-
 def first_kernel(
-    devices, capacity, recv_ref, kept_ref, swapped_ref, sums_ref, spread_ref, own_ref,
+    devices, capacity, recv_ref, fields_ref, rates_ref, spread_ref, own_ref,
     post_ref, near_ref, far_ref, push_ref, held_ref, line_ref, slot_ref, wide_ref,
 ):
     width = recv_ref.shape[1]
     block, slots = capacity + 2, devices * capacity
-    depth, length = kept_ref.shape[1], kept_ref.shape[2]
+    depth, length = fields_ref.shape[1], fields_ref.shape[2]
     lines = depth * length
+    rate = [rates_ref[:, a : a + 1] for a in range(27)]
     wide_ref[...] = recv_ref[...].astype(f32)
     facts = wide_ref[pl.ds(capacity, devices, stride=block), :]
     slot_rows = jnp.concatenate(
@@ -228,10 +214,8 @@
         jnp.concatenate(gather, axis=0).astype(bf16), slot_rows, preferred_element_type=f32
     )
     for z in range(depth):
-        sums = [sums_ref[n, z] for n in range(4)]
-        kept, swapped = [kept_ref[i, z] for i in range(27)], [swapped_ref[i, z] for i in range(27)]
-        grains = grains_at(held_ref, z, depth, length)
-        post, push = exchange(sums[0], sums[1:], kept, swapped, *grains)
+        relaxed = relax([fields_ref[i, z] for i in range(27)], rate)
+        post, push = exchange(*relaxed, *grains_at(held_ref, z, depth, length))
         for i in range(27):
             post_ref[i, z] = post[i]
         for k in range(3):
@@ -247,7 +231,7 @@
     at_rank_ref[...] = jnp.where(iota(at_rank_ref.shape, 0) == rank, 1.0, 0.0)
 
 
-def ends_kernel(post_ref, near_ref, far_ref, inner_ref, outer_ref):
+def ends_kernel(post_ref, far_ref, near_ref, inner_ref, outer_ref):
     depth, length = post_ref.shape[1], post_ref.shape[2]
     even = even_place("gx")
 
@@ -302,7 +286,7 @@
 
 
 def second_kernel(
-    capacity, rates_ref, post_ref, near_ref, far_ref, inner_ref, outer_ref,
+    capacity, rates_ref, post_ref, far_ref, near_ref, outer_ref, inner_ref,
     held_ref, push_ref, line_ref, turned_ref,
     next_ref, next_near_ref, next_far_ref, next_inner_ref, next_outer_ref, back_ref, right_ref, left_ref,
 ):
@@ -310,7 +294,7 @@
     lines = depth * length
     slots = turned_ref.shape[1]
     halo = (near_ref, far_ref, inner_ref, outer_ref)
-    rate = [rates_ref[a : a + 1] for a in range(27)]
+    rate = [rates_ref[:, a : a + 1] for a in range(27)]
     pushes = []
     for z in range(depth):
         relaxed = relax(streamed(post_ref, *halo, z), rate)
@@ -365,7 +349,7 @@
 
 
 def last_kernel(
-    capacity, post_ref, near_ref, far_ref, inner_ref, outer_ref, back_ref, hot_ref, at_rank_ref,
+    capacity, post_ref, outer_ref, far_ref, near_ref, inner_ref, back_ref, hot_ref, at_rank_ref,
     scaled_ref, force_ref,
 ):
     for z in range(post_ref.shape[1]):
@@ -429,18 +413,16 @@
     recv = lax.all_to_all(
         send.reshape(devices, capacity // 2 + 1, 2, width), both, split_axis=0, concat_axis=0, tiled=True
     ).reshape(rows, width)
-    state, sums = shape(populations.shape, f32), shape((4, depth, length, width), f32)
+    state = shape(populations.shape, f32)
     face, ends = shape((9, length, width), f32), shape((9 * depth, width), f32)
-    kept, swapped, sums, rate_rows = call(
-        relax_kernel, [state, state, sums, shape((27, width), f32)], rates, populations, smem=(0,)
-    )
+    rates = rates.reshape(1, 27)
     post, near, far, push, held, slot_line, slot_rows = call(
         functools.partial(first_kernel, devices, capacity),
         [
             state, face, face, shape((3, depth, length, width), f32),
             shape((4 * lines, width), f32), shape((1, slots), i32), shape((slots, width), bf16),
         ],
-        recv, kept, swapped, sums, spread, own, scratch=[pltpu.VMEM((rows, width), f32)],
+        recv, populations, rates, spread, own, scratch=[pltpu.VMEM((rows, width), f32)],
     )
     near, far = swap_faces(near, far)
     turned, hot, at_rank = call(
@@ -448,12 +430,12 @@
         [shape((width, slots), bf16), shape((devices, grains), bf16), shape((capacity, grains), f32)],
         slot_rows, dest, earlier,
     )
-    inner, outer = call(ends_kernel, [ends, ends], post, near, far)
-    inner, outer = swap_inner(inner), swap_outer(outer)
+    inner, outer = call(ends_kernel, [ends, ends], post, far, near)
+    outer, inner = swap_outer(outer), swap_inner(inner)
     post, next_near, next_far, inner, outer, back = call(
         functools.partial(second_kernel, capacity),
         [state, face, face, ends, ends, shape((4 * devices, LANES), f32)],
-        rate_rows, post, near, far, inner, outer, held, push, slot_line, turned,
+        rates, post, far, near, outer, inner, held, push, slot_line, turned,
         scratch=[pltpu.VMEM(ends.shape, f32)] * 2,
     )
     back = lax.all_to_all(
@@ -465,7 +447,7 @@
     scaled, grain_force = call(
         functools.partial(last_kernel, capacity),
         [state, shape((3, grains), f32)],
-        post, near, far, inner, outer, back, hot, at_rank,
+        post, outer, far, near, inner, back, hot, at_rank,
     )
     return (scaled, grain_force)
 

time: 44.5 us -> 44.2 us (level)
  blocking collectives: 0 us -> 18.2 us
  waiting for transfers between devices: 20.6 us -> 9.16 us
  starting transfers between devices: 17 us -> 10.8 us
  Pallas kernels: 5.04 us -> 3.64 us
  local copies, waits for them, and re-layouts: 0.82 us -> 1.47 us
    all_to_all x0 -> x1, blocking collectives: none -> 18.2 us  [per_device(): lax.all_to_all(send.reshape(devices, capacity // 2 + 1, 2, width), both,...]
    all_to_all x1 -> x0, waiting for transfers between devices: 10.3 us -> none  [per_device(): lax.all_to_all(send.reshape(devices, capacity // 2 + 1, 2, width), both,...]
    all_to_all x1 -> x0, starting transfers between devices: 7.3 us -> none  [per_device(): lax.all_to_all(send.reshape(devices, capacity // 2 + 1, 2, width), both,...]
    ppermute x4, starting transfers between devices: 2.48 us -> 5.24 us  [swap_faces(): received.append(lax.ppermute(face, ('gz', 'gx'), pairs))]
    pallas_call x8 -> x7, Pallas kernels: 5.04 us -> 3.64 us  [call(): pl.pallas_call(kernel, out_shape=list(outs), in_specs=[pl.BlockSpec(memor...]
    all_to_all x1, starting transfers between devices: 3.67 us -> 2.57 us  [per_device(): lax.all_to_all(back.reshape(devices, 4, LANES), both, split_axis=0, conca...]
    ppermute x4, waiting for transfers between devices: 3.38 us -> 2.48 us  [swap_faces(): received.append(lax.ppermute(face, ('gz', 'gx'), pairs))]
    ppermute x2, waiting for transfers between devices: 0.89 us -> 0.01 us  [swap_inner(): lax.ppermute(inner, 'gx', [(i, i ^ 1) for i in range(lax.axis_size('gx'))])]
  transfers between devices with their start and end apart: 10 -> 9, of which waited for: 6 -> 3; matrix products, arithmetic and copies ran while one was open for 0% -> 0% of each run, Pallas kernels for 2% -> 0%
where the time goes in v5:
time: 44.2 us; the launch traced here: 44 us
  blocking collectives  18.2 us (41%)
  starting transfers between devices  10.8 us (24%)
  waiting for transfers between devices  9.16 us (21%)
  Pallas kernels  3.64 us (8%)
  local copies, waits for them, and re-layouts  1.47 us (3%)
  between operations  0.74 us (2%)
    all_to_all x1, blocking collectives, per_device(): lax.all_to_all(send.reshape(devices, capacity // 2 + 1, 2, width), both,...  18.2 us
    ppermute x2, waiting for transfers between devices, swap_outer(): return lax.ppermute(outer, 'gx', pairs)  6.67 us
    ppermute x4, starting transfers between devices, swap_faces(): received.append(lax.ppermute(face, ('gz', 'gx'), pairs))  5.24 us
    pallas_call x7, Pallas kernels, call(): pl.pallas_call(kernel, out_shape=list(outs), in_specs=[pl.BlockSpec(memor...  3.64 us
    ppermute x2, starting transfers between devices, swap_outer(): return lax.ppermute(outer, 'gx', pairs)  2.73 us
    all_to_all x1, starting transfers between devices, per_device(): lax.all_to_all(back.reshape(devices, 4, LANES), both, split_axis=0, conca...  2.57 us
    ppermute x4, waiting for transfers between devices, swap_faces(): received.append(lax.ppermute(face, ('gz', 'gx'), pairs))  2.48 us
    unnamed x12, local copies, waits for them, and re-layouts  1.47 us
  transfers between devices with their start and end apart: 9, of which 3 were waited for; matrix products, arithmetic and copies ran while one was open for 0% of the time, Pallas kernels for 0%

profile of v5, /device:TPU:0, one launch (start us, length us, event | category | flops | bytes accessed | tf_op | source)
XLA Modules:
  0.0 44.0 jit_solution(8694168893765814412)
XLA Ops:
  0.6 0.0 copy-start.1
  0.6 0.0 copy-start.3
  0.6 0.1 shard_map.77
  0.7 0.0 copy-start.4
  0.7 0.0 copy-start.2
  0.7 0.8 %copy-done.1 = bf16[512,128]{1,0:T(8,128)(2,1)S(1)} copy-done((bf16[512,128]{1,0:T(8,128)(2,1)S(1)}, bf16[512,128]{1,0:T(8,128)(2,1)}, u32[]{:S(2)}) %copy-start.1) | copy-done | bytes 131096
  1.5 0.7 %shard_map.78 = bf16[1088,128]{1,0:T(8,128)(2,1)S(1)} custom-call(s32[1,512]{1,0:T(1,128)S(1)} %bitcast.10, s32[1,512]{1,0:T(1,128)S(1)} %bitcast.12, bf16[3,512]{1,0:T(4,128)(2,1)S(1)} %copy-done.3, bf16[512,128]{1,0:T(8,128)(2,1)S(1)} %copy-done.1, bf16[128,128]{1,0:T(8,128)(2,1)S(1)} %get-tuple-element.23.earlier_ref), custom_call_target="tpu_custom_call" | custom-call | bytes 449536 | tf_op jit(solution)/shard_map/pallas_call | solution.py:27
  2.2 0.0 copy-start
  2.2 18.2 %all_to_all.10 = bf16[32,17,2,128]{3,2,1,0:T(2,128)(2,1)S(1)} all-to-all(bf16[32,17,2,128]{3,2,1,0:T(2,128)(2,1)S(1)} %bitcast.7), channel_id=1, replica_groups=mesh['gz'=4,'gx'=8] {'gz','gx'}, dimensions={0} | all-to-all | bytes 557056 | tf_op jit(solution)/shard_map/all_to_all | solution.py:413
  20.4 0.7 %copy-done.5 = f32[27]{0:T(128)S(1)} copy-done((f32[27]{0:T(128)S(1)}, f32[27]{0:T(128)}, u32[]{:S(2)}) %copy-start.5) | copy-done | bytes 132
  21.1 0.5 %shard_map.79 = (f32[27,2,8,128]{3,2,1,0:T(8,128)S(1)}, f32[9,8,128]{2,1,0:T(8,128)S(1)}, f32[9,8,128]{2,1,0:T(8,128)S(1)}, f32[3,2,8,128]{3,2,1,0:T(8,128)S(1)}...) custom-call(bf16[1088,128]{1,0:T(8,128)(2,1)S(1)} %bitcast.8, ...), custom_call_target="tpu_custom_call" | custom-call | bytes 1511532 | tf_op jit(solution)/shard_map/pallas_call | solution.py:27
  21.6 0.2 collective-permute-start
  21.8 1.9 %collective-permute-start.1 = (f32[9,8,128]{2,1,0:T(8,128)S(1)}, f32[9,8,128]{2,1,0:T(8,128)S(1)}, u32[]{:S(2)}, u32[]{:S(2)}) collective-permute-start(f32[9,8,128]{2,1,0:T(8,128)S(1)} %get-tuple-element.28), channel_id=1, source_target_pairs={{0,8},{1,9},{2,10},{3,11},{4,12},{5,13},{6,14},{7,15},{8,0},{9,1},... | collective-permute-start | bytes 110600 | tf_op jit(solution)/shard_map/ppermute | solution.py:378
  23.6 0.0 collective-permute-done.far_ref
  23.7 2.5 %collective-permute-done.1.near_ref = f32[9,8,128]{2,1,0:T(8,128)S(1)} collective-permute-done((f32[9,8,128]{2,1,0:T(8,128)S(1)}, f32[9,8,128]{2,1,0:T(8,128)S(1)}, u32[]{:S(2)}, u32[]{:S(2)}) %collective-permute-start.1) | collective-permute-done | bytes 36896 | tf_op jit(solution)/shard_map/ppermute | solution.py:378
  26.1 0.1 collective-permute-start.2
  26.2 0.3 collective-permute-start.3
  26.5 0.2 shard_map.81
  26.7 4.4 %collective-permute-done.2.outer_ref = f32[18,128]{1,0:T(8,128)S(1)} collective-permute-done((f32[18,128]{1,0:T(8,128)S(1)}, f32[18,128]{1,0:T(8,128)S(1)}, u32[]{:S(2)}, u32[]{:S(2)}) %collective-permute-start.2) | collective-permute-done | bytes 9248 | tf_op jit(solution)/shard_map/ppermute | solution.py:389
  31.1 0.0 collective-permute-done.3.inner_ref
  31.1 1.3 %shard_map.82 = (f32[27,2,8,128]{3,2,1,0:T(8,128)S(1)}, f32[9,8,128]{2,1,0:T(8,128)S(1)}, f32[9,8,128]{2,1,0:T(8,128)S(1)}, f32[18,128]{1,0:T(8,128)S(1)}, f32[18,128]{1,0:T(8,128)S(1)}, /*index=5*/f32[128,128]{1,0:T(8,128)}) custom-call(f32[1,27]{1,0:T(1,128)S(1)} %bitcast.14, f32[27,2,8,128]{3,2,1,0:T(8,128)S(1)} %get-tuple-element.26.post_ref, ...), custom_call_target="tpu_custom_call" | custom-call | bytes 1015916 | tf_op jit(solution)/shard_map/pallas_call | solution.py:27
  32.4 2.6 %all-to-all-start.1 = ((f32[32,4,128]{2,1,0:T(4,128)}), f32[32,4,128]{2,1,0:T(4,128)S(1)}, u32[]{:S(2)}, u32[]{:S(2)}) async-start(f32[32,4,128]{2,1,0:T(4,128)} %bitcast.5), calls=%async_computation.1 | async-start | bytes 131072 | tf_op jit(solution)/shard_map/all_to_all | solution.py:441
  35.0 0.2 collective-permute-start.5
  35.1 3.0 %collective-permute-start.6 = (f32[9,8,128]{2,1,0:T(8,128)S(1)}, f32[9,8,128]{2,1,0:T(8,128)S(1)}, u32[]{:S(2)}, u32[]{:S(2)}) collective-permute-start(f32[9,8,128]{2,1,0:T(8,128)S(1)} %get-tuple-element.39), channel_id=1, source_target_pairs={{0,8},{1,9},{2,10},{3,11},{4,12},{5,13},{6,14},{7,15},{8,0},{9,1},... | collective-permute-start | bytes 110600 | tf_op jit(solution)/shard_map/ppermute | solution.py:378
  38.1 2.7 %collective-permute-start.4 = (f32[18,128]{1,0:T(8,128)S(1)}, f32[18,128]{1,0:T(8,128)S(1)}, u32[]{:S(2)}, u32[]{:S(2)}) collective-permute-start(f32[18,128]{1,0:T(8,128)S(1)} %get-tuple-element.37), channel_id=1, source_target_pairs={{0,7},{1,2},{2,1},{3,4},{4,3},{5,6},{6,5},{7,0},{8,15},{9,10},{10,... | collective-permute-start | bytes 27656 | tf_op jit(solution)/shard_map/ppermute | solution.py:389
  40.8 0.0 collective-permute-start.7
  40.8 2.3 %collective-permute-done.4.outer_ref = f32[18,128]{1,0:T(8,128)S(1)} collective-permute-done((f32[18,128]{1,0:T(8,128)S(1)}, f32[18,128]{1,0:T(8,128)S(1)}, u32[]{:S(2)}, u32[]{:S(2)}) %collective-permute-start.4) | collective-permute-done | bytes 9248 | tf_op jit(solution)/shard_map/ppermute | solution.py:389
  43.1 0.0 collective-permute-done.7.inner_ref
  43.1 0.0 collective-permute-done.5.far_ref
  43.1 0.0 collective-permute-done.6.near_ref
  43.1 0.0 all-to-all-done.1
  43.1 0.9 %shard_map.83 = (f32[27,2,8,128]{3,2,1,0:T(8,128)}, f32[3,512]{1,0:T(4,128)}) custom-call(f32[27,2,8,128]{3,2,1,0:T(8,128)S(1)} %get-tuple-element.36.post_ref, f32[18,128]{1,0:T(8,128)S(1)} %collective-permute-done.4.outer_ref, f32[9,8,128]{2,1,0:T(8,128)S(1)} %collective-permute-done.5.far_ref, f32[9,8,128]{2,1,0:T(8,128)S(1)} %collective-permute-done.6.near_ref, ...), custom_call_target="tpu_custom_call" | custom-call | bytes 704512 | tf_op jit(solution)/shard_map/pallas_call | solution.py:27
  (6 shorter events, 0.0 us)
Async XLA Ops:
  0.6 0.9 %copy-start.1 = (bf16[512,128]{1,0:T(8,128)(2,1)S(1)}, bf16[512,128]{1,0:T(8,128)(2,1)}, u32[]{:S(2)}) copy-start(bf16[512,128]{1,0:T(8,128)(2,1)} %fraction_ref.1) | copy-start | bytes 393220
  0.6 0.9 %copy-start.3 = (bf16[3,512]{1,0:T(4,128)(2,1)S(1)}, bf16[3,512]{1,0:T(4,128)(2,1)}, u32[]{:S(2)}) copy-start(bf16[3,512]{1,0:T(4,128)(2,1)} %speed_ref.1) | copy-start | bytes 9220
  0.7 0.8 %copy-start.4 = (s32[512]{0:T(512)S(1)}, s32[512]{0:T(512)}, u32[]{:S(2)}) copy-start(s32[512]{0:T(512)} %param.11) | copy-start | bytes 6148
  0.7 0.8 %copy-start.2 = (s32[512,1]{0,1:T(1,128)S(1)}, s32[512,1]{0,1:T(1,128)}, u32[]{:S(2)}) copy-start(s32[512,1]{0,1:T(1,128)} %param.10) | copy-start | bytes 6148
  2.2 18.2 %copy-start = (f32[27,2,8,128]{3,2,1,0:T(8,128)S(1)}, f32[27,2,8,128]{3,2,1,0:T(8,128)}, u32[]{:S(2)}) copy-start(f32[27,2,8,128]{3,2,1,0:T(8,128)} %fields_ref.1) | copy-start | bytes 663556
  20.4 0.7 %copy-start.5 = (f32[27]{0:T(128)S(1)}, f32[27]{0:T(128)}, u32[]{:S(2)}) copy-start(f32[27]{0:T(128)} %param.7) | copy-start | bytes 328
  21.6 2.1 %collective-permute-start = (f32[9,8,128]{2,1,0:T(8,128)S(1)}, f32[9,8,128]{2,1,0:T(8,128)S(1)}, u32[]{:S(2)}, u32[]{:S(2)}) collective-permute-start(f32[9,8,128]{2,1,0:T(8,128)S(1)} %get-tuple-element.27), channel_id=1, source_target_pairs={{0,1},{1,0},{2,3},{3,2},{4,5},{5,4},{6,7},{7,6},{8,16},{9,17},{10,... | collective-permute-start | bytes 110600 | tf_op jit(solution)/shard_map/ppermute | solution.py:378
  21.8 4.4 %collective-permute-start.1 = (f32[9,8,128]{2,1,0:T(8,128)S(1)}, f32[9,8,128]{2,1,0:T(8,128)S(1)}, u32[]{:S(2)}, u32[]{:S(2)}) collective-permute-start(f32[9,8,128]{2,1,0:T(8,128)S(1)} %get-tuple-element.28), channel_id=1, source_target_pairs={{0,8},{1,9},{2,10},{3,11},{4,12},{5,13},{6,14},{7,15},{8,0},{9,1},... | collective-permute-start | bytes 110600 | tf_op jit(solution)/shard_map/ppermute | solution.py:378
  26.1 5.0 %collective-permute-start.2 = (f32[18,128]{1,0:T(8,128)S(1)}, f32[18,128]{1,0:T(8,128)S(1)}, u32[]{:S(2)}, u32[]{:S(2)}) collective-permute-start(f32[18,128]{1,0:T(8,128)S(1)} %get-tuple-element.29), channel_id=1, source_target_pairs={{0,7},{1,2},{2,1},{3,4},{4,3},{5,6},{6,5},{7,0},{8,15},{9,10},{10,... | collective-permute-start | bytes 27656 | tf_op jit(solution)/shard_map/ppermute | solution.py:389
  26.2 4.9 %collective-permute-start.3 = (f32[18,128]{1,0:T(8,128)S(1)}, f32[18,128]{1,0:T(8,128)S(1)}, u32[]{:S(2)}, u32[]{:S(2)}) collective-permute-start(f32[18,128]{1,0:T(8,128)S(1)} %get-tuple-element.30), channel_id=1, source_target_pairs={{0,1},{1,0},{2,3},{3,2},{4,5},{5,4},{6,7},{7,6},{8,9},{9,8},{10,11... | collective-permute-start | bytes 27656 | tf_op jit(solution)/shard_map/ppermute | solution.py:383
  32.4 10.7 %all-to-all-start.1 = ((f32[32,4,128]{2,1,0:T(4,128)}), f32[32,4,128]{2,1,0:T(4,128)S(1)}, u32[]{:S(2)}, u32[]{:S(2)}) async-start(f32[32,4,128]{2,1,0:T(4,128)} %bitcast.5), calls=%async_computation.1 | async-start | bytes 131072 | tf_op jit(solution)/shard_map/all_to_all | solution.py:441
  35.0 8.1 %collective-permute-start.5 = (f32[9,8,128]{2,1,0:T(8,128)S(1)}, f32[9,8,128]{2,1,0:T(8,128)S(1)}, u32[]{:S(2)}, u32[]{:S(2)}) collective-permute-start(f32[9,8,128]{2,1,0:T(8,128)S(1)} %get-tuple-element.38), channel_id=1, source_target_pairs={{0,1},{1,0},{2,3},{3,2},{4,5},{5,4},{6,7},{7,6},{8,16},{9,17},{10,... | collective-permute-start | bytes 110600 | tf_op jit(solution)/shard_map/ppermute | solution.py:378
  35.1 7.9 %collective-permute-start.6 = (f32[9,8,128]{2,1,0:T(8,128)S(1)}, f32[9,8,128]{2,1,0:T(8,128)S(1)}, u32[]{:S(2)}, u32[]{:S(2)}) collective-permute-start(f32[9,8,128]{2,1,0:T(8,128)S(1)} %get-tuple-element.39), channel_id=1, source_target_pairs={{0,8},{1,9},{2,10},{3,11},{4,12},{5,13},{6,14},{7,15},{8,0},{9,1},... | collective-permute-start | bytes 110600 | tf_op jit(solution)/shard_map/ppermute | solution.py:378
  38.1 4.9 %collective-permute-start.4 = (f32[18,128]{1,0:T(8,128)S(1)}, f32[18,128]{1,0:T(8,128)S(1)}, u32[]{:S(2)}, u32[]{:S(2)}) collective-permute-start(f32[18,128]{1,0:T(8,128)S(1)} %get-tuple-element.37), channel_id=1, source_target_pairs={{0,7},{1,2},{2,1},{3,4},{4,3},{5,6},{6,5},{7,0},{8,15},{9,10},{10,... | collective-permute-start | bytes 27656 | tf_op jit(solution)/shard_map/ppermute | solution.py:389
  40.8 2.3 %collective-permute-start.7 = (f32[18,128]{1,0:T(8,128)S(1)}, f32[18,128]{1,0:T(8,128)S(1)}, u32[]{:S(2)}, u32[]{:S(2)}) collective-permute-start(f32[18,128]{1,0:T(8,128)S(1)} %get-tuple-element.40), channel_id=1, source_target_pairs={{0,1},{1,0},{2,3},{3,2},{4,5},{5,4},{6,7},{7,6},{8,9},{9,8},{10,11... | collective-permute-start | bytes 27656 | tf_op jit(solution)/shard_map/ppermute | solution.py:383

commit v6 on v5

--- a/solution.py
+++ b/solution.py
@@ -70,27 +70,34 @@
     return jnp.concatenate(parts, axis=1)
 
 
-def pack_kernel(devices, capacity, dest_ref, line_ref, speed_ref, fraction_ref, earlier_ref, send_ref, rows_ref):
-    grains, width = fraction_ref.shape
-    block = capacity + 2
+def rank_kernel(
+    devices, capacity, dest_ref, line_ref, speed_ref, rates_ref, earlier_ref, position_ref, facts_ref, rates_out_ref
+):
+    grains, width = dest_ref.shape[1], facts_ref.shape[1]
     dest = dest_ref[...]
     hot = jnp.where(iota((devices, grains), 0) == dest, 1.0, 0.0)
     rank = ranks(hot, earlier_ref[...]).astype(i32)
+    position_ref[...] = dest * (capacity + 2) + rank
     speed = speed_ref[...].astype(f32)
     values = [speed[0:1], speed[1:2], speed[2:3], line_ref[...].astype(f32)]
     at_rank = iota((capacity, grains), 0) == rank
     facts = [jnp.where(at_rank, value, 0.0) for value in values]
     if 4 * capacity < width:
         facts.append(jnp.zeros((width - 4 * capacity, grains), f32))
-    fact_rows = lax.dot_general(
+    facts_ref[...] = lax.dot_general(
         hot.astype(bf16),
         jnp.concatenate(facts, axis=0).astype(bf16),
         (((1,), (1,)), ((), ())),
         preferred_element_type=f32,
     )
-    place = jnp.where(iota((devices * block, grains), 0) == dest * block + rank, 1.0, 0.0).astype(bf16)
+    rates_out_ref[...] = rates_ref[...]
+
+
+def pack_kernel(capacity, position_ref, facts_ref, fraction_ref, send_ref, rows_ref):
+    rows, grains = rows_ref.shape[0], fraction_ref.shape[0]
+    place = jnp.where(iota((rows, grains), 0) == position_ref[...], 1.0, 0.0).astype(bf16)
     rows_ref[...] = jnp.dot(place, fraction_ref[...], preferred_element_type=f32)
-    rows_ref[pl.ds(capacity, devices, stride=block), :] = fact_rows
+    rows_ref[pl.ds(capacity, facts_ref.shape[0], stride=capacity + 2), :] = facts_ref[...]
     send_ref[...] = rows_ref[...].astype(bf16)
 
 
@@ -404,10 +411,15 @@
         [shape((LANES, LANES), bf16), shape((width, slots), bf16), shape((devices, slots), f32)],
         flops=10**9,
     )
+    position, facts, rates = call(
+        functools.partial(rank_kernel, devices, capacity),
+        [shape((1, grains), i32), shape((devices, width), f32), shape((1, 27), f32)],
+        dest, line, grain_velocity, rates.reshape(1, 27), earlier,
+    )
     (send,) = call(
-        functools.partial(pack_kernel, devices, capacity),
+        functools.partial(pack_kernel, capacity),
         [shape((rows, width), bf16)],
-        dest, line, grain_velocity, grain_fraction, earlier,
+        position, facts, grain_fraction,
         scratch=[pltpu.VMEM((rows, width), f32)],
     )
     recv = lax.all_to_all(
@@ -415,7 +427,6 @@
     ).reshape(rows, width)
     state = shape(populations.shape, f32)
     face, ends = shape((9, length, width), f32), shape((9 * depth, width), f32)
-    rates = rates.reshape(1, 27)
     post, near, far, push, held, slot_line, slot_rows = call(
         functools.partial(first_kernel, devices, capacity),
         [

time: 44.2 us -> 43.6 us (0.986)
  local copies, waits for them, and re-layouts: 1.47 us -> 0.69 us
    unnamed x12, local copies, waits for them, and re-layouts: 1.47 us -> 0.69 us
    pallas_call x7 -> x8, Pallas kernels: 3.64 us -> 3.71 us  [call(): pl.pallas_call(kernel, out_shape=list(outs), in_specs=[pl.BlockSpec(memor...]
where the time goes in v6:
time: 43.6 us; the launch traced here: 43.4 us
  blocking collectives  18.2 us (42%)
  starting transfers between devices  10.8 us (25%)
  waiting for transfers between devices  9.16 us (21%)
  Pallas kernels  3.71 us (9%)
  between operations  0.78 us (2%)
  local copies, waits for them, and re-layouts  0.69 us (2%)
    all_to_all x1, blocking collectives, per_device(): lax.all_to_all(send.reshape(devices, capacity // 2 + 1, 2, width), both,...  18.2 us
    ppermute x2, waiting for transfers between devices, swap_outer(): return lax.ppermute(outer, 'gx', pairs)  6.67 us
    ppermute x4, starting transfers between devices, swap_faces(): received.append(lax.ppermute(face, ('gz', 'gx'), pairs))  5.25 us
    pallas_call x8, Pallas kernels, call(): pl.pallas_call(kernel, out_shape=list(outs), in_specs=[pl.BlockSpec(memor...  3.71 us
    ppermute x2, starting transfers between devices, swap_outer(): return lax.ppermute(outer, 'gx', pairs)  2.73 us
    all_to_all x1, starting transfers between devices, per_device(): lax.all_to_all(back.reshape(devices, 4, LANES), both, split_axis=0, conca...  2.57 us
    ppermute x4, waiting for transfers between devices, swap_faces(): received.append(lax.ppermute(face, ('gz', 'gx'), pairs))  2.48 us
  transfers between devices with their start and end apart: 9, of which 3 were waited for; matrix products, arithmetic and copies ran while one was open for 0% of the time, Pallas kernels for 0%

profile of v6, /device:TPU:0, one launch (start us, length us, event | category | flops | bytes accessed | tf_op | source)
XLA Modules:
  0.0 43.4 jit_solution(16081272835129115253)
XLA Ops:
  0.6 0.1 shard_map.77
  0.7 0.0 copy-start.3
  0.7 0.0 copy-start.2
  0.7 0.0 copy-start.5
  0.8 0.6 %copy-done.4 = s32[512]{0:T(512)S(1)} copy-done((s32[512]{0:T(512)S(1)}, s32[512]{0:T(512)}, u32[]{:S(2)}) %copy-start.4) | copy-done | bytes 2072
  1.3 0.1 copy-done.3
  1.4 0.0 copy-done.2
  1.4 0.3 shard_map.78
  1.7 0.0 copy-done.1
  1.7 0.5 %shard_map.79 = bf16[1088,128]{1,0:T(8,128)(2,1)S(1)} custom-call(s32[1,512]{1,0:T(1,128)S(1)} %get-tuple-element.28.position_ref, f32[32,128]{1,0:T(8,128)S(1)} %get-tuple-element.29.facts_ref, bf16[512,128]{1,0:T(8,128)(2,1)S(1)} %copy-done.1), custom_call_target="tpu_custom_call" | custom-call | bytes 428032 | tf_op jit(solution)/shard_map/pallas_call | solution.py:27
  2.2 0.0 copy-start
  2.2 18.2 %all_to_all.10 = bf16[32,17,2,128]{3,2,1,0:T(2,128)(2,1)S(1)} all-to-all(bf16[32,17,2,128]{3,2,1,0:T(2,128)(2,1)S(1)} %bitcast.8), channel_id=1, replica_groups=mesh['gz'=4,'gx'=8] {'gz','gx'}, dimensions={0} | all-to-all | bytes 557056 | tf_op jit(solution)/shard_map/all_to_all | solution.py:425
  20.4 0.5 %shard_map.80 = (f32[27,2,8,128]{3,2,1,0:T(8,128)S(1)}, f32[9,8,128]{2,1,0:T(8,128)S(1)}, f32[9,8,128]{2,1,0:T(8,128)S(1)}, f32[3,2,8,128]{3,2,1,0:T(8,128)S(1)}...) custom-call(bf16[1088,128]{1,0:T(8,128)(2,1)S(1)} %bitcast.7, ...), custom_call_target="tpu_custom_call" | custom-call | bytes 1511532 | tf_op jit(solution)/shard_map/pallas_call | solution.py:27
  20.9 0.2 collective-permute-start
  21.1 1.9 %collective-permute-start.1 = (f32[9,8,128]{2,1,0:T(8,128)S(1)}, f32[9,8,128]{2,1,0:T(8,128)S(1)}, u32[]{:S(2)}, u32[]{:S(2)}) collective-permute-start(f32[9,8,128]{2,1,0:T(8,128)S(1)} %get-tuple-element.34), channel_id=1, source_target_pairs={{0,8},{1,9},{2,10},{3,11},{4,12},{5,13},{6,14},{7,15},{8,0},{9,1},... | collective-permute-start | bytes 110600 | tf_op jit(solution)/shard_map/ppermute | solution.py:385
  23.0 0.0 collective-permute-done.far_ref
  23.0 2.5 %collective-permute-done.1.near_ref = f32[9,8,128]{2,1,0:T(8,128)S(1)} collective-permute-done((f32[9,8,128]{2,1,0:T(8,128)S(1)}, f32[9,8,128]{2,1,0:T(8,128)S(1)}, u32[]{:S(2)}, u32[]{:S(2)}) %collective-permute-start.1) | collective-permute-done | bytes 36896 | tf_op jit(solution)/shard_map/ppermute | solution.py:385
  25.5 0.1 collective-permute-start.2
  25.6 0.3 collective-permute-start.3
  25.9 0.2 shard_map.82
  26.1 4.4 %collective-permute-done.2.outer_ref = f32[18,128]{1,0:T(8,128)S(1)} collective-permute-done((f32[18,128]{1,0:T(8,128)S(1)}, f32[18,128]{1,0:T(8,128)S(1)}, u32[]{:S(2)}, u32[]{:S(2)}) %collective-permute-start.2) | collective-permute-done | bytes 9248 | tf_op jit(solution)/shard_map/ppermute | solution.py:396
  30.5 0.0 collective-permute-done.3.inner_ref
  30.5 1.2 %shard_map.83 = (f32[27,2,8,128]{3,2,1,0:T(8,128)S(1)}, f32[9,8,128]{2,1,0:T(8,128)S(1)}, f32[9,8,128]{2,1,0:T(8,128)S(1)}, f32[18,128]{1,0:T(8,128)S(1)}, f32[18,128]{1,0:T(8,128)S(1)}, /*index=5*/f32[128,128]{1,0:T(8,128)}) custom-call(f32[1,27]{1,0:T(1,128)S(1)} %get-tuple-element.27.rates_ref, f32[27,2,8,128]{3,2,1,0:T(8,128)S(1)} %get-tuple-element.32.post_ref, ...), custom_call_target="tpu_custom_call" | custom-call | bytes 1015916 | tf_op jit(solution)/shard_map/pallas_call | solution.py:27
  31.7 2.6 %all-to-all-start.1 = ((f32[32,4,128]{2,1,0:T(4,128)}), f32[32,4,128]{2,1,0:T(4,128)S(1)}, u32[]{:S(2)}, u32[]{:S(2)}) async-start(f32[32,4,128]{2,1,0:T(4,128)} %bitcast.5), calls=%async_computation.1 | async-start | bytes 131072 | tf_op jit(solution)/shard_map/all_to_all | solution.py:452
  34.3 0.2 collective-permute-start.5
  34.5 3.0 %collective-permute-start.6 = (f32[9,8,128]{2,1,0:T(8,128)S(1)}, f32[9,8,128]{2,1,0:T(8,128)S(1)}, u32[]{:S(2)}, u32[]{:S(2)}) collective-permute-start(f32[9,8,128]{2,1,0:T(8,128)S(1)} %get-tuple-element.45), channel_id=1, source_target_pairs={{0,8},{1,9},{2,10},{3,11},{4,12},{5,13},{6,14},{7,15},{8,0},{9,1},... | collective-permute-start | bytes 110600 | tf_op jit(solution)/shard_map/ppermute | solution.py:385
  37.5 2.7 %collective-permute-start.4 = (f32[18,128]{1,0:T(8,128)S(1)}, f32[18,128]{1,0:T(8,128)S(1)}, u32[]{:S(2)}, u32[]{:S(2)}) collective-permute-start(f32[18,128]{1,0:T(8,128)S(1)} %get-tuple-element.43), channel_id=1, source_target_pairs={{0,7},{1,2},{2,1},{3,4},{4,3},{5,6},{6,5},{7,0},{8,15},{9,10},{10,... | collective-permute-start | bytes 27656 | tf_op jit(solution)/shard_map/ppermute | solution.py:396
  40.1 0.0 collective-permute-start.7
  40.1 2.3 %collective-permute-done.4.outer_ref = f32[18,128]{1,0:T(8,128)S(1)} collective-permute-done((f32[18,128]{1,0:T(8,128)S(1)}, f32[18,128]{1,0:T(8,128)S(1)}, u32[]{:S(2)}, u32[]{:S(2)}) %collective-permute-start.4) | collective-permute-done | bytes 9248 | tf_op jit(solution)/shard_map/ppermute | solution.py:396
  42.4 0.0 collective-permute-done.7.inner_ref
  42.4 0.0 collective-permute-done.5.far_ref
  42.4 0.9 %shard_map.84 = (f32[27,2,8,128]{3,2,1,0:T(8,128)}, f32[3,512]{1,0:T(4,128)}) custom-call(f32[27,2,8,128]{3,2,1,0:T(8,128)S(1)} %get-tuple-element.42.post_ref, f32[18,128]{1,0:T(8,128)S(1)} %collective-permute-done.4.outer_ref, f32[9,8,128]{2,1,0:T(8,128)S(1)} %collective-permute-done.5.far_ref, f32[9,8,128]{2,1,0:T(8,128)S(1)} %collective-permute-done.6.near_ref, ...), custom_call_target="tpu_custom_call" | custom-call | bytes 704512 | tf_op jit(solution)/shard_map/pallas_call | solution.py:27
  (7 shorter events, 0.0 us)
Async XLA Ops:
  0.6 0.7 %copy-start.4 = (s32[512]{0:T(512)S(1)}, s32[512]{0:T(512)}, u32[]{:S(2)}) copy-start(s32[512]{0:T(512)} %param.11) | copy-start | bytes 6148
  0.6 1.1 %copy-start.1 = (bf16[512,128]{1,0:T(8,128)(2,1)S(1)}, bf16[512,128]{1,0:T(8,128)(2,1)}, u32[]{:S(2)}) copy-start(bf16[512,128]{1,0:T(8,128)(2,1)} %fraction_ref.1) | copy-start | bytes 393220
  0.7 0.7 %copy-start.3 = (bf16[3,512]{1,0:T(4,128)(2,1)S(1)}, bf16[3,512]{1,0:T(4,128)(2,1)}, u32[]{:S(2)}) copy-start(bf16[3,512]{1,0:T(4,128)(2,1)} %speed_ref.1) | copy-start | bytes 9220
  0.7 0.7 %copy-start.2 = (s32[512,1]{0,1:T(1,128)S(1)}, s32[512,1]{0,1:T(1,128)}, u32[]{:S(2)}) copy-start(s32[512,1]{0,1:T(1,128)} %param.10) | copy-start | bytes 6148
  0.7 0.7 %copy-start.5 = (f32[27]{0:T(128)S(1)}, f32[27]{0:T(128)}, u32[]{:S(2)}) copy-start(f32[27]{0:T(128)} %param.7) | copy-start | bytes 328
  2.2 18.2 %copy-start = (f32[27,2,8,128]{3,2,1,0:T(8,128)S(1)}, f32[27,2,8,128]{3,2,1,0:T(8,128)}, u32[]{:S(2)}) copy-start(f32[27,2,8,128]{3,2,1,0:T(8,128)} %fields_ref.1) | copy-start | bytes 663556
  20.9 2.1 %collective-permute-start = (f32[9,8,128]{2,1,0:T(8,128)S(1)}, f32[9,8,128]{2,1,0:T(8,128)S(1)}, u32[]{:S(2)}, u32[]{:S(2)}) collective-permute-start(f32[9,8,128]{2,1,0:T(8,128)S(1)} %get-tuple-element.33), channel_id=1, source_target_pairs={{0,1},{1,0},{2,3},{3,2},{4,5},{5,4},{6,7},{7,6},{8,16},{9,17},{10,... | collective-permute-start | bytes 110600 | tf_op jit(solution)/shard_map/ppermute | solution.py:385
  21.1 4.4 %collective-permute-start.1 = (f32[9,8,128]{2,1,0:T(8,128)S(1)}, f32[9,8,128]{2,1,0:T(8,128)S(1)}, u32[]{:S(2)}, u32[]{:S(2)}) collective-permute-start(f32[9,8,128]{2,1,0:T(8,128)S(1)} %get-tuple-element.34), channel_id=1, source_target_pairs={{0,8},{1,9},{2,10},{3,11},{4,12},{5,13},{6,14},{7,15},{8,0},{9,1},... | collective-permute-start | bytes 110600 | tf_op jit(solution)/shard_map/ppermute | solution.py:385
  25.5 5.0 %collective-permute-start.2 = (f32[18,128]{1,0:T(8,128)S(1)}, f32[18,128]{1,0:T(8,128)S(1)}, u32[]{:S(2)}, u32[]{:S(2)}) collective-permute-start(f32[18,128]{1,0:T(8,128)S(1)} %get-tuple-element.35), channel_id=1, source_target_pairs={{0,7},{1,2},{2,1},{3,4},{4,3},{5,6},{6,5},{7,0},{8,15},{9,10},{10,... | collective-permute-start | bytes 27656 | tf_op jit(solution)/shard_map/ppermute | solution.py:396
  25.6 4.9 %collective-permute-start.3 = (f32[18,128]{1,0:T(8,128)S(1)}, f32[18,128]{1,0:T(8,128)S(1)}, u32[]{:S(2)}, u32[]{:S(2)}) collective-permute-start(f32[18,128]{1,0:T(8,128)S(1)} %get-tuple-element.36), channel_id=1, source_target_pairs={{0,1},{1,0},{2,3},{3,2},{4,5},{5,4},{6,7},{7,6},{8,9},{9,8},{10,11... | collective-permute-start | bytes 27656 | tf_op jit(solution)/shard_map/ppermute | solution.py:390
  31.7 10.7 %all-to-all-start.1 = ((f32[32,4,128]{2,1,0:T(4,128)}), f32[32,4,128]{2,1,0:T(4,128)S(1)}, u32[]{:S(2)}, u32[]{:S(2)}) async-start(f32[32,4,128]{2,1,0:T(4,128)} %bitcast.5), calls=%async_computation.1 | async-start | bytes 131072 | tf_op jit(solution)/shard_map/all_to_all | solution.py:452
  34.3 8.1 %collective-permute-start.5 = (f32[9,8,128]{2,1,0:T(8,128)S(1)}, f32[9,8,128]{2,1,0:T(8,128)S(1)}, u32[]{:S(2)}, u32[]{:S(2)}) collective-permute-start(f32[9,8,128]{2,1,0:T(8,128)S(1)} %get-tuple-element.44), channel_id=1, source_target_pairs={{0,1},{1,0},{2,3},{3,2},{4,5},{5,4},{6,7},{7,6},{8,16},{9,17},{10,... | collective-permute-start | bytes 110600 | tf_op jit(solution)/shard_map/ppermute | solution.py:385
  34.5 7.9 %collective-permute-start.6 = (f32[9,8,128]{2,1,0:T(8,128)S(1)}, f32[9,8,128]{2,1,0:T(8,128)S(1)}, u32[]{:S(2)}, u32[]{:S(2)}) collective-permute-start(f32[9,8,128]{2,1,0:T(8,128)S(1)} %get-tuple-element.45), channel_id=1, source_target_pairs={{0,8},{1,9},{2,10},{3,11},{4,12},{5,13},{6,14},{7,15},{8,0},{9,1},... | collective-permute-start | bytes 110600 | tf_op jit(solution)/shard_map/ppermute | solution.py:385
  37.5 4.9 %collective-permute-start.4 = (f32[18,128]{1,0:T(8,128)S(1)}, f32[18,128]{1,0:T(8,128)S(1)}, u32[]{:S(2)}, u32[]{:S(2)}) collective-permute-start(f32[18,128]{1,0:T(8,128)S(1)} %get-tuple-element.43), channel_id=1, source_target_pairs={{0,7},{1,2},{2,1},{3,4},{4,3},{5,6},{6,5},{7,0},{8,15},{9,10},{10,... | collective-permute-start | bytes 27656 | tf_op jit(solution)/shard_map/ppermute | solution.py:396
  40.1 2.3 %collective-permute-start.7 = (f32[18,128]{1,0:T(8,128)S(1)}, f32[18,128]{1,0:T(8,128)S(1)}, u32[]{:S(2)}, u32[]{:S(2)}) collective-permute-start(f32[18,128]{1,0:T(8,128)S(1)} %get-tuple-element.46), channel_id=1, source_target_pairs={{0,1},{1,0},{2,3},{3,2},{4,5},{5,4},{6,7},{7,6},{8,9},{9,8},{10,11... | collective-permute-start | bytes 27656 | tf_op jit(solution)/shard_map/ppermute | solution.py:390

commit v7 on v5

--- a/solution.py
+++ b/solution.py
@@ -70,27 +70,29 @@
     return jnp.concatenate(parts, axis=1)
 
 
-def pack_kernel(devices, capacity, dest_ref, line_ref, speed_ref, fraction_ref, earlier_ref, send_ref, rows_ref):
+def rank_kernel(devices, dest_ref, rates_ref, earlier_ref, rank_ref, rates_out_ref):
+    hot = jnp.where(iota((devices, dest_ref.shape[1]), 0) == dest_ref[...], 1.0, 0.0)
+    rank_ref[...] = ranks(hot, earlier_ref[...]).astype(i32)
+    rates_out_ref[...] = rates_ref[...]
+
+
+def pack_kernel(devices, capacity, dest_ref, rank_ref, line_ref, speed_ref, fraction_ref, send_ref, rows_ref):
     grains, width = fraction_ref.shape
-    block = capacity + 2
-    dest = dest_ref[...]
-    hot = jnp.where(iota((devices, grains), 0) == dest, 1.0, 0.0)
-    rank = ranks(hot, earlier_ref[...]).astype(i32)
+    dest, rank = dest_ref[...], rank_ref[...]
+    place = jnp.where(iota((rows_ref.shape[0], grains), 0) == dest * (capacity + 2) + rank, 1.0, 0.0)
+    rows_ref[...] = jnp.dot(place.astype(bf16), fraction_ref[...], preferred_element_type=f32)
     speed = speed_ref[...].astype(f32)
     values = [speed[0:1], speed[1:2], speed[2:3], line_ref[...].astype(f32)]
     at_rank = iota((capacity, grains), 0) == rank
     facts = [jnp.where(at_rank, value, 0.0) for value in values]
     if 4 * capacity < width:
         facts.append(jnp.zeros((width - 4 * capacity, grains), f32))
-    fact_rows = lax.dot_general(
-        hot.astype(bf16),
+    rows_ref[pl.ds(capacity, devices, stride=capacity + 2), :] = lax.dot_general(
+        jnp.where(iota((devices, grains), 0) == dest, 1.0, 0.0).astype(bf16),
         jnp.concatenate(facts, axis=0).astype(bf16),
         (((1,), (1,)), ((), ())),
         preferred_element_type=f32,
     )
-    place = jnp.where(iota((devices * block, grains), 0) == dest * block + rank, 1.0, 0.0).astype(bf16)
-    rows_ref[...] = jnp.dot(place, fraction_ref[...], preferred_element_type=f32)
-    rows_ref[pl.ds(capacity, devices, stride=block), :] = fact_rows
     send_ref[...] = rows_ref[...].astype(bf16)
 
 
@@ -223,12 +225,10 @@
     store_faces(post_ref, near_ref, far_ref)
 
 
-def turn_kernel(slot_ref, dest_ref, earlier_ref, turned_ref, hot_ref, at_rank_ref):
+def turn_kernel(slot_ref, dest_ref, rank_ref, turned_ref, hot_ref, at_rank_ref):
     turned_ref[...] = slot_ref[...].astype(f32).T.astype(bf16)
-    hot = jnp.where(iota(hot_ref.shape, 0) == dest_ref[...], 1.0, 0.0)
-    hot_ref[...] = hot.astype(bf16)
-    rank = ranks(hot, earlier_ref[...]).astype(i32)
-    at_rank_ref[...] = jnp.where(iota(at_rank_ref.shape, 0) == rank, 1.0, 0.0)
+    hot_ref[...] = jnp.where(iota(hot_ref.shape, 0) == dest_ref[...], 1.0, 0.0).astype(bf16)
+    at_rank_ref[...] = jnp.where(iota(at_rank_ref.shape, 0) == rank_ref[...], 1.0, 0.0)
 
 
 def ends_kernel(post_ref, far_ref, near_ref, inner_ref, outer_ref):
@@ -349,7 +349,7 @@
 
 
 def last_kernel(
-    capacity, post_ref, outer_ref, far_ref, near_ref, inner_ref, back_ref, hot_ref, at_rank_ref,
+    capacity, post_ref, near_ref, far_ref, outer_ref, inner_ref, back_ref, hot_ref, at_rank_ref,
     scaled_ref, force_ref,
 ):
     for z in range(post_ref.shape[1]):
@@ -404,10 +404,15 @@
         [shape((LANES, LANES), bf16), shape((width, slots), bf16), shape((devices, slots), f32)],
         flops=10**9,
     )
+    rank, rates = call(
+        functools.partial(rank_kernel, devices),
+        [shape((1, grains), i32), shape((1, 27), f32)],
+        dest, rates.reshape(1, 27), earlier,
+    )
     (send,) = call(
         functools.partial(pack_kernel, devices, capacity),
         [shape((rows, width), bf16)],
-        dest, line, grain_velocity, grain_fraction, earlier,
+        dest, rank, line, grain_velocity, grain_fraction,
         scratch=[pltpu.VMEM((rows, width), f32)],
     )
     recv = lax.all_to_all(
@@ -415,7 +420,6 @@
     ).reshape(rows, width)
     state = shape(populations.shape, f32)
     face, ends = shape((9, length, width), f32), shape((9 * depth, width), f32)
-    rates = rates.reshape(1, 27)
     post, near, far, push, held, slot_line, slot_rows = call(
         functools.partial(first_kernel, devices, capacity),
         [
@@ -428,7 +432,7 @@
     turned, hot, at_rank = call(
         turn_kernel,
         [shape((width, slots), bf16), shape((devices, grains), bf16), shape((capacity, grains), f32)],
-        slot_rows, dest, earlier,
+        slot_rows, dest, rank,
     )
     inner, outer = call(ends_kernel, [ends, ends], post, far, near)
     outer, inner = swap_outer(outer), swap_inner(inner)
@@ -447,7 +451,7 @@
     scaled, grain_force = call(
         functools.partial(last_kernel, capacity),
         [state, shape((3, grains), f32)],
-        post, outer, far, near, inner, back, hot, at_rank,
+        post, near, far, outer, inner, back, hot, at_rank,
     )
     return (scaled, grain_force)
 

time: 44.2 us -> 43.4 us (0.982)
  starting transfers between devices: 10.8 us -> 10.3 us
    ppermute x4, starting transfers between devices: 5.24 us -> 3.77 us  [swap_faces(): received.append(lax.ppermute(face, ('gz', 'gx'), pairs))]
    ppermute x2, starting transfers between devices: 2.73 us -> 3.65 us  [swap_outer(): return lax.ppermute(outer, 'gx', pairs)]
    ppermute x2, waiting for transfers between devices: 6.67 us -> 5.87 us  [swap_outer(): return lax.ppermute(outer, 'gx', pairs)]
    all_to_all x1, waiting for transfers between devices: 0.01 us -> 0.69 us  [per_device(): lax.all_to_all(back.reshape(devices, 4, LANES), both, split_axis=0, conca...]
    pallas_call x7 -> x8, Pallas kernels: 3.64 us -> 3.56 us  [call(): pl.pallas_call(kernel, out_shape=list(outs), in_specs=[pl.BlockSpec(memor...]
  transfers between devices with their start and end apart: 9 -> 9, of which waited for: 3 -> 4; matrix products, arithmetic and copies ran while one was open for 0% -> 0% of each run, Pallas kernels for 0% -> 0%
where the time goes in v7:
time: 43.4 us; the launch traced here: 43.2 us
  blocking collectives  18.2 us (42%)
  starting transfers between devices  10.3 us (24%)
  waiting for transfers between devices  9.04 us (21%)
  Pallas kernels  3.56 us (8%)
  local copies, waits for them, and re-layouts  1.35 us (3%)
  between operations  0.75 us (2%)
    all_to_all x1, blocking collectives, per_device(): lax.all_to_all(send.reshape(devices, capacity // 2 + 1, 2, width), both,...  18.2 us
    ppermute x2, waiting for transfers between devices, swap_outer(): return lax.ppermute(outer, 'gx', pairs)  5.87 us
    ppermute x4, starting transfers between devices, swap_faces(): received.append(lax.ppermute(face, ('gz', 'gx'), pairs))  3.77 us
    ppermute x2, starting transfers between devices, swap_outer(): return lax.ppermute(outer, 'gx', pairs)  3.65 us
    pallas_call x8, Pallas kernels, call(): pl.pallas_call(kernel, out_shape=list(outs), in_specs=[pl.BlockSpec(memor...  3.56 us
    all_to_all x1, starting transfers between devices, per_device(): lax.all_to_all(back.reshape(devices, 4, LANES), both, split_axis=0, conca...  2.57 us
    ppermute x4, waiting for transfers between devices, swap_faces(): received.append(lax.ppermute(face, ('gz', 'gx'), pairs))  2.48 us
    unnamed x12, local copies, waits for them, and re-layouts  1.35 us
  transfers between devices with their start and end apart: 9, of which 4 were waited for; matrix products, arithmetic and copies ran while one was open for 0% of the time, Pallas kernels for 0%

profile of v7, /device:TPU:0, one launch (start us, length us, event | category | flops | bytes accessed | tf_op | source)
XLA Modules:
  0.0 43.2 jit_solution(531937214519284745)
XLA Ops:
  0.6 0.1 shard_map.77
  0.7 0.0 copy-start.2
  0.7 0.0 copy-start.5
  0.7 0.7 %copy-done.2 = s32[512,1]{0,1:T(1,128)S(1)} copy-done((s32[512,1]{0,1:T(1,128)S(1)}, s32[512,1]{0,1:T(1,128)}, u32[]{:S(2)}) %copy-start.2) | copy-done | bytes 2072
  1.4 0.2 shard_map.78
  1.6 0.0 copy-start.4
  1.6 0.5 %copy-done.3 = bf16[3,512]{1,0:T(4,128)(2,1)S(1)} copy-done((bf16[3,512]{1,0:T(4,128)(2,1)S(1)}, bf16[3,512]{1,0:T(4,128)(2,1)}, u32[]{:S(2)}) %copy-start.3) | copy-done | bytes 3096
  2.1 0.1 copy-done.4
  2.3 0.5 %shard_map.79 = bf16[1088,128]{1,0:T(8,128)(2,1)S(1)} custom-call(s32[1,512]{1,0:T(1,128)S(1)} %bitcast.11, s32[1,512]{1,0:T(1,128)S(1)} %get-tuple-element.27.rank_ref, s32[1,512]{1,0:T(1,128)S(1)} %bitcast.13, bf16[3,512]{1,0:T(4,128)(2,1)S(1)} %copy-done.3, bf16[512,128]{1,0:T(8,128)(2,1)S(1)} %copy-done.1), custom_call_target="tpu_custom_call" | custom-call | bytes 418816 | tf_op jit(solution)/shard_map/pallas_call | solution.py:27
  2.7 0.0 copy-start
  2.8 18.2 %all_to_all.10 = bf16[32,17,2,128]{3,2,1,0:T(2,128)(2,1)S(1)} all-to-all(bf16[32,17,2,128]{3,2,1,0:T(2,128)(2,1)S(1)} %bitcast.8), channel_id=1, replica_groups=mesh['gz'=4,'gx'=8] {'gz','gx'}, dimensions={0} | all-to-all | bytes 557056 | tf_op jit(solution)/shard_map/all_to_all | solution.py:418
  21.0 0.5 %shard_map.80 = (f32[27,2,8,128]{3,2,1,0:T(8,128)S(1)}, f32[9,8,128]{2,1,0:T(8,128)S(1)}, f32[9,8,128]{2,1,0:T(8,128)S(1)}, f32[3,2,8,128]{3,2,1,0:T(8,128)S(1)}...) custom-call(bf16[1088,128]{1,0:T(8,128)(2,1)S(1)} %bitcast.7, ...), custom_call_target="tpu_custom_call" | custom-call | bytes 1511532 | tf_op jit(solution)/shard_map/pallas_call | solution.py:27
  21.5 0.2 collective-permute-start
  21.6 1.9 %collective-permute-start.1 = (f32[9,8,128]{2,1,0:T(8,128)S(1)}, f32[9,8,128]{2,1,0:T(8,128)S(1)}, u32[]{:S(2)}, u32[]{:S(2)}) collective-permute-start(f32[9,8,128]{2,1,0:T(8,128)S(1)} %get-tuple-element.32), channel_id=1, source_target_pairs={{0,8},{1,9},{2,10},{3,11},{4,12},{5,13},{6,14},{7,15},{8,0},{9,1},... | collective-permute-start | bytes 110600 | tf_op jit(solution)/shard_map/ppermute | solution.py:378
  23.5 0.0 collective-permute-done.far_ref
  23.5 2.5 %collective-permute-done.1.near_ref = f32[9,8,128]{2,1,0:T(8,128)S(1)} collective-permute-done((f32[9,8,128]{2,1,0:T(8,128)S(1)}, f32[9,8,128]{2,1,0:T(8,128)S(1)}, u32[]{:S(2)}, u32[]{:S(2)}) %collective-permute-start.1) | collective-permute-done | bytes 36896 | tf_op jit(solution)/shard_map/ppermute | solution.py:378
  26.0 0.1 collective-permute-start.2
  26.1 0.3 collective-permute-start.3
  26.4 0.1 shard_map.82
  26.5 4.5 %collective-permute-done.2.outer_ref = f32[18,128]{1,0:T(8,128)S(1)} collective-permute-done((f32[18,128]{1,0:T(8,128)S(1)}, f32[18,128]{1,0:T(8,128)S(1)}, u32[]{:S(2)}, u32[]{:S(2)}) %collective-permute-start.2) | collective-permute-done | bytes 9248 | tf_op jit(solution)/shard_map/ppermute | solution.py:389
  31.0 0.0 collective-permute-done.3.inner_ref
  31.0 1.3 %shard_map.83 = (f32[27,2,8,128]{3,2,1,0:T(8,128)S(1)}, f32[9,8,128]{2,1,0:T(8,128)S(1)}, f32[9,8,128]{2,1,0:T(8,128)S(1)}, f32[18,128]{1,0:T(8,128)S(1)}, f32[18,128]{1,0:T(8,128)S(1)}, /*index=5*/f32[128,128]{1,0:T(8,128)}) custom-call(f32[1,27]{1,0:T(1,128)S(1)} %get-tuple-element.26.rates_ref, f32[27,2,8,128]{3,2,1,0:T(8,128)S(1)} %get-tuple-element.30.post_ref, ...), custom_call_target="tpu_custom_call" | custom-call | bytes 1015916 | tf_op jit(solution)/shard_map/pallas_call | solution.py:27
  32.3 2.6 %all-to-all-start.1 = ((f32[32,4,128]{2,1,0:T(4,128)}), f32[32,4,128]{2,1,0:T(4,128)S(1)}, u32[]{:S(2)}, u32[]{:S(2)}) async-start(f32[32,4,128]{2,1,0:T(4,128)} %bitcast.5), calls=%async_computation.1 | async-start | bytes 131072 | tf_op jit(solution)/shard_map/all_to_all | solution.py:445
  34.8 1.7 %collective-permute-start.4 = (f32[9,8,128]{2,1,0:T(8,128)S(1)}, f32[9,8,128]{2,1,0:T(8,128)S(1)}, u32[]{:S(2)}, u32[]{:S(2)}) collective-permute-start(f32[9,8,128]{2,1,0:T(8,128)S(1)} %get-tuple-element.41), channel_id=1, source_target_pairs={{0,8},{1,9},{2,10},{3,11},{4,12},{5,13},{6,14},{7,15},{8,0},{9,1},... | collective-permute-start | bytes 110600 | tf_op jit(solution)/shard_map/ppermute | solution.py:378
  36.5 0.0 collective-permute-start.5
  36.5 3.6 %collective-permute-start.6 = (f32[18,128]{1,0:T(8,128)S(1)}, f32[18,128]{1,0:T(8,128)S(1)}, u32[]{:S(2)}, u32[]{:S(2)}) collective-permute-start(f32[18,128]{1,0:T(8,128)S(1)} %get-tuple-element.43), channel_id=1, source_target_pairs={{0,7},{1,2},{2,1},{3,4},{4,3},{5,6},{6,5},{7,0},{8,15},{9,10},{10,... | collective-permute-start | bytes 27656 | tf_op jit(solution)/shard_map/ppermute | solution.py:389
  40.1 1.4 %collective-permute-done.6.outer_ref = f32[18,128]{1,0:T(8,128)S(1)} collective-permute-done((f32[18,128]{1,0:T(8,128)S(1)}, f32[18,128]{1,0:T(8,128)S(1)}, u32[]{:S(2)}, u32[]{:S(2)}) %collective-permute-start.6) | collective-permute-done | bytes 9248 | tf_op jit(solution)/shard_map/ppermute | solution.py:389
  41.5 0.0 collective-permute-done.7.inner_ref
  41.5 0.0 collective-permute-done.4.near_ref
  41.5 0.0 collective-permute-done.5.far_ref
  41.5 0.7 %all-to-all-done.1 = f32[32,4,128]{2,1,0:T(4,128)S(1)} async-done(((f32[32,4,128]{2,1,0:T(4,128)}), f32[32,4,128]{2,1,0:T(4,128)S(1)}, u32[]{:S(2)}, u32[]{:S(2)}) %all-to-all-start.1) | async-done | bytes 65568 | tf_op jit(solution)/shard_map/all_to_all | solution.py:445
  42.2 0.9 %shard_map.84 = (f32[27,2,8,128]{3,2,1,0:T(8,128)}, f32[3,512]{1,0:T(4,128)}) custom-call(f32[27,2,8,128]{3,2,1,0:T(8,128)S(1)} %get-tuple-element.40.post_ref, f32[9,8,128]{2,1,0:T(8,128)S(1)} %collective-permute-done.4.near_ref, f32[9,8,128]{2,1,0:T(8,128)S(1)} %collective-permute-done.5.far_ref, f32[18,128]{1,0:T(8,128)S(1)} %collective-permute-done.6.outer_ref, ...), custom_call_target="tpu_custom_call" | custom-call | bytes 704512 | tf_op jit(solution)/shard_map/pallas_call | solution.py:27
  (7 shorter events, 0.0 us)
Async XLA Ops:
  0.6 0.9 %copy-start.1 = (bf16[512,128]{1,0:T(8,128)(2,1)S(1)}, bf16[512,128]{1,0:T(8,128)(2,1)}, u32[]{:S(2)}) copy-start(bf16[512,128]{1,0:T(8,128)(2,1)} %fraction_ref.1) | copy-start | bytes 393220
  0.7 0.7 %copy-start.2 = (s32[512,1]{0,1:T(1,128)S(1)}, s32[512,1]{0,1:T(1,128)}, u32[]{:S(2)}) copy-start(s32[512,1]{0,1:T(1,128)} %param.10) | copy-start | bytes 6148
  0.7 0.7 %copy-start.5 = (f32[27]{0:T(128)S(1)}, f32[27]{0:T(128)}, u32[]{:S(2)}) copy-start(f32[27]{0:T(128)} %param.7) | copy-start | bytes 328
  1.4 0.7 %copy-start.3 = (bf16[3,512]{1,0:T(4,128)(2,1)S(1)}, bf16[3,512]{1,0:T(4,128)(2,1)}, u32[]{:S(2)}) copy-start(bf16[3,512]{1,0:T(4,128)(2,1)} %speed_ref.1) | copy-start | bytes 9220
  1.6 0.7 %copy-start.4 = (s32[512]{0:T(512)S(1)}, s32[512]{0:T(512)}, u32[]{:S(2)}) copy-start(s32[512]{0:T(512)} %param.11) | copy-start | bytes 6148
  2.7 18.2 %copy-start = (f32[27,2,8,128]{3,2,1,0:T(8,128)S(1)}, f32[27,2,8,128]{3,2,1,0:T(8,128)}, u32[]{:S(2)}) copy-start(f32[27,2,8,128]{3,2,1,0:T(8,128)} %fields_ref.1) | copy-start | bytes 663556
  21.5 2.1 %collective-permute-start = (f32[9,8,128]{2,1,0:T(8,128)S(1)}, f32[9,8,128]{2,1,0:T(8,128)S(1)}, u32[]{:S(2)}, u32[]{:S(2)}) collective-permute-start(f32[9,8,128]{2,1,0:T(8,128)S(1)} %get-tuple-element.31), channel_id=1, source_target_pairs={{0,1},{1,0},{2,3},{3,2},{4,5},{5,4},{6,7},{7,6},{8,16},{9,17},{10,... | collective-permute-start | bytes 110600 | tf_op jit(solution)/shard_map/ppermute | solution.py:378
  21.6 4.4 %collective-permute-start.1 = (f32[9,8,128]{2,1,0:T(8,128)S(1)}, f32[9,8,128]{2,1,0:T(8,128)S(1)}, u32[]{:S(2)}, u32[]{:S(2)}) collective-permute-start(f32[9,8,128]{2,1,0:T(8,128)S(1)} %get-tuple-element.32), channel_id=1, source_target_pairs={{0,8},{1,9},{2,10},{3,11},{4,12},{5,13},{6,14},{7,15},{8,0},{9,1},... | collective-permute-start | bytes 110600 | tf_op jit(solution)/shard_map/ppermute | solution.py:378
  26.0 5.0 %collective-permute-start.2 = (f32[18,128]{1,0:T(8,128)S(1)}, f32[18,128]{1,0:T(8,128)S(1)}, u32[]{:S(2)}, u32[]{:S(2)}) collective-permute-start(f32[18,128]{1,0:T(8,128)S(1)} %get-tuple-element.33), channel_id=1, source_target_pairs={{0,7},{1,2},{2,1},{3,4},{4,3},{5,6},{6,5},{7,0},{8,15},{9,10},{10,... | collective-permute-start | bytes 27656 | tf_op jit(solution)/shard_map/ppermute | solution.py:389
  26.1 4.9 %collective-permute-start.3 = (f32[18,128]{1,0:T(8,128)S(1)}, f32[18,128]{1,0:T(8,128)S(1)}, u32[]{:S(2)}, u32[]{:S(2)}) collective-permute-start(f32[18,128]{1,0:T(8,128)S(1)} %get-tuple-element.34), channel_id=1, source_target_pairs={{0,1},{1,0},{2,3},{3,2},{4,5},{5,4},{6,7},{7,6},{8,9},{9,8},{10,11... | collective-permute-start | bytes 27656 | tf_op jit(solution)/shard_map/ppermute | solution.py:383
  32.3 10.0 %all-to-all-start.1 = ((f32[32,4,128]{2,1,0:T(4,128)}), f32[32,4,128]{2,1,0:T(4,128)S(1)}, u32[]{:S(2)}, u32[]{:S(2)}) async-start(f32[32,4,128]{2,1,0:T(4,128)} %bitcast.5), calls=%async_computation.1 | async-start | bytes 131072 | tf_op jit(solution)/shard_map/all_to_all | solution.py:445
  34.8 6.7 %collective-permute-start.4 = (f32[9,8,128]{2,1,0:T(8,128)S(1)}, f32[9,8,128]{2,1,0:T(8,128)S(1)}, u32[]{:S(2)}, u32[]{:S(2)}) collective-permute-start(f32[9,8,128]{2,1,0:T(8,128)S(1)} %get-tuple-element.41), channel_id=1, source_target_pairs={{0,8},{1,9},{2,10},{3,11},{4,12},{5,13},{6,14},{7,15},{8,0},{9,1},... | collective-permute-start | bytes 110600 | tf_op jit(solution)/shard_map/ppermute | solution.py:378
  36.5 5.0 %collective-permute-start.5 = (f32[9,8,128]{2,1,0:T(8,128)S(1)}, f32[9,8,128]{2,1,0:T(8,128)S(1)}, u32[]{:S(2)}, u32[]{:S(2)}) collective-permute-start(f32[9,8,128]{2,1,0:T(8,128)S(1)} %get-tuple-element.42), channel_id=1, source_target_pairs={{0,1},{1,0},{2,3},{3,2},{4,5},{5,4},{6,7},{7,6},{8,16},{9,17},{10,... | collective-permute-start | bytes 110600 | tf_op jit(solution)/shard_map/ppermute | solution.py:378
  36.5 5.0 %collective-permute-start.6 = (f32[18,128]{1,0:T(8,128)S(1)}, f32[18,128]{1,0:T(8,128)S(1)}, u32[]{:S(2)}, u32[]{:S(2)}) collective-permute-start(f32[18,128]{1,0:T(8,128)S(1)} %get-tuple-element.43), channel_id=1, source_target_pairs={{0,7},{1,2},{2,1},{3,4},{4,3},{5,6},{6,5},{7,0},{8,15},{9,10},{10,... | collective-permute-start | bytes 27656 | tf_op jit(solution)/shard_map/ppermute | solution.py:389
  40.1 1.4 %collective-permute-start.7 = (f32[18,128]{1,0:T(8,128)S(1)}, f32[18,128]{1,0:T(8,128)S(1)}, u32[]{:S(2)}, u32[]{:S(2)}) collective-permute-start(f32[18,128]{1,0:T(8,128)S(1)} %get-tuple-element.44), channel_id=1, source_target_pairs={{0,1},{1,0},{2,3},{3,2},{4,5},{5,4},{6,7},{7,6},{8,9},{9,8},{10,11... | collective-permute-start | bytes 27656 | tf_op jit(solution)/shard_map/ppermute | solution.py:383

commit v8 on v7

--- a/solution.py
+++ b/solution.py
@@ -70,21 +70,23 @@
     return jnp.concatenate(parts, axis=1)
 
 
-def rank_kernel(devices, dest_ref, rates_ref, earlier_ref, rank_ref, rates_out_ref):
+def rank_kernel(
+    devices, dest_ref, line_ref, speed_ref, rates_ref, earlier_ref, rank_ref, facts_ref, rates_out_ref
+):
     hot = jnp.where(iota((devices, dest_ref.shape[1]), 0) == dest_ref[...], 1.0, 0.0)
     rank_ref[...] = ranks(hot, earlier_ref[...]).astype(i32)
+    facts_ref[0:3] = speed_ref[...].astype(f32)
+    facts_ref[3:4] = line_ref[...].astype(f32)
     rates_out_ref[...] = rates_ref[...]
 
 
-def pack_kernel(devices, capacity, dest_ref, rank_ref, line_ref, speed_ref, fraction_ref, send_ref, rows_ref):
+def pack_kernel(devices, capacity, dest_ref, rank_ref, facts_ref, fraction_ref, send_ref, rows_ref):
     grains, width = fraction_ref.shape
     dest, rank = dest_ref[...], rank_ref[...]
     place = jnp.where(iota((rows_ref.shape[0], grains), 0) == dest * (capacity + 2) + rank, 1.0, 0.0)
     rows_ref[...] = jnp.dot(place.astype(bf16), fraction_ref[...], preferred_element_type=f32)
-    speed = speed_ref[...].astype(f32)
-    values = [speed[0:1], speed[1:2], speed[2:3], line_ref[...].astype(f32)]
     at_rank = iota((capacity, grains), 0) == rank
-    facts = [jnp.where(at_rank, value, 0.0) for value in values]
+    facts = [jnp.where(at_rank, facts_ref[m : m + 1], 0.0) for m in range(4)]
     if 4 * capacity < width:
         facts.append(jnp.zeros((width - 4 * capacity, grains), f32))
     rows_ref[pl.ds(capacity, devices, stride=capacity + 2), :] = lax.dot_general(
@@ -172,24 +174,53 @@
     return lax.axis_index(axis) % 2 == 0
 
 
-def store_faces(post_ref, near_ref, far_ref):
-    top = post_ref.shape[1] - 1
+def store_faces(ups, downs, near_ref, far_ref):
     for n in range(9):
-        up, down = post_ref[n + 18, top], post_ref[n, 0]
-        near_ref[n] = jnp.where(even_place("gz"), up, down)
-        far_ref[n] = jnp.where(even_place("gz"), down, up)
-
-
-def across(near_ref, far_ref, i, x=slice(None)):
+        near_ref[n] = jnp.where(even_place("gz"), ups[n], downs[n])
+        far_ref[n] = jnp.where(even_place("gz"), downs[n], ups[n])
+
+
+def end_row(i, z, depth):
+    return ((STEP[i][0] + 1) * 3 + STEP[i][2] + 1) * depth + z
+
+
+def store_ends(post_ref, inner_ref, outer_ref):
+    depth, length = post_ref.shape[1], post_ref.shape[2]
+    for i in range(27):
+        if STEP[i][1] == 1:
+            for z in range(depth):
+                n = end_row(i, z, depth)
+                right, left = post_ref[i, z, length - 1 : length], post_ref[i - 6, z, 0:1]
+                inner_ref[n : n + 1] = jnp.where(even_place("gx"), right, left)
+                outer_ref[n : n + 1] = jnp.where(even_place("gx"), left, right)
+
+
+def moved_along_x(field, i, z, depth, outer_ref, inner_ref, corner=None):
+    cx = STEP[i][1]
+    if not cx:
+        return field
+    n, length = end_row(i, z, depth), field.shape[0]
+    outer, inner = outer_ref[n : n + 1], inner_ref[n : n + 1]
+    if corner is not None:
+        end = corner
+    elif cx > 0:
+        end = jnp.where(even_place("gx"), outer, inner)
+    else:
+        end = jnp.where(even_place("gx"), inner, outer)
+    place = 0 if cx > 0 else length - 1
+    return jnp.where(iota(field.shape, 0) == place, end, pltpu.roll(field, cx % length, 0))
+
+
+def across(near_ref, far_ref, i):
     n = i % 9
     if STEP[i][0] > 0:
-        return jnp.where(even_place("gz"), far_ref[n, x], near_ref[n, x])
-    return jnp.where(even_place("gz"), near_ref[n, x], far_ref[n, x])
+        return jnp.where(even_place("gz"), far_ref[n], near_ref[n])
+    return jnp.where(even_place("gz"), near_ref[n], far_ref[n])
 
 
 def first_kernel(
     devices, capacity, recv_ref, fields_ref, rates_ref, spread_ref, own_ref,
-    post_ref, near_ref, far_ref, push_ref, held_ref, line_ref, slot_ref, wide_ref,
+    post_ref, outer_ref, inner_ref, push_ref, held_ref, line_ref, slot_ref, wide_ref,
 ):
     width = recv_ref.shape[1]
     block, slots = capacity + 2, devices * capacity
@@ -222,7 +253,7 @@
             post_ref[i, z] = post[i]
         for k in range(3):
             push_ref[k, z] = push[k]
-    store_faces(post_ref, near_ref, far_ref)
+    store_ends(post_ref, inner_ref, outer_ref)
 
 
 def turn_kernel(slot_ref, dest_ref, rank_ref, turned_ref, hot_ref, at_rank_ref):
@@ -231,69 +262,44 @@
     at_rank_ref[...] = jnp.where(iota(at_rank_ref.shape, 0) == rank_ref[...], 1.0, 0.0)
 
 
-def ends_kernel(post_ref, far_ref, near_ref, inner_ref, outer_ref):
-    depth, length = post_ref.shape[1], post_ref.shape[2]
-    even = even_place("gx")
-
-    def row(i, z, x):
-        source = z - STEP[i][0]
-        if 0 <= source < depth:
-            return post_ref[i, source, x : x + 1]
-        return across(near_ref, far_ref, i, slice(x, x + 1))
-
-    for i in range(27):
-        if STEP[i][1] != 1:
-            continue
-        j = i - 6
-        for z in range(depth):
-            n = end_row(i, z, depth)
-            right, left = row(i, z, length - 1), row(j, z, 0)
-            inner_ref[n : n + 1] = jnp.where(even, right, left)
-            outer_ref[n : n + 1] = jnp.where(even, left, right)
-
-
-def end_row(i, z, depth):
-    return ((STEP[i][0] + 1) * 3 + STEP[i][2] + 1) * depth + z
-
-
-def streamed(post_ref, near_ref, far_ref, inner_ref, outer_ref, z, back_ref=None):
-    depth, length, width = post_ref.shape[1:]
-    even = even_place("gx")
-    rows = iota((length, width), 0)
+def faces_kernel(post_ref, outer_ref, inner_ref, near_ref, far_ref):
+    depth = post_ref.shape[1]
+    move = lambda i, z: moved_along_x(post_ref[i, z], i, z, depth, outer_ref, inner_ref)
+    ups, downs = [move(n + 18, depth - 1) for n in range(9)], [move(n, 0) for n in range(9)]
+    store_faces(ups, downs, near_ref, far_ref)
+
+
+def streamed(post_ref, outer_ref, inner_ref, far_ref, near_ref, z, back_ref=None):
+    depth, width = post_ref.shape[1], post_ref.shape[3]
     moved_list = []
     for i in range(27):
         cz, cx, cy = STEP[i]
         source = z - cz
         inside = 0 <= source < depth
         moved = post_ref[i, source] if inside else across(near_ref, far_ref, i)
-        if cx:
-            n = end_row(i, z, depth)
-            inner, outer = inner_ref[n : n + 1], outer_ref[n : n + 1]
-            edge = jnp.where(even, outer, inner) if cx > 0 else jnp.where(even, inner, outer)
-            if not inside and back_ref is not None:
-                edge = back_ref[pl.ds(4 * device_at(-cz, -cx) + 2 + cy, 1)]
-            moved = pltpu.roll(moved, cx % length, 0)
-            moved = jnp.where(rows == (0 if cx > 0 else length - 1), edge, moved)
+        if inside:
+            moved = moved_along_x(moved, i, source, depth, outer_ref, inner_ref)
+        elif cx and back_ref is not None:
+            corner = back_ref[pl.ds(4 * device_at(-cz, -cx) + 2 + cy, 1)]
+            moved = moved_along_x(moved, i, 0, depth, outer_ref, inner_ref, corner)
         if cy:
             moved = pltpu.roll(moved, cy % width, 1)
-        if source < 0:
-            moved = jnp.where(lax.axis_index("gz") == 0, post_ref[26 - i, z], moved)
-        elif source >= depth:
-            top = lax.axis_size("gz") - 1
-            moved = jnp.where(lax.axis_index("gz") == top, post_ref[26 - i, z], moved)
+        if not inside:
+            wall = 0 if cz > 0 else lax.axis_size("gz") - 1
+            moved = jnp.where(lax.axis_index("gz") == wall, post_ref[26 - i, z], moved)
         moved_list.append(moved)
     return moved_list
 
 
 def second_kernel(
-    capacity, rates_ref, post_ref, far_ref, near_ref, outer_ref, inner_ref,
+    capacity, rates_ref, post_ref, outer_ref, inner_ref, far_ref, near_ref,
     held_ref, push_ref, line_ref, turned_ref,
-    next_ref, next_near_ref, next_far_ref, next_inner_ref, next_outer_ref, back_ref, right_ref, left_ref,
+    next_ref, next_near_ref, next_far_ref, next_inner_ref, next_outer_ref, back_ref,
 ):
     depth, length, width = post_ref.shape[1:]
     lines = depth * length
     slots = turned_ref.shape[1]
-    halo = (near_ref, far_ref, inner_ref, outer_ref)
+    halo = (outer_ref, inner_ref, far_ref, near_ref)
     rate = [rates_ref[:, a : a + 1] for a in range(27)]
     pushes = []
     for z in range(depth):
@@ -302,27 +308,15 @@
         for i in range(27):
             next_ref[i, z] = post[i]
         pushes.append(push)
-    store_faces(next_ref, next_near_ref, next_far_ref)
+    ups, downs = [next_ref[n + 18, depth - 1] for n in range(9)], [next_ref[n, 0] for n in range(9)]
+    store_faces(ups, downs, next_near_ref, next_far_ref)
+    store_ends(next_ref, next_inner_ref, next_outer_ref)
     back_ref[...] = jnp.zeros(back_ref.shape, f32)
-    right_ref[...] = jnp.zeros(right_ref.shape, f32)
-    left_ref[...] = jnp.zeros(left_ref.shape, f32)
     for i in range(27):
         cz, cx, cy = STEP[i]
-        if cx == 0:
-            continue
-        x = length - 1 if cx > 0 else 0
-        face_ref = right_ref if cx > 0 else left_ref
-        for z in range(depth):
-            if 0 <= z - cz < depth:
-                n = end_row(i, z, depth)
-                face_ref[n : n + 1] = next_ref[i, z - cz, x : x + 1]
-        if cz:
-            z = depth - 1 if cz > 0 else 0
+        if cz and cx:
+            z, x = depth - 1 if cz > 0 else 0, length - 1 if cx > 0 else 0
             back_ref[pl.ds(4 * device_at(cz, cx) + 2 + cy, 1)] = next_ref[i, z, x : x + 1]
-    even = even_place("gx")
-    right, left = right_ref[...], left_ref[...]
-    next_inner_ref[...] = jnp.where(even, right, left)
-    next_outer_ref[...] = jnp.where(even, left, right)
     total = jnp.concatenate(
         [push_ref[k, z] + pushes[z][k] for k in range(3) for z in range(depth)], axis=0
     )
@@ -353,7 +347,7 @@
     scaled_ref, force_ref,
 ):
     for z in range(post_ref.shape[1]):
-        fields = streamed(post_ref, near_ref, far_ref, inner_ref, outer_ref, z, back_ref)
+        fields = streamed(post_ref, outer_ref, inner_ref, far_ref, near_ref, z, back_ref)
         for i in range(27):
             scaled_ref[i, z] = fields[i] * (1.0 / WEIGHT[i])
     back = back_ref[pl.ds(0, hot_ref.shape[0], stride=4), :]
@@ -404,15 +398,15 @@
         [shape((LANES, LANES), bf16), shape((width, slots), bf16), shape((devices, slots), f32)],
         flops=10**9,
     )
-    rank, rates = call(
+    rank, facts, rates = call(
         functools.partial(rank_kernel, devices),
-        [shape((1, grains), i32), shape((1, 27), f32)],
-        dest, rates.reshape(1, 27), earlier,
+        [shape((1, grains), i32), shape((4, grains), f32), shape((1, 27), f32)],
+        dest, line, grain_velocity, rates.reshape(1, 27), earlier,
     )
     (send,) = call(
         functools.partial(pack_kernel, devices, capacity),
         [shape((rows, width), bf16)],
-        dest, rank, line, grain_velocity, grain_fraction,
+        dest, rank, facts, grain_fraction,
         scratch=[pltpu.VMEM((rows, width), f32)],
     )
     recv = lax.all_to_all(
@@ -420,27 +414,25 @@
     ).reshape(rows, width)
     state = shape(populations.shape, f32)
     face, ends = shape((9, length, width), f32), shape((9 * depth, width), f32)
-    post, near, far, push, held, slot_line, slot_rows = call(
+    post, outer, inner, push, held, slot_line, slot_rows = call(
         functools.partial(first_kernel, devices, capacity),
         [
-            state, face, face, shape((3, depth, length, width), f32),
+            state, ends, ends, shape((3, depth, length, width), f32),
             shape((4 * lines, width), f32), shape((1, slots), i32), shape((slots, width), bf16),
         ],
         recv, populations, rates, spread, own, scratch=[pltpu.VMEM((rows, width), f32)],
     )
-    near, far = swap_faces(near, far)
+    outer, inner = swap_outer(outer), swap_inner(inner)
     turned, hot, at_rank = call(
         turn_kernel,
         [shape((width, slots), bf16), shape((devices, grains), bf16), shape((capacity, grains), f32)],
         slot_rows, dest, rank,
     )
-    inner, outer = call(ends_kernel, [ends, ends], post, far, near)
-    outer, inner = swap_outer(outer), swap_inner(inner)
+    near, far = swap_faces(*call(faces_kernel, [face, face], post, outer, inner))
     post, next_near, next_far, inner, outer, back = call(
         functools.partial(second_kernel, capacity),
         [state, face, face, ends, ends, shape((4 * devices, LANES), f32)],
-        rates, post, far, near, outer, inner, held, push, slot_line, turned,
-        scratch=[pltpu.VMEM(ends.shape, f32)] * 2,
+        rates, post, outer, inner, far, near, held, push, slot_line, turned,
     )
     back = lax.all_to_all(
         back.reshape(devices, 4, LANES), both, split_axis=0, concat_axis=0, tiled=True

time: 43.4 us -> 42.6 us (0.982)
  waiting for transfers between devices: 9.04 us -> 8.33 us
  local copies, waits for them, and re-layouts: 1.35 us -> 0.69 us
  starting transfers between devices: 10.3 us -> 10.8 us
    ppermute x2, starting transfers between devices: 3.65 us -> 4.5 us  [swap_outer(): return lax.ppermute(outer, 'gx', pairs)]
    unnamed x12, local copies, waits for them, and re-layouts: 1.35 us -> 0.69 us
where the time goes in v8:
time: 42.6 us; the launch traced here: 42.4 us
  blocking collectives  18.2 us (43%)
  starting transfers between devices  10.8 us (25%)
  waiting for transfers between devices  8.33 us (20%)
  Pallas kernels  3.59 us (8%)
  between operations  0.76 us (2%)
  local copies, waits for them, and re-layouts  0.69 us (2%)
    all_to_all x1, blocking collectives, per_device(): lax.all_to_all(send.reshape(devices, capacity // 2 + 1, 2, width), both,...  18.2 us
    ppermute x2, waiting for transfers between devices, swap_outer(): return lax.ppermute(outer, 'gx', pairs)  5.45 us
    ppermute x2, starting transfers between devices, swap_outer(): return lax.ppermute(outer, 'gx', pairs)  4.5 us
    ppermute x4, starting transfers between devices, swap_faces(): received.append(lax.ppermute(face, ('gz', 'gx'), pairs))  3.76 us
    pallas_call x8, Pallas kernels, call(): pl.pallas_call(kernel, out_shape=list(outs), in_specs=[pl.BlockSpec(memor...  3.59 us
    all_to_all x1, starting transfers between devices, per_device(): lax.all_to_all(back.reshape(devices, 4, LANES), both, split_axis=0, conca...  2.57 us
    ppermute x4, waiting for transfers between devices, swap_faces(): received.append(lax.ppermute(face, ('gz', 'gx'), pairs))  2.18 us
  transfers between devices with their start and end apart: 9, of which 4 were waited for; matrix products, arithmetic and copies ran while one was open for 0% of the time, Pallas kernels for 0%

profile of v8, /device:TPU:0, one launch (start us, length us, event | category | flops | bytes accessed | tf_op | source)
XLA Modules:
  0.0 42.4 jit_solution(14632498894916305382)
XLA Ops:
  0.6 0.1 shard_map.77
  0.7 0.0 copy-start.3
  0.7 0.0 copy-start.2
  0.7 0.0 copy-start.5
  0.8 0.6 %copy-done.4 = s32[512]{0:T(512)S(1)} copy-done((s32[512]{0:T(512)S(1)}, s32[512]{0:T(512)}, u32[]{:S(2)}) %copy-start.4) | copy-done | bytes 2072
  1.3 0.1 copy-done.3
  1.4 0.0 copy-done.2
  1.4 0.2 shard_map.78
  1.6 0.5 %shard_map.79 = bf16[1088,128]{1,0:T(8,128)(2,1)S(1)} custom-call(s32[1,512]{1,0:T(1,128)S(1)} %bitcast.11, s32[1,512]{1,0:T(1,128)S(1)} %get-tuple-element.28.rank_ref, f32[4,512]{1,0:T(4,128)S(1)} %get-tuple-element.29.facts_ref, bf16[512,128]{1,0:T(8,128)(2,1)S(1)} %copy-done.1), custom_call_target="tpu_custom_call" | custom-call | bytes 421888 | tf_op jit(solution)/shard_map/pallas_call | solution.py:27
  2.1 0.0 copy-start
  2.1 18.2 %all_to_all.10 = bf16[32,17,2,128]{3,2,1,0:T(2,128)(2,1)S(1)} all-to-all(bf16[32,17,2,128]{3,2,1,0:T(2,128)(2,1)S(1)} %bitcast.8), channel_id=1, replica_groups=mesh['gz'=4,'gx'=8] {'gz','gx'}, dimensions={0} | all-to-all | bytes 557056 | tf_op jit(solution)/shard_map/all_to_all | solution.py:412
  20.3 0.5 %shard_map.80 = (f32[27,2,8,128]{3,2,1,0:T(8,128)S(1)}, f32[18,128]{1,0:T(8,128)S(1)}, f32[18,128]{1,0:T(8,128)S(1)}, f32[3,2,8,128]{3,2,1,0:T(8,128)S(1)}, f32[...) custom-call(bf16[1088,128]{1,0:T(8,128)(2,1)S(1)} %bitcast.7, ...), custom_call_target="tpu_custom_call" | custom-call | bytes 1456236 | tf_op jit(solution)/shard_map/pallas_call | solution.py:27
  20.8 0.9 %collective-permute-start = (f32[18,128]{1,0:T(8,128)S(1)}, f32[18,128]{1,0:T(8,128)S(1)}, u32[]{:S(2)}, u32[]{:S(2)}) collective-permute-start(f32[18,128]{1,0:T(8,128)S(1)} %get-tuple-element.33), channel_id=1, source_target_pairs={{0,7},{1,2},{2,1},{3,4},{4,3},{5,6},{6,5},{7,0},{8,15},{9,10},{10,... | collective-permute-start | bytes 27656 | tf_op jit(solution)/shard_map/ppermute | solution.py:383
  21.8 0.0 collective-permute-start.1
  21.8 4.0 %collective-permute-done.outer_ref = f32[18,128]{1,0:T(8,128)S(1)} collective-permute-done((f32[18,128]{1,0:T(8,128)S(1)}, f32[18,128]{1,0:T(8,128)S(1)}, u32[]{:S(2)}, u32[]{:S(2)}) %collective-permute-start) | collective-permute-done | bytes 9248 | tf_op jit(solution)/shard_map/ppermute | solution.py:383
  25.8 0.0 collective-permute-done.1.inner_ref
  25.8 0.1 collective-permute-start.2
  25.9 2.0 %collective-permute-start.3 = (f32[9,8,128]{2,1,0:T(8,128)S(1)}, f32[9,8,128]{2,1,0:T(8,128)S(1)}, u32[]{:S(2)}, u32[]{:S(2)}) collective-permute-start(f32[9,8,128]{2,1,0:T(8,128)S(1)} %get-tuple-element.36), channel_id=1, source_target_pairs={{0,8},{1,9},{2,10},{3,11},{4,12},{5,13},{6,14},{7,15},{8,0},{9,1},... | collective-permute-start | bytes 110600 | tf_op jit(solution)/shard_map/ppermute | solution.py:372
  27.9 0.1 shard_map.82
  28.0 0.0 collective-permute-done.2.far_ref
  28.1 2.2 %collective-permute-done.3.near_ref = f32[9,8,128]{2,1,0:T(8,128)S(1)} collective-permute-done((f32[9,8,128]{2,1,0:T(8,128)S(1)}, f32[9,8,128]{2,1,0:T(8,128)S(1)}, u32[]{:S(2)}, u32[]{:S(2)}) %collective-permute-start.3) | collective-permute-done | bytes 36896 | tf_op jit(solution)/shard_map/ppermute | solution.py:372
  30.2 1.2 %shard_map.83 = (f32[27,2,8,128]{3,2,1,0:T(8,128)S(1)}, f32[9,8,128]{2,1,0:T(8,128)S(1)}, f32[9,8,128]{2,1,0:T(8,128)S(1)}, f32[18,128]{1,0:T(8,128)S(1)}, f32[18,128]{1,0:T(8,128)S(1)}, /*index=5*/f32[128,128]{1,0:T(8,128)}) custom-call(f32[1,27]{1,0:T(1,128)S(1)} %get-tuple-element.27.rates_ref, f32[27,2,8,128]{3,2,1,0:T(8,128)S(1)} %get-tuple-element.32.post_ref, ...), custom_call_target="tpu_custom_call" | custom-call | bytes 1015916 | tf_op jit(solution)/shard_map/pallas_call | solution.py:27
  31.5 2.6 %all-to-all-start.1 = ((f32[32,4,128]{2,1,0:T(4,128)}), f32[32,4,128]{2,1,0:T(4,128)S(1)}, u32[]{:S(2)}, u32[]{:S(2)}) async-start(f32[32,4,128]{2,1,0:T(4,128)} %bitcast.5), calls=%async_computation.1 | async-start | bytes 131072 | tf_op jit(solution)/shard_map/all_to_all | solution.py:437
  34.1 1.7 %collective-permute-start.4 = (f32[9,8,128]{2,1,0:T(8,128)S(1)}, f32[9,8,128]{2,1,0:T(8,128)S(1)}, u32[]{:S(2)}, u32[]{:S(2)}) collective-permute-start(f32[9,8,128]{2,1,0:T(8,128)S(1)} %get-tuple-element.43), channel_id=1, source_target_pairs={{0,8},{1,9},{2,10},{3,11},{4,12},{5,13},{6,14},{7,15},{8,0},{9,1},... | collective-permute-start | bytes 110600 | tf_op jit(solution)/shard_map/ppermute | solution.py:372
  35.8 0.0 collective-permute-start.5
  35.8 3.6 %collective-permute-start.6 = (f32[18,128]{1,0:T(8,128)S(1)}, f32[18,128]{1,0:T(8,128)S(1)}, u32[]{:S(2)}, u32[]{:S(2)}) collective-permute-start(f32[18,128]{1,0:T(8,128)S(1)} %get-tuple-element.45), channel_id=1, source_target_pairs={{0,7},{1,2},{2,1},{3,4},{4,3},{5,6},{6,5},{7,0},{8,15},{9,10},{10,... | collective-permute-start | bytes 27656 | tf_op jit(solution)/shard_map/ppermute | solution.py:383
  39.3 1.4 %collective-permute-done.6.outer_ref = f32[18,128]{1,0:T(8,128)S(1)} collective-permute-done((f32[18,128]{1,0:T(8,128)S(1)}, f32[18,128]{1,0:T(8,128)S(1)}, u32[]{:S(2)}, u32[]{:S(2)}) %collective-permute-start.6) | collective-permute-done | bytes 9248 | tf_op jit(solution)/shard_map/ppermute | solution.py:383
  40.7 0.0 collective-permute-done.7.inner_ref
  40.7 0.0 collective-permute-done.4.near_ref
  40.7 0.0 collective-permute-done.5.far_ref
  40.8 0.7 %all-to-all-done.1 = f32[32,4,128]{2,1,0:T(4,128)S(1)} async-done(((f32[32,4,128]{2,1,0:T(4,128)}), f32[32,4,128]{2,1,0:T(4,128)S(1)}, u32[]{:S(2)}, u32[]{:S(2)}) %all-to-all-start.1) | async-done | bytes 65568 | tf_op jit(solution)/shard_map/all_to_all | solution.py:437
  41.4 1.0 %shard_map.84 = (f32[27,2,8,128]{3,2,1,0:T(8,128)}, f32[3,512]{1,0:T(4,128)}) custom-call(f32[27,2,8,128]{3,2,1,0:T(8,128)S(1)} %get-tuple-element.42.post_ref, f32[9,8,128]{2,1,0:T(8,128)S(1)} %collective-permute-done.4.near_ref, f32[9,8,128]{2,1,0:T(8,128)S(1)} %collective-permute-done.5.far_ref, f32[18,128]{1,0:T(8,128)S(1)} %collective-permute-done.6.outer_ref, ...), custom_call_target="tpu_custom_call" | custom-call | bytes 704512 | tf_op jit(solution)/shard_map/pallas_call | solution.py:27
  (7 shorter events, 0.0 us)
Async XLA Ops:
  0.6 0.7 %copy-start.4 = (s32[512]{0:T(512)S(1)}, s32[512]{0:T(512)}, u32[]{:S(2)}) copy-start(s32[512]{0:T(512)} %param.11) | copy-start | bytes 6148
  0.6 1.0 %copy-start.1 = (bf16[512,128]{1,0:T(8,128)(2,1)S(1)}, bf16[512,128]{1,0:T(8,128)(2,1)}, u32[]{:S(2)}) copy-start(bf16[512,128]{1,0:T(8,128)(2,1)} %fraction_ref.1) | copy-start | bytes 393220
  0.7 0.7 %copy-start.3 = (bf16[3,512]{1,0:T(4,128)(2,1)S(1)}, bf16[3,512]{1,0:T(4,128)(2,1)}, u32[]{:S(2)}) copy-start(bf16[3,512]{1,0:T(4,128)(2,1)} %speed_ref.1) | copy-start | bytes 9220
  0.7 0.7 %copy-start.2 = (s32[512,1]{0,1:T(1,128)S(1)}, s32[512,1]{0,1:T(1,128)}, u32[]{:S(2)}) copy-start(s32[512,1]{0,1:T(1,128)} %param.10) | copy-start | bytes 6148
  0.7 0.7 %copy-start.5 = (f32[27]{0:T(128)S(1)}, f32[27]{0:T(128)}, u32[]{:S(2)}) copy-start(f32[27]{0:T(128)} %param.7) | copy-start | bytes 328
  2.1 18.2 %copy-start = (f32[27,2,8,128]{3,2,1,0:T(8,128)S(1)}, f32[27,2,8,128]{3,2,1,0:T(8,128)}, u32[]{:S(2)}) copy-start(f32[27,2,8,128]{3,2,1,0:T(8,128)} %fields_ref.1) | copy-start | bytes 663556
  20.8 5.0 %collective-permute-start = (f32[18,128]{1,0:T(8,128)S(1)}, f32[18,128]{1,0:T(8,128)S(1)}, u32[]{:S(2)}, u32[]{:S(2)}) collective-permute-start(f32[18,128]{1,0:T(8,128)S(1)} %get-tuple-element.33), channel_id=1, source_target_pairs={{0,7},{1,2},{2,1},{3,4},{4,3},{5,6},{6,5},{7,0},{8,15},{9,10},{10,... | collective-permute-start | bytes 27656 | tf_op jit(solution)/shard_map/ppermute | solution.py:383
  21.8 4.1 %collective-permute-start.1 = (f32[18,128]{1,0:T(8,128)S(1)}, f32[18,128]{1,0:T(8,128)S(1)}, u32[]{:S(2)}, u32[]{:S(2)}) collective-permute-start(f32[18,128]{1,0:T(8,128)S(1)} %get-tuple-element.34), channel_id=1, source_target_pairs={{0,1},{1,0},{2,3},{3,2},{4,5},{5,4},{6,7},{7,6},{8,9},{9,8},{10,11... | collective-permute-start | bytes 27656 | tf_op jit(solution)/shard_map/ppermute | solution.py:377
  25.8 2.2 %collective-permute-start.2 = (f32[9,8,128]{2,1,0:T(8,128)S(1)}, f32[9,8,128]{2,1,0:T(8,128)S(1)}, u32[]{:S(2)}, u32[]{:S(2)}) collective-permute-start(f32[9,8,128]{2,1,0:T(8,128)S(1)} %get-tuple-element.35), channel_id=1, source_target_pairs={{0,1},{1,0},{2,3},{3,2},{4,5},{5,4},{6,7},{7,6},{8,16},{9,17},{10,... | collective-permute-start | bytes 110600 | tf_op jit(solution)/shard_map/ppermute | solution.py:372
  25.9 4.3 %collective-permute-start.3 = (f32[9,8,128]{2,1,0:T(8,128)S(1)}, f32[9,8,128]{2,1,0:T(8,128)S(1)}, u32[]{:S(2)}, u32[]{:S(2)}) collective-permute-start(f32[9,8,128]{2,1,0:T(8,128)S(1)} %get-tuple-element.36), channel_id=1, source_target_pairs={{0,8},{1,9},{2,10},{3,11},{4,12},{5,13},{6,14},{7,15},{8,0},{9,1},... | collective-permute-start | bytes 110600 | tf_op jit(solution)/shard_map/ppermute | solution.py:372
  31.5 10.0 %all-to-all-start.1 = ((f32[32,4,128]{2,1,0:T(4,128)}), f32[32,4,128]{2,1,0:T(4,128)S(1)}, u32[]{:S(2)}, u32[]{:S(2)}) async-start(f32[32,4,128]{2,1,0:T(4,128)} %bitcast.5), calls=%async_computation.1 | async-start | bytes 131072 | tf_op jit(solution)/shard_map/all_to_all | solution.py:437
  34.1 6.7 %collective-permute-start.4 = (f32[9,8,128]{2,1,0:T(8,128)S(1)}, f32[9,8,128]{2,1,0:T(8,128)S(1)}, u32[]{:S(2)}, u32[]{:S(2)}) collective-permute-start(f32[9,8,128]{2,1,0:T(8,128)S(1)} %get-tuple-element.43), channel_id=1, source_target_pairs={{0,8},{1,9},{2,10},{3,11},{4,12},{5,13},{6,14},{7,15},{8,0},{9,1},... | collective-permute-start | bytes 110600 | tf_op jit(solution)/shard_map/ppermute | solution.py:372
  35.8 5.0 %collective-permute-start.5 = (f32[9,8,128]{2,1,0:T(8,128)S(1)}, f32[9,8,128]{2,1,0:T(8,128)S(1)}, u32[]{:S(2)}, u32[]{:S(2)}) collective-permute-start(f32[9,8,128]{2,1,0:T(8,128)S(1)} %get-tuple-element.44), channel_id=1, source_target_pairs={{0,1},{1,0},{2,3},{3,2},{4,5},{5,4},{6,7},{7,6},{8,16},{9,17},{10,... | collective-permute-start | bytes 110600 | tf_op jit(solution)/shard_map/ppermute | solution.py:372
  35.8 5.0 %collective-permute-start.6 = (f32[18,128]{1,0:T(8,128)S(1)}, f32[18,128]{1,0:T(8,128)S(1)}, u32[]{:S(2)}, u32[]{:S(2)}) collective-permute-start(f32[18,128]{1,0:T(8,128)S(1)} %get-tuple-element.45), channel_id=1, source_target_pairs={{0,7},{1,2},{2,1},{3,4},{4,3},{5,6},{6,5},{7,0},{8,15},{9,10},{10,... | collective-permute-start | bytes 27656 | tf_op jit(solution)/shard_map/ppermute | solution.py:383
  39.3 1.4 %collective-permute-start.7 = (f32[18,128]{1,0:T(8,128)S(1)}, f32[18,128]{1,0:T(8,128)S(1)}, u32[]{:S(2)}, u32[]{:S(2)}) collective-permute-start(f32[18,128]{1,0:T(8,128)S(1)} %get-tuple-element.46), channel_id=1, source_target_pairs={{0,1},{1,0},{2,3},{3,2},{4,5},{5,4},{6,7},{7,6},{8,9},{9,8},{10,11... | collective-permute-start | bytes 27656 | tf_op jit(solution)/shard_map/ppermute | solution.py:377

commit v9 on v8

--- a/solution.py
+++ b/solution.py
@@ -42,20 +42,15 @@
     return z * length + x
 
 
-def split3(x):
+def split2(x):
     high = x.astype(bf16)
-    rest = x - high.astype(f32)
-    mid = rest.astype(bf16)
-    return high, mid, (rest - mid.astype(f32)).astype(bf16)
-
-
-def tables_kernel(capacity, earlier_ref, spread_ref, own_ref):
-    width, slots = spread_ref.shape
-    order = iota(earlier_ref.shape, 0) < iota(earlier_ref.shape, 1)
-    earlier_ref[...] = jnp.where(order, 1.0, 0.0).astype(bf16)
-    same = iota((width, slots), 0) % capacity == iota((width, slots), 1) % capacity
-    spread_ref[...] = jnp.where(same, 1.0, 0.0).astype(bf16)
-    own_ref[...] = jnp.where(iota(own_ref.shape, 0) == iota(own_ref.shape, 1) // capacity, 1.0, 0.0)
+    return high, (x - high.astype(f32)).astype(bf16)
+
+
+def tables_kernel(capacity, earlier_ref, spread_ref):
+    row, column = iota(earlier_ref.shape, 0), iota(earlier_ref.shape, 1)
+    earlier_ref[...] = jnp.where(row < column, 1.0, 0.0).astype(bf16)
+    spread_ref[...] = jnp.where(row % capacity == column % capacity, 1.0, 0.0).astype(bf16)
 
 
 def ranks(hot, earlier):
@@ -219,7 +214,7 @@
 
 
 def first_kernel(
-    devices, capacity, recv_ref, fields_ref, rates_ref, spread_ref, own_ref,
+    devices, capacity, recv_ref, fields_ref, rates_ref, spread_ref,
     post_ref, outer_ref, inner_ref, push_ref, held_ref, line_ref, slot_ref, wide_ref,
 ):
     width = recv_ref.shape[1]
@@ -228,24 +223,38 @@
     lines = depth * length
     rate = [rates_ref[:, a : a + 1] for a in range(27)]
     wide_ref[...] = recv_ref[...].astype(f32)
-    facts = wide_ref[pl.ds(capacity, devices, stride=block), :]
     slot_rows = jnp.concatenate(
         [wide_ref[j * block : j * block + capacity] for j in range(devices)], axis=0
     ).astype(bf16)
     slot_ref[...] = slot_rows
-    group = iota((devices, width), 1) // capacity
-    stacked = jnp.concatenate([jnp.where(group == m, facts, 0.0) for m in range(4)], axis=0)
-    wide = jnp.dot(stacked.astype(bf16), spread_ref[...], preferred_element_type=f32)
-    own = own_ref[...]
-    fact = [
-        jnp.sum(own * wide[m * devices : (m + 1) * devices], axis=0, keepdims=True) for m in range(4)
-    ]
+    tiles, shared = slots // LANES, LANES // capacity
+    group = iota((tiles, width), 1) // capacity
+    rows = [wide_ref[pl.ds(capacity + a * block, tiles, stride=shared * block), :] for a in range(shared)]
+    picked = jnp.concatenate([jnp.where(group == m, row, 0.0) for m in range(4) for row in rows], axis=0)
+    placed = jnp.dot(picked.astype(bf16), spread_ref[...], preferred_element_type=f32)
+    fact = []
+    for m in range(4):
+        first = m * shared * tiles
+        fact.append(
+            total_of(
+                [
+                    jnp.where(group == a, placed[first + a * tiles : first + (a + 1) * tiles], 0.0)
+                    for a in range(shared)
+                ]
+            )
+        )
     line_ref[...] = fact[3].astype(i32)
-    on_line = iota((lines, slots), 0) == fact[3].astype(i32)
-    gather = [jnp.where(on_line, 1.0, 0.0)] + [jnp.where(on_line, fact[k], 0.0) for k in range(3)]
-    held_ref[...] = jnp.dot(
-        jnp.concatenate(gather, axis=0).astype(bf16), slot_rows, preferred_element_type=f32
-    )
+    gather = []
+    for t in range(tiles):
+        on_line = iota((lines, LANES), 0) == fact[3][t : t + 1].astype(i32)
+        gather.append(
+            jnp.concatenate(
+                [jnp.where(on_line, 1.0, 0.0)]
+                + [jnp.where(on_line, fact[k][t : t + 1], 0.0) for k in range(3)],
+                axis=0,
+            ).astype(bf16)
+        )
+    held_ref[...] = jnp.dot(jnp.concatenate(gather, axis=1), slot_rows, preferred_element_type=f32)
     for z in range(depth):
         relaxed = relax([fields_ref[i, z] for i in range(27)], rate)
         post, push = exchange(*relaxed, *grains_at(held_ref, z, depth, length))
@@ -258,7 +267,8 @@
 
 def turn_kernel(slot_ref, dest_ref, rank_ref, turned_ref, hot_ref, at_rank_ref):
     turned_ref[...] = slot_ref[...].astype(f32).T.astype(bf16)
-    hot_ref[...] = jnp.where(iota(hot_ref.shape, 0) == dest_ref[...], 1.0, 0.0).astype(bf16)
+    devices = hot_ref.shape[0] // 2
+    hot_ref[...] = jnp.where(iota(hot_ref.shape, 0) % devices == dest_ref[...], 1.0, 0.0).astype(bf16)
     at_rank_ref[...] = jnp.where(iota(at_rank_ref.shape, 0) == rank_ref[...], 1.0, 0.0)
 
 
@@ -321,18 +331,18 @@
         [push_ref[k, z] + pushes[z][k] for k in range(3) for z in range(depth)], axis=0
     )
     along_y = jnp.dot(
-        jnp.concatenate(split3(total), axis=0), turned_ref[...], preferred_element_type=f32
-    )
-    along_y = along_y[: 3 * lines] + along_y[3 * lines : 6 * lines] + along_y[6 * lines :]
-    on_line = iota((lines, slots), 0) == line_ref[...]
+        jnp.concatenate(split2(total), axis=0), turned_ref[...], preferred_element_type=f32
+    )
+    along_y = along_y[: 3 * lines] + along_y[3 * lines :]
     tiles, per_tile = slots // LANES, LANES // capacity
     group = iota((tiles, LANES), 1) // capacity
-    force = []
-    for k in range(3):
-        picked = -jnp.sum(jnp.where(on_line, along_y[k * lines : (k + 1) * lines], 0.0), axis=0, keepdims=True)
-        force.append(
-            jnp.concatenate([picked[:, t * LANES : (t + 1) * LANES] for t in range(tiles)], axis=0)
-        )
+    force = [[], [], []]
+    for t in range(tiles):
+        on_line = iota((lines, LANES), 0) == line_ref[t : t + 1]
+        for k in range(3):
+            part = along_y[k * lines : (k + 1) * lines, t * LANES : (t + 1) * LANES]
+            force[k].append(-jnp.sum(jnp.where(on_line, part, 0.0), axis=0, keepdims=True))
+    force = [jnp.concatenate(parts, axis=0) for parts in force]
     for a in range(per_tile):
         block = jnp.zeros((tiles, LANES), f32)
         for k in range(3):
@@ -350,10 +360,9 @@
         fields = streamed(post_ref, outer_ref, inner_ref, far_ref, near_ref, z, back_ref)
         for i in range(27):
             scaled_ref[i, z] = fields[i] * (1.0 / WEIGHT[i])
-    back = back_ref[pl.ds(0, hot_ref.shape[0], stride=4), :]
-    parts = jnp.concatenate([part.astype(f32) for part in split3(back)], axis=1).T
+    back = back_ref[pl.ds(0, hot_ref.shape[0] // 2, stride=4), :]
+    parts = jnp.concatenate([part.astype(f32) for part in split2(back)], axis=0).T
     picked = jnp.dot(parts.astype(bf16), hot_ref[...], preferred_element_type=f32)
-    picked = picked[:LANES] + picked[LANES : 2 * LANES] + picked[2 * LANES :]
     for k in range(3):
         mine = at_rank_ref[...] * picked[k * capacity : (k + 1) * capacity]
         force_ref[k : k + 1] = jnp.sum(mine, axis=0, keepdims=True)
@@ -393,10 +402,8 @@
     shape, both = jax.ShapeDtypeStruct, ("gz", "gx")
     dest, line = grain_dest.reshape(1, grains), grain_line.reshape(1, grains)
     rows = devices * (capacity + 2)
-    earlier, spread, own = call(
-        functools.partial(tables_kernel, capacity),
-        [shape((LANES, LANES), bf16), shape((width, slots), bf16), shape((devices, slots), f32)],
-        flops=10**9,
+    earlier, spread = call(
+        functools.partial(tables_kernel, capacity), [shape((LANES, LANES), bf16)] * 2, flops=10**9
     )
     rank, facts, rates = call(
         functools.partial(rank_kernel, devices),
@@ -418,14 +425,14 @@
         functools.partial(first_kernel, devices, capacity),
         [
             state, ends, ends, shape((3, depth, length, width), f32),
-            shape((4 * lines, width), f32), shape((1, slots), i32), shape((slots, width), bf16),
+            shape((4 * lines, width), f32), shape((slots // LANES, LANES), i32), shape((slots, width), bf16),
         ],
-        recv, populations, rates, spread, own, scratch=[pltpu.VMEM((rows, width), f32)],
+        recv, populations, rates, spread, scratch=[pltpu.VMEM((rows, width), f32)],
     )
     outer, inner = swap_outer(outer), swap_inner(inner)
     turned, hot, at_rank = call(
         turn_kernel,
-        [shape((width, slots), bf16), shape((devices, grains), bf16), shape((capacity, grains), f32)],
+        [shape((width, slots), bf16), shape((2 * devices, grains), bf16), shape((capacity, grains), f32)],
         slot_rows, dest, rank,
     )
     near, far = swap_faces(*call(faces_kernel, [face, face], post, outer, inner))

time: 42.6 us -> 42.4 us (level)
  no operation moved by 1% of the time
where the time goes in v9:
time: 42.4 us; the launch traced here: 42.1 us
  blocking collectives  18.2 us (43%)
  starting transfers between devices  10.8 us (25%)
  waiting for transfers between devices  8.33 us (20%)
  Pallas kernels  3.28 us (8%)
  between operations  0.76 us (2%)
  local copies, waits for them, and re-layouts  0.72 us (2%)
    all_to_all x1, blocking collectives, per_device(): lax.all_to_all(send.reshape(devices, capacity // 2 + 1, 2, width), both,...  18.2 us
    ppermute x2, waiting for transfers between devices, swap_outer(): return lax.ppermute(outer, 'gx', pairs)  5.46 us
    ppermute x2, starting transfers between devices, swap_outer(): return lax.ppermute(outer, 'gx', pairs)  4.5 us
    ppermute x4, starting transfers between devices, swap_faces(): received.append(lax.ppermute(face, ('gz', 'gx'), pairs))  3.76 us
    pallas_call x8, Pallas kernels, call(): pl.pallas_call(kernel, out_shape=list(outs), in_specs=[pl.BlockSpec(memor...  3.28 us
    all_to_all x1, starting transfers between devices, per_device(): lax.all_to_all(back.reshape(devices, 4, LANES), both, split_axis=0, conca...  2.57 us
    ppermute x4, waiting for transfers between devices, swap_faces(): received.append(lax.ppermute(face, ('gz', 'gx'), pairs))  2.18 us
  transfers between devices with their start and end apart: 9, of which 4 were waited for; matrix products, arithmetic and copies ran while one was open for 0% of the time, Pallas kernels for 0%

profile of v9, /device:TPU:0, one launch (start us, length us, event | category | flops | bytes accessed | tf_op | source)
XLA Modules:
  0.0 42.1 jit_solution(9201665156619121265)
XLA Ops:
  0.7 0.0 copy-start.3
  0.7 0.0 copy-start.2
  0.7 0.0 copy-start.5
  0.7 0.6 %copy-done.4 = s32[512]{0:T(512)S(1)} copy-done((s32[512]{0:T(512)S(1)}, s32[512]{0:T(512)}, u32[]{:S(2)}) %copy-start.4) | copy-done | bytes 2072
  1.3 0.1 copy-done.3
  1.4 0.0 copy-done.2
  1.4 0.2 shard_map.78
  1.6 0.5 %shard_map.79 = bf16[1088,128]{1,0:T(8,128)(2,1)S(1)} custom-call(s32[1,512]{1,0:T(1,128)S(1)} %bitcast.11, s32[1,512]{1,0:T(1,128)S(1)} %get-tuple-element.27.rank_ref, f32[4,512]{1,0:T(4,128)S(1)} %get-tuple-element.28.facts_ref, bf16[512,128]{1,0:T(8,128)(2,1)S(1)} %copy-done.1), custom_call_target="tpu_custom_call" | custom-call | bytes 421888 | tf_op jit(solution)/shard_map/pallas_call | solution.py:27
  2.1 0.0 copy-start
  2.1 18.2 %all_to_all.10 = bf16[32,17,2,128]{3,2,1,0:T(2,128)(2,1)S(1)} all-to-all(bf16[32,17,2,128]{3,2,1,0:T(2,128)(2,1)S(1)} %bitcast.8), channel_id=1, replica_groups=mesh['gz'=4,'gx'=8] {'gz','gx'}, dimensions={0} | all-to-all | bytes 557056 | tf_op jit(solution)/shard_map/all_to_all | solution.py:419
  20.3 0.4 %shard_map.80 = (f32[27,2,8,128]{3,2,1,0:T(8,128)S(1)}, f32[18,128]{1,0:T(8,128)S(1)}, f32[18,128]{1,0:T(8,128)S(1)}, f32[3,2,8,128]{3,2,1,0:T(8,128)S(1)}, f32[...) custom-call(bf16[1088,128]{1,0:T(8,128)(2,1)S(1)} %bitcast.7, ...), custom_call_target="tpu_custom_call" | custom-call | bytes 1095788 | tf_op jit(solution)/shard_map/pallas_call | solution.py:27
  20.7 0.9 %collective-permute-start = (f32[18,128]{1,0:T(8,128)S(1)}, f32[18,128]{1,0:T(8,128)S(1)}, u32[]{:S(2)}, u32[]{:S(2)}) collective-permute-start(f32[18,128]{1,0:T(8,128)S(1)} %get-tuple-element.31), channel_id=1, source_target_pairs={{0,7},{1,2},{2,1},{3,4},{4,3},{5,6},{6,5},{7,0},{8,15},{9,10},{10,... | collective-permute-start | bytes 27656 | tf_op jit(solution)/shard_map/ppermute | solution.py:392
  21.6 0.0 collective-permute-start.1
  21.7 4.1 %collective-permute-done.outer_ref = f32[18,128]{1,0:T(8,128)S(1)} collective-permute-done((f32[18,128]{1,0:T(8,128)S(1)}, f32[18,128]{1,0:T(8,128)S(1)}, u32[]{:S(2)}, u32[]{:S(2)}) %collective-permute-start) | collective-permute-done | bytes 9248 | tf_op jit(solution)/shard_map/ppermute | solution.py:392
  25.7 0.0 collective-permute-done.1.inner_ref
  25.7 0.1 collective-permute-start.2
  25.8 2.0 %collective-permute-start.3 = (f32[9,8,128]{2,1,0:T(8,128)S(1)}, f32[9,8,128]{2,1,0:T(8,128)S(1)}, u32[]{:S(2)}, u32[]{:S(2)}) collective-permute-start(f32[9,8,128]{2,1,0:T(8,128)S(1)} %get-tuple-element.34), channel_id=1, source_target_pairs={{0,8},{1,9},{2,10},{3,11},{4,12},{5,13},{6,14},{7,15},{8,0},{9,1},... | collective-permute-start | bytes 110600 | tf_op jit(solution)/shard_map/ppermute | solution.py:381
  27.8 0.1 shard_map.82
  27.9 0.0 collective-permute-done.2.far_ref
  28.0 2.2 %collective-permute-done.3.near_ref = f32[9,8,128]{2,1,0:T(8,128)S(1)} collective-permute-done((f32[9,8,128]{2,1,0:T(8,128)S(1)}, f32[9,8,128]{2,1,0:T(8,128)S(1)}, u32[]{:S(2)}, u32[]{:S(2)}) %collective-permute-start.3) | collective-permute-done | bytes 36896 | tf_op jit(solution)/shard_map/ppermute | solution.py:381
  30.1 1.2 %shard_map.83 = (f32[27,2,8,128]{3,2,1,0:T(8,128)S(1)}, f32[9,8,128]{2,1,0:T(8,128)S(1)}, f32[9,8,128]{2,1,0:T(8,128)S(1)}, f32[18,128]{1,0:T(8,128)S(1)}, f32[18,128]{1,0:T(8,128)S(1)}, /*index=5*/f32[128,128]{1,0:T(8,128)}) custom-call(f32[1,27]{1,0:T(1,128)S(1)} %get-tuple-element.26.rates_ref, f32[27,2,8,128]{3,2,1,0:T(8,128)S(1)} %get-tuple-element.30.post_ref, ...), custom_call_target="tpu_custom_call" | custom-call | bytes 1015916 | tf_op jit(solution)/shard_map/pallas_call | solution.py:27
  31.3 2.6 %all-to-all-start.1 = ((f32[32,4,128]{2,1,0:T(4,128)}), f32[32,4,128]{2,1,0:T(4,128)S(1)}, u32[]{:S(2)}, u32[]{:S(2)}) async-start(f32[32,4,128]{2,1,0:T(4,128)} %bitcast.5), calls=%async_computation.1 | async-start | bytes 131072 | tf_op jit(solution)/shard_map/all_to_all | solution.py:444
  33.9 1.7 %collective-permute-start.4 = (f32[9,8,128]{2,1,0:T(8,128)S(1)}, f32[9,8,128]{2,1,0:T(8,128)S(1)}, u32[]{:S(2)}, u32[]{:S(2)}) collective-permute-start(f32[9,8,128]{2,1,0:T(8,128)S(1)} %get-tuple-element.41), channel_id=1, source_target_pairs={{0,8},{1,9},{2,10},{3,11},{4,12},{5,13},{6,14},{7,15},{8,0},{9,1},... | collective-permute-start | bytes 110600 | tf_op jit(solution)/shard_map/ppermute | solution.py:381
  35.6 0.0 collective-permute-start.5
  35.6 3.6 %collective-permute-start.6 = (f32[18,128]{1,0:T(8,128)S(1)}, f32[18,128]{1,0:T(8,128)S(1)}, u32[]{:S(2)}, u32[]{:S(2)}) collective-permute-start(f32[18,128]{1,0:T(8,128)S(1)} %get-tuple-element.43), channel_id=1, source_target_pairs={{0,7},{1,2},{2,1},{3,4},{4,3},{5,6},{6,5},{7,0},{8,15},{9,10},{10,... | collective-permute-start | bytes 27656 | tf_op jit(solution)/shard_map/ppermute | solution.py:392
  39.2 0.0 collective-permute-start.7
  39.2 1.4 %collective-permute-done.6.outer_ref = f32[18,128]{1,0:T(8,128)S(1)} collective-permute-done((f32[18,128]{1,0:T(8,128)S(1)}, f32[18,128]{1,0:T(8,128)S(1)}, u32[]{:S(2)}, u32[]{:S(2)}) %collective-permute-start.6) | collective-permute-done | bytes 9248 | tf_op jit(solution)/shard_map/ppermute | solution.py:392
  40.6 0.0 collective-permute-done.7.inner_ref
  40.6 0.0 collective-permute-done.4.near_ref
  40.6 0.0 collective-permute-done.5.far_ref
  40.6 0.7 %all-to-all-done.1 = f32[32,4,128]{2,1,0:T(4,128)S(1)} async-done(((f32[32,4,128]{2,1,0:T(4,128)}), f32[32,4,128]{2,1,0:T(4,128)S(1)}, u32[]{:S(2)}, u32[]{:S(2)}) %all-to-all-start.1) | async-done | bytes 65568 | tf_op jit(solution)/shard_map/all_to_all | solution.py:444
  41.3 0.9 %shard_map.84 = (f32[27,2,8,128]{3,2,1,0:T(8,128)}, f32[3,512]{1,0:T(4,128)}) custom-call(f32[27,2,8,128]{3,2,1,0:T(8,128)S(1)} %get-tuple-element.40.post_ref, f32[9,8,128]{2,1,0:T(8,128)S(1)} %collective-permute-done.4.near_ref, f32[9,8,128]{2,1,0:T(8,128)S(1)} %collective-permute-done.5.far_ref, f32[18,128]{1,0:T(8,128)S(1)} %collective-permute-done.6.outer_ref, ...), custom_call_target="tpu_custom_call" | custom-call | bytes 737280 | tf_op jit(solution)/shard_map/pallas_call | solution.py:27
  (7 shorter events, 0.1 us)
Async XLA Ops:
  0.6 0.7 %copy-start.4 = (s32[512]{0:T(512)S(1)}, s32[512]{0:T(512)}, u32[]{:S(2)}) copy-start(s32[512]{0:T(512)} %param.11) | copy-start | bytes 6148
  0.6 0.9 %copy-start.1 = (bf16[512,128]{1,0:T(8,128)(2,1)S(1)}, bf16[512,128]{1,0:T(8,128)(2,1)}, u32[]{:S(2)}) copy-start(bf16[512,128]{1,0:T(8,128)(2,1)} %fraction_ref.1) | copy-start | bytes 393220
  0.7 0.7 %copy-start.3 = (bf16[3,512]{1,0:T(4,128)(2,1)S(1)}, bf16[3,512]{1,0:T(4,128)(2,1)}, u32[]{:S(2)}) copy-start(bf16[3,512]{1,0:T(4,128)(2,1)} %speed_ref.1) | copy-start | bytes 9220
  0.7 0.7 %copy-start.2 = (s32[512,1]{0,1:T(1,128)S(1)}, s32[512,1]{0,1:T(1,128)}, u32[]{:S(2)}) copy-start(s32[512,1]{0,1:T(1,128)} %param.10) | copy-start | bytes 6148
  0.7 0.7 %copy-start.5 = (f32[27]{0:T(128)S(1)}, f32[27]{0:T(128)}, u32[]{:S(2)}) copy-start(f32[27]{0:T(128)} %param.7) | copy-start | bytes 328
  2.1 18.2 %copy-start = (f32[27,2,8,128]{3,2,1,0:T(8,128)S(1)}, f32[27,2,8,128]{3,2,1,0:T(8,128)}, u32[]{:S(2)}) copy-start(f32[27,2,8,128]{3,2,1,0:T(8,128)} %fields_ref.1) | copy-start | bytes 663556
  20.7 5.0 %collective-permute-start = (f32[18,128]{1,0:T(8,128)S(1)}, f32[18,128]{1,0:T(8,128)S(1)}, u32[]{:S(2)}, u32[]{:S(2)}) collective-permute-start(f32[18,128]{1,0:T(8,128)S(1)} %get-tuple-element.31), channel_id=1, source_target_pairs={{0,7},{1,2},{2,1},{3,4},{4,3},{5,6},{6,5},{7,0},{8,15},{9,10},{10,... | collective-permute-start | bytes 27656 | tf_op jit(solution)/shard_map/ppermute | solution.py:392
  21.6 4.1 %collective-permute-start.1 = (f32[18,128]{1,0:T(8,128)S(1)}, f32[18,128]{1,0:T(8,128)S(1)}, u32[]{:S(2)}, u32[]{:S(2)}) collective-permute-start(f32[18,128]{1,0:T(8,128)S(1)} %get-tuple-element.32), channel_id=1, source_target_pairs={{0,1},{1,0},{2,3},{3,2},{4,5},{5,4},{6,7},{7,6},{8,9},{9,8},{10,11... | collective-permute-start | bytes 27656 | tf_op jit(solution)/shard_map/ppermute | solution.py:386
  25.7 2.2 %collective-permute-start.2 = (f32[9,8,128]{2,1,0:T(8,128)S(1)}, f32[9,8,128]{2,1,0:T(8,128)S(1)}, u32[]{:S(2)}, u32[]{:S(2)}) collective-permute-start(f32[9,8,128]{2,1,0:T(8,128)S(1)} %get-tuple-element.33), channel_id=1, source_target_pairs={{0,1},{1,0},{2,3},{3,2},{4,5},{5,4},{6,7},{7,6},{8,16},{9,17},{10,... | collective-permute-start | bytes 110600 | tf_op jit(solution)/shard_map/ppermute | solution.py:381
  25.8 4.3 %collective-permute-start.3 = (f32[9,8,128]{2,1,0:T(8,128)S(1)}, f32[9,8,128]{2,1,0:T(8,128)S(1)}, u32[]{:S(2)}, u32[]{:S(2)}) collective-permute-start(f32[9,8,128]{2,1,0:T(8,128)S(1)} %get-tuple-element.34), channel_id=1, source_target_pairs={{0,8},{1,9},{2,10},{3,11},{4,12},{5,13},{6,14},{7,15},{8,0},{9,1},... | collective-permute-start | bytes 110600 | tf_op jit(solution)/shard_map/ppermute | solution.py:381
  31.3 10.0 %all-to-all-start.1 = ((f32[32,4,128]{2,1,0:T(4,128)}), f32[32,4,128]{2,1,0:T(4,128)S(1)}, u32[]{:S(2)}, u32[]{:S(2)}) async-start(f32[32,4,128]{2,1,0:T(4,128)} %bitcast.5), calls=%async_computation.1 | async-start | bytes 131072 | tf_op jit(solution)/shard_map/all_to_all | solution.py:444
  33.9 6.7 %collective-permute-start.4 = (f32[9,8,128]{2,1,0:T(8,128)S(1)}, f32[9,8,128]{2,1,0:T(8,128)S(1)}, u32[]{:S(2)}, u32[]{:S(2)}) collective-permute-start(f32[9,8,128]{2,1,0:T(8,128)S(1)} %get-tuple-element.41), channel_id=1, source_target_pairs={{0,8},{1,9},{2,10},{3,11},{4,12},{5,13},{6,14},{7,15},{8,0},{9,1},... | collective-permute-start | bytes 110600 | tf_op jit(solution)/shard_map/ppermute | solution.py:381
  35.6 5.0 %collective-permute-start.5 = (f32[9,8,128]{2,1,0:T(8,128)S(1)}, f32[9,8,128]{2,1,0:T(8,128)S(1)}, u32[]{:S(2)}, u32[]{:S(2)}) collective-permute-start(f32[9,8,128]{2,1,0:T(8,128)S(1)} %get-tuple-element.42), channel_id=1, source_target_pairs={{0,1},{1,0},{2,3},{3,2},{4,5},{5,4},{6,7},{7,6},{8,16},{9,17},{10,... | collective-permute-start | bytes 110600 | tf_op jit(solution)/shard_map/ppermute | solution.py:381
  35.6 5.0 %collective-permute-start.6 = (f32[18,128]{1,0:T(8,128)S(1)}, f32[18,128]{1,0:T(8,128)S(1)}, u32[]{:S(2)}, u32[]{:S(2)}) collective-permute-start(f32[18,128]{1,0:T(8,128)S(1)} %get-tuple-element.43), channel_id=1, source_target_pairs={{0,7},{1,2},{2,1},{3,4},{4,3},{5,6},{6,5},{7,0},{8,15},{9,10},{10,... | collective-permute-start | bytes 27656 | tf_op jit(solution)/shard_map/ppermute | solution.py:392
  39.2 1.4 %collective-permute-start.7 = (f32[18,128]{1,0:T(8,128)S(1)}, f32[18,128]{1,0:T(8,128)S(1)}, u32[]{:S(2)}, u32[]{:S(2)}) collective-permute-start(f32[18,128]{1,0:T(8,128)S(1)} %get-tuple-element.44), channel_id=1, source_target_pairs={{0,1},{1,0},{2,3},{3,2},{4,5},{5,4},{6,7},{7,6},{8,9},{9,8},{10,11... | collective-permute-start | bytes 27656 | tf_op jit(solution)/shard_map/ppermute | solution.py:386

commit v10 on v9

--- a/solution.py
+++ b/solution.py
@@ -169,10 +169,12 @@
     return lax.axis_index(axis) % 2 == 0
 
 
-def store_faces(ups, downs, near_ref, far_ref):
+def store_faces(post_ref, near_ref, far_ref):
+    top = post_ref.shape[1] - 1
     for n in range(9):
-        near_ref[n] = jnp.where(even_place("gz"), ups[n], downs[n])
-        far_ref[n] = jnp.where(even_place("gz"), downs[n], ups[n])
+        up, down = post_ref[n + 18, top], post_ref[n, 0]
+        near_ref[n] = jnp.where(even_place("gz"), up, down)
+        far_ref[n] = jnp.where(even_place("gz"), down, up)
 
 
 def end_row(i, z, depth):
@@ -190,32 +192,27 @@
                 outer_ref[n : n + 1] = jnp.where(even_place("gx"), left, right)
 
 
-def moved_along_x(field, i, z, depth, outer_ref, inner_ref, corner=None):
-    cx = STEP[i][1]
-    if not cx:
-        return field
-    n, length = end_row(i, z, depth), field.shape[0]
-    outer, inner = outer_ref[n : n + 1], inner_ref[n : n + 1]
-    if corner is not None:
-        end = corner
-    elif cx > 0:
-        end = jnp.where(even_place("gx"), outer, inner)
-    else:
-        end = jnp.where(even_place("gx"), inner, outer)
+def end_from(i, outer, inner):
+    if STEP[i][1] > 0:
+        return jnp.where(even_place("gx"), outer, inner)
+    return jnp.where(even_place("gx"), inner, outer)
+
+
+def moved_along_x(field, i, end):
+    cx, length = STEP[i][1], field.shape[0]
     place = 0 if cx > 0 else length - 1
     return jnp.where(iota(field.shape, 0) == place, end, pltpu.roll(field, cx % length, 0))
 
 
-def across(near_ref, far_ref, i):
-    n = i % 9
+def across(near, far, i):
     if STEP[i][0] > 0:
-        return jnp.where(even_place("gz"), far_ref[n], near_ref[n])
-    return jnp.where(even_place("gz"), near_ref[n], far_ref[n])
+        return jnp.where(even_place("gz"), far, near)
+    return jnp.where(even_place("gz"), near, far)
 
 
 def first_kernel(
     devices, capacity, recv_ref, fields_ref, rates_ref, spread_ref,
-    post_ref, outer_ref, inner_ref, push_ref, held_ref, line_ref, slot_ref, wide_ref,
+    post_ref, outer_ref, inner_ref, far_ref, near_ref, push_ref, held_ref, line_ref, slot_ref, wide_ref,
 ):
     width = recv_ref.shape[1]
     block, slots = capacity + 2, devices * capacity
@@ -263,6 +260,7 @@
         for k in range(3):
             push_ref[k, z] = push[k]
     store_ends(post_ref, inner_ref, outer_ref)
+    store_faces(post_ref, near_ref, far_ref)
 
 
 def turn_kernel(slot_ref, dest_ref, rank_ref, turned_ref, hot_ref, at_rank_ref):
@@ -272,26 +270,35 @@
     at_rank_ref[...] = jnp.where(iota(at_rank_ref.shape, 0) == rank_ref[...], 1.0, 0.0)
 
 
-def faces_kernel(post_ref, outer_ref, inner_ref, near_ref, far_ref):
-    depth = post_ref.shape[1]
-    move = lambda i, z: moved_along_x(post_ref[i, z], i, z, depth, outer_ref, inner_ref)
-    ups, downs = [move(n + 18, depth - 1) for n in range(9)], [move(n, 0) for n in range(9)]
-    store_faces(ups, downs, near_ref, far_ref)
-
-
-def streamed(post_ref, outer_ref, inner_ref, far_ref, near_ref, z, back_ref=None):
+def corners_kernel(depth, outer_ref, inner_ref, far_ref, near_ref):
+    for i in range(9):
+        if STEP[i][1]:
+            up, down = [
+                end_from(i, outer_ref[n : n + 1], inner_ref[n : n + 1])
+                for n in (end_row(18 + i, depth - 1, depth), end_row(i, 0, depth))
+            ]
+            n = corner_row(i)
+            near_ref[n : n + 1] = jnp.where(even_place("gz"), up, down)
+            far_ref[n : n + 1] = jnp.where(even_place("gz"), down, up)
+
+
+def corner_row(i):
+    return (3 if STEP[i][1] > 0 else 0) + STEP[i][2] + 1
+
+
+def streamed(post_ref, outer_ref, inner_ref, far_ref, near_ref, z, corner):
     depth, width = post_ref.shape[1], post_ref.shape[3]
     moved_list = []
     for i in range(27):
         cz, cx, cy = STEP[i]
         source = z - cz
         inside = 0 <= source < depth
-        moved = post_ref[i, source] if inside else across(near_ref, far_ref, i)
-        if inside:
-            moved = moved_along_x(moved, i, source, depth, outer_ref, inner_ref)
-        elif cx and back_ref is not None:
-            corner = back_ref[pl.ds(4 * device_at(-cz, -cx) + 2 + cy, 1)]
-            moved = moved_along_x(moved, i, 0, depth, outer_ref, inner_ref, corner)
+        moved = post_ref[i, source] if inside else across(near_ref[i % 9], far_ref[i % 9], i)
+        if cx and inside:
+            n = end_row(i, source, depth)
+            moved = moved_along_x(moved, i, end_from(i, outer_ref[n : n + 1], inner_ref[n : n + 1]))
+        elif cx:
+            moved = moved_along_x(moved, i, corner(i))
         if cy:
             moved = pltpu.roll(moved, cy % width, 1)
         if not inside:
@@ -302,7 +309,7 @@
 
 
 def second_kernel(
-    capacity, rates_ref, post_ref, outer_ref, inner_ref, far_ref, near_ref,
+    capacity, rates_ref, post_ref, outer_ref, inner_ref, far_ref, near_ref, far_rows_ref, near_rows_ref,
     held_ref, push_ref, line_ref, turned_ref,
     next_ref, next_near_ref, next_far_ref, next_inner_ref, next_outer_ref, back_ref,
 ):
@@ -311,15 +318,19 @@
     slots = turned_ref.shape[1]
     halo = (outer_ref, inner_ref, far_ref, near_ref)
     rate = [rates_ref[:, a : a + 1] for a in range(27)]
+
+    def corner(i):
+        n = corner_row(i)
+        return across(near_rows_ref[n : n + 1], far_rows_ref[n : n + 1], i)
+
     pushes = []
     for z in range(depth):
-        relaxed = relax(streamed(post_ref, *halo, z), rate)
+        relaxed = relax(streamed(post_ref, *halo, z, corner), rate)
         post, push = exchange(*relaxed, *grains_at(held_ref, z, depth, length))
         for i in range(27):
             next_ref[i, z] = post[i]
         pushes.append(push)
-    ups, downs = [next_ref[n + 18, depth - 1] for n in range(9)], [next_ref[n, 0] for n in range(9)]
-    store_faces(ups, downs, next_near_ref, next_far_ref)
+    store_faces(next_ref, next_near_ref, next_far_ref)
     store_ends(next_ref, next_inner_ref, next_outer_ref)
     back_ref[...] = jnp.zeros(back_ref.shape, f32)
     for i in range(27):
@@ -356,8 +367,12 @@
     capacity, post_ref, near_ref, far_ref, outer_ref, inner_ref, back_ref, hot_ref, at_rank_ref,
     scaled_ref, force_ref,
 ):
+    def corner(i):
+        cz, cx, cy = STEP[i]
+        return back_ref[pl.ds(4 * device_at(-cz, -cx) + 2 + cy, 1)]
+
     for z in range(post_ref.shape[1]):
-        fields = streamed(post_ref, outer_ref, inner_ref, far_ref, near_ref, z, back_ref)
+        fields = streamed(post_ref, outer_ref, inner_ref, far_ref, near_ref, z, corner)
         for i in range(27):
             scaled_ref[i, z] = fields[i] * (1.0 / WEIGHT[i])
     back = back_ref[pl.ds(0, hot_ref.shape[0] // 2, stride=4), :]
@@ -421,25 +436,30 @@
     ).reshape(rows, width)
     state = shape(populations.shape, f32)
     face, ends = shape((9, length, width), f32), shape((9 * depth, width), f32)
-    post, outer, inner, push, held, slot_line, slot_rows = call(
+    post, outer, inner, far, near, push, held, slot_line, slot_rows = call(
         functools.partial(first_kernel, devices, capacity),
         [
-            state, ends, ends, shape((3, depth, length, width), f32),
+            state, ends, ends, face, face, shape((3, depth, length, width), f32),
             shape((4 * lines, width), f32), shape((slots // LANES, LANES), i32), shape((slots, width), bf16),
         ],
         recv, populations, rates, spread, scratch=[pltpu.VMEM((rows, width), f32)],
     )
     outer, inner = swap_outer(outer), swap_inner(inner)
+    near, far = swap_faces(near, far)
     turned, hot, at_rank = call(
         turn_kernel,
         [shape((width, slots), bf16), shape((2 * devices, grains), bf16), shape((capacity, grains), f32)],
         slot_rows, dest, rank,
     )
-    near, far = swap_faces(*call(faces_kernel, [face, face], post, outer, inner))
+    corners = shape((6, width), f32)
+    far_rows, near_rows = call(
+        functools.partial(corners_kernel, depth), [corners, corners], outer, inner, flops=10**10
+    )
+    near_rows, far_rows = swap_faces(near_rows, far_rows)
     post, next_near, next_far, inner, outer, back = call(
         functools.partial(second_kernel, capacity),
         [state, face, face, ends, ends, shape((4 * devices, LANES), f32)],
-        rates, post, outer, inner, far, near, held, push, slot_line, turned,
+        rates, post, outer, inner, far, near, far_rows, near_rows, held, push, slot_line, turned,
     )
     back = lax.all_to_all(
         back.reshape(devices, 4, LANES), both, split_axis=0, concat_axis=0, tiled=True

time: 42.4 us -> 41.7 us (0.983)
  waiting for transfers between devices: 8.33 us -> 5.67 us
  starting transfers between devices: 10.8 us -> 12.9 us
    ppermute x4 -> x6, starting transfers between devices: 3.76 us -> 5.8 us  [swap_faces(): received.append(lax.ppermute(face, ('gz', 'gx'), pairs))]
    ppermute x2, waiting for transfers between devices: 5.46 us -> 3.43 us  [swap_outer(): return lax.ppermute(outer, 'gx', pairs)]
    ppermute x4 -> x6, waiting for transfers between devices: 2.18 us -> 1.55 us  [swap_faces(): received.append(lax.ppermute(face, ('gz', 'gx'), pairs))]
  transfers between devices with their start and end apart: 9 -> 11, of which waited for: 4 -> 4; matrix products, arithmetic and copies ran while one was open for 0% -> 0% of each run, Pallas kernels for 0% -> 0%
where the time goes in v10:
time: 41.7 us; the launch traced here: 41.5 us
  blocking collectives  18.2 us (44%)
  starting transfers between devices  12.9 us (31%)
  waiting for transfers between devices  5.67 us (14%)
  Pallas kernels  3.27 us (8%)
  between operations  0.76 us (2%)
  local copies, waits for them, and re-layouts  0.72 us (2%)
    all_to_all x1, blocking collectives, per_device(): lax.all_to_all(send.reshape(devices, capacity // 2 + 1, 2, width), both,...  18.2 us
    ppermute x6, starting transfers between devices, swap_faces(): received.append(lax.ppermute(face, ('gz', 'gx'), pairs))  5.8 us
    ppermute x2, starting transfers between devices, swap_outer(): return lax.ppermute(outer, 'gx', pairs)  4.48 us
    ppermute x2, waiting for transfers between devices, swap_outer(): return lax.ppermute(outer, 'gx', pairs)  3.43 us
    pallas_call x8, Pallas kernels, call(): pl.pallas_call(kernel, out_shape=list(outs), in_specs=[pl.BlockSpec(memor...  3.27 us
    all_to_all x1, starting transfers between devices, per_device(): lax.all_to_all(back.reshape(devices, 4, LANES), both, split_axis=0, conca...  2.57 us
    ppermute x6, waiting for transfers between devices, swap_faces(): received.append(lax.ppermute(face, ('gz', 'gx'), pairs))  1.55 us
  transfers between devices with their start and end apart: 11, of which 4 were waited for; matrix products, arithmetic and copies ran while one was open for 0% of the time, Pallas kernels for 0%

profile of v10, /device:TPU:0, one launch (start us, length us, event | category | flops | bytes accessed | tf_op | source)
XLA Modules:
  0.0 41.5 jit_solution(14036680741273697556)
XLA Ops:
  0.7 0.0 copy-start.3
  0.7 0.0 copy-start.2
  0.7 0.0 copy-start.5
  0.7 0.6 %copy-done.4 = s32[512]{0:T(512)S(1)} copy-done((s32[512]{0:T(512)S(1)}, s32[512]{0:T(512)}, u32[]{:S(2)}) %copy-start.4) | copy-done | bytes 2072
  1.3 0.1 copy-done.3
  1.4 0.0 copy-done.2
  1.4 0.2 shard_map.78
  1.6 0.5 %shard_map.79 = bf16[1088,128]{1,0:T(8,128)(2,1)S(1)} custom-call(s32[1,512]{1,0:T(1,128)S(1)} %bitcast.11, s32[1,512]{1,0:T(1,128)S(1)} %get-tuple-element.29.rank_ref, f32[4,512]{1,0:T(4,128)S(1)} %get-tuple-element.30.facts_ref, bf16[512,128]{1,0:T(8,128)(2,1)S(1)} %copy-done.1), custom_call_target="tpu_custom_call" | custom-call | bytes 421888 | tf_op jit(solution)/shard_map/pallas_call | solution.py:27
  2.1 0.0 copy-start
  2.1 18.2 %all_to_all.10 = bf16[32,17,2,128]{3,2,1,0:T(2,128)(2,1)S(1)} all-to-all(bf16[32,17,2,128]{3,2,1,0:T(2,128)(2,1)S(1)} %bitcast.8), channel_id=1, replica_groups=mesh['gz'=4,'gx'=8] {'gz','gx'}, dimensions={0} | all-to-all | bytes 557056 | tf_op jit(solution)/shard_map/all_to_all | solution.py:434
  20.3 0.4 %shard_map.80 = (f32[27,2,8,128]{3,2,1,0:T(8,128)S(1)}, f32[18,128]{1,0:T(8,128)S(1)}, f32[18,128]{1,0:T(8,128)S(1)}, f32[9,8,128]{2,1,0:T(8,128)S(1)}, f32[9,8,...) custom-call(bf16[1088,128]{1,0:T(8,128)(2,1)S(1)} %bitcast.7, ...), custom_call_target="tpu_custom_call" | custom-call | bytes 1169516 | tf_op jit(solution)/shard_map/pallas_call | solution.py:27
  20.7 0.9 %collective-permute-start = (f32[18,128]{1,0:T(8,128)S(1)}, f32[18,128]{1,0:T(8,128)S(1)}, u32[]{:S(2)}, u32[]{:S(2)}) collective-permute-start(f32[18,128]{1,0:T(8,128)S(1)} %get-tuple-element.33), channel_id=1, source_target_pairs={{0,7},{1,2},{2,1},{3,4},{4,3},{5,6},{6,5},{7,0},{8,15},{9,10},{10,... | collective-permute-start | bytes 27656 | tf_op jit(solution)/shard_map/ppermute | solution.py:407
  21.7 0.0 collective-permute-start.1
  21.7 0.5 %collective-permute-start.2 = (f32[9,8,128]{2,1,0:T(8,128)S(1)}, f32[9,8,128]{2,1,0:T(8,128)S(1)}, u32[]{:S(2)}, u32[]{:S(2)}) collective-permute-start(f32[9,8,128]{2,1,0:T(8,128)S(1)} %get-tuple-element.35), channel_id=1, source_target_pairs={{0,1},{1,0},{2,3},{3,2},{4,5},{5,4},{6,7},{7,6},{8,16},{9,17},{10,... | collective-permute-start | bytes 110600 | tf_op jit(solution)/shard_map/ppermute | solution.py:396
  22.2 1.5 %collective-permute-start.3 = (f32[9,8,128]{2,1,0:T(8,128)S(1)}, f32[9,8,128]{2,1,0:T(8,128)S(1)}, u32[]{:S(2)}, u32[]{:S(2)}) collective-permute-start(f32[9,8,128]{2,1,0:T(8,128)S(1)} %get-tuple-element.36), channel_id=1, source_target_pairs={{0,8},{1,9},{2,10},{3,11},{4,12},{5,13},{6,14},{7,15},{8,0},{9,1},... | collective-permute-start | bytes 110600 | tf_op jit(solution)/shard_map/ppermute | solution.py:396
  23.7 2.0 %collective-permute-done.outer_ref = f32[18,128]{1,0:T(8,128)S(1)} collective-permute-done((f32[18,128]{1,0:T(8,128)S(1)}, f32[18,128]{1,0:T(8,128)S(1)}, u32[]{:S(2)}, u32[]{:S(2)}) %collective-permute-start) | collective-permute-done | bytes 9248 | tf_op jit(solution)/shard_map/ppermute | solution.py:407
  25.7 0.0 collective-permute-done.1.inner_ref
  25.7 0.1 collective-permute-start.4
  25.8 2.0 %collective-permute-start.5 = (f32[6,128]{1,0:T(8,128)S(1)}, f32[6,128]{1,0:T(8,128)S(1)}, u32[]{:S(2)}, u32[]{:S(2)}) collective-permute-start(f32[6,128]{1,0:T(8,128)S(1)} %get-tuple-element.38), channel_id=1, source_target_pairs={{0,8},{1,9},{2,10},{3,11},{4,12},{5,13},{6,14},{7,15},{8,0},{9,1},... | collective-permute-start | bytes 9224 | tf_op jit(solution)/shard_map/ppermute | solution.py:396
  27.8 0.1 shard_map.82
  27.9 1.5 %collective-permute-done.5.near_rows_ref = f32[6,128]{1,0:T(8,128)S(1)} collective-permute-done((f32[6,128]{1,0:T(8,128)S(1)}, f32[6,128]{1,0:T(8,128)S(1)}, u32[]{:S(2)}, u32[]{:S(2)}) %collective-permute-start.5) | collective-permute-done | bytes 3104 | tf_op jit(solution)/shard_map/ppermute | solution.py:396
  29.5 0.0 collective-permute-done.2.far_ref
  29.5 1.2 %shard_map.83 = (f32[27,2,8,128]{3,2,1,0:T(8,128)S(1)}, f32[9,8,128]{2,1,0:T(8,128)S(1)}, f32[9,8,128]{2,1,0:T(8,128)S(1)}, f32[18,128]{1,0:T(8,128)S(1)}, f32[18,128]{1,0:T(8,128)S(1)}, /*index=5*/f32[128,128]{1,0:T(8,128)}) custom-call(f32[1,27]{1,0:T(1,128)S(1)} %get-tuple-element.28.rates_ref, f32[27,2,8,128]{3,2,1,0:T(8,128)S(1)} %get-tuple-element.32.post_ref, ...), custom_call_target="tpu_custom_call" | custom-call | bytes 1022060 | tf_op jit(solution)/shard_map/pallas_call | solution.py:27
  30.6 2.6 %all-to-all-start.1 = ((f32[32,4,128]{2,1,0:T(4,128)}), f32[32,4,128]{2,1,0:T(4,128)S(1)}, u32[]{:S(2)}, u32[]{:S(2)}) async-start(f32[32,4,128]{2,1,0:T(4,128)} %bitcast.5), calls=%async_computation.1 | async-start | bytes 131072 | tf_op jit(solution)/shard_map/all_to_all | solution.py:464
  33.2 1.7 %collective-permute-start.6 = (f32[9,8,128]{2,1,0:T(8,128)S(1)}, f32[9,8,128]{2,1,0:T(8,128)S(1)}, u32[]{:S(2)}, u32[]{:S(2)}) collective-permute-start(f32[9,8,128]{2,1,0:T(8,128)S(1)} %get-tuple-element.45), channel_id=1, source_target_pairs={{0,8},{1,9},{2,10},{3,11},{4,12},{5,13},{6,14},{7,15},{8,0},{9,1},... | collective-permute-start | bytes 110600 | tf_op jit(solution)/shard_map/ppermute | solution.py:396
  35.0 0.0 collective-permute-start.7
  35.0 3.6 %collective-permute-start.8 = (f32[18,128]{1,0:T(8,128)S(1)}, f32[18,128]{1,0:T(8,128)S(1)}, u32[]{:S(2)}, u32[]{:S(2)}) collective-permute-start(f32[18,128]{1,0:T(8,128)S(1)} %get-tuple-element.47), channel_id=1, source_target_pairs={{0,7},{1,2},{2,1},{3,4},{4,3},{5,6},{6,5},{7,0},{8,15},{9,10},{10,... | collective-permute-start | bytes 27656 | tf_op jit(solution)/shard_map/ppermute | solution.py:407
  38.5 1.4 %collective-permute-done.8.outer_ref = f32[18,128]{1,0:T(8,128)S(1)} collective-permute-done((f32[18,128]{1,0:T(8,128)S(1)}, f32[18,128]{1,0:T(8,128)S(1)}, u32[]{:S(2)}, u32[]{:S(2)}) %collective-permute-start.8) | collective-permute-done | bytes 9248 | tf_op jit(solution)/shard_map/ppermute | solution.py:407
  39.9 0.0 collective-permute-done.9.inner_ref
  39.9 0.0 collective-permute-done.6.near_ref
  39.9 0.7 %all-to-all-done.1 = f32[32,4,128]{2,1,0:T(4,128)S(1)} async-done(((f32[32,4,128]{2,1,0:T(4,128)}), f32[32,4,128]{2,1,0:T(4,128)S(1)}, u32[]{:S(2)}, u32[]{:S(2)}) %all-to-all-start.1) | async-done | bytes 65568 | tf_op jit(solution)/shard_map/all_to_all | solution.py:464
  40.6 0.9 %shard_map.84 = (f32[27,2,8,128]{3,2,1,0:T(8,128)}, f32[3,512]{1,0:T(4,128)}) custom-call(f32[27,2,8,128]{3,2,1,0:T(8,128)S(1)} %get-tuple-element.44.post_ref, f32[9,8,128]{2,1,0:T(8,128)S(1)} %collective-permute-done.6.near_ref, f32[9,8,128]{2,1,0:T(8,128)S(1)} %collective-permute-done.7.far_ref, f32[18,128]{1,0:T(8,128)S(1)} %collective-permute-done.8.outer_ref, ...), custom_call_target="tpu_custom_call" | custom-call | bytes 737280 | tf_op jit(solution)/shard_map/pallas_call | solution.py:27
  (11 shorter events, 0.1 us)
Async XLA Ops:
  0.6 0.7 %copy-start.4 = (s32[512]{0:T(512)S(1)}, s32[512]{0:T(512)}, u32[]{:S(2)}) copy-start(s32[512]{0:T(512)} %param.11) | copy-start | bytes 6148
  0.6 0.9 %copy-start.1 = (bf16[512,128]{1,0:T(8,128)(2,1)S(1)}, bf16[512,128]{1,0:T(8,128)(2,1)}, u32[]{:S(2)}) copy-start(bf16[512,128]{1,0:T(8,128)(2,1)} %fraction_ref.1) | copy-start | bytes 393220
  0.7 0.7 %copy-start.3 = (bf16[3,512]{1,0:T(4,128)(2,1)S(1)}, bf16[3,512]{1,0:T(4,128)(2,1)}, u32[]{:S(2)}) copy-start(bf16[3,512]{1,0:T(4,128)(2,1)} %speed_ref.1) | copy-start | bytes 9220
  0.7 0.7 %copy-start.2 = (s32[512,1]{0,1:T(1,128)S(1)}, s32[512,1]{0,1:T(1,128)}, u32[]{:S(2)}) copy-start(s32[512,1]{0,1:T(1,128)} %param.10) | copy-start | bytes 6148
  0.7 0.7 %copy-start.5 = (f32[27]{0:T(128)S(1)}, f32[27]{0:T(128)}, u32[]{:S(2)}) copy-start(f32[27]{0:T(128)} %param.7) | copy-start | bytes 328
  2.1 18.2 %copy-start = (f32[27,2,8,128]{3,2,1,0:T(8,128)S(1)}, f32[27,2,8,128]{3,2,1,0:T(8,128)}, u32[]{:S(2)}) copy-start(f32[27,2,8,128]{3,2,1,0:T(8,128)} %fields_ref.1) | copy-start | bytes 663556
  20.7 5.0 %collective-permute-start = (f32[18,128]{1,0:T(8,128)S(1)}, f32[18,128]{1,0:T(8,128)S(1)}, u32[]{:S(2)}, u32[]{:S(2)}) collective-permute-start(f32[18,128]{1,0:T(8,128)S(1)} %get-tuple-element.33), channel_id=1, source_target_pairs={{0,7},{1,2},{2,1},{3,4},{4,3},{5,6},{6,5},{7,0},{8,15},{9,10},{10,... | collective-permute-start | bytes 27656 | tf_op jit(solution)/shard_map/ppermute | solution.py:407
  21.7 4.1 %collective-permute-start.1 = (f32[18,128]{1,0:T(8,128)S(1)}, f32[18,128]{1,0:T(8,128)S(1)}, u32[]{:S(2)}, u32[]{:S(2)}) collective-permute-start(f32[18,128]{1,0:T(8,128)S(1)} %get-tuple-element.34), channel_id=1, source_target_pairs={{0,1},{1,0},{2,3},{3,2},{4,5},{5,4},{6,7},{7,6},{8,9},{9,8},{10,11... | collective-permute-start | bytes 27656 | tf_op jit(solution)/shard_map/ppermute | solution.py:401
  21.7 7.8 %collective-permute-start.2 = (f32[9,8,128]{2,1,0:T(8,128)S(1)}, f32[9,8,128]{2,1,0:T(8,128)S(1)}, u32[]{:S(2)}, u32[]{:S(2)}) collective-permute-start(f32[9,8,128]{2,1,0:T(8,128)S(1)} %get-tuple-element.35), channel_id=1, source_target_pairs={{0,1},{1,0},{2,3},{3,2},{4,5},{5,4},{6,7},{7,6},{8,16},{9,17},{10,... | collective-permute-start | bytes 110600 | tf_op jit(solution)/shard_map/ppermute | solution.py:396
  22.2 7.3 %collective-permute-start.3 = (f32[9,8,128]{2,1,0:T(8,128)S(1)}, f32[9,8,128]{2,1,0:T(8,128)S(1)}, u32[]{:S(2)}, u32[]{:S(2)}) collective-permute-start(f32[9,8,128]{2,1,0:T(8,128)S(1)} %get-tuple-element.36), channel_id=1, source_target_pairs={{0,8},{1,9},{2,10},{3,11},{4,12},{5,13},{6,14},{7,15},{8,0},{9,1},... | collective-permute-start | bytes 110600 | tf_op jit(solution)/shard_map/ppermute | solution.py:396
  25.7 2.2 %collective-permute-start.4 = (f32[6,128]{1,0:T(8,128)S(1)}, f32[6,128]{1,0:T(8,128)S(1)}, u32[]{:S(2)}, u32[]{:S(2)}) collective-permute-start(f32[6,128]{1,0:T(8,128)S(1)} %get-tuple-element.37), channel_id=1, source_target_pairs={{0,1},{1,0},{2,3},{3,2},{4,5},{5,4},{6,7},{7,6},{8,16},{9,17},{10,... | collective-permute-start | bytes 9224 | tf_op jit(solution)/shard_map/ppermute | solution.py:396
  25.8 3.7 %collective-permute-start.5 = (f32[6,128]{1,0:T(8,128)S(1)}, f32[6,128]{1,0:T(8,128)S(1)}, u32[]{:S(2)}, u32[]{:S(2)}) collective-permute-start(f32[6,128]{1,0:T(8,128)S(1)} %get-tuple-element.38), channel_id=1, source_target_pairs={{0,8},{1,9},{2,10},{3,11},{4,12},{5,13},{6,14},{7,15},{8,0},{9,1},... | collective-permute-start | bytes 9224 | tf_op jit(solution)/shard_map/ppermute | solution.py:396
  30.6 10.0 %all-to-all-start.1 = ((f32[32,4,128]{2,1,0:T(4,128)}), f32[32,4,128]{2,1,0:T(4,128)S(1)}, u32[]{:S(2)}, u32[]{:S(2)}) async-start(f32[32,4,128]{2,1,0:T(4,128)} %bitcast.5), calls=%async_computation.1 | async-start | bytes 131072 | tf_op jit(solution)/shard_map/all_to_all | solution.py:464
  33.2 6.7 %collective-permute-start.6 = (f32[9,8,128]{2,1,0:T(8,128)S(1)}, f32[9,8,128]{2,1,0:T(8,128)S(1)}, u32[]{:S(2)}, u32[]{:S(2)}) collective-permute-start(f32[9,8,128]{2,1,0:T(8,128)S(1)} %get-tuple-element.45), channel_id=1, source_target_pairs={{0,8},{1,9},{2,10},{3,11},{4,12},{5,13},{6,14},{7,15},{8,0},{9,1},... | collective-permute-start | bytes 110600 | tf_op jit(solution)/shard_map/ppermute | solution.py:396
  35.0 5.0 %collective-permute-start.7 = (f32[9,8,128]{2,1,0:T(8,128)S(1)}, f32[9,8,128]{2,1,0:T(8,128)S(1)}, u32[]{:S(2)}, u32[]{:S(2)}) collective-permute-start(f32[9,8,128]{2,1,0:T(8,128)S(1)} %get-tuple-element.46), channel_id=1, source_target_pairs={{0,1},{1,0},{2,3},{3,2},{4,5},{5,4},{6,7},{7,6},{8,16},{9,17},{10,... | collective-permute-start | bytes 110600 | tf_op jit(solution)/shard_map/ppermute | solution.py:396
  35.0 5.0 %collective-permute-start.8 = (f32[18,128]{1,0:T(8,128)S(1)}, f32[18,128]{1,0:T(8,128)S(1)}, u32[]{:S(2)}, u32[]{:S(2)}) collective-permute-start(f32[18,128]{1,0:T(8,128)S(1)} %get-tuple-element.47), channel_id=1, source_target_pairs={{0,7},{1,2},{2,1},{3,4},{4,3},{5,6},{6,5},{7,0},{8,15},{9,10},{10,... | collective-permute-start | bytes 27656 | tf_op jit(solution)/shard_map/ppermute | solution.py:407
  38.5 1.4 %collective-permute-start.9 = (f32[18,128]{1,0:T(8,128)S(1)}, f32[18,128]{1,0:T(8,128)S(1)}, u32[]{:S(2)}, u32[]{:S(2)}) collective-permute-start(f32[18,128]{1,0:T(8,128)S(1)} %get-tuple-element.48), channel_id=1, source_target_pairs={{0,1},{1,0},{2,3},{3,2},{4,5},{5,4},{6,7},{7,6},{8,9},{9,8},{10,11... | collective-permute-start | bytes 27656 | tf_op jit(solution)/shard_map/ppermute | solution.py:401

commit v11 on v10

--- a/solution.py
+++ b/solution.py
@@ -363,21 +363,34 @@
         back_ref[pl.ds(4 * a, tiles, stride=4 * per_tile), :] = block
 
 
-def last_kernel(
-    capacity, post_ref, near_ref, far_ref, outer_ref, inner_ref, back_ref, hot_ref, at_rank_ref,
-    scaled_ref, force_ref,
-):
-    def corner(i):
-        cz, cx, cy = STEP[i]
-        return back_ref[pl.ds(4 * device_at(-cz, -cx) + 2 + cy, 1)]
-
+def scale_kernel(post_ref, near_ref, far_ref, outer_ref, inner_ref, staged_ref):
+    none = jnp.zeros((1, post_ref.shape[3]), f32)
     for z in range(post_ref.shape[1]):
-        fields = streamed(post_ref, outer_ref, inner_ref, far_ref, near_ref, z, corner)
+        fields = streamed(post_ref, outer_ref, inner_ref, far_ref, near_ref, z, lambda i: none)
         for i in range(27):
-            scaled_ref[i, z] = fields[i] * (1.0 / WEIGHT[i])
+            staged_ref[i, z] = fields[i] * (1.0 / WEIGHT[i])
+
+
+def last_kernel(capacity, staged_ref, back_ref, hot_ref, at_rank_ref, scaled_ref, force_ref):
+    depth, length, width = staged_ref.shape[1:]
+    for z in range(depth):
+        for i in range(27):
+            cz, cx, cy = STEP[i]
+            value = staged_ref[i, z]
+            if cx and not 0 <= z - cz < depth:
+                row = back_ref[pl.ds(4 * device_at(-cz, -cx) + 2 + cy, 1)] * (1.0 / WEIGHT[i])
+                row = pltpu.roll(row, cy % width, 1) if cy else row
+                wall = 0 if cz > 0 else lax.axis_size("gz") - 1
+                place = jnp.where(lax.axis_index("gz") == wall, -1, 0 if cx > 0 else length - 1)
+                value = jnp.where(iota(value.shape, 0) == place, row, value)
+            scaled_ref[i, z] = value
     back = back_ref[pl.ds(0, hot_ref.shape[0] // 2, stride=4), :]
-    parts = jnp.concatenate([part.astype(f32) for part in split2(back)], axis=0).T
-    picked = jnp.dot(parts.astype(bf16), hot_ref[...], preferred_element_type=f32)
+    picked = lax.dot_general(
+        jnp.concatenate(split2(back), axis=0),
+        hot_ref[...],
+        (((0,), (0,)), ((), ())),
+        preferred_element_type=f32,
+    )
     for k in range(3):
         mine = at_rank_ref[...] * picked[k * capacity : (k + 1) * capacity]
         force_ref[k : k + 1] = jnp.sum(mine, axis=0, keepdims=True)
@@ -467,10 +480,11 @@
     outer = swap_outer(outer)
     near, far = swap_faces(next_near, next_far)
     inner = swap_inner(inner)
+    (staged,) = call(scale_kernel, [state], post, near, far, outer, inner)
     scaled, grain_force = call(
         functools.partial(last_kernel, capacity),
         [state, shape((3, grains), f32)],
-        post, near, far, outer, inner, back, hot, at_rank,
+        staged, back, hot, at_rank,
     )
     return (scaled, grain_force)
 

time: 41.7 us -> 41.7 us (level)
    pallas_call x8 -> x9, Pallas kernels: 3.27 us -> 3.35 us  [call(): pl.pallas_call(kernel, out_shape=list(outs), in_specs=[pl.BlockSpec(memor...]
  transfers between devices with their start and end apart: 11 -> 11, of which waited for: 4 -> 4; matrix products, arithmetic and copies ran while one was open for 0% -> 0% of each run, Pallas kernels for 0% -> 1%
where the time goes in v11:
time: 41.7 us; the launch traced here: 41.4 us
  blocking collectives  18.2 us (44%)
  starting transfers between devices  12.9 us (31%)
  waiting for transfers between devices  5.54 us (13%)
  Pallas kernels  3.35 us (8%)
  between operations  0.77 us (2%)
  local copies, waits for them, and re-layouts  0.72 us (2%)
    all_to_all x1, blocking collectives, per_device(): lax.all_to_all(send.reshape(devices, capacity // 2 + 1, 2, width), both,...  18.2 us
    ppermute x6, starting transfers between devices, swap_faces(): received.append(lax.ppermute(face, ('gz', 'gx'), pairs))  5.81 us
    ppermute x2, starting transfers between devices, swap_outer(): return lax.ppermute(outer, 'gx', pairs)  4.48 us
    ppermute x2, waiting for transfers between devices, swap_outer(): return lax.ppermute(outer, 'gx', pairs)  3.43 us
    pallas_call x9, Pallas kernels, call(): pl.pallas_call(kernel, out_shape=list(outs), in_specs=[pl.BlockSpec(memor...  3.35 us
    all_to_all x1, starting transfers between devices, per_device(): lax.all_to_all(back.reshape(devices, 4, LANES), both, split_axis=0, conca...  2.57 us
    ppermute x6, waiting for transfers between devices, swap_faces(): received.append(lax.ppermute(face, ('gz', 'gx'), pairs))  1.55 us
  transfers between devices with their start and end apart: 11, of which 4 were waited for; matrix products, arithmetic and copies ran while one was open for 0% of the time, Pallas kernels for 1%

profile of v11, /device:TPU:0, one launch (start us, length us, event | category | flops | bytes accessed | tf_op | source)
XLA Modules:
  0.0 41.4 jit_solution(1494210249803957075)
XLA Ops:
  0.7 0.0 copy-start.3
  0.7 0.0 copy-start.2
  0.7 0.0 copy-start.5
  0.7 0.6 %copy-done.4 = s32[512]{0:T(512)S(1)} copy-done((s32[512]{0:T(512)S(1)}, s32[512]{0:T(512)}, u32[]{:S(2)}) %copy-start.4) | copy-done | bytes 2072
  1.3 0.1 copy-done.3
  1.4 0.0 copy-done.2
  1.4 0.2 shard_map.78
  1.6 0.5 %shard_map.79 = bf16[1088,128]{1,0:T(8,128)(2,1)S(1)} custom-call(s32[1,512]{1,0:T(1,128)S(1)} %bitcast.11, s32[1,512]{1,0:T(1,128)S(1)} %get-tuple-element.29.rank_ref, f32[4,512]{1,0:T(4,128)S(1)} %get-tuple-element.30.facts_ref, bf16[512,128]{1,0:T(8,128)(2,1)S(1)} %copy-done.1), custom_call_target="tpu_custom_call" | custom-call | bytes 421888 | tf_op jit(solution)/shard_map/pallas_call | solution.py:27
  2.1 0.0 copy-start
  2.1 18.2 %all_to_all.10 = bf16[32,17,2,128]{3,2,1,0:T(2,128)(2,1)S(1)} all-to-all(bf16[32,17,2,128]{3,2,1,0:T(2,128)(2,1)S(1)} %bitcast.8), channel_id=1, replica_groups=mesh['gz'=4,'gx'=8] {'gz','gx'}, dimensions={0} | all-to-all | bytes 557056 | tf_op jit(solution)/shard_map/all_to_all | solution.py:447
  20.3 0.4 %shard_map.80 = (f32[27,2,8,128]{3,2,1,0:T(8,128)S(1)}, f32[18,128]{1,0:T(8,128)S(1)}, f32[18,128]{1,0:T(8,128)S(1)}, f32[9,8,128]{2,1,0:T(8,128)S(1)}, f32[9,8,...) custom-call(bf16[1088,128]{1,0:T(8,128)(2,1)S(1)} %bitcast.7, ...), custom_call_target="tpu_custom_call" | custom-call | bytes 1169516 | tf_op jit(solution)/shard_map/pallas_call | solution.py:27
  20.7 0.9 %collective-permute-start = (f32[18,128]{1,0:T(8,128)S(1)}, f32[18,128]{1,0:T(8,128)S(1)}, u32[]{:S(2)}, u32[]{:S(2)}) collective-permute-start(f32[18,128]{1,0:T(8,128)S(1)} %get-tuple-element.33), channel_id=1, source_target_pairs={{0,7},{1,2},{2,1},{3,4},{4,3},{5,6},{6,5},{7,0},{8,15},{9,10},{10,... | collective-permute-start | bytes 27656 | tf_op jit(solution)/shard_map/ppermute | solution.py:420
  21.7 0.5 %collective-permute-start.2 = (f32[9,8,128]{2,1,0:T(8,128)S(1)}, f32[9,8,128]{2,1,0:T(8,128)S(1)}, u32[]{:S(2)}, u32[]{:S(2)}) collective-permute-start(f32[9,8,128]{2,1,0:T(8,128)S(1)} %get-tuple-element.35), channel_id=1, source_target_pairs={{0,1},{1,0},{2,3},{3,2},{4,5},{5,4},{6,7},{7,6},{8,16},{9,17},{10,... | collective-permute-start | bytes 110600 | tf_op jit(solution)/shard_map/ppermute | solution.py:409
  22.2 1.5 %collective-permute-start.3 = (f32[9,8,128]{2,1,0:T(8,128)S(1)}, f32[9,8,128]{2,1,0:T(8,128)S(1)}, u32[]{:S(2)}, u32[]{:S(2)}) collective-permute-start(f32[9,8,128]{2,1,0:T(8,128)S(1)} %get-tuple-element.36), channel_id=1, source_target_pairs={{0,8},{1,9},{2,10},{3,11},{4,12},{5,13},{6,14},{7,15},{8,0},{9,1},... | collective-permute-start | bytes 110600 | tf_op jit(solution)/shard_map/ppermute | solution.py:409
  23.7 2.0 %collective-permute-done.outer_ref = f32[18,128]{1,0:T(8,128)S(1)} collective-permute-done((f32[18,128]{1,0:T(8,128)S(1)}, f32[18,128]{1,0:T(8,128)S(1)}, u32[]{:S(2)}, u32[]{:S(2)}) %collective-permute-start) | collective-permute-done | bytes 9248 | tf_op jit(solution)/shard_map/ppermute | solution.py:420
  25.7 0.1 collective-permute-start.4
  25.8 2.0 %collective-permute-start.5 = (f32[6,128]{1,0:T(8,128)S(1)}, f32[6,128]{1,0:T(8,128)S(1)}, u32[]{:S(2)}, u32[]{:S(2)}) collective-permute-start(f32[6,128]{1,0:T(8,128)S(1)} %get-tuple-element.38), channel_id=1, source_target_pairs={{0,8},{1,9},{2,10},{3,11},{4,12},{5,13},{6,14},{7,15},{8,0},{9,1},... | collective-permute-start | bytes 9224 | tf_op jit(solution)/shard_map/ppermute | solution.py:409
  27.8 0.1 shard_map.82
  27.9 0.0 collective-permute-done.4.far_rows_ref
  27.9 1.5 %collective-permute-done.5.near_rows_ref = f32[6,128]{1,0:T(8,128)S(1)} collective-permute-done((f32[6,128]{1,0:T(8,128)S(1)}, f32[6,128]{1,0:T(8,128)S(1)}, u32[]{:S(2)}, u32[]{:S(2)}) %collective-permute-start.5) | collective-permute-done | bytes 3104 | tf_op jit(solution)/shard_map/ppermute | solution.py:409
  29.5 0.0 collective-permute-done.2.far_ref
  29.5 0.0 collective-permute-done.3.near_ref
  29.5 1.2 %shard_map.83 = (f32[27,2,8,128]{3,2,1,0:T(8,128)S(1)}, f32[9,8,128]{2,1,0:T(8,128)S(1)}, f32[9,8,128]{2,1,0:T(8,128)S(1)}, f32[18,128]{1,0:T(8,128)S(1)}, f32[18,128]{1,0:T(8,128)S(1)}, /*index=5*/f32[128,128]{1,0:T(8,128)}) custom-call(f32[1,27]{1,0:T(1,128)S(1)} %get-tuple-element.28.rates_ref, f32[27,2,8,128]{3,2,1,0:T(8,128)S(1)} %get-tuple-element.32.post_ref, ...), custom_call_target="tpu_custom_call" | custom-call | bytes 1022060 | tf_op jit(solution)/shard_map/pallas_call | solution.py:27
  30.7 2.6 %all-to-all-start.1 = ((f32[32,4,128]{2,1,0:T(4,128)}), f32[32,4,128]{2,1,0:T(4,128)S(1)}, u32[]{:S(2)}, u32[]{:S(2)}) async-start(f32[32,4,128]{2,1,0:T(4,128)} %bitcast.5), calls=%async_computation.1 | async-start | bytes 131072 | tf_op jit(solution)/shard_map/all_to_all | solution.py:477
  33.2 1.7 %collective-permute-start.6 = (f32[9,8,128]{2,1,0:T(8,128)S(1)}, f32[9,8,128]{2,1,0:T(8,128)S(1)}, u32[]{:S(2)}, u32[]{:S(2)}) collective-permute-start(f32[9,8,128]{2,1,0:T(8,128)S(1)} %get-tuple-element.45), channel_id=1, source_target_pairs={{0,8},{1,9},{2,10},{3,11},{4,12},{5,13},{6,14},{7,15},{8,0},{9,1},... | collective-permute-start | bytes 110600 | tf_op jit(solution)/shard_map/ppermute | solution.py:409
  35.0 0.0 collective-permute-start.7
  35.0 3.6 %collective-permute-start.8 = (f32[18,128]{1,0:T(8,128)S(1)}, f32[18,128]{1,0:T(8,128)S(1)}, u32[]{:S(2)}, u32[]{:S(2)}) collective-permute-start(f32[18,128]{1,0:T(8,128)S(1)} %get-tuple-element.47), channel_id=1, source_target_pairs={{0,7},{1,2},{2,1},{3,4},{4,3},{5,6},{6,5},{7,0},{8,15},{9,10},{10,... | collective-permute-start | bytes 27656 | tf_op jit(solution)/shard_map/ppermute | solution.py:420
  38.5 0.0 collective-permute-start.9
  38.5 1.4 %collective-permute-done.8.outer_ref = f32[18,128]{1,0:T(8,128)S(1)} collective-permute-done((f32[18,128]{1,0:T(8,128)S(1)}, f32[18,128]{1,0:T(8,128)S(1)}, u32[]{:S(2)}, u32[]{:S(2)}) %collective-permute-start.8) | collective-permute-done | bytes 9248 | tf_op jit(solution)/shard_map/ppermute | solution.py:420
  39.9 0.1 shard_map.84.staged_ref
  40.1 0.6 %all-to-all-done.1 = f32[32,4,128]{2,1,0:T(4,128)S(1)} async-done(((f32[32,4,128]{2,1,0:T(4,128)}), f32[32,4,128]{2,1,0:T(4,128)S(1)}, u32[]{:S(2)}, u32[]{:S(2)}) %all-to-all-start.1) | async-done | bytes 65568 | tf_op jit(solution)/shard_map/all_to_all | solution.py:477
  40.6 0.8 %shard_map.85 = (f32[27,2,8,128]{3,2,1,0:T(8,128)}, f32[3,512]{1,0:T(4,128)}) custom-call(f32[27,2,8,128]{3,2,1,0:T(8,128)S(1)} %shard_map.84.staged_ref, f32[128,128]{1,0:T(8,128)S(1)} %bitcast.9, bf16[64,512]{1,0:T(8,128)(2,1)S(1)} %get-tuple-element.50.hot_ref, f32[32,512]{1,0:T(8,128)S(1)} %get-tuple-element.51.at_rank_ref), custom_call_target="tpu_custom_call" | custom-call | bytes 645120 | tf_op jit(solution)/shard_map/pallas_call | solution.py:27
  (12 shorter events, 0.1 us)
Async XLA Ops:
  0.6 0.7 %copy-start.4 = (s32[512]{0:T(512)S(1)}, s32[512]{0:T(512)}, u32[]{:S(2)}) copy-start(s32[512]{0:T(512)} %param.11) | copy-start | bytes 6148
  0.6 0.9 %copy-start.1 = (bf16[512,128]{1,0:T(8,128)(2,1)S(1)}, bf16[512,128]{1,0:T(8,128)(2,1)}, u32[]{:S(2)}) copy-start(bf16[512,128]{1,0:T(8,128)(2,1)} %fraction_ref.1) | copy-start | bytes 393220
  0.7 0.7 %copy-start.3 = (bf16[3,512]{1,0:T(4,128)(2,1)S(1)}, bf16[3,512]{1,0:T(4,128)(2,1)}, u32[]{:S(2)}) copy-start(bf16[3,512]{1,0:T(4,128)(2,1)} %speed_ref.1) | copy-start | bytes 9220
  0.7 0.7 %copy-start.2 = (s32[512,1]{0,1:T(1,128)S(1)}, s32[512,1]{0,1:T(1,128)}, u32[]{:S(2)}) copy-start(s32[512,1]{0,1:T(1,128)} %param.10) | copy-start | bytes 6148
  0.7 0.7 %copy-start.5 = (f32[27]{0:T(128)S(1)}, f32[27]{0:T(128)}, u32[]{:S(2)}) copy-start(f32[27]{0:T(128)} %param.7) | copy-start | bytes 328
  2.1 18.2 %copy-start = (f32[27,2,8,128]{3,2,1,0:T(8,128)S(1)}, f32[27,2,8,128]{3,2,1,0:T(8,128)}, u32[]{:S(2)}) copy-start(f32[27,2,8,128]{3,2,1,0:T(8,128)} %fields_ref.1) | copy-start | bytes 663556
  20.7 5.0 %collective-permute-start = (f32[18,128]{1,0:T(8,128)S(1)}, f32[18,128]{1,0:T(8,128)S(1)}, u32[]{:S(2)}, u32[]{:S(2)}) collective-permute-start(f32[18,128]{1,0:T(8,128)S(1)} %get-tuple-element.33), channel_id=1, source_target_pairs={{0,7},{1,2},{2,1},{3,4},{4,3},{5,6},{6,5},{7,0},{8,15},{9,10},{10,... | collective-permute-start | bytes 27656 | tf_op jit(solution)/shard_map/ppermute | solution.py:420
  21.7 4.1 %collective-permute-start.1 = (f32[18,128]{1,0:T(8,128)S(1)}, f32[18,128]{1,0:T(8,128)S(1)}, u32[]{:S(2)}, u32[]{:S(2)}) collective-permute-start(f32[18,128]{1,0:T(8,128)S(1)} %get-tuple-element.34), channel_id=1, source_target_pairs={{0,1},{1,0},{2,3},{3,2},{4,5},{5,4},{6,7},{7,6},{8,9},{9,8},{10,11... | collective-permute-start | bytes 27656 | tf_op jit(solution)/shard_map/ppermute | solution.py:414
  21.7 7.8 %collective-permute-start.2 = (f32[9,8,128]{2,1,0:T(8,128)S(1)}, f32[9,8,128]{2,1,0:T(8,128)S(1)}, u32[]{:S(2)}, u32[]{:S(2)}) collective-permute-start(f32[9,8,128]{2,1,0:T(8,128)S(1)} %get-tuple-element.35), channel_id=1, source_target_pairs={{0,1},{1,0},{2,3},{3,2},{4,5},{5,4},{6,7},{7,6},{8,16},{9,17},{10,... | collective-permute-start | bytes 110600 | tf_op jit(solution)/shard_map/ppermute | solution.py:409
  22.2 7.3 %collective-permute-start.3 = (f32[9,8,128]{2,1,0:T(8,128)S(1)}, f32[9,8,128]{2,1,0:T(8,128)S(1)}, u32[]{:S(2)}, u32[]{:S(2)}) collective-permute-start(f32[9,8,128]{2,1,0:T(8,128)S(1)} %get-tuple-element.36), channel_id=1, source_target_pairs={{0,8},{1,9},{2,10},{3,11},{4,12},{5,13},{6,14},{7,15},{8,0},{9,1},... | collective-permute-start | bytes 110600 | tf_op jit(solution)/shard_map/ppermute | solution.py:409
  25.7 2.2 %collective-permute-start.4 = (f32[6,128]{1,0:T(8,128)S(1)}, f32[6,128]{1,0:T(8,128)S(1)}, u32[]{:S(2)}, u32[]{:S(2)}) collective-permute-start(f32[6,128]{1,0:T(8,128)S(1)} %get-tuple-element.37), channel_id=1, source_target_pairs={{0,1},{1,0},{2,3},{3,2},{4,5},{5,4},{6,7},{7,6},{8,16},{9,17},{10,... | collective-permute-start | bytes 9224 | tf_op jit(solution)/shard_map/ppermute | solution.py:409
  25.8 3.7 %collective-permute-start.5 = (f32[6,128]{1,0:T(8,128)S(1)}, f32[6,128]{1,0:T(8,128)S(1)}, u32[]{:S(2)}, u32[]{:S(2)}) collective-permute-start(f32[6,128]{1,0:T(8,128)S(1)} %get-tuple-element.38), channel_id=1, source_target_pairs={{0,8},{1,9},{2,10},{3,11},{4,12},{5,13},{6,14},{7,15},{8,0},{9,1},... | collective-permute-start | bytes 9224 | tf_op jit(solution)/shard_map/ppermute | solution.py:409
  30.7 10.0 %all-to-all-start.1 = ((f32[32,4,128]{2,1,0:T(4,128)}), f32[32,4,128]{2,1,0:T(4,128)S(1)}, u32[]{:S(2)}, u32[]{:S(2)}) async-start(f32[32,4,128]{2,1,0:T(4,128)} %bitcast.5), calls=%async_computation.1 | async-start | bytes 131072 | tf_op jit(solution)/shard_map/all_to_all | solution.py:477
  33.2 6.7 %collective-permute-start.6 = (f32[9,8,128]{2,1,0:T(8,128)S(1)}, f32[9,8,128]{2,1,0:T(8,128)S(1)}, u32[]{:S(2)}, u32[]{:S(2)}) collective-permute-start(f32[9,8,128]{2,1,0:T(8,128)S(1)} %get-tuple-element.45), channel_id=1, source_target_pairs={{0,8},{1,9},{2,10},{3,11},{4,12},{5,13},{6,14},{7,15},{8,0},{9,1},... | collective-permute-start | bytes 110600 | tf_op jit(solution)/shard_map/ppermute | solution.py:409
  35.0 5.0 %collective-permute-start.7 = (f32[9,8,128]{2,1,0:T(8,128)S(1)}, f32[9,8,128]{2,1,0:T(8,128)S(1)}, u32[]{:S(2)}, u32[]{:S(2)}) collective-permute-start(f32[9,8,128]{2,1,0:T(8,128)S(1)} %get-tuple-element.46), channel_id=1, source_target_pairs={{0,1},{1,0},{2,3},{3,2},{4,5},{5,4},{6,7},{7,6},{8,16},{9,17},{10,... | collective-permute-start | bytes 110600 | tf_op jit(solution)/shard_map/ppermute | solution.py:409
  35.0 5.0 %collective-permute-start.8 = (f32[18,128]{1,0:T(8,128)S(1)}, f32[18,128]{1,0:T(8,128)S(1)}, u32[]{:S(2)}, u32[]{:S(2)}) collective-permute-start(f32[18,128]{1,0:T(8,128)S(1)} %get-tuple-element.47), channel_id=1, source_target_pairs={{0,7},{1,2},{2,1},{3,4},{4,3},{5,6},{6,5},{7,0},{8,15},{9,10},{10,... | collective-permute-start | bytes 27656 | tf_op jit(solution)/shard_map/ppermute | solution.py:420
  38.5 1.4 %collective-permute-start.9 = (f32[18,128]{1,0:T(8,128)S(1)}, f32[18,128]{1,0:T(8,128)S(1)}, u32[]{:S(2)}, u32[]{:S(2)}) collective-permute-start(f32[18,128]{1,0:T(8,128)S(1)} %get-tuple-element.48), channel_id=1, source_target_pairs={{0,1},{1,0},{2,3},{3,2},{4,5},{5,4},{6,7},{7,6},{8,9},{9,8},{10,11... | collective-permute-start | bytes 27656 | tf_op jit(solution)/shard_map/ppermute | solution.py:414

commit v12 on v11

--- a/solution.py
+++ b/solution.py
@@ -47,10 +47,9 @@
     return high, (x - high.astype(f32)).astype(bf16)
 
 
-def tables_kernel(capacity, earlier_ref, spread_ref):
+def tables_kernel(earlier_ref):
     row, column = iota(earlier_ref.shape, 0), iota(earlier_ref.shape, 1)
     earlier_ref[...] = jnp.where(row < column, 1.0, 0.0).astype(bf16)
-    spread_ref[...] = jnp.where(row % capacity == column % capacity, 1.0, 0.0).astype(bf16)
 
 
 def ranks(hot, earlier):
@@ -70,20 +69,25 @@
 ):
     hot = jnp.where(iota((devices, dest_ref.shape[1]), 0) == dest_ref[...], 1.0, 0.0)
     rank_ref[...] = ranks(hot, earlier_ref[...]).astype(i32)
-    facts_ref[0:3] = speed_ref[...].astype(f32)
-    facts_ref[3:4] = line_ref[...].astype(f32)
+    shared = facts_ref.shape[0]
+    place = device_at(0, 0) % shared
+    speed = speed_ref[...].astype(f32)
+    values = [speed[0:1], speed[1:2], speed[2:3], line_ref[...].astype(f32)]
+    for group in range(shared):
+        row = jnp.zeros(values[3].shape, f32)
+        for m, value in enumerate(values):
+            row = jnp.where(place == (group - m) % shared, value, row)
+        facts_ref[group : group + 1] = row
     rates_out_ref[...] = rates_ref[...]
 
 
 def pack_kernel(devices, capacity, dest_ref, rank_ref, facts_ref, fraction_ref, send_ref, rows_ref):
     grains, width = fraction_ref.shape
     dest, rank = dest_ref[...], rank_ref[...]
-    place = jnp.where(iota((rows_ref.shape[0], grains), 0) == dest * (capacity + 2) + rank, 1.0, 0.0)
-    rows_ref[...] = jnp.dot(place.astype(bf16), fraction_ref[...], preferred_element_type=f32)
+    chosen = jnp.where(iota((rows_ref.shape[0], grains), 0) == dest * (capacity + 2) + rank, 1.0, 0.0)
+    rows_ref[...] = jnp.dot(chosen.astype(bf16), fraction_ref[...], preferred_element_type=f32)
     at_rank = iota((capacity, grains), 0) == rank
-    facts = [jnp.where(at_rank, facts_ref[m : m + 1], 0.0) for m in range(4)]
-    if 4 * capacity < width:
-        facts.append(jnp.zeros((width - 4 * capacity, grains), f32))
+    facts = [jnp.where(at_rank, facts_ref[m : m + 1], 0.0) for m in range(facts_ref.shape[0])]
     rows_ref[pl.ds(capacity, devices, stride=capacity + 2), :] = lax.dot_general(
         jnp.where(iota((devices, grains), 0) == dest, 1.0, 0.0).astype(bf16),
         jnp.concatenate(facts, axis=0).astype(bf16),
@@ -211,7 +215,7 @@
 
 
 def first_kernel(
-    devices, capacity, recv_ref, fields_ref, rates_ref, spread_ref,
+    devices, capacity, recv_ref, fields_ref, rates_ref,
     post_ref, outer_ref, inner_ref, far_ref, near_ref, push_ref, held_ref, line_ref, slot_ref, wide_ref,
 ):
     width = recv_ref.shape[1]
@@ -227,19 +231,10 @@
     tiles, shared = slots // LANES, LANES // capacity
     group = iota((tiles, width), 1) // capacity
     rows = [wide_ref[pl.ds(capacity + a * block, tiles, stride=shared * block), :] for a in range(shared)]
-    picked = jnp.concatenate([jnp.where(group == m, row, 0.0) for m in range(4) for row in rows], axis=0)
-    placed = jnp.dot(picked.astype(bf16), spread_ref[...], preferred_element_type=f32)
     fact = []
     for m in range(4):
-        first = m * shared * tiles
-        fact.append(
-            total_of(
-                [
-                    jnp.where(group == a, placed[first + a * tiles : first + (a + 1) * tiles], 0.0)
-                    for a in range(shared)
-                ]
-            )
-        )
+        mixed = total_of([jnp.where(group == (a + m) % shared, rows[a], 0.0) for a in range(shared)])
+        fact.append(pltpu.roll(mixed, LANES - m * capacity, 1) if m else mixed)
     line_ref[...] = fact[3].astype(i32)
     gather = []
     for t in range(tiles):
@@ -430,12 +425,10 @@
     shape, both = jax.ShapeDtypeStruct, ("gz", "gx")
     dest, line = grain_dest.reshape(1, grains), grain_line.reshape(1, grains)
     rows = devices * (capacity + 2)
-    earlier, spread = call(
-        functools.partial(tables_kernel, capacity), [shape((LANES, LANES), bf16)] * 2, flops=10**9
-    )
+    (earlier,) = call(tables_kernel, [shape((LANES, LANES), bf16)], flops=10**9)
     rank, facts, rates = call(
         functools.partial(rank_kernel, devices),
-        [shape((1, grains), i32), shape((4, grains), f32), shape((1, 27), f32)],
+        [shape((1, grains), i32), shape((LANES // capacity, grains), f32), shape((1, 27), f32)],
         dest, line, grain_velocity, rates.reshape(1, 27), earlier,
     )
     (send,) = call(
@@ -455,7 +448,7 @@
             state, ends, ends, face, face, shape((3, depth, length, width), f32),
             shape((4 * lines, width), f32), shape((slots // LANES, LANES), i32), shape((slots, width), bf16),
         ],
-        recv, populations, rates, spread, scratch=[pltpu.VMEM((rows, width), f32)],
+        recv, populations, rates, scratch=[pltpu.VMEM((rows, width), f32)],
     )
     outer, inner = swap_outer(outer), swap_inner(inner)
     near, far = swap_faces(near, far)

time: 41.7 us -> 41.6 us (level)
  no operation moved by 1% of the time
where the time goes in v12:
time: 41.6 us; the launch traced here: 41.4 us
  blocking collectives  18.2 us (44%)
  starting transfers between devices  12.9 us (31%)
  waiting for transfers between devices  5.54 us (13%)
  Pallas kernels  3.28 us (8%)
  between operations  0.77 us (2%)
  local copies, waits for them, and re-layouts  0.73 us (2%)
    all_to_all x1, blocking collectives, per_device(): lax.all_to_all(send.reshape(devices, capacity // 2 + 1, 2, width), both,...  18.2 us
    ppermute x6, starting transfers between devices, swap_faces(): received.append(lax.ppermute(face, ('gz', 'gx'), pairs))  5.81 us
    ppermute x2, starting transfers between devices, swap_outer(): return lax.ppermute(outer, 'gx', pairs)  4.48 us
    ppermute x2, waiting for transfers between devices, swap_outer(): return lax.ppermute(outer, 'gx', pairs)  3.43 us
    pallas_call x9, Pallas kernels, call(): pl.pallas_call(kernel, out_shape=list(outs), in_specs=[pl.BlockSpec(memor...  3.28 us
    all_to_all x1, starting transfers between devices, per_device(): lax.all_to_all(back.reshape(devices, 4, LANES), both, split_axis=0, conca...  2.57 us
    ppermute x6, waiting for transfers between devices, swap_faces(): received.append(lax.ppermute(face, ('gz', 'gx'), pairs))  1.55 us
  transfers between devices with their start and end apart: 11, of which 4 were waited for; matrix products, arithmetic and copies ran while one was open for 0% of the time, Pallas kernels for 1%

profile of v12, /device:TPU:0, one launch (start us, length us, event | category | flops | bytes accessed | tf_op | source)
XLA Modules:
  0.0 41.4 jit_solution(12054639700991852508)
XLA Ops:
  0.7 0.0 copy-start.4
  0.7 0.0 copy-start.2
  0.7 0.0 copy-start.5
  0.7 0.6 %copy-done.3 = bf16[3,512]{1,0:T(4,128)(2,1)S(1)} copy-done((bf16[3,512]{1,0:T(4,128)(2,1)S(1)}, bf16[3,512]{1,0:T(4,128)(2,1)}, u32[]{:S(2)}) %copy-start.3) | copy-done | bytes 3096
  1.3 0.1 copy-done.4
  1.4 0.0 copy-done.2
  1.4 0.2 shard_map.78
  1.6 0.5 %shard_map.79 = bf16[1088,128]{1,0:T(8,128)(2,1)S(1)} custom-call(s32[1,512]{1,0:T(1,128)S(1)} %bitcast.11, s32[1,512]{1,0:T(1,128)S(1)} %get-tuple-element.26.rank_ref, f32[4,512]{1,0:T(4,128)S(1)} %get-tuple-element.27.facts_ref, bf16[512,128]{1,0:T(8,128)(2,1)S(1)} %copy-done.1), custom_call_target="tpu_custom_call" | custom-call | bytes 421888 | tf_op jit(solution)/shard_map/pallas_call | solution.py:27
  2.1 0.0 copy-start
  2.1 18.2 %all_to_all.10 = bf16[32,17,2,128]{3,2,1,0:T(2,128)(2,1)S(1)} all-to-all(bf16[32,17,2,128]{3,2,1,0:T(2,128)(2,1)S(1)} %bitcast.8), channel_id=1, replica_groups=mesh['gz'=4,'gx'=8] {'gz','gx'}, dimensions={0} | all-to-all | bytes 557056 | tf_op jit(solution)/shard_map/all_to_all | solution.py:440
  20.3 0.4 shard_map.80
  20.7 0.9 %collective-permute-start = (f32[18,128]{1,0:T(8,128)S(1)}, f32[18,128]{1,0:T(8,128)S(1)}, u32[]{:S(2)}, u32[]{:S(2)}) collective-permute-start(f32[18,128]{1,0:T(8,128)S(1)} %get-tuple-element.29), channel_id=1, source_target_pairs={{0,7},{1,2},{2,1},{3,4},{4,3},{5,6},{6,5},{7,0},{8,15},{9,10},{10,... | collective-permute-start | bytes 27656 | tf_op jit(solution)/shard_map/ppermute | solution.py:415
  21.6 0.0 collective-permute-start.1
  21.6 0.5 %collective-permute-start.2 = (f32[9,8,128]{2,1,0:T(8,128)S(1)}, f32[9,8,128]{2,1,0:T(8,128)S(1)}, u32[]{:S(2)}, u32[]{:S(2)}) collective-permute-start(f32[9,8,128]{2,1,0:T(8,128)S(1)} %get-tuple-element.31), channel_id=1, source_target_pairs={{0,1},{1,0},{2,3},{3,2},{4,5},{5,4},{6,7},{7,6},{8,16},{9,17},{10,... | collective-permute-start | bytes 110600 | tf_op jit(solution)/shard_map/ppermute | solution.py:404
  22.1 1.5 %collective-permute-start.3 = (f32[9,8,128]{2,1,0:T(8,128)S(1)}, f32[9,8,128]{2,1,0:T(8,128)S(1)}, u32[]{:S(2)}, u32[]{:S(2)}) collective-permute-start(f32[9,8,128]{2,1,0:T(8,128)S(1)} %get-tuple-element.32), channel_id=1, source_target_pairs={{0,8},{1,9},{2,10},{3,11},{4,12},{5,13},{6,14},{7,15},{8,0},{9,1},... | collective-permute-start | bytes 110600 | tf_op jit(solution)/shard_map/ppermute | solution.py:404
  23.6 2.0 %collective-permute-done.outer_ref = f32[18,128]{1,0:T(8,128)S(1)} collective-permute-done((f32[18,128]{1,0:T(8,128)S(1)}, f32[18,128]{1,0:T(8,128)S(1)}, u32[]{:S(2)}, u32[]{:S(2)}) %collective-permute-start) | collective-permute-done | bytes 9248 | tf_op jit(solution)/shard_map/ppermute | solution.py:415
  25.6 0.0 collective-permute-done.1.inner_ref
  25.7 0.1 collective-permute-start.4
  25.7 2.0 %collective-permute-start.5 = (f32[6,128]{1,0:T(8,128)S(1)}, f32[6,128]{1,0:T(8,128)S(1)}, u32[]{:S(2)}, u32[]{:S(2)}) collective-permute-start(f32[6,128]{1,0:T(8,128)S(1)} %get-tuple-element.34), channel_id=1, source_target_pairs={{0,8},{1,9},{2,10},{3,11},{4,12},{5,13},{6,14},{7,15},{8,0},{9,1},... | collective-permute-start | bytes 9224 | tf_op jit(solution)/shard_map/ppermute | solution.py:404
  27.7 0.1 shard_map.82
  27.9 1.5 %collective-permute-done.5.near_rows_ref = f32[6,128]{1,0:T(8,128)S(1)} collective-permute-done((f32[6,128]{1,0:T(8,128)S(1)}, f32[6,128]{1,0:T(8,128)S(1)}, u32[]{:S(2)}, u32[]{:S(2)}) %collective-permute-start.5) | collective-permute-done | bytes 3104 | tf_op jit(solution)/shard_map/ppermute | solution.py:404
  29.4 1.2 %shard_map.83 = (f32[27,2,8,128]{3,2,1,0:T(8,128)S(1)}, f32[9,8,128]{2,1,0:T(8,128)S(1)}, f32[9,8,128]{2,1,0:T(8,128)S(1)}, f32[18,128]{1,0:T(8,128)S(1)}, f32[18,128]{1,0:T(8,128)S(1)}, /*index=5*/f32[128,128]{1,0:T(8,128)}) custom-call(f32[1,27]{1,0:T(1,128)S(1)} %get-tuple-element.25.rates_ref, f32[27,2,8,128]{3,2,1,0:T(8,128)S(1)} %get-tuple-element.28.post_ref, ...), custom_call_target="tpu_custom_call" | custom-call | bytes 1022060 | tf_op jit(solution)/shard_map/pallas_call | solution.py:27
  30.6 2.6 %all-to-all-start.1 = ((f32[32,4,128]{2,1,0:T(4,128)}), f32[32,4,128]{2,1,0:T(4,128)S(1)}, u32[]{:S(2)}, u32[]{:S(2)}) async-start(f32[32,4,128]{2,1,0:T(4,128)} %bitcast.5), calls=%async_computation.1 | async-start | bytes 131072 | tf_op jit(solution)/shard_map/all_to_all | solution.py:470
  33.2 1.7 %collective-permute-start.6 = (f32[9,8,128]{2,1,0:T(8,128)S(1)}, f32[9,8,128]{2,1,0:T(8,128)S(1)}, u32[]{:S(2)}, u32[]{:S(2)}) collective-permute-start(f32[9,8,128]{2,1,0:T(8,128)S(1)} %get-tuple-element.41), channel_id=1, source_target_pairs={{0,8},{1,9},{2,10},{3,11},{4,12},{5,13},{6,14},{7,15},{8,0},{9,1},... | collective-permute-start | bytes 110600 | tf_op jit(solution)/shard_map/ppermute | solution.py:404
  34.9 0.0 collective-permute-start.7
  34.9 3.5 %collective-permute-start.8 = (f32[18,128]{1,0:T(8,128)S(1)}, f32[18,128]{1,0:T(8,128)S(1)}, u32[]{:S(2)}, u32[]{:S(2)}) collective-permute-start(f32[18,128]{1,0:T(8,128)S(1)} %get-tuple-element.43), channel_id=1, source_target_pairs={{0,7},{1,2},{2,1},{3,4},{4,3},{5,6},{6,5},{7,0},{8,15},{9,10},{10,... | collective-permute-start | bytes 27656 | tf_op jit(solution)/shard_map/ppermute | solution.py:415
  38.4 1.4 %collective-permute-done.8.outer_ref = f32[18,128]{1,0:T(8,128)S(1)} collective-permute-done((f32[18,128]{1,0:T(8,128)S(1)}, f32[18,128]{1,0:T(8,128)S(1)}, u32[]{:S(2)}, u32[]{:S(2)}) %collective-permute-start.8) | collective-permute-done | bytes 9248 | tf_op jit(solution)/shard_map/ppermute | solution.py:415
  39.9 0.0 collective-permute-done.9.inner_ref
  39.9 0.0 collective-permute-done.6.near_ref
  39.9 0.1 shard_map.84.staged_ref
  40.0 0.6 %all-to-all-done.1 = f32[32,4,128]{2,1,0:T(4,128)S(1)} async-done(((f32[32,4,128]{2,1,0:T(4,128)}), f32[32,4,128]{2,1,0:T(4,128)S(1)}, u32[]{:S(2)}, u32[]{:S(2)}) %all-to-all-start.1) | async-done | bytes 65568 | tf_op jit(solution)/shard_map/all_to_all | solution.py:470
  40.6 0.8 %shard_map.85 = (f32[27,2,8,128]{3,2,1,0:T(8,128)}, f32[3,512]{1,0:T(4,128)}) custom-call(f32[27,2,8,128]{3,2,1,0:T(8,128)S(1)} %shard_map.84.staged_ref, f32[128,128]{1,0:T(8,128)S(1)} %bitcast.9, bf16[64,512]{1,0:T(8,128)(2,1)S(1)} %get-tuple-element.46.hot_ref, f32[32,512]{1,0:T(8,128)S(1)} %get-tuple-element.47.at_rank_ref), custom_call_target="tpu_custom_call" | custom-call | bytes 645120 | tf_op jit(solution)/shard_map/pallas_call | solution.py:27
  (12 shorter events, 0.0 us)
Async XLA Ops:
  0.6 0.7 %copy-start.3 = (bf16[3,512]{1,0:T(4,128)(2,1)S(1)}, bf16[3,512]{1,0:T(4,128)(2,1)}, u32[]{:S(2)}) copy-start(bf16[3,512]{1,0:T(4,128)(2,1)} %speed_ref.1) | copy-start | bytes 9220
  0.6 0.9 %copy-start.1 = (bf16[512,128]{1,0:T(8,128)(2,1)S(1)}, bf16[512,128]{1,0:T(8,128)(2,1)}, u32[]{:S(2)}) copy-start(bf16[512,128]{1,0:T(8,128)(2,1)} %fraction_ref.1) | copy-start | bytes 393220
  0.7 0.7 %copy-start.4 = (s32[512]{0:T(512)S(1)}, s32[512]{0:T(512)}, u32[]{:S(2)}) copy-start(s32[512]{0:T(512)} %param.11) | copy-start | bytes 6148
  0.7 0.7 %copy-start.2 = (s32[512,1]{0,1:T(1,128)S(1)}, s32[512,1]{0,1:T(1,128)}, u32[]{:S(2)}) copy-start(s32[512,1]{0,1:T(1,128)} %param.10) | copy-start | bytes 6148
  0.7 0.7 %copy-start.5 = (f32[27]{0:T(128)S(1)}, f32[27]{0:T(128)}, u32[]{:S(2)}) copy-start(f32[27]{0:T(128)} %param.7) | copy-start | bytes 328
  2.1 18.2 %copy-start = (f32[27,2,8,128]{3,2,1,0:T(8,128)S(1)}, f32[27,2,8,128]{3,2,1,0:T(8,128)}, u32[]{:S(2)}) copy-start(f32[27,2,8,128]{3,2,1,0:T(8,128)} %fields_ref.1) | copy-start | bytes 663556
  20.7 5.0 %collective-permute-start = (f32[18,128]{1,0:T(8,128)S(1)}, f32[18,128]{1,0:T(8,128)S(1)}, u32[]{:S(2)}, u32[]{:S(2)}) collective-permute-start(f32[18,128]{1,0:T(8,128)S(1)} %get-tuple-element.29), channel_id=1, source_target_pairs={{0,7},{1,2},{2,1},{3,4},{4,3},{5,6},{6,5},{7,0},{8,15},{9,10},{10,... | collective-permute-start | bytes 27656 | tf_op jit(solution)/shard_map/ppermute | solution.py:415
  21.6 4.1 %collective-permute-start.1 = (f32[18,128]{1,0:T(8,128)S(1)}, f32[18,128]{1,0:T(8,128)S(1)}, u32[]{:S(2)}, u32[]{:S(2)}) collective-permute-start(f32[18,128]{1,0:T(8,128)S(1)} %get-tuple-element.30), channel_id=1, source_target_pairs={{0,1},{1,0},{2,3},{3,2},{4,5},{5,4},{6,7},{7,6},{8,9},{9,8},{10,11... | collective-permute-start | bytes 27656 | tf_op jit(solution)/shard_map/ppermute | solution.py:409
  21.6 7.8 %collective-permute-start.2 = (f32[9,8,128]{2,1,0:T(8,128)S(1)}, f32[9,8,128]{2,1,0:T(8,128)S(1)}, u32[]{:S(2)}, u32[]{:S(2)}) collective-permute-start(f32[9,8,128]{2,1,0:T(8,128)S(1)} %get-tuple-element.31), channel_id=1, source_target_pairs={{0,1},{1,0},{2,3},{3,2},{4,5},{5,4},{6,7},{7,6},{8,16},{9,17},{10,... | collective-permute-start | bytes 110600 | tf_op jit(solution)/shard_map/ppermute | solution.py:404
  22.1 7.3 %collective-permute-start.3 = (f32[9,8,128]{2,1,0:T(8,128)S(1)}, f32[9,8,128]{2,1,0:T(8,128)S(1)}, u32[]{:S(2)}, u32[]{:S(2)}) collective-permute-start(f32[9,8,128]{2,1,0:T(8,128)S(1)} %get-tuple-element.32), channel_id=1, source_target_pairs={{0,8},{1,9},{2,10},{3,11},{4,12},{5,13},{6,14},{7,15},{8,0},{9,1},... | collective-permute-start | bytes 110600 | tf_op jit(solution)/shard_map/ppermute | solution.py:404
  25.7 2.2 %collective-permute-start.4 = (f32[6,128]{1,0:T(8,128)S(1)}, f32[6,128]{1,0:T(8,128)S(1)}, u32[]{:S(2)}, u32[]{:S(2)}) collective-permute-start(f32[6,128]{1,0:T(8,128)S(1)} %get-tuple-element.33), channel_id=1, source_target_pairs={{0,1},{1,0},{2,3},{3,2},{4,5},{5,4},{6,7},{7,6},{8,16},{9,17},{10,... | collective-permute-start | bytes 9224 | tf_op jit(solution)/shard_map/ppermute | solution.py:404
  25.7 3.7 %collective-permute-start.5 = (f32[6,128]{1,0:T(8,128)S(1)}, f32[6,128]{1,0:T(8,128)S(1)}, u32[]{:S(2)}, u32[]{:S(2)}) collective-permute-start(f32[6,128]{1,0:T(8,128)S(1)} %get-tuple-element.34), channel_id=1, source_target_pairs={{0,8},{1,9},{2,10},{3,11},{4,12},{5,13},{6,14},{7,15},{8,0},{9,1},... | collective-permute-start | bytes 9224 | tf_op jit(solution)/shard_map/ppermute | solution.py:404
  30.6 10.0 %all-to-all-start.1 = ((f32[32,4,128]{2,1,0:T(4,128)}), f32[32,4,128]{2,1,0:T(4,128)S(1)}, u32[]{:S(2)}, u32[]{:S(2)}) async-start(f32[32,4,128]{2,1,0:T(4,128)} %bitcast.5), calls=%async_computation.1 | async-start | bytes 131072 | tf_op jit(solution)/shard_map/all_to_all | solution.py:470
  33.2 6.7 %collective-permute-start.6 = (f32[9,8,128]{2,1,0:T(8,128)S(1)}, f32[9,8,128]{2,1,0:T(8,128)S(1)}, u32[]{:S(2)}, u32[]{:S(2)}) collective-permute-start(f32[9,8,128]{2,1,0:T(8,128)S(1)} %get-tuple-element.41), channel_id=1, source_target_pairs={{0,8},{1,9},{2,10},{3,11},{4,12},{5,13},{6,14},{7,15},{8,0},{9,1},... | collective-permute-start | bytes 110600 | tf_op jit(solution)/shard_map/ppermute | solution.py:404
  34.9 5.0 %collective-permute-start.7 = (f32[9,8,128]{2,1,0:T(8,128)S(1)}, f32[9,8,128]{2,1,0:T(8,128)S(1)}, u32[]{:S(2)}, u32[]{:S(2)}) collective-permute-start(f32[9,8,128]{2,1,0:T(8,128)S(1)} %get-tuple-element.42), channel_id=1, source_target_pairs={{0,1},{1,0},{2,3},{3,2},{4,5},{5,4},{6,7},{7,6},{8,16},{9,17},{10,... | collective-permute-start | bytes 110600 | tf_op jit(solution)/shard_map/ppermute | solution.py:404
  34.9 5.0 %collective-permute-start.8 = (f32[18,128]{1,0:T(8,128)S(1)}, f32[18,128]{1,0:T(8,128)S(1)}, u32[]{:S(2)}, u32[]{:S(2)}) collective-permute-start(f32[18,128]{1,0:T(8,128)S(1)} %get-tuple-element.43), channel_id=1, source_target_pairs={{0,7},{1,2},{2,1},{3,4},{4,3},{5,6},{6,5},{7,0},{8,15},{9,10},{10,... | collective-permute-start | bytes 27656 | tf_op jit(solution)/shard_map/ppermute | solution.py:415
  38.4 1.4 %collective-permute-start.9 = (f32[18,128]{1,0:T(8,128)S(1)}, f32[18,128]{1,0:T(8,128)S(1)}, u32[]{:S(2)}, u32[]{:S(2)}) collective-permute-start(f32[18,128]{1,0:T(8,128)S(1)} %get-tuple-element.44), channel_id=1, source_target_pairs={{0,1},{1,0},{2,3},{3,2},{4,5},{5,4},{6,7},{7,6},{8,9},{9,8},{10,11... | collective-permute-start | bytes 27656 | tf_op jit(solution)/shard_map/ppermute | solution.py:409

commit v13 on v12

--- a/solution.py
+++ b/solution.py
@@ -144,22 +144,26 @@
     return density, momentum, kept, swapped
 
 
-def exchange(density, momentum, kept, swapped, solid, carried):
+def pull(solid, carried):
     inverse = 1.0 / (1.0 + solid)
     share = solid * inverse
     speed = [c * inverse for c in carried]
     base = 1.0 - 1.5 * total_of([v * v for v in speed])
-    push = [(density * v - m) * inverse for v, m in zip(speed, momentum)]
-    post = [None] * 27
+    pulled = [None] * 27
     for i in range(13, 27):
-        scale = WEIGHT[i] * density
+        scale = WEIGHT[i] * share
         if i == 13:
-            post[i] = kept[i] + share * (swapped[i] + scale * base)
+            pulled[i] = scale * base
             continue
         dot = along(speed, i)
         even, odd = scale * (base + 4.5 * dot * dot), scale * (3.0 * dot)
-        post[i] = kept[i] + share * (swapped[i] + (even + odd))
-        post[26 - i] = kept[26 - i] + share * (swapped[26 - i] + (even - odd))
+        pulled[i], pulled[26 - i] = even + odd, even - odd
+    return share, inverse, [v * inverse for v in speed], pulled
+
+
+def exchange(density, momentum, kept, swapped, share, inverse, drag, pulled):
+    push = [density * d - m * inverse for d, m in zip(drag, momentum)]
+    post = [kept[i] + (share * swapped[i] + density * pulled[i]) for i in range(27)]
     return post, push
 
 
@@ -249,7 +253,7 @@
     held_ref[...] = jnp.dot(jnp.concatenate(gather, axis=1), slot_rows, preferred_element_type=f32)
     for z in range(depth):
         relaxed = relax([fields_ref[i, z] for i in range(27)], rate)
-        post, push = exchange(*relaxed, *grains_at(held_ref, z, depth, length))
+        post, push = exchange(*relaxed, *pull(*grains_at(held_ref, z, depth, length)))
         for i in range(27):
             post_ref[i, z] = post[i]
         for k in range(3):
@@ -258,7 +262,12 @@
     store_faces(post_ref, near_ref, far_ref)
 
 
-def turn_kernel(slot_ref, dest_ref, rank_ref, turned_ref, hot_ref, at_rank_ref):
+def turn_kernel(slot_ref, dest_ref, rank_ref, held_ref, turned_ref, hot_ref, at_rank_ref, pulled_ref):
+    _, depth, length, _ = pulled_ref.shape
+    for z in range(depth):
+        share, inverse, drag, pulled = pull(*grains_at(held_ref, z, depth, length))
+        for n, value in enumerate(pulled + [share, inverse] + drag):
+            pulled_ref[n, z] = value
     turned_ref[...] = slot_ref[...].astype(f32).T.astype(bf16)
     devices = hot_ref.shape[0] // 2
     hot_ref[...] = jnp.where(iota(hot_ref.shape, 0) % devices == dest_ref[...], 1.0, 0.0).astype(bf16)
@@ -305,7 +314,7 @@
 
 def second_kernel(
     capacity, rates_ref, post_ref, outer_ref, inner_ref, far_ref, near_ref, far_rows_ref, near_rows_ref,
-    held_ref, push_ref, line_ref, turned_ref,
+    pulled_ref, push_ref, line_ref, turned_ref,
     next_ref, next_near_ref, next_far_ref, next_inner_ref, next_outer_ref, back_ref,
 ):
     depth, length, width = post_ref.shape[1:]
@@ -321,7 +330,13 @@
     pushes = []
     for z in range(depth):
         relaxed = relax(streamed(post_ref, *halo, z, corner), rate)
-        post, push = exchange(*relaxed, *grains_at(held_ref, z, depth, length))
+        post, push = exchange(
+            *relaxed,
+            pulled_ref[27, z],
+            pulled_ref[28, z],
+            [pulled_ref[29 + k, z] for k in range(3)],
+            [pulled_ref[i, z] for i in range(27)],
+        )
         for i in range(27):
             next_ref[i, z] = post[i]
         pushes.append(push)
@@ -452,10 +467,10 @@
     )
     outer, inner = swap_outer(outer), swap_inner(inner)
     near, far = swap_faces(near, far)
-    turned, hot, at_rank = call(
+    turned, hot, at_rank, pulled = call(
         turn_kernel,
-        [shape((width, slots), bf16), shape((2 * devices, grains), bf16), shape((capacity, grains), f32)],
-        slot_rows, dest, rank,
+        [shape((width, slots), bf16), shape((2 * devices, grains), bf16), shape((capacity, grains), f32), shape((32, depth, length, width), f32)],
+        slot_rows, dest, rank, held,
     )
     corners = shape((6, width), f32)
     far_rows, near_rows = call(
@@ -465,7 +480,7 @@
     post, next_near, next_far, inner, outer, back = call(
         functools.partial(second_kernel, capacity),
         [state, face, face, ends, ends, shape((4 * devices, LANES), f32)],
-        rates, post, outer, inner, far, near, far_rows, near_rows, held, push, slot_line, turned,
+        rates, post, outer, inner, far, near, far_rows, near_rows, pulled, push, slot_line, turned,
     )
     back = lax.all_to_all(
         back.reshape(devices, 4, LANES), both, split_axis=0, concat_axis=0, tiled=True

time: 41.6 us -> 41.6 us (level)
  no operation moved by 1% of the time
where the time goes in v13:
time: 41.6 us; the launch traced here: 41.4 us
  blocking collectives  18.2 us (44%)
  starting transfers between devices  12.9 us (31%)
  waiting for transfers between devices  5.52 us (13%)
  Pallas kernels  3.3 us (8%)
  between operations  0.77 us (2%)
  local copies, waits for them, and re-layouts  0.73 us (2%)
    all_to_all x1, blocking collectives, per_device(): lax.all_to_all(send.reshape(devices, capacity // 2 + 1, 2, width), both,...  18.2 us
    ppermute x6, starting transfers between devices, swap_faces(): received.append(lax.ppermute(face, ('gz', 'gx'), pairs))  5.81 us
    ppermute x2, starting transfers between devices, swap_outer(): return lax.ppermute(outer, 'gx', pairs)  4.48 us
    ppermute x2, waiting for transfers between devices, swap_outer(): return lax.ppermute(outer, 'gx', pairs)  3.43 us
    pallas_call x9, Pallas kernels, call(): pl.pallas_call(kernel, out_shape=list(outs), in_specs=[pl.BlockSpec(memor...  3.3 us
    all_to_all x1, starting transfers between devices, per_device(): lax.all_to_all(back.reshape(devices, 4, LANES), both, split_axis=0, conca...  2.57 us
    ppermute x6, waiting for transfers between devices, swap_faces(): received.append(lax.ppermute(face, ('gz', 'gx'), pairs))  1.53 us
  transfers between devices with their start and end apart: 11, of which 4 were waited for; matrix products, arithmetic and copies ran while one was open for 0% of the time, Pallas kernels for 1%

profile of v13, /device:TPU:0, one launch (start us, length us, event | category | flops | bytes accessed | tf_op | source)
XLA Modules:
  0.0 41.4 jit_solution(8244185448098643254)
XLA Ops:
  0.7 0.0 copy-start.4
  0.7 0.0 copy-start.2
  0.7 0.0 copy-start.5
  0.7 0.6 %copy-done.3 = bf16[3,512]{1,0:T(4,128)(2,1)S(1)} copy-done((bf16[3,512]{1,0:T(4,128)(2,1)S(1)}, bf16[3,512]{1,0:T(4,128)(2,1)}, u32[]{:S(2)}) %copy-start.3) | copy-done | bytes 3096
  1.3 0.1 copy-done.4
  1.4 0.0 copy-done.2
  1.4 0.2 shard_map.78
  1.6 0.5 %shard_map.79 = bf16[1088,128]{1,0:T(8,128)(2,1)S(1)} custom-call(s32[1,512]{1,0:T(1,128)S(1)} %bitcast.11, s32[1,512]{1,0:T(1,128)S(1)} %get-tuple-element.27.rank_ref, f32[4,512]{1,0:T(4,128)S(1)} %get-tuple-element.28.facts_ref, bf16[512,128]{1,0:T(8,128)(2,1)S(1)} %copy-done.1), custom_call_target="tpu_custom_call" | custom-call | bytes 421888 | tf_op jit(solution)/shard_map/pallas_call | solution.py:27
  2.1 0.0 copy-start
  2.1 18.2 %all_to_all.10 = bf16[32,17,2,128]{3,2,1,0:T(2,128)(2,1)S(1)} all-to-all(bf16[32,17,2,128]{3,2,1,0:T(2,128)(2,1)S(1)} %bitcast.8), channel_id=1, replica_groups=mesh['gz'=4,'gx'=8] {'gz','gx'}, dimensions={0} | all-to-all | bytes 557056 | tf_op jit(solution)/shard_map/all_to_all | solution.py:455
  20.3 0.4 shard_map.80
  20.7 0.9 %collective-permute-start = (f32[18,128]{1,0:T(8,128)S(1)}, f32[18,128]{1,0:T(8,128)S(1)}, u32[]{:S(2)}, u32[]{:S(2)}) collective-permute-start(f32[18,128]{1,0:T(8,128)S(1)} %get-tuple-element.30), channel_id=1, source_target_pairs={{0,7},{1,2},{2,1},{3,4},{4,3},{5,6},{6,5},{7,0},{8,15},{9,10},{10,... | collective-permute-start | bytes 27656 | tf_op jit(solution)/shard_map/ppermute | solution.py:430
  21.6 0.5 %collective-permute-start.2 = (f32[9,8,128]{2,1,0:T(8,128)S(1)}, f32[9,8,128]{2,1,0:T(8,128)S(1)}, u32[]{:S(2)}, u32[]{:S(2)}) collective-permute-start(f32[9,8,128]{2,1,0:T(8,128)S(1)} %get-tuple-element.32), channel_id=1, source_target_pairs={{0,1},{1,0},{2,3},{3,2},{4,5},{5,4},{6,7},{7,6},{8,16},{9,17},{10,... | collective-permute-start | bytes 110600 | tf_op jit(solution)/shard_map/ppermute | solution.py:419
  22.1 1.5 %collective-permute-start.3 = (f32[9,8,128]{2,1,0:T(8,128)S(1)}, f32[9,8,128]{2,1,0:T(8,128)S(1)}, u32[]{:S(2)}, u32[]{:S(2)}) collective-permute-start(f32[9,8,128]{2,1,0:T(8,128)S(1)} %get-tuple-element.33), channel_id=1, source_target_pairs={{0,8},{1,9},{2,10},{3,11},{4,12},{5,13},{6,14},{7,15},{8,0},{9,1},... | collective-permute-start | bytes 110600 | tf_op jit(solution)/shard_map/ppermute | solution.py:419
  23.6 2.0 %collective-permute-done.outer_ref = f32[18,128]{1,0:T(8,128)S(1)} collective-permute-done((f32[18,128]{1,0:T(8,128)S(1)}, f32[18,128]{1,0:T(8,128)S(1)}, u32[]{:S(2)}, u32[]{:S(2)}) %collective-permute-start) | collective-permute-done | bytes 9248 | tf_op jit(solution)/shard_map/ppermute | solution.py:430
  25.7 0.1 collective-permute-start.4
  25.8 2.0 %collective-permute-start.5 = (f32[6,128]{1,0:T(8,128)S(1)}, f32[6,128]{1,0:T(8,128)S(1)}, u32[]{:S(2)}, u32[]{:S(2)}) collective-permute-start(f32[6,128]{1,0:T(8,128)S(1)} %get-tuple-element.35), channel_id=1, source_target_pairs={{0,8},{1,9},{2,10},{3,11},{4,12},{5,13},{6,14},{7,15},{8,0},{9,1},... | collective-permute-start | bytes 9224 | tf_op jit(solution)/shard_map/ppermute | solution.py:419
  27.7 0.2 shard_map.82
  27.9 0.0 collective-permute-done.4.far_rows_ref
  27.9 1.5 %collective-permute-done.5.near_rows_ref = f32[6,128]{1,0:T(8,128)S(1)} collective-permute-done((f32[6,128]{1,0:T(8,128)S(1)}, f32[6,128]{1,0:T(8,128)S(1)}, u32[]{:S(2)}, u32[]{:S(2)}) %collective-permute-start.5) | collective-permute-done | bytes 3104 | tf_op jit(solution)/shard_map/ppermute | solution.py:419
  29.4 0.0 collective-permute-done.2.far_ref
  29.4 0.0 collective-permute-done.3.near_ref
  29.4 1.2 %shard_map.83 = (f32[27,2,8,128]{3,2,1,0:T(8,128)S(1)}, f32[9,8,128]{2,1,0:T(8,128)S(1)}, f32[9,8,128]{2,1,0:T(8,128)S(1)}, f32[18,128]{1,0:T(8,128)S(1)}, f32[18,128]{1,0:T(8,128)S(1)}, /*index=5*/f32[128,128]{1,0:T(8,128)}) custom-call(f32[1,27]{1,0:T(1,128)S(1)} %get-tuple-element.26.rates_ref, f32[27,2,8,128]{3,2,1,0:T(8,128)S(1)} %get-tuple-element.29.post_ref, ...), custom_call_target="tpu_custom_call" | custom-call | bytes 1251436 | tf_op jit(solution)/shard_map/pallas_call | solution.py:27
  30.6 2.6 %all-to-all-start.1 = ((f32[32,4,128]{2,1,0:T(4,128)}), f32[32,4,128]{2,1,0:T(4,128)S(1)}, u32[]{:S(2)}, u32[]{:S(2)}) async-start(f32[32,4,128]{2,1,0:T(4,128)} %bitcast.5), calls=%async_computation.1 | async-start | bytes 131072 | tf_op jit(solution)/shard_map/all_to_all | solution.py:485
  33.2 1.7 %collective-permute-start.6 = (f32[9,8,128]{2,1,0:T(8,128)S(1)}, f32[9,8,128]{2,1,0:T(8,128)S(1)}, u32[]{:S(2)}, u32[]{:S(2)}) collective-permute-start(f32[9,8,128]{2,1,0:T(8,128)S(1)} %get-tuple-element.43), channel_id=1, source_target_pairs={{0,8},{1,9},{2,10},{3,11},{4,12},{5,13},{6,14},{7,15},{8,0},{9,1},... | collective-permute-start | bytes 110600 | tf_op jit(solution)/shard_map/ppermute | solution.py:419
  34.9 0.0 collective-permute-start.7
  34.9 3.5 %collective-permute-start.8 = (f32[18,128]{1,0:T(8,128)S(1)}, f32[18,128]{1,0:T(8,128)S(1)}, u32[]{:S(2)}, u32[]{:S(2)}) collective-permute-start(f32[18,128]{1,0:T(8,128)S(1)} %get-tuple-element.45), channel_id=1, source_target_pairs={{0,7},{1,2},{2,1},{3,4},{4,3},{5,6},{6,5},{7,0},{8,15},{9,10},{10,... | collective-permute-start | bytes 27656 | tf_op jit(solution)/shard_map/ppermute | solution.py:430
  38.5 1.4 %collective-permute-done.8.outer_ref = f32[18,128]{1,0:T(8,128)S(1)} collective-permute-done((f32[18,128]{1,0:T(8,128)S(1)}, f32[18,128]{1,0:T(8,128)S(1)}, u32[]{:S(2)}, u32[]{:S(2)}) %collective-permute-start.8) | collective-permute-done | bytes 9248 | tf_op jit(solution)/shard_map/ppermute | solution.py:430
  39.9 0.0 collective-permute-done.9.inner_ref
  39.9 0.1 shard_map.84.staged_ref
  40.0 0.6 %all-to-all-done.1 = f32[32,4,128]{2,1,0:T(4,128)S(1)} async-done(((f32[32,4,128]{2,1,0:T(4,128)}), f32[32,4,128]{2,1,0:T(4,128)S(1)}, u32[]{:S(2)}, u32[]{:S(2)}) %all-to-all-start.1) | async-done | bytes 65568 | tf_op jit(solution)/shard_map/all_to_all | solution.py:485
  40.6 0.8 %shard_map.85 = (f32[27,2,8,128]{3,2,1,0:T(8,128)}, f32[3,512]{1,0:T(4,128)}) custom-call(f32[27,2,8,128]{3,2,1,0:T(8,128)S(1)} %shard_map.84.staged_ref, f32[128,128]{1,0:T(8,128)S(1)} %bitcast.9, bf16[64,512]{1,0:T(8,128)(2,1)S(1)} %get-tuple-element.48.hot_ref, f32[32,512]{1,0:T(8,128)S(1)} %get-tuple-element.49.at_rank_ref), custom_call_target="tpu_custom_call" | custom-call | bytes 645120 | tf_op jit(solution)/shard_map/pallas_call | solution.py:27
  (12 shorter events, 0.0 us)
Async XLA Ops:
  0.6 0.7 %copy-start.3 = (bf16[3,512]{1,0:T(4,128)(2,1)S(1)}, bf16[3,512]{1,0:T(4,128)(2,1)}, u32[]{:S(2)}) copy-start(bf16[3,512]{1,0:T(4,128)(2,1)} %speed_ref.1) | copy-start | bytes 9220
  0.6 0.9 %copy-start.1 = (bf16[512,128]{1,0:T(8,128)(2,1)S(1)}, bf16[512,128]{1,0:T(8,128)(2,1)}, u32[]{:S(2)}) copy-start(bf16[512,128]{1,0:T(8,128)(2,1)} %fraction_ref.1) | copy-start | bytes 393220
  0.7 0.7 %copy-start.4 = (s32[512]{0:T(512)S(1)}, s32[512]{0:T(512)}, u32[]{:S(2)}) copy-start(s32[512]{0:T(512)} %param.11) | copy-start | bytes 6148
  0.7 0.7 %copy-start.2 = (s32[512,1]{0,1:T(1,128)S(1)}, s32[512,1]{0,1:T(1,128)}, u32[]{:S(2)}) copy-start(s32[512,1]{0,1:T(1,128)} %param.10) | copy-start | bytes 6148
  0.7 0.7 %copy-start.5 = (f32[27]{0:T(128)S(1)}, f32[27]{0:T(128)}, u32[]{:S(2)}) copy-start(f32[27]{0:T(128)} %param.7) | copy-start | bytes 328
  2.1 18.2 %copy-start = (f32[27,2,8,128]{3,2,1,0:T(8,128)S(1)}, f32[27,2,8,128]{3,2,1,0:T(8,128)}, u32[]{:S(2)}) copy-start(f32[27,2,8,128]{3,2,1,0:T(8,128)} %fields_ref.1) | copy-start | bytes 663556
  20.7 5.0 %collective-permute-start = (f32[18,128]{1,0:T(8,128)S(1)}, f32[18,128]{1,0:T(8,128)S(1)}, u32[]{:S(2)}, u32[]{:S(2)}) collective-permute-start(f32[18,128]{1,0:T(8,128)S(1)} %get-tuple-element.30), channel_id=1, source_target_pairs={{0,7},{1,2},{2,1},{3,4},{4,3},{5,6},{6,5},{7,0},{8,15},{9,10},{10,... | collective-permute-start | bytes 27656 | tf_op jit(solution)/shard_map/ppermute | solution.py:430
  21.6 4.1 %collective-permute-start.1 = (f32[18,128]{1,0:T(8,128)S(1)}, f32[18,128]{1,0:T(8,128)S(1)}, u32[]{:S(2)}, u32[]{:S(2)}) collective-permute-start(f32[18,128]{1,0:T(8,128)S(1)} %get-tuple-element.31), channel_id=1, source_target_pairs={{0,1},{1,0},{2,3},{3,2},{4,5},{5,4},{6,7},{7,6},{8,9},{9,8},{10,11... | collective-permute-start | bytes 27656 | tf_op jit(solution)/shard_map/ppermute | solution.py:424
  21.6 7.8 %collective-permute-start.2 = (f32[9,8,128]{2,1,0:T(8,128)S(1)}, f32[9,8,128]{2,1,0:T(8,128)S(1)}, u32[]{:S(2)}, u32[]{:S(2)}) collective-permute-start(f32[9,8,128]{2,1,0:T(8,128)S(1)} %get-tuple-element.32), channel_id=1, source_target_pairs={{0,1},{1,0},{2,3},{3,2},{4,5},{5,4},{6,7},{7,6},{8,16},{9,17},{10,... | collective-permute-start | bytes 110600 | tf_op jit(solution)/shard_map/ppermute | solution.py:419
  22.1 7.3 %collective-permute-start.3 = (f32[9,8,128]{2,1,0:T(8,128)S(1)}, f32[9,8,128]{2,1,0:T(8,128)S(1)}, u32[]{:S(2)}, u32[]{:S(2)}) collective-permute-start(f32[9,8,128]{2,1,0:T(8,128)S(1)} %get-tuple-element.33), channel_id=1, source_target_pairs={{0,8},{1,9},{2,10},{3,11},{4,12},{5,13},{6,14},{7,15},{8,0},{9,1},... | collective-permute-start | bytes 110600 | tf_op jit(solution)/shard_map/ppermute | solution.py:419
  25.7 2.2 %collective-permute-start.4 = (f32[6,128]{1,0:T(8,128)S(1)}, f32[6,128]{1,0:T(8,128)S(1)}, u32[]{:S(2)}, u32[]{:S(2)}) collective-permute-start(f32[6,128]{1,0:T(8,128)S(1)} %get-tuple-element.34), channel_id=1, source_target_pairs={{0,1},{1,0},{2,3},{3,2},{4,5},{5,4},{6,7},{7,6},{8,16},{9,17},{10,... | collective-permute-start | bytes 9224 | tf_op jit(solution)/shard_map/ppermute | solution.py:419
  25.8 3.7 %collective-permute-start.5 = (f32[6,128]{1,0:T(8,128)S(1)}, f32[6,128]{1,0:T(8,128)S(1)}, u32[]{:S(2)}, u32[]{:S(2)}) collective-permute-start(f32[6,128]{1,0:T(8,128)S(1)} %get-tuple-element.35), channel_id=1, source_target_pairs={{0,8},{1,9},{2,10},{3,11},{4,12},{5,13},{6,14},{7,15},{8,0},{9,1},... | collective-permute-start | bytes 9224 | tf_op jit(solution)/shard_map/ppermute | solution.py:419
  30.6 10.0 %all-to-all-start.1 = ((f32[32,4,128]{2,1,0:T(4,128)}), f32[32,4,128]{2,1,0:T(4,128)S(1)}, u32[]{:S(2)}, u32[]{:S(2)}) async-start(f32[32,4,128]{2,1,0:T(4,128)} %bitcast.5), calls=%async_computation.1 | async-start | bytes 131072 | tf_op jit(solution)/shard_map/all_to_all | solution.py:485
  33.2 6.7 %collective-permute-start.6 = (f32[9,8,128]{2,1,0:T(8,128)S(1)}, f32[9,8,128]{2,1,0:T(8,128)S(1)}, u32[]{:S(2)}, u32[]{:S(2)}) collective-permute-start(f32[9,8,128]{2,1,0:T(8,128)S(1)} %get-tuple-element.43), channel_id=1, source_target_pairs={{0,8},{1,9},{2,10},{3,11},{4,12},{5,13},{6,14},{7,15},{8,0},{9,1},... | collective-permute-start | bytes 110600 | tf_op jit(solution)/shard_map/ppermute | solution.py:419
  34.9 5.0 %collective-permute-start.7 = (f32[9,8,128]{2,1,0:T(8,128)S(1)}, f32[9,8,128]{2,1,0:T(8,128)S(1)}, u32[]{:S(2)}, u32[]{:S(2)}) collective-permute-start(f32[9,8,128]{2,1,0:T(8,128)S(1)} %get-tuple-element.44), channel_id=1, source_target_pairs={{0,1},{1,0},{2,3},{3,2},{4,5},{5,4},{6,7},{7,6},{8,16},{9,17},{10,... | collective-permute-start | bytes 110600 | tf_op jit(solution)/shard_map/ppermute | solution.py:419
  34.9 5.0 %collective-permute-start.8 = (f32[18,128]{1,0:T(8,128)S(1)}, f32[18,128]{1,0:T(8,128)S(1)}, u32[]{:S(2)}, u32[]{:S(2)}) collective-permute-start(f32[18,128]{1,0:T(8,128)S(1)} %get-tuple-element.45), channel_id=1, source_target_pairs={{0,7},{1,2},{2,1},{3,4},{4,3},{5,6},{6,5},{7,0},{8,15},{9,10},{10,... | collective-permute-start | bytes 27656 | tf_op jit(solution)/shard_map/ppermute | solution.py:430
  38.5 1.4 %collective-permute-start.9 = (f32[18,128]{1,0:T(8,128)S(1)}, f32[18,128]{1,0:T(8,128)S(1)}, u32[]{:S(2)}, u32[]{:S(2)}) collective-permute-start(f32[18,128]{1,0:T(8,128)S(1)} %get-tuple-element.46), channel_id=1, source_target_pairs={{0,1},{1,0},{2,3},{3,2},{4,5},{5,4},{6,7},{7,6},{8,9},{9,8},{10,11... | collective-permute-start | bytes 27656 | tf_op jit(solution)/shard_map/ppermute | solution.py:424
